TPU v7x, 256 devices: a whole 4x4x8 slice. The times are simulated.
256 devices in a mesh: dp: 32 (over z_hi, x, core), fsdp: 8 (over y, z_lo).
Axes of the slice: x: 4, y: 4, z: 8 (z_hi: 4, z_lo: 2; z = z_hi * 2 + z_lo), core: 2. Of those that a mesh axis runs over, the one named last changes fastest.
Arguments:
- waveform_rows: bfloat16 [32768, 1024], P(('dp', 'fsdp')), may hold values from -6 to 6
- conv_weight: bfloat16 [1024, 512], P('fsdp'), may hold values from -0.1875 to 0.1875
- proj_weight: bfloat16 [512, 1280], P('fsdp'), may hold values from -0.25 to 0.25
- ffn_pair: bfloat16 [2560, 2, 1280], P('fsdp', None, 'dp'), may hold values from -0.15625 to 0.15625
- owner: int32 [32768, 1], P(('dp', 'fsdp')), may hold values from 0 to 31; in each aligned block of 128 rows (0 to 127, 128 to 255, ...) at most 6 rows name the same one
- frame_live: int32 [32768], P(('dp', 'fsdp')), may hold values 0 or 1
- cotangent: bfloat16 [49152, 1280], P(('dp', 'fsdp')), may hold values from -0.125 to 0.125
Outputs:
- encoded: bfloat16 [49152, 1280], P(('dp', 'fsdp'))
- grad_pair: float32 [2560, 2, 1280], P('fsdp', None, 'dp')
Inputs may be any that keep to these rules, and one draw needn't show every extreme that they name: In the rows of one device no owner is named more than 6 times, a bound that some block reaches.
All inputs are finite; a program needn't handle non-finite values. No bound on the sum of `frame_live` on one device may be relied on, other than what follows from the above.
Results may differ from a plain program's by a relative error of at most 0.038.
Values may be sent and summed in bfloat16 or wider, within the bound.
No kernel may reach another device: no remote copies, remote signals or barrier semaphores. Data moves between devices by JAX's collectives and lax.ppermute only.
A program may use at most 192 MiB of HBM per device.

v0:
```python
import jax
import jax.numpy as jnp
from jax import lax
from jax.sharding import PartitionSpec as P

epsilon = 1e-05


def gelu_exact(values):
    return jax.nn.gelu(values, approximate=False)


def gelu_slope(values):
    cumulative = 0.5 * (1.0 + lax.erf(values * 0.7071067811865476))
    density = jnp.exp(-0.5 * values * values) * 0.3989422804014327
    return cumulative + values * density


def normalize(values):
    mean_value = jnp.mean(values, axis=-1, keepdims=True)
    centered = values - mean_value
    variance = jnp.mean(centered * centered, axis=-1, keepdims=True)
    return centered * lax.rsqrt(variance + epsilon)


def front_end(row_block, conv_full):
    conv_out = jnp.dot(row_block, conv_full, preferred_element_type=jnp.float32)
    return normalize(gelu_exact(conv_out)).astype(jnp.bfloat16)


def per_device(waveform_rows, conv_weight, proj_weight, ffn_pair, owner, frame_live, cotangent):
    dp_size = lax.axis_size("dp")
    slots = cotangent.shape[0]
    capacity = slots // dp_size
    conv_full, proj_full, pair_units = (
        lax.all_gather(conv_weight, "fsdp", axis=0, tiled=True),
        lax.all_gather(proj_weight, "fsdp", axis=0, tiled=True),
        lax.all_gather(ffn_pair, "fsdp", axis=0, tiled=True),
    )
    pair_full = lax.all_gather(pair_units, "dp", axis=2, tiled=True)
    target = owner[:, 0]
    onehot = (target[:, None] == jnp.arange(dp_size, dtype=jnp.int32)[None, :]).astype(jnp.int32)
    before = jnp.cumsum(onehot, axis=0) - onehot
    position = jnp.sum(before * onehot, axis=1)
    slot_index = target * capacity + position
    matches = slot_index[None, :] == jnp.arange(slots, dtype=jnp.int32)[:, None]
    placement = matches.astype(jnp.bfloat16)
    outgoing_flags = jnp.sum(jnp.where(matches, (1 + frame_live)[None, :], 0), axis=1)
    outgoing_flags = outgoing_flags.reshape(dp_size, capacity)
    outgoing = jnp.dot(placement, waveform_rows, preferred_element_type=jnp.float32).astype(
        jnp.bfloat16
    )
    outgoing = outgoing.reshape(dp_size, capacity, waveform_rows.shape[1])
    incoming, slot_flags = (
        lax.all_to_all(outgoing, "dp", split_axis=0, concat_axis=0, tiled=True),
        lax.all_to_all(outgoing_flags, "dp", split_axis=0, concat_axis=0, tiled=True),
    )
    features = front_end(incoming.reshape(slots, waveform_rows.shape[1]), conv_full)
    slot_flags = slot_flags.reshape(slots)
    up_rows = pair_full[:, 0, :]
    down_rows = pair_full[:, 1, :]
    stream = jnp.dot(features, proj_full, preferred_element_type=jnp.float32).astype(jnp.bfloat16)
    stream_wide = stream.astype(jnp.float32)
    normed = normalize(stream_wide).astype(jnp.bfloat16)
    contract_last = (((1,), (1,)), ((), ()))
    hidden_pre = lax.dot_general(normed, up_rows, contract_last, preferred_element_type=jnp.float32)
    hidden = gelu_exact(hidden_pre).astype(jnp.bfloat16)
    mixed = stream_wide + jnp.dot(hidden, down_rows, preferred_element_type=jnp.float32)
    occupied = (slot_flags > 0).astype(jnp.float32)
    encoded = (mixed * occupied[:, None]).astype(jnp.bfloat16)
    live_mask = (slot_flags == 2).astype(jnp.bfloat16)
    grad_out = cotangent * live_mask[:, None]
    grad_hidden = lax.dot_general(
        grad_out, down_rows, contract_last, preferred_element_type=jnp.float32
    )
    grad_pre = (grad_hidden * gelu_slope(hidden_pre)).astype(jnp.bfloat16)
    contract_first = (((0,), (0,)), ((), ()))
    up_term = lax.dot_general(grad_pre, normed, contract_first, preferred_element_type=jnp.float32)
    down_term = lax.dot_general(
        hidden, grad_out, contract_first, preferred_element_type=jnp.float32
    )
    group_sums = lax.psum_scatter(
        jnp.stack([up_term, down_term], axis=1).astype(jnp.bfloat16),
        "fsdp",
        scatter_dimension=0,
        tiled=True,
    )
    grad_pair = lax.psum_scatter(group_sums, "dp", scatter_dimension=2, tiled=True).astype(
        jnp.float32
    )
    return (encoded, grad_pair)


def solution(mesh):
    return jax.shard_map(
        per_device,
        mesh=mesh,
        in_specs=(
            P(("dp", "fsdp"), None),
            P("fsdp", None),
            P("fsdp", None),
            P("fsdp", None, "dp"),
            P(("dp", "fsdp"), None),
            P(("dp", "fsdp")),
            P(("dp", "fsdp"), None),
        ),
        out_specs=(P(("dp", "fsdp"), None), P("fsdp", None, "dp")),
        check_vma=False,
    )
```

profile of v0, /device:TPU:2, one launch (start us, length us, event | category | flops | bytes accessed | tf_op | source)
XLA Modules:
  0.0 890.9 jit_solution(2477698793832742333)
XLA Ops:
  7.2 0.0 copy-start
  7.2 0.0 all-gather.4.cloned.1.call-start
  7.2 0.7 all-gather.4.cloned.1.call-update
  7.9 0.0 copy-start.2
  7.9 0.0 all-gather.6.cloned.1.call-start
  8.0 0.7 all-gather.6.cloned.1.call-update
  8.7 0.0 all-gather.8.cloned.1.call-start
  8.7 1.0 copy.27
  9.7 0.0 copy-start.3
  9.7 48.5 %all_gather.14 = bf16[2560,2,40]{2,1,0:T(2,128)(2,1)S(1)} all-gather(bf16[320,2,40]{2,1,0:T(2,128)(2,1)S(1)} %copy.27), channel_id=1, replica_groups=mesh['dp'=32,'fsdp'=8] {'fsdp'}, dimensions={0}, use_global_device_ids=true | all-gather | bytes 460800 | tf_op jit(solution)/shard_map/all_gather | solution.py:38
  58.2 2.4 copy.28
  60.6 0.0 all-gather.8.cloned.1.call-update
  60.7 0.0 copy-done.2
  60.7 0.1 fusion.57
  60.8 0.2 reduce_window_sum.11
  60.9 0.2 select_reduce_fusion.1
  61.1 0.0 copy-done.3
  61.1 0.1 select_reduce_fusion
  61.2 0.7 all_to_all.10
  62.0 11.1 %all-to-all-start.1 = ((s32[32,1,6]{2,1,0:T(1,128)}), s32[32,1,6]{2,1,0:T(1,128)S(1)}, u32[]{:S(2)}, u32[]{:S(2)}) async-start(s32[32,1,6]{2,1,0:T(1,128)} %bitcast.3), calls=%async_computation.1 | async-start | bytes 32768 | tf_op jit(solution)/shard_map/all_to_all | solution.py:56
  73.1 0.0 copy-done
  73.1 0.3 convolution_convert_fusion.3
  73.3 1.0 reshape.70
  74.3 7.3 all-to-all-done.1
  81.5 5.0 all-to-all-start
  86.6 0.2 reduce-scatter.2.cloned.1.call-start
  86.8 0.1 fusion.60
  86.9 0.1 reshape.73
  87.0 21.3 %all-to-all-done = bf16[32,6,1024]{2,1,0:T(8,128)(2,1)S(1)} async-done(((bf16[32,6,1024]{2,1,0:T(8,128)(2,1)}), bf16[32,6,1024]{2,1,0:T(8,128)(2,1)S(1)}, u32[]{:S(2)}, u32[]{:S(2)}) %all-to-all-start) | async-done | bytes 393248 | tf_op jit(solution)/shard_map/all_to_all | solution.py:55
  108.2 0.1 reshape.71
  108.4 0.0 all-gather.4.cloned.1.call-done
  108.4 2.5 fusion.66
  110.9 0.2 multiply_reduce_fusion.1
  111.1 8.1 all-gather.6.cloned.1.call-done
  119.2 1.9 fusion.69
  121.1 0.2 multiply_reduce_fusion
  121.4 92.7 %all-gather.8.cloned.1.call-done = bf16[2560,2,1280]{0,1,2:T(2,128)(2,1)} async-done(((bf16[2560,2,40]{0,1,2:T(2,128)(2,1)}), bf16[2560,2,1280]{0,1,2:T(2,128)(2,1)}) %all-gather.8.cloned.1.call-update) | async-done | bytes 13107216 | tf_op jit(solution)/shard_map/all_gather | solution.py:40
  214.1 25.6 %fusion.68 = (bf16[2560,1,1280]{0,1,2:T(2,128)(2,1)}, bf16[2560,1,1280]{0,1,2:T(2,128)(2,1)}) fusion(bf16[2560,2,1280]{0,1,2:T(2,128)(2,1)} %all-gather.8.cloned.1.call-done), kind=kLoop, calls=%fused_computation.94 | loop fusion | bytes 26214400 | tf_op jit(solution)/shard_map/slice | solution.py:61
  239.7 25.9 %copy.34 = bf16[2560,1,1280]{2,0,1:T(8,128)(2,1)} copy(bf16[2560,1,1280]{0,1,2:T(2,128)(2,1)} %get-tuple-element.17) | data formatting | bytes 13107200
  265.7 25.9 %copy.35 = bf16[2560,1,1280]{2,0,1:T(8,128)(2,1)} copy(bf16[2560,1,1280]{0,1,2:T(2,128)(2,1)} %get-tuple-element.16) | data formatting | bytes 13107200
  291.6 0.0 copy-start.4
  291.6 8.8 fusion.26
  300.4 0.0 copy-done.4
  300.4 4.6 fusion.1
  305.1 8.6 fusion
  313.7 10.9 %pad_maximum_fusion = bf16[2560,2,1280]{2,0,1:T(8,128)(2,1)} fusion(bf16[2560,1,1280]{2,0,1:T(8,128)(2,1)} %fusion.1, bf16[2560,1,1280]{2,0,1:T(8,128)(2,1)} %fusion), kind=kLoop, calls=%fused_computation | loop fusion | flops 6553600 | bytes 26214400 | tf_op jit(solution)/shard_map/stack | solution.py:83
  324.5 0.0 reduce-scatter.2.cloned.1.call-update
  324.6 0.0 copy-start.5
  324.6 0.0 all-reduce.3.cloned.1.call-start
  324.6 266.7 %reduce-scatter.2.cloned.1.call-done = bf16[320,2,1280]{2,0,1:T(8,128)(2,1)} async-done(((bf16[2560,2,1280]{2,0,1:T(8,128)(2,1)}), bf16[320,2,1280]{2,0,1:T(8,128)(2,1)}) %reduce-scatter.2.cloned.1.call-update) | async-done | bytes 1638416 | tf_op jit(solution)/shard_map/reduce_scatter | solution.py:82
  591.4 6.6 copy.32
  598.0 0.0 all-reduce.3.cloned.1.call-update
  598.0 0.0 copy-done.5
  598.0 0.6 dynamic-slice
  599.2 0.1 fusion.59
  599.3 0.1 reshape.72
  599.4 0.0 copy-start.1
  599.4 5.1 fusion.20
  604.5 278.3 %all-reduce.3.cloned.1.call-done = bf16[320,2,1280]{0,1,2:T(2,128)(2,1)} async-done(((bf16[320,2,1280]{0,1,2:T(2,128)(2,1)}), bf16[320,2,1280]{0,1,2:T(2,128)(2,1)}) %all-reduce.3.cloned.1.call-update) | async-done | bytes 1638416
  882.9 0.9 dynamic-slice_convert_fusion
  883.8 0.7 copy.33
  884.4 0.0 copy-done.1
  (5 shorter events, 0.0 us)
Async XLA Ops:
  7.2 65.9 %copy-start = (bf16[128,1024]{1,0:T(8,128)(2,1)S(1)}, bf16[128,1024]{1,0:T(8,128)(2,1)}, u32[]{:S(2)}) copy-start(bf16[128,1024]{1,0:T(8,128)(2,1)} %param.7) | copy-start | bytes 786436
  7.2 101.2 %all-gather.4.cloned.1.call-start = ((), (), s32[]{:S(2)}) async-start(), calls=%async_computation.3 | async-start | bytes 1179648 | tf_op jit(solution)/shard_map/all_gather | solution.py:36
  7.9 52.7 %copy-start.2 = (s32[128,1]{0,1:T(1,128)S(1)}, s32[128,1]{0,1:T(1,128)}, u32[]{:S(2)}) copy-start(s32[128,1]{0,1:T(1,128)} %param.11) | copy-start | bytes 1540
  7.9 111.3 %all-gather.6.cloned.1.call-start = ((), (), s32[]{:S(2)}) async-start(), calls=%async_computation.4 | async-start | bytes 1474560 | tf_op jit(solution)/shard_map/all_gather | solution.py:37
  8.7 205.4 %all-gather.8.cloned.1.call-start = ((), (), s32[]{:S(2)}) async-start(), calls=%async_computation.5 | async-start | bytes 13516800 | tf_op jit(solution)/shard_map/all_gather | solution.py:40
  9.7 51.4 %copy-start.3 = (s32[128]{0:T(128)S(1)}, s32[128]{0:T(128)}, u32[]{:S(2)}) copy-start(s32[128]{0:T(128)} %param.12) | copy-start | bytes 1540
  62.0 19.6 %all-to-all-start.1 = ((s32[32,1,6]{2,1,0:T(1,128)}), s32[32,1,6]{2,1,0:T(1,128)S(1)}, u32[]{:S(2)}, u32[]{:S(2)}) async-start(s32[32,1,6]{2,1,0:T(1,128)} %bitcast.3), calls=%async_computation.1 | async-start | bytes 32768 | tf_op jit(solution)/shard_map/all_to_all | solution.py:56
  81.5 26.7 %all-to-all-start = ((bf16[32,6,1024]{2,1,0:T(8,128)(2,1)}), bf16[32,6,1024]{2,1,0:T(8,128)(2,1)S(1)}, u32[]{:S(2)}, u32[]{:S(2)}) async-start(bf16[32,6,1024]{2,1,0:T(8,128)(2,1)} %reshape.70), calls=%async_computation | async-start | bytes 1048576 | tf_op jit(solution)/shard_map/all_to_all | solution.py:55
  86.6 504.8 %reduce-scatter.2.cloned.1.call-start = ((), (), s32[]{:S(2)}) async-start(), calls=%async_computation.6 | async-start | bytes 14745600 | tf_op jit(solution)/shard_map/reduce_scatter | solution.py:82
  291.6 8.8 copy-start.4
  324.6 273.4 %copy-start.5 = (u32[256]{0:T(256)S(1)}, u32[256]{0:T(256)}, u32[]{:S(2)}) copy-start(u32[256]{0:T(256)} %constant.20) | copy-start | bytes 3076
  324.6 558.3 %all-reduce.3.cloned.1.call-start = ((), (), s32[]{:S(2)}) async-start(), calls=%async_computation.7 | async-start | bytes 3932160
  599.4 285.0 %copy-start.1 = (bf16[128,1024]{1,0:T(8,128)(2,1)S(1)}, bf16[128,1024]{1,0:T(8,128)(2,1)}, u32[]{:S(2)}) copy-start(bf16[128,1024]{1,0:T(8,128)(2,1)} %param.7) | copy-start | bytes 786436
Sparse Core Ops, SparseCore 0:
  9.8 53.2 all-gather.3
  64.9 54.3 all-gather.5
  122.4 91.6 all-gather.7
  324.7 266.6 reduce-scatter.1
  598.1 284.7 all-reduce.2
where the time goes:
time: 898 us; the launch traced here: 891 us
  waiting for transfers between devices  676 us (75%)
  local copies, waits for them, and re-layouts  90.8 us (10%)
  blocking collectives  48.5 us (5%)
  matrix products  31.8 us (4%)
  starting transfers between devices  16.5 us (2%)
  between operations  14.6 us (2%)
  other arithmetic  12.9 us (1%)
    unnamed x6, waiting for transfers between devices  280 us
    reduce_scatter x1, waiting for transfers between devices, per_device(): lax.psum_scatter(jnp.stack([up_term, down_term], axis=1).astype(jnp.bfloa...  267 us
    all_gather x1, waiting for transfers between devices, per_device(): pair_full = lax.all_gather(pair_units, 'dp', axis=2, tiled=True)  92.7 us
    unnamed x17, local copies, waits for them, and re-layouts  54.1 us
    all_gather x1, blocking collectives, per_device(): lax.all_gather(ffn_pair, 'fsdp', axis=0, tiled=True)  48.5 us
    slice x1, local copies, waits for them, and re-layouts, per_device(): down_rows = pair_full[:, 1, :]  25.6 us
    all_to_all x1, waiting for transfers between devices, per_device(): lax.all_to_all(outgoing, 'dp', split_axis=0, concat_axis=0, tiled=True)  21.3 us
  transfers between devices with their start and end apart: 7, of which 6 were waited for; matrix products, arithmetic and copies ran while one was open for 2% of the time, Pallas kernels for 0%

commit v1 on v0

v1 whole, which is shorter than its diff:
```python
import jax
import jax.numpy as jnp
import numpy as np
from jax import lax
from jax.sharding import Mesh
from jax.sharding import PartitionSpec as P

epsilon = 1e-05
bf16 = jnp.bfloat16
f32 = jnp.float32

CAP = 6
PAD = 8


def gelu_exact(values):
    return jax.nn.gelu(values, approximate=False)


def gelu_slope(values):
    cumulative = 0.5 * (1.0 + lax.erf(values * 0.7071067811865476))
    density = jnp.exp(-0.5 * values * values) * 0.3989422804014327
    return cumulative + values * density


def normalize(values):
    mean_value = jnp.mean(values, axis=-1, keepdims=True)
    centered = values - mean_value
    variance = jnp.mean(centered * centered, axis=-1, keepdims=True)
    return centered * lax.rsqrt(variance + epsilon)


def gathered(values, axis, count):
    spread = jnp.broadcast_to(values[None], (count,) + values.shape)
    return lax.all_to_all(spread, axis, split_axis=0, concat_axis=0, tiled=True)


def dot(a, b, dims=((1,), (0,))):
    return lax.dot_general(a, b, (dims, ((), ())), preferred_element_type=f32)


def per_device(waveform_rows, conv_weight, proj_weight, ffn_pair, owner, frame_live, cotangent):
    n_dp = 32
    slots = n_dp * CAP
    dp = ("zh", "x", "c")
    fsdp = ("y", "zl")
    z = ("zh", "zl")
    local_pair = jnp.transpose(ffn_pair, (2, 1, 0)).reshape(40, 640)
    pair = lax.all_gather(local_pair, ("zh", "x", "c", "zl"), axis=0, tiled=True)
    cot_all = lax.all_gather(cotangent, "y", axis=0, tiled=True)

    target = owner[:, 0]
    onehot = (target[:, None] == jnp.arange(n_dp, dtype=jnp.int32)[None, :]).astype(jnp.int32)
    before = jnp.cumsum(onehot, axis=0) - onehot
    position = jnp.sum(before * onehot, axis=1)
    slot_index = target * PAD + position
    matches = slot_index[None, :] == jnp.arange(n_dp * PAD, dtype=jnp.int32)[:, None]
    outgoing = dot(matches.astype(bf16), waveform_rows).astype(bf16)
    flags = jnp.sum(jnp.where(matches, (1 + frame_live)[None, :], 0), axis=1).astype(bf16)
    flags = jnp.pad(flags.reshape(n_dp, 1, PAD), ((0, 0), (0, 0), (0, 1024 - PAD)))
    outgoing = jnp.concatenate(
        [outgoing.reshape(n_dp, PAD, 1024)[:, :CAP], flags, jnp.zeros_like(flags)], axis=1
    )
    incoming = lax.all_to_all(outgoing, dp, split_axis=0, concat_axis=0, tiled=True)
    conv_full = gathered(conv_weight, fsdp, 8).reshape(1024, 512)
    proj_full = gathered(proj_weight, fsdp, 8).reshape(512, 1280)

    slot_flags = incoming[:, CAP, :CAP].reshape(1, slots)
    rows = incoming[:, :CAP].reshape(slots, 1024)
    own_features = normalize(gelu_exact(dot(rows, conv_full))).astype(bf16)
    flag_rows = jnp.pad(slot_flags, ((0, 15), (0, 512 - slots)))
    block = jnp.concatenate([own_features, flag_rows], axis=0)
    blocks = gathered(block, "y", 4)
    features = blocks[:, :slots].reshape(4 * slots, 512)
    all_flags = blocks[:, slots, :slots].reshape(4 * slots)

    stream = dot(features, proj_full).astype(bf16)
    normed = normalize(stream.astype(f32)).astype(bf16)
    pair = pair.reshape(32, 2, 40, 2, 320)
    weights = jnp.transpose(pair, (3, 0, 2, 1, 4)).reshape(2, 1280, 640)
    up, down = weights[0], weights[1]
    hidden_pre = dot(normed, up)
    hidden = gelu_exact(hidden_pre).astype(bf16)
    partial = dot(hidden, down, ((1,), (1,))).reshape(4, slots, 1280)
    y = lax.axis_index("y")
    own = lax.dynamic_index_in_dim(partial, y, 0, keepdims=False)
    own = own + lax.dynamic_slice_in_dim(stream, y * slots, slots, 0).astype(f32)
    rest = partial.astype(bf16)
    for step in range(1, 4):
        piece = lax.dynamic_index_in_dim(rest, lax.rem(y + step, 4), 0, keepdims=False)
        arrived = lax.ppermute(piece, "y", [(k, (k + step) % 4) for k in range(4)])
        own = own + arrived.astype(f32)
    occupied = (slot_flags.reshape(slots) > 0).astype(f32)
    encoded = (own * occupied[:, None]).astype(bf16)

    live_mask = (all_flags == 2).astype(bf16)
    grad_out = cot_all * live_mask[:, None]
    grad_hidden = dot(grad_out, down)
    grad_pre = (grad_hidden * gelu_slope(hidden_pre)).astype(bf16)
    first = ((0,), (0,))
    up_term = dot(normed, grad_pre, first)
    down_term = dot(grad_out, hidden, first)
    terms = jnp.stack([up_term, down_term]).astype(bf16).reshape(2, 4, 4, 2, 40, 2, 320)
    terms = jnp.transpose(terms, (3, 2, 1, 5, 4, 0, 6)).reshape(2, 1280, 640)
    c = lax.axis_index("c")
    away = lax.dynamic_index_in_dim(terms, 1 - c, 0, keepdims=False)
    kept = lax.dynamic_index_in_dim(terms, c, 0, keepdims=False)
    arrived = lax.ppermute(away, "c", [(0, 1), (1, 0)])
    total = (kept.astype(f32) + arrived.astype(f32)).astype(bf16).reshape(4, 320, 640)
    total = lax.all_to_all(total, "x", split_axis=0, concat_axis=0, tiled=True)
    total = jnp.sum(total.astype(f32), axis=0).astype(bf16).reshape(8, 40, 640)
    total = lax.all_to_all(total, z, split_axis=0, concat_axis=0, tiled=True)
    total = jnp.sum(total.astype(f32), axis=0)
    grad_pair = jnp.transpose(total.reshape(40, 2, 320), (2, 1, 0))
    return (encoded, grad_pair)


def solution(mesh):
    names = ("zh", "x", "c", "y", "zl")
    fine = Mesh(np.asarray(mesh.devices).reshape(4, 4, 2, 4, 2), names)
    dp = ("zh", "x", "c")
    fsdp = ("y", "zl")
    everyone = dp + fsdp
    return jax.shard_map(
        per_device,
        mesh=fine,
        in_specs=(
            P(everyone, None),
            P(fsdp, None),
            P(fsdp, None),
            P(fsdp, None, dp),
            P(everyone, None),
            P(everyone),
            P(everyone, None),
        ),
        out_specs=(P(everyone, None), P(fsdp, None, dp)),
        check_vma=False,
    )
```

time: 898 us -> 390 us (0.43)
  waiting for transfers between devices: 676 us -> 184 us
  blocking collectives: 48.5 us -> 14 us
  starting transfers between devices: 16.5 us -> 37.6 us
  other arithmetic: 12.9 us -> 29.1 us
  local copies, waits for them, and re-layouts: 90.8 us -> 75.3 us
    unnamed x6 -> x2, waiting for transfers between devices: 280 us -> 0.71 us
    reduce_scatter x1 -> x0, waiting for transfers between devices: 267 us -> none  [per_device(): lax.psum_scatter(jnp.stack([up_term, down_term], axis=1).astype(jnp.bfloa...]
    unnamed x17 -> x21, local copies, waits for them, and re-layouts: 54.1 us -> 1.77 us
    all_gather x1 -> x0, blocking collectives: 48.5 us -> none  [per_device(): lax.all_gather(ffn_pair, 'fsdp', axis=0, tiled=True)]
    all_to_all x2 -> x5, waiting for transfers between devices: 28.5 us -> 66.2 us  [the longest x2 30.5 us: gathered(): return lax.all_to_all(spread, axis, split_axis=0, concat_axis=0, tiled=True)]
    another operation x0 -> x5, local copies, waits for them, and re-layouts: none -> 25.1 us  [the longest x4 25 us: per_device(): jnp.stack([up_term, down_term]).astype(bf16).reshape(2, 4, 4, 2, 40, 2, 320)]
    reshape x2 -> x5, local copies, waits for them, and re-layouts: 1.09 us -> 19.4 us  [the longest x1 9.62 us: per_device(): pair = pair.reshape(32, 2, 40, 2, 320)]
    all_to_all x2 -> x5, starting transfers between devices: 16.1 us -> 34.3 us  [the longest x1 11.6 us: per_device(): lax.all_to_all(outgoing, dp, split_axis=0, concat_axis=0, tiled=True)]
  transfers between devices with their start and end apart: 7 -> 11, of which waited for: 6 -> 9; matrix products, arithmetic and copies ran while one was open for 2% -> 15% of each run, Pallas kernels for 0% -> 0%
where the time goes in v1:
time: 390 us; the launch traced here: 384 us
  waiting for transfers between devices  184 us (47%)
  local copies, waits for them, and re-layouts  75.3 us (19%)
  starting transfers between devices  37.6 us (10%)
  matrix products  29.5 us (8%)
  other arithmetic  29.1 us (7%)
  between operations  14.7 us (4%)
  blocking collectives  14 us (4%)
    all_gather x1, waiting for transfers between devices, per_device(): lax.all_gather(local_pair, ('zh', 'x', 'c', 'zl'), axis=0, tiled=True)  108 us
    all_to_all x2, waiting for transfers between devices, gathered(): return lax.all_to_all(spread, axis, split_axis=0, concat_axis=0, tiled=True)  30.5 us
    dot_general x7, matrix products, dot(): return lax.dot_general(a, b, (dims, ((), ())), preferred_element_type=f32)  29.5 us
    another operation x4, local copies, waits for them, and re-layouts, per_device(): jnp.stack([up_term, down_term]).astype(bf16).reshape(2, 4, 4, 2, 40, 2, 320)  25 us
    all_to_all x1, waiting for transfers between devices, per_device(): lax.all_to_all(outgoing, dp, split_axis=0, concat_axis=0, tiled=True)  16 us
    slice x3, local copies, waits for them, and re-layouts, per_device(): up, down = (weights[0], weights[1])  15.4 us
    transpose x1, other arithmetic, per_device(): terms = jnp.transpose(terms, (3, 2, 1, 5, 4, 0, 6)).reshape(2, 1280, 640)  14.9 us
    all_to_all x1, blocking collectives, gathered(): return lax.all_to_all(spread, axis, split_axis=0, concat_axis=0, tiled=True)  14 us
  transfers between devices with their start and end apart: 11, of which 9 were waited for; matrix products, arithmetic and copies ran while one was open for 15% of the time, Pallas kernels for 0%

profile of v1, /device:TPU:2, one launch (start us, length us, event | category | flops | bytes accessed | tf_op | source)
XLA Modules:
  0.0 384.0 jit_solution(13348409572992079334)
XLA Ops:
  7.2 0.8 fusion.52
  8.0 0.2 reduce_window_sum.11
  8.2 0.8 select_reduce_fusion.1
  9.0 0.7 multiply_add_fusion
  9.7 0.1 select_reduce_fusion
  9.8 0.1 convert_element_type.127
  9.9 0.3 fusion.24
  10.3 1.0 fusion.39
  11.3 11.6 %all-to-all-start = ((bf16[32,8,1024]{2,1,0:T(8,128)(2,1)}), bf16[32,8,1024]{2,1,0:T(8,128)(2,1)S(1)}, u32[]{:S(2)}, u32[]{:S(2)}) async-start(bf16[32,8,1024]{2,1,0:T(8,128)(2,1)} %fusion.39), calls=%async_computation | async-start | bytes 1048576 | tf_op jit(solution)/shard_map/all_to_all | solution.py:64
  23.0 0.7 reshape.126
  23.8 16.0 %all-to-all-done = bf16[32,8,1024]{2,1,0:T(8,128)(2,1)S(1)} async-done(((bf16[32,8,1024]{2,1,0:T(8,128)(2,1)}), bf16[32,8,1024]{2,1,0:T(8,128)(2,1)S(1)}, u32[]{:S(2)}, u32[]{:S(2)}) %all-to-all-start) | async-done | bytes 524320 | tf_op jit(solution)/shard_map/all_to_all | solution.py:64
  39.8 1.1 broadcast_in_dim.23
  40.9 5.4 %all-to-all-start.1 = ((bf16[8,128,512]{2,1,0:T(8,128)(2,1)}), bf16[8,128,512]{2,1,0:T(8,128)(2,1)S(1)}, u32[]{:S(2)}, u32[]{:S(2)}) async-start(bf16[8,128,512]{2,1,0:T(8,128)(2,1)} %broadcast_in_dim.23), calls=%async_computation.1 | async-start | bytes 2097152 | tf_op jit(solution)/shard_map/all_to_all | solution.py:35
  46.3 0.1 reshape_squeeze.4
  46.5 0.1 reshape.122
  46.6 15.2 %all-to-all-done.1 = bf16[8,128,512]{2,1,0:T(8,128)(2,1)S(1)} async-done(((bf16[8,128,512]{2,1,0:T(8,128)(2,1)}), bf16[8,128,512]{2,1,0:T(8,128)(2,1)S(1)}, u32[]{:S(2)}, u32[]{:S(2)}) %all-to-all-start.1) | async-done | bytes 1048608 | tf_op jit(solution)/shard_map/all_to_all | solution.py:35
  61.8 1.3 fusion.63
  63.1 0.2 multiply_reduce_fusion
  63.4 0.1 multiply_convert_fusion
  63.6 14.0 %all_to_all.30 = bf16[4,208,512]{2,1,0:T(8,128)(2,1)S(1)} all-to-all(bf16[4,208,512]{2,1,0:T(8,128)(2,1)S(1)} %broadcast_in_dim.24), channel_id=1, replica_groups=mesh['zh'=4,'x'=4,'c'=2,'y'=4,'zl'=2] {'y'}, dimensions={0} | all-to-all | bytes 1703936 | tf_op jit(solution)/shard_map/all_to_all | solution.py:35
  77.6 1.2 broadcast_in_dim.25
  78.8 4.1 %all-to-all-start.3 = ((bf16[8,64,1280]{2,1,0:T(8,128)(2,1)}), bf16[8,64,1280]{2,1,0:T(8,128)(2,1)S(1)}, u32[]{:S(2)}, u32[]{:S(2)}) async-start(bf16[8,64,1280]{2,1,0:T(8,128)(2,1)} %broadcast_in_dim.25), calls=%async_computation.3 | async-start | bytes 2621440 | tf_op jit(solution)/shard_map/all_to_all | solution.py:35
  82.9 0.7 all-gather.5.cloned.1.call-update
  83.6 1.0 slice.33
  84.6 15.3 %all-to-all-done.3 = bf16[8,64,1280]{2,1,0:T(8,128)(2,1)S(1)} async-done(((bf16[8,64,1280]{2,1,0:T(8,128)(2,1)}), bf16[8,64,1280]{2,1,0:T(8,128)(2,1)S(1)}, u32[]{:S(2)}, u32[]{:S(2)}) %all-to-all-start.3) | async-done | bytes 1310752 | tf_op jit(solution)/shard_map/all_to_all | solution.py:35
  99.8 1.1 copy-done.6
  100.9 2.8 convert_reduce_fusion
  103.9 0.6 fusion.2
  104.5 107.8 %all-gather.3.cloned.1.call-done = bf16[2560,640]{1,0:T(8,128)(2,1)} async-done(((bf16[40,640]{1,0:T(8,128)(2,1)}), bf16[2560,640]{1,0:T(8,128)(2,1)}) %all-gather.3.cloned.1.call-update) | async-done | bytes 3276816 | tf_op jit(solution)/shard_map/all_gather | solution.py:49
  212.3 9.6 %reshape.127 = bf16[32,2,40,2,320]{4,3,2,1,0:T(2,128)(2,1)} reshape(bf16[2560,640]{1,0:T(8,128)(2,1)} %all-gather.3.cloned.1.call-done) | data formatting | bytes 6553600 | tf_op jit(solution)/shard_map/reshape | solution.py:79
  221.9 9.1 %fusion.65 = (bf16[1,32,40,2,320]{4,0,2,3,1:T(2,128)(2,1)}, bf16[1,32,40,2,320]{4,0,2,3,1:T(2,128)(2,1)S(1)}) fusion(bf16[2,32,40,2,320]{4,0,2,3,1:T(2,128)(2,1)} %bitcast.51), kind=kLoop, calls=%fused_computation.109 | loop fusion | bytes 6553600 | tf_op jit(solution)/shard_map/slice | solution.py:81
  231.0 2.0 copy.33
  233.0 2.3 squeeze.29
  235.3 4.3 %copy.34 = bf16[1,32,40,2,320]{4,3,2,1,0:T(2,128)(2,1)S(1)} copy(bf16[1,32,40,2,320]{4,0,2,3,1:T(2,128)(2,1)} %get-tuple-element.12) | data formatting | bytes 3276800 | tf_op jit(solution)/shard_map/slice | solution.py:81
  239.6 7.2 %fusion.7 = (bf16[768,640]{1,0:T(8,128)(2,1)S(1)}, f32[768,640]{1,0:T(8,128)}) fusion(bf16[1280,640]{1,0:T(8,128)(2,1)S(1)} %copy-done.5, bf16[768,1280]{1,0:T(8,128)(2,1)S(1)} %copy-done.3, f32[768]{0:T(1024)S(1)} %add_rsqrt_fusion, f32[768]{0:T(1024)S(1)} %broadcast_multiply_fusion), kind=kOutput, calls=%fused_computation.16 | convolution fusion | flops 1294172160 | bytes 6559744 | tf_op jit(solution)/shard_map/dot_general | solution.py:39
  246.8 4.1 %all-gather.5.cloned.1.call-done = bf16[768,1280]{1,0:T(8,128)(2,1)} async-done(((bf16[192,1280]{1,0:T(8,128)(2,1)}), bf16[768,1280]{1,0:T(8,128)(2,1)}) %all-gather.5.cloned.1.call-update) | async-done | bytes 1966096 | tf_op jit(solution)/shard_map/all_gather | solution.py:50
  250.9 4.5 %convolution_convert_fusion.1 = bf16[1280,640]{1,0:T(8,128)(2,1)} fusion(bf16[768,640]{1,0:T(8,128)(2,1)S(1)} %get-tuple-element.19, bf16[768,1280]{1,0:T(8,128)(2,1)} %all-gather.5.cloned.1.call-done, bf16[768]{0:T(1024)(128)(2,1)S(1)} %reshape.133), kind=kOutput, calls=%fused_computation.10 | convolution fusion | flops 1260093440 | bytes 4589056 | tf_op jit(solution)/shard_map/dot_general | solution.py:39
  255.4 5.5 %stack.10 = bf16[1,4,4,2,40,2,320]{6,5,4,3,2,1,0:T(2,128)(2,1)} reshape(bf16[1280,640]{1,0:T(8,128)(2,1)} %convolution_convert_fusion.1) | data formatting | bytes 3276800 | tf_op jit(solution)/shard_map/stack | solution.py:103
  260.9 7.0 %copy.36 = bf16[1,4,4,2,40,2,320]{6,0,4,5,1,2,3:T(2,128)(2,1)} copy(bf16[1,4,4,2,40,2,320]{6,5,4,3,2,1,0:T(2,128)(2,1)} %stack.10) | data formatting | bytes 3276800 | tf_op jit(solution)/shard_map/stack | solution.py:103
  267.9 2.3 squeeze.30
  270.2 8.4 %convolution_convert_fusion.2 = bf16[1280,640]{1,0:T(8,128)(2,1)} fusion(f32[768,640]{1,0:T(8,128)} %get-tuple-element.20, bf16[1280,640]{1,0:T(8,128)(2,1)} %squeeze.30, bf16[768,1280]{1,0:T(8,128)(2,1)} %all-gather.5.cloned.1.call-done, bf16[768]{0:T(1024)(128)(2,1)S(1)} %reshape.133, bf16[768,1280]{1,0:T(8,128)(2,1)} %copy-done.2, ...), kind=kOutput, calls=%fused_computation.11 | convolution fusion | flops 2527232000 | bytes 9182720 | tf_op jit(solution)/shard_map/dot_general | solution.py:39
  278.6 5.5 %stack.9 = bf16[1,4,4,2,40,2,320]{6,5,4,3,2,1,0:T(2,128)(2,1)} reshape(bf16[1280,640]{1,0:T(8,128)(2,1)} %convolution_convert_fusion.2) | data formatting | bytes 3276800 | tf_op jit(solution)/shard_map/stack | solution.py:103
  284.1 7.1 %copy.35 = bf16[1,4,4,2,40,2,320]{6,0,4,5,1,2,3:T(2,128)(2,1)} copy(bf16[1,4,4,2,40,2,320]{6,5,4,3,2,1,0:T(2,128)(2,1)} %stack.9) | data formatting | bytes 3276800 | tf_op jit(solution)/shard_map/stack | solution.py:103
  291.1 14.9 %maximum_bitcast_fusion = bf16[2,4,4,2,40,2,320]{6,5,4,3,2,1,0:T(2,128)(2,1)} fusion(bf16[1,4,4,2,40,2,320]{6,0,4,5,1,2,3:T(2,128)(2,1)} %copy.36, bf16[1,4,4,2,40,2,320]{6,0,4,5,1,2,3:T(2,128)(2,1)} %copy.35), kind=kLoop, calls=%fused_computation.6 | loop fusion | flops 6553600 | bytes 6553600 | tf_op jit(solution)/shard_map/transpose | solution.py:104
  306.0 8.8 %reshape.128 = bf16[2,1280,640]{2,1,0:T(8,128)(2,1)} reshape(bf16[2,4,4,2,40,2,320]{6,5,4,3,2,1,0:T(2,128)(2,1)} %maximum_bitcast_fusion) | data formatting | bytes 6553600 | tf_op jit(solution)/shard_map/reshape | solution.py:104
  314.8 2.7 dynamic-slice_bitcast_fusion
  317.6 3.8 %collective-permute-done.3 = bf16[1280,640]{1,0:T(8,128)(2,1)} collective-permute-done((bf16[1280,640]{1,0:T(8,128)(2,1)}, bf16[1280,640]{1,0:T(8,128)(2,1)}, u32[]{:S(2)}, u32[]{:S(2)}) %collective-permute-start.3) | collective-permute-done | bytes 1638432 | tf_op jit(solution)/shard_map/ppermute | solution.py:108
  321.4 3.5 fusion.4
  324.9 4.9 %all-to-all-start.4 = ((bf16[4,320,640]{2,1,0:T(8,128)(2,1)}), bf16[4,320,640]{2,1,0:T(8,128)(2,1)}, u32[]{:S(2)}, u32[]{:S(2)}) async-start(bf16[4,320,640]{2,1,0:T(8,128)(2,1)} %bitcast.52), calls=%async_computation.4 | async-start | bytes 3276800 | tf_op jit(solution)/shard_map/all_to_all | solution.py:110
  329.8 2.4 reshape.135
  332.2 5.0 %fusion.66 = (bf16[4,192,1280]{2,1,0:T(8,128)(2,1)S(1)}, f32[4,192,1280]{2,1,0:T(8,128)}) fusion(bf16[4,192,640]{2,1,0:T(8,128)(2,1)S(1)} %bitcast.57, bf16[1280,640,1]{1,0,2:T(8,128)(2,1)} %reshape.135), kind=kOutput, calls=%fused_computation.110 | convolution fusion | flops 1259274240 | bytes 8519680 | tf_op jit(solution)/shard_map/dot_general | solution.py:39
  337.3 1.3 collective-permute-start.2
  338.7 1.3 collective-permute-start.1
  340.0 0.6 collective-permute-start
  340.5 9.9 %all-to-all-done.4 = bf16[4,320,640]{2,1,0:T(8,128)(2,1)} async-done(((bf16[4,320,640]{2,1,0:T(8,128)(2,1)}), bf16[4,320,640]{2,1,0:T(8,128)(2,1)}, u32[]{:S(2)}, u32[]{:S(2)}) %all-to-all-start.4) | async-done | bytes 1638432 | tf_op jit(solution)/shard_map/all_to_all | solution.py:110
  350.5 2.5 reduce_sum.81
  353.0 8.3 %all-to-all-start.5 = ((bf16[8,40,640]{2,1,0:T(8,128)(2,1)}), bf16[8,40,640]{2,1,0:T(8,128)(2,1)S(1)}, u32[]{:S(2)}, u32[]{:S(2)}) async-start(bf16[8,40,640]{2,1,0:T(8,128)(2,1)} %bitcast.16), calls=%async_computation.5 | async-start | bytes 819200 | tf_op jit(solution)/shard_map/all_to_all | solution.py:112
  361.3 0.9 fusion.53
  362.2 0.1 reshape.132
  362.4 1.1 collective-permute-done
  363.5 2.6 fusion.33
  366.1 9.8 %all-to-all-done.5 = bf16[8,40,640]{2,1,0:T(8,128)(2,1)S(1)} async-done(((bf16[8,40,640]{2,1,0:T(8,128)(2,1)}), bf16[8,40,640]{2,1,0:T(8,128)(2,1)S(1)}, u32[]{:S(2)}, u32[]{:S(2)}) %all-to-all-start.5) | async-done | bytes 409632 | tf_op jit(solution)/shard_map/all_to_all | solution.py:112
  376.0 0.1 reshape.131
  376.1 0.7 copy.37
  (39 shorter events, 0.7 us)
Async XLA Ops:
  7.2 2.7 copy-start
  7.2 15.8 %copy-start.9 = (bf16[320,2,40]{0,2,1:T(8,128)(2,1)S(1)}, bf16[320,2,40]{0,2,1:T(8,128)(2,1)}, u32[]{:S(2)}) copy-start(bf16[320,2,40]{0,2,1:T(8,128)(2,1)} %param.10) | copy-start | bytes 153604
  7.2 32.6 %copy-start.8 = (bf16[128,512]{1,0:T(8,128)(2,1)S(1)}, bf16[128,512]{1,0:T(8,128)(2,1)}, u32[]{:S(2)}) copy-start(bf16[128,512]{1,0:T(8,128)(2,1)} %param.8) | copy-start | bytes 393220
  11.3 28.5 %all-to-all-start = ((bf16[32,8,1024]{2,1,0:T(8,128)(2,1)}), bf16[32,8,1024]{2,1,0:T(8,128)(2,1)S(1)}, u32[]{:S(2)}, u32[]{:S(2)}) async-start(bf16[32,8,1024]{2,1,0:T(8,128)(2,1)} %fusion.39), calls=%async_computation | async-start | bytes 1048576 | tf_op jit(solution)/shard_map/all_to_all | solution.py:64
  22.9 189.4 %all-gather.3.cloned.1.call-start = ((), (), s32[]{:S(2)}) async-start(), calls=%async_computation.6 | async-start | bytes 3328000 | tf_op jit(solution)/shard_map/all_gather | solution.py:49
  39.8 6.8 %copy-start.4 = (bf16[32,8,1024]{2,1,0:T(8,128)(2,1)}, bf16[32,8,1024]{2,1,0:T(8,128)(2,1)S(1)}, u32[]{:S(2)}) copy-start(bf16[32,8,1024]{2,1,0:T(8,128)(2,1)S(1)} %all-to-all-done) | copy-start | bytes 1572868
  40.9 20.9 %all-to-all-start.1 = ((bf16[8,128,512]{2,1,0:T(8,128)(2,1)}), bf16[8,128,512]{2,1,0:T(8,128)(2,1)S(1)}, u32[]{:S(2)}, u32[]{:S(2)}) async-start(bf16[8,128,512]{2,1,0:T(8,128)(2,1)} %broadcast_in_dim.23), calls=%async_computation.1 | async-start | bytes 2097152 | tf_op jit(solution)/shard_map/all_to_all | solution.py:35
  63.3 14.3 %copy-start.7 = (bf16[64,1280]{1,0:T(8,128)(2,1)S(1)}, bf16[64,1280]{1,0:T(8,128)(2,1)}, u32[]{:S(2)}) copy-start(bf16[64,1280]{1,0:T(8,128)(2,1)} %param.9) | copy-start | bytes 491524
  78.8 21.1 %all-to-all-start.3 = ((bf16[8,64,1280]{2,1,0:T(8,128)(2,1)}), bf16[8,64,1280]{2,1,0:T(8,128)(2,1)S(1)}, u32[]{:S(2)}, u32[]{:S(2)}) async-start(bf16[8,64,1280]{2,1,0:T(8,128)(2,1)} %broadcast_in_dim.25), calls=%async_computation.3 | async-start | bytes 2621440 | tf_op jit(solution)/shard_map/all_to_all | solution.py:35
  82.8 168.1 %all-gather.5.cloned.1.call-start = ((), (), s32[]{:S(2)}) async-start(), calls=%async_computation.7 | async-start | bytes 2457600 | tf_op jit(solution)/shard_map/all_gather | solution.py:50
  99.8 1.1 copy-start.6
  103.7 118.2 %copy-start.2 = (bf16[768,1280]{1,0:T(8,128)(2,1)}, bf16[768,1280]{1,0:T(8,128)(2,1)S(1)}, u32[]{:S(2)}) copy-start(bf16[768,1280]{1,0:T(8,128)(2,1)S(1)} %get-tuple-element.18) | copy-start | bytes 5898244
  235.3 4.3 %copy-start.3 = (bf16[768,1280]{1,0:T(8,128)(2,1)S(1)}, bf16[768,1280]{1,0:T(8,128)(2,1)}, u32[]{:S(2)}) copy-start(bf16[768,1280]{1,0:T(8,128)(2,1)} %copy-done.2) | copy-start | bytes 5898244
  235.3 4.3 %copy-start.5 = (bf16[1280,640]{1,0:T(8,128)(2,1)S(1)}, bf16[1280,640]{1,0:T(8,128)(2,1)}, u32[]{:S(2)}) copy-start(bf16[1280,640]{1,0:T(8,128)(2,1)} %squeeze.29) | copy-start | bytes 4915204
  317.6 3.8 %collective-permute-start.3 = (bf16[1280,640]{1,0:T(8,128)(2,1)}, bf16[1280,640]{1,0:T(8,128)(2,1)}, u32[]{:S(2)}, u32[]{:S(2)}) collective-permute-start(bf16[1280,640]{1,0:T(8,128)(2,1)} %dynamic-slice_bitcast_fusion), channel_id=1, source_target_pairs={{0,8},{8,0},{1,9},{9,1},{2,10},{10,2},{3,11},{11,3},{4,12},{12,4},... | collective-permute-start | bytes 4915208 | tf_op jit(solution)/shard_map/ppermute | solution.py:108
  324.9 25.5 %all-to-all-start.4 = ((bf16[4,320,640]{2,1,0:T(8,128)(2,1)}), bf16[4,320,640]{2,1,0:T(8,128)(2,1)}, u32[]{:S(2)}, u32[]{:S(2)}) async-start(bf16[4,320,640]{2,1,0:T(8,128)(2,1)} %bitcast.52), calls=%async_computation.4 | async-start | bytes 3276800 | tf_op jit(solution)/shard_map/all_to_all | solution.py:110
  337.3 25.0 %collective-permute-start.2 = (bf16[192,1280]{1,0:T(8,128)(2,1)S(1)}, bf16[192,1280]{1,0:T(8,128)(2,1)S(1)}, u32[]{:S(2)}, u32[]{:S(2)}) collective-permute-start(bf16[192,1280]{1,0:T(8,128)(2,1)S(1)} %get-tuple-element.15), channel_id=1, source_target_pairs={{0,6},{2,0},{4,2},{6,4},{1,7},{3,1},{5,3},{7,5},{8,14},{10,8},{12,... | collective-permute-start | bytes 1474568 | tf_op jit(solution)/shard_map/ppermute | solution.py:91
  338.7 23.7 %collective-permute-start.1 = (bf16[192,1280]{1,0:T(8,128)(2,1)S(1)}, bf16[192,1280]{1,0:T(8,128)(2,1)S(1)}, u32[]{:S(2)}, u32[]{:S(2)}) collective-permute-start(bf16[192,1280]{1,0:T(8,128)(2,1)S(1)} %get-tuple-element.16), channel_id=1, source_target_pairs={{0,4},{2,6},{4,0},{6,2},{1,5},{3,7},{5,1},{7,3},{8,12},{10,14},{12... | collective-permute-start | bytes 1474568 | tf_op jit(solution)/shard_map/ppermute | solution.py:91
  340.0 23.5 %collective-permute-start = (bf16[192,1280]{1,0:T(8,128)(2,1)S(1)}, bf16[192,1280]{1,0:T(8,128)(2,1)}, u32[]{:S(2)}, u32[]{:S(2)}) collective-permute-start(bf16[192,1280]{1,0:T(8,128)(2,1)S(1)} %get-tuple-element.14), channel_id=1, source_target_pairs={{0,2},{2,4},{4,6},{6,0},{1,3},{3,5},{5,7},{7,1},{8,10},{10,12},{12... | collective-permute-start | bytes 1474568 | tf_op jit(solution)/shard_map/ppermute | solution.py:91
  353.0 22.9 %all-to-all-start.5 = ((bf16[8,40,640]{2,1,0:T(8,128)(2,1)}), bf16[8,40,640]{2,1,0:T(8,128)(2,1)S(1)}, u32[]{:S(2)}, u32[]{:S(2)}) async-start(bf16[8,40,640]{2,1,0:T(8,128)(2,1)} %bitcast.16), calls=%async_computation.5 | async-start | bytes 819200 | tf_op jit(solution)/shard_map/all_to_all | solution.py:112
  363.5 13.2 %copy-start.1 = (bf16[128,1024]{1,0:T(8,128)(2,1)S(1)}, bf16[128,1024]{1,0:T(8,128)(2,1)}, u32[]{:S(2)}) copy-start(bf16[128,1024]{1,0:T(8,128)(2,1)} %param.7) | copy-start | bytes 786436
Sparse Core Ops, SparseCore 0:
  26.1 186.0 all-gather.2
  214.1 36.7 all-gather.4

commit v2 on v1

v2 whole, which is shorter than its diff:
```python
import functools

import jax
import jax.numpy as jnp
import numpy as np
from jax import lax
from jax.experimental import pallas as pl
from jax.experimental.pallas import tpu as pltpu
from jax.sharding import Mesh
from jax.sharding import PartitionSpec as P

epsilon = 1e-05
bf16 = jnp.bfloat16
f32 = jnp.float32
i32 = jnp.int32

N_DP = 32
CAP = 6
PAD = 8
SLOTS = 192
CH = 512
D = 1280
UNITS = 320
LANES = 384
WIDE = 2 * LANES
BLOCK = 40
ZX = ("zh", "zl")

VMEM = pl.BlockSpec(memory_space=pltpu.VMEM)
SMEM = pl.BlockSpec(memory_space=pltpu.SMEM)


def dot(a, b, dims=((1,), (0,))):
    return lax.dot_general(a, b, (dims, ((), ())), preferred_element_type=f32)


def iota(shape, dim):
    return lax.broadcasted_iota(i32, shape, dim)


def normalize(values):
    mean_value = jnp.mean(values, axis=-1, keepdims=True)
    centered = values - mean_value
    variance = jnp.mean(centered * centered, axis=-1, keepdims=True)
    return centered * lax.rsqrt(variance + epsilon)


def call(kernel, out_shape, args, flops, bytes_accessed, scratch=(), vmem=48 << 20, smem=0, name=None):
    return pl.pallas_call(
        kernel,
        out_shape=out_shape,
        in_specs=[SMEM] * smem + [VMEM] * (len(args) - smem),
        out_specs=jax.tree.map(lambda _: VMEM, out_shape),
        scratch_shapes=list(scratch),
        compiler_params=pltpu.CompilerParams(vmem_limit_bytes=vmem),
        cost_estimate=pl.CostEstimate(
            flops=flops, bytes_accessed=bytes_accessed, transcendentals=0
        ),
        name=name,
    )(*args)


def pack_kernel(pair, packed):
    up = pair[0].astype(f32)
    down = pair[1].astype(f32)
    blank = jnp.zeros((BLOCK, LANES - UNITS), f32)
    up = jnp.concatenate([up, blank], axis=1)
    down = jnp.concatenate([down, blank], axis=1)
    packed[...] = pack_pair(up, down).astype(bf16)


def pack_pair(up, down):
    turned = pltpu.roll(down, 64, 1)
    lane = iota((BLOCK, 128), 1)
    middle = jnp.where(lane < 64, up[:, 256:], turned[:, :128])
    return jnp.concatenate([up[:, :256], middle, turned[:, 128:]], axis=1)


def unpack_pair(packed):
    used = iota((BLOCK, LANES), 1) < UNITS
    up = jnp.where(used, packed[:, :LANES], 0.0)
    down = pltpu.roll(packed[:, 256:], LANES - 64, 1)
    return up, jnp.where(used, down, 0.0)


def route_kernel(owner, live, rows, outgoing):
    count = rows.shape[0]
    target = owner[...]
    onehot = (target == iota((count, 128), 1)).astype(f32)
    earlier = (iota((count, count), 1) < iota((count, count), 0)).astype(bf16)
    before = dot(earlier, onehot.astype(bf16))
    position = jnp.sum(before * onehot, axis=1, keepdims=True).astype(i32)
    diagonal = iota((count, count), 0) == iota((count, count), 1)
    state = 1.0 + jnp.sum(
        jnp.where(diagonal, live[...].astype(f32), 0.0), axis=1, keepdims=True
    )
    slot = iota((count, N_DP * PAD), 1)
    placement = (target * PAD + position == slot).astype(bf16)
    flag_row = (target * PAD + CAP == slot).astype(bf16)
    flag_value = jnp.where(position == iota((count, 128), 1), state, 0.0).astype(bf16)
    first = ((0,), (0,))
    outgoing[...] = dot(placement, rows[...], first).astype(bf16)
    flags = dot(flag_row, flag_value, first)
    outgoing[:, :128] = (outgoing[:, :128].astype(f32) + flags).astype(bf16)


def front_kernel(place, incoming, *refs):
    pieces, (block, flags_out, conv) = refs[:4], refs[4:]
    y, zl = place[0], place[1]
    for step in range(4):
        for other in range(2):
            start = lax.rem(y - step + 4, 4) * 256 + lax.rem(zl + other, 2) * 128
            conv[pl.ds(pl.multiple_of(start, 128), 128), :] = pieces[step][
                other * 128 : other * 128 + 128, :
            ]
    raw = incoming[...]
    conv_out = dot(raw, conv[...])
    active = 0.5 * conv_out * (1.0 + lax.erf(conv_out * 0.7071067811865476))
    features = normalize(active).astype(bf16)
    slot = iota((SLOTS, N_DP * PAD), 0)
    row = iota((SLOTS, N_DP * PAD), 1)
    owner, rank = slot // CAP, slot % CAP
    compact = (row == owner * PAD + rank).astype(bf16)
    block[:SLOTS, :] = dot(compact, features).astype(bf16)
    flag_rows = dot((row == owner * PAD + CAP).astype(bf16), raw[:, :128])
    lane = iota((SLOTS, 128), 1)
    flags = jnp.sum(
        jnp.where(lane == iota((SLOTS, 128), 0) % CAP, flag_rows, 0.0), axis=1, keepdims=True
    )
    flags_out[...] = flags
    wide = iota((SLOTS, CH), 1) == iota((SLOTS, CH), 0)
    as_row = jnp.sum(jnp.where(wide, flags, 0.0), axis=0, keepdims=True)
    block[SLOTS:, :] = jnp.broadcast_to(as_row, (16, CH)).astype(bf16)


def weights_kernel(place, *refs):
    pieces, (up, down, wide_up, wide_down) = refs[:8], refs[8:]
    zh, x, c, zl = place[0], place[1], place[2], place[3]
    for core in range(2):
        for step in range(4):
            piece = pieces[core * 4 + step]
            base = lax.rem(x - step + 4, 4) * 80 + lax.rem(c + core, 2) * 40

            def one(k, carry):
                row = lax.rem(zh - k // 2 + 4, 4) * 320 + base
                half = lax.rem(zl + k, 2)
                rows = pl.ds(pl.multiple_of(row, 8), BLOCK)
                a, b = unpack_pair(piece[k].astype(f32))
                wide_up[half, rows, :] = a
                wide_down[half, rows, :] = b
                return carry

            lax.fori_loop(0, 8, one, 0)
    for half in range(2):
        up[:, half * LANES : (half + 1) * LANES] = wide_up[half].astype(bf16)
        down[:, half * LANES : (half + 1) * LANES] = wide_down[half].astype(bf16)


def ffn_kernel(place, cot, up, down, *refs):
    blocks, protos, refs = refs[:4], refs[4:8], refs[8:]
    own, away1, away2, away3, kept, sent, refs = *refs[:6], refs[6:]
    proj, feats, live, normed, hidden, grad_pre, grad_out, wide_up, wide_down = refs
    y, zl, c = place[0], place[1], place[2]
    for step in range(4):
        for other in range(2):
            start = lax.rem(y - step + 4, 4) * 128 + lax.rem(zl + other, 2) * 64
            proj[pl.ds(pl.multiple_of(start, 64), 64), :] = protos[step][
                other * 64 : other * 64 + 64, :
            ]
        feats[step] = blocks[step][:SLOTS, :]
        flags = blocks[step][SLOTS : SLOTS + 16, :].astype(f32)[:1, :]
        wide = iota((SLOTS, CH), 1) == iota((SLOTS, CH), 0)
        flags = jnp.sum(jnp.where(wide, flags, 0.0), axis=1, keepdims=True)
        live[step] = (flags == 2.0).astype(f32)

    def forward(step, carry):
        rows = pl.ds(pl.multiple_of(step * SLOTS, SLOTS), SLOTS)
        stream = dot(feats[step], proj[...]).astype(bf16).astype(f32)
        normed[rows, :] = normalize(stream).astype(bf16)
        pre = dot(normed[rows, :], up[...])
        cumulative = 0.5 * (1.0 + lax.erf(pre * 0.7071067811865476))
        density = jnp.exp(-0.5 * pre * pre) * 0.3989422804014327
        hidden[rows, :] = (pre * cumulative).astype(bf16)
        slope = cumulative + pre * density
        partial = dot(hidden[rows, :], down[...], ((1,), (1,)))

        @pl.when(step == 0)
        def _():
            own[...] = partial + stream

        for k, away in enumerate((away1, away2, away3)):

            @pl.when(step == k + 1)
            def _():
                away[...] = partial.astype(bf16)

        there = lax.rem(y - step + 4, 4) * SLOTS
        masked = cot[pl.ds(pl.multiple_of(there, SLOTS), SLOTS), :].astype(f32) * live[step]
        grad_out[rows, :] = masked.astype(bf16)
        grad_hidden = dot(grad_out[rows, :], down[...])
        grad_pre[rows, :] = (grad_hidden * slope).astype(bf16)
        return carry

    lax.fori_loop(0, 4, forward, 0)

    def backward(part, carry):
        columns = pl.ds(pl.multiple_of(part * 640, 640), 640)
        first = ((0,), (0,))
        wide_up[...] = dot(normed[:, columns], grad_pre[...], first)
        wide_down[...] = dot(grad_out[:, columns], hidden[...], first)

        def place_block(k, carry):
            zh, x = k // 4, lax.rem(k, 4)
            for other, out in enumerate((kept, sent)):
                row = zh * 320 + x * 80 + lax.rem(c + other, 2) * BLOCK
                rows = pl.ds(pl.multiple_of(row, 8), BLOCK)
                for half in range(2):
                    lanes = slice(half * LANES, (half + 1) * LANES)
                    block = pack_pair(wide_up[rows, lanes], wide_down[rows, lanes])
                    out[x, (part * 2 + zh) * 2 + half] = block.astype(bf16)
            return carry

        lax.fori_loop(0, 8, place_block, 0)
        return carry

    lax.fori_loop(0, 2, backward, 0)


def last_kernel(arrived, out):
    total = arrived[0].astype(f32)
    for k in range(1, 8):
        total = total + arrived[k].astype(f32)
    up, down = unpack_pair(total)
    out[0] = up[:, :UNITS]
    out[1] = down[:, :UNITS]


def ring(values, axis, size, step):
    return lax.ppermute(values, axis, [(k, (k + step) % size) for k in range(size)])


def around(values, axis, size):
    return [values] + [ring(values, axis, size, step) for step in range(1, size)]


def per_device(waveform_rows, conv_weight, proj_weight, ffn_pair, owner, frame_live, cotangent):
    dp = ("zh", "x", "c")
    zh, x, c, y, zl = (lax.axis_index(name).astype(i32) for name in ("zh", "x", "c", "y", "zl"))
    cot_all = lax.all_gather(cotangent, "y", axis=0, tiled=True)

    packed = call(
        pack_kernel,
        jax.ShapeDtypeStruct((BLOCK, 2 * UNITS), bf16),
        [jnp.transpose(ffn_pair, (1, 2, 0))],
        1 << 16, 1 << 17, name="pack",
    )
    both = jnp.stack([packed, ring(packed, "zl", 2, 1)])
    along_z = jnp.concatenate(around(both, "zh", 4), axis=0)
    along_x = around(along_z, "x", 4)
    pieces = along_x + [ring(piece, "c", 2, 1) for piece in along_x]

    conv_pair = jnp.concatenate([conv_weight, ring(conv_weight, "zl", 2, 1)], axis=0)
    conv_pieces = around(conv_pair, "y", 4)
    proj_pair = jnp.concatenate([proj_weight, ring(proj_weight, "zl", 2, 1)], axis=0)
    proj_pieces = around(proj_pair, "y", 4)

    outgoing = call(
        route_kernel,
        jax.ShapeDtypeStruct((N_DP * PAD, 1024), bf16),
        [owner, frame_live.reshape(1, -1), waveform_rows],
        2 * 256 * 128 * 1152, 1 << 20, name="route",
    )
    incoming = lax.all_to_all(
        outgoing.reshape(N_DP, PAD, 1024), dp, split_axis=0, concat_axis=0, tiled=True
    ).reshape(N_DP * PAD, 1024)

    block, flags = call(
        front_kernel,
        (
            jax.ShapeDtypeStruct((SLOTS + 16, CH), bf16),
            jax.ShapeDtypeStruct((SLOTS, 1), f32),
        ),
        [jnp.stack([y, zl]), incoming, *conv_pieces],
        2 * 256 * 1024 * 512, 2 << 20,
        scratch=[pltpu.VMEM((1024, CH), bf16)], smem=1, name="front",
    )
    blocks = around(block, "y", 4)

    up, down = call(
        weights_kernel,
        (jax.ShapeDtypeStruct((D, WIDE), bf16),) * 2,
        [jnp.stack([zh, x, c, zl]), *pieces],
        1 << 22, 8 << 20,
        scratch=[pltpu.VMEM((2, D, LANES), f32)] * 2, smem=1, name="weights",
    )
    rows = 4 * SLOTS
    piece = jax.ShapeDtypeStruct((SLOTS, D), bf16)
    terms = jax.ShapeDtypeStruct((4, 8, BLOCK, 2 * UNITS), bf16)
    own, away1, away2, away3, kept, sent = call(
        ffn_kernel,
        (jax.ShapeDtypeStruct((SLOTS, D), f32), piece, piece, piece, terms, terms),
        [jnp.stack([y, zl, c]), cot_all, up, down, *blocks, *proj_pieces],
        2 * rows * D * (CH + 5 * WIDE), 16 << 20,
        scratch=[
            pltpu.VMEM((CH, D), bf16),
            pltpu.VMEM((4, SLOTS, CH), bf16),
            pltpu.VMEM((4, SLOTS, 1), f32),
            pltpu.VMEM((rows, D), bf16),
            pltpu.VMEM((rows, WIDE), bf16),
            pltpu.VMEM((rows, WIDE), bf16),
            pltpu.VMEM((rows, D), bf16),
            pltpu.VMEM((640, WIDE), f32),
            pltpu.VMEM((640, WIDE), f32),
        ],
        smem=1, name="ffn",
    )
    for step, away in ((1, away1), (2, away2), (3, away3)):
        own = own + ring(away, "y", 4, 4 - step).astype(f32)
    encoded = (own * (flags > 0).astype(f32)).astype(bf16)

    total = kept.astype(f32) + ring(sent, "c", 2, 1).astype(f32)
    total = lax.all_to_all(total.astype(bf16), "x", split_axis=0, concat_axis=0, tiled=True)
    total = jnp.sum(total.astype(f32), axis=0).astype(bf16)
    total = lax.all_to_all(total, ZX, split_axis=0, concat_axis=0, tiled=True)
    grad_pair = call(
        last_kernel,
        jax.ShapeDtypeStruct((2, BLOCK, UNITS), f32),
        [total],
        1 << 18, 1 << 19, name="last",
    )
    return (encoded, jnp.transpose(grad_pair, (2, 0, 1)))


def solution(mesh):
    names = ("zh", "x", "c", "y", "zl")
    fine = Mesh(np.asarray(mesh.devices).reshape(4, 4, 2, 4, 2), names)
    dp = ("zh", "x", "c")
    fsdp = ("y", "zl")
    everyone = dp + fsdp
    return jax.shard_map(
        per_device,
        mesh=fine,
        in_specs=(
            P(everyone, None),
            P(fsdp, None),
            P(fsdp, None),
            P(fsdp, None, dp),
            P(everyone, None),
            P(everyone),
            P(everyone, None),
        ),
        out_specs=(P(everyone, None), P(fsdp, None, dp)),
        check_vma=False,
    )
```

time: 390 us -> 192 us (0.49); the launches traced: 384 us -> 192 us
  waiting for transfers between devices: 184 us -> 65.8 us
  local copies, waits for them, and re-layouts: 75.3 us -> 13.6 us
  Pallas kernels: 0 us -> 33.4 us
  matrix products: 29.5 us -> 0 us
  other arithmetic: 29.1 us -> 8.11 us
  starting transfers between devices: 37.6 us -> 56.3 us
  blocking collectives: 14 us -> 0 us
    all_gather x1 -> x0, waiting for transfers between devices: 108 us -> none  [per_device(): lax.all_gather(local_pair, ('zh', 'x', 'c', 'zl'), axis=0, tiled=True)]
    all_to_all x5 -> x3, waiting for transfers between devices: 66.2 us -> 29.5 us  [the longest x1 17.4 us: per_device(): lax.all_to_all(total.astype(bf16), 'x', split_axis=0, concat_axis=0, tile...]
    pallas_call x0 -> x6, Pallas kernels: none -> 33.4 us  [call(): pl.pallas_call(kernel, out_shape=out_shape, in_specs=[SMEM] * smem + [VME...]
    ppermute x4 -> x26, starting transfers between devices: 3.21 us -> 34.5 us  [ring(): lax.ppermute(values, axis, [(k, (k + step) % size) for k in range(size)])]
    ppermute x4 -> x26, waiting for transfers between devices: 4.99 us -> 35.6 us  [ring(): lax.ppermute(values, axis, [(k, (k + step) % size) for k in range(size)])]
    dot_general x7 -> x0, matrix products: 29.5 us -> none  [dot(): return lax.dot_general(a, b, (dims, ((), ())), preferred_element_type=f32)]
    another operation x5 -> x0, local copies, waits for them, and re-layouts: 25.1 us -> none  [the longest x4 25 us: per_device(): jnp.stack([up_term, down_term]).astype(bf16).reshape(2, 4, 4, 2, 40, 2, 320)]
    reshape x5 -> x0, local copies, waits for them, and re-layouts: 19.4 us -> none  [the longest x1 9.62 us: per_device(): pair = pair.reshape(32, 2, 40, 2, 320)]
  transfers between devices with their start and end apart: 11 -> 30, of which waited for: 9 -> 12; matrix products, arithmetic and copies ran while one was open for 15% -> 5% of each run, Pallas kernels for 0% -> 6%
where the time goes in v2:
time: 192 us
  waiting for transfers between devices  65.8 us (34%)
  starting transfers between devices  56.3 us (29%)
  Pallas kernels  33.4 us (17%)
  between operations  14.2 us (7%)
  local copies, waits for them, and re-layouts  13.6 us (7%)
  other arithmetic  8.11 us (4%)
    ppermute x26, waiting for transfers between devices, ring(): lax.ppermute(values, axis, [(k, (k + step) % size) for k in range(size)])  35.6 us
    ppermute x26, starting transfers between devices, ring(): lax.ppermute(values, axis, [(k, (k + step) % size) for k in range(size)])  34.5 us
    pallas_call x6, Pallas kernels, call(): pl.pallas_call(kernel, out_shape=out_shape, in_specs=[SMEM] * smem + [VME...  33.4 us
    all_to_all x1, waiting for transfers between devices, per_device(): lax.all_to_all(total.astype(bf16), 'x', split_axis=0, concat_axis=0, tile...  17.4 us
    all_to_all x1, waiting for transfers between devices, per_device(): total = lax.all_to_all(total, ZX, split_axis=0, concat_axis=0, tiled=True)  12.2 us
    unnamed x37, local copies, waits for them, and re-layouts  12 us
    all_to_all x1, starting transfers between devices, per_device(): lax.all_to_all(outgoing.reshape(N_DP, PAD, 1024), dp, split_axis=0, conca...  10.7 us
    all_to_all x1, starting transfers between devices, per_device(): lax.all_to_all(total.astype(bf16), 'x', split_axis=0, concat_axis=0, tile...  6.98 us
  transfers between devices with their start and end apart: 30, of which 12 were waited for; matrix products, arithmetic and copies ran while one was open for 5% of the time, Pallas kernels for 6%

profile of v2, /device:TPU:2, one launch (start us, length us, event | category | flops | bytes accessed | tf_op | source)
XLA Modules:
  0.0 191.5 jit_solution(9260633565944842403)
XLA Ops:
  7.2 0.7 all-gather.2.cloned.1.call-update
  7.9 0.8 copy-done.7
  8.7 0.1 pack.1
  8.8 2.0 %collective-permute-start = (bf16[40,640]{1,0:T(8,128)(2,1)S(1)}, bf16[40,640]{1,0:T(8,128)(2,1)S(1)}, u32[]{:S(2)}, u32[]{:S(2)}) collective-permute-start(bf16[40,640]{1,0:T(8,128)(2,1)S(1)} %pack.1), channel_id=1, source_target_pairs={{0,1},{1,0},{2,3},{3,2},{4,5},{5,4},{6,7},{7,6},{8,9},{9,8},{10,11... | collective-permute-start | bytes 153608 | tf_op jit(solution)/shard_map/ppermute | solution.py:239
  10.8 0.1 collective-permute-start.11
  10.9 1.9 %collective-permute-start.18 = (bf16[64,1280]{1,0:T(8,128)(2,1)}, bf16[64,1280]{1,0:T(8,128)(2,1)}, u32[]{:S(2)}, u32[]{:S(2)}) collective-permute-start(bf16[64,1280]{1,0:T(8,128)(2,1)} %param.9), channel_id=1, source_target_pairs={{0,1},{1,0},{2,3},{3,2},{4,5},{5,4},{6,7},{7,6},{8,9},{9,8},{10,11... | collective-permute-start | bytes 491528 | tf_op jit(solution)/shard_map/ppermute | solution.py:239
  12.9 0.8 copy.10.owner
  13.6 0.9 copy-done
  14.6 0.7 copy-done.8
  15.2 1.5 route.1
  16.7 10.7 %all-to-all-start = ((bf16[32,8,1024]{2,1,0:T(8,128)(2,1)}), bf16[32,8,1024]{2,1,0:T(8,128)(2,1)S(1)}, u32[]{:S(2)}, u32[]{:S(2)}) async-start(bf16[32,8,1024]{2,1,0:T(8,128)(2,1)} %bitcast.9), calls=%async_computation | async-start | bytes 1048576 | tf_op jit(solution)/shard_map/all_to_all | solution.py:273
  27.5 3.7 %collective-permute-start.3 = (bf16[2,40,640]{2,1,0:T(8,128)(2,1)S(1)}, bf16[2,40,640]{2,1,0:T(8,128)(2,1)S(1)}, u32[]{:S(2)}, u32[]{:S(2)}) collective-permute-start(bf16[2,40,640]{2,1,0:T(8,128)(2,1)S(1)} %pad_maximum_fusion), channel_id=1, source_target_pairs={{0,192},{64,0},{128,64},{192,128},{1,193},{65,1},{129,65},{193,129... | collective-permute-start | bytes 307208 | tf_op jit(solution)/shard_map/ppermute | solution.py:239
  31.2 2.3 %collective-permute-start.2 = (bf16[2,40,640]{2,1,0:T(8,128)(2,1)S(1)}, bf16[2,40,640]{2,1,0:T(8,128)(2,1)S(1)}, u32[]{:S(2)}, u32[]{:S(2)}) collective-permute-start(bf16[2,40,640]{2,1,0:T(8,128)(2,1)S(1)} %pad_maximum_fusion), channel_id=1, source_target_pairs={{0,128},{64,192},{128,0},{192,64},{1,129},{65,193},{129,1},{193,65... | collective-permute-start | bytes 307208 | tf_op jit(solution)/shard_map/ppermute | solution.py:239
  33.5 2.4 %collective-permute-start.1 = (bf16[2,40,640]{2,1,0:T(8,128)(2,1)S(1)}, bf16[2,40,640]{2,1,0:T(8,128)(2,1)S(1)}, u32[]{:S(2)}, u32[]{:S(2)}) collective-permute-start(bf16[2,40,640]{2,1,0:T(8,128)(2,1)S(1)} %pad_maximum_fusion), channel_id=1, source_target_pairs={{0,64},{64,128},{128,192},{192,0},{1,65},{65,129},{129,193},{193,1... | collective-permute-start | bytes 307208 | tf_op jit(solution)/shard_map/ppermute | solution.py:239
  35.9 3.1 %collective-permute-start.14 = (bf16[256,512]{1,0:T(8,128)(2,1)S(1)}, bf16[256,512]{1,0:T(8,128)(2,1)S(1)}, u32[]{:S(2)}, u32[]{:S(2)}) collective-permute-start(bf16[256,512]{1,0:T(8,128)(2,1)S(1)} %constant_dynamic-update-slice_fusion.5.refs_0_), channel_id=1, source_target_pairs={{0,6},{2,0},{4,2},{6,4},{1,7},{3,1},{5,3},{7,5},{8,14},{10,8},{12,... | collective-permute-start | bytes 786440 | tf_op jit(solution)/shard_map/ppermute | solution.py:239
  39.0 11.9 %collective-permute-done.1 = bf16[2,40,640]{2,1,0:T(8,128)(2,1)S(1)} collective-permute-done((bf16[2,40,640]{2,1,0:T(8,128)(2,1)S(1)}, bf16[2,40,640]{2,1,0:T(8,128)(2,1)S(1)}, u32[]{:S(2)}, u32[]{:S(2)}) %collective-permute-start.1) | collective-permute-done | bytes 102432 | tf_op jit(solution)/shard_map/ppermute | solution.py:239
  50.9 3.3 %collective-permute-start.13 = (bf16[256,512]{1,0:T(8,128)(2,1)S(1)}, bf16[256,512]{1,0:T(8,128)(2,1)S(1)}, u32[]{:S(2)}, u32[]{:S(2)}) collective-permute-start(bf16[256,512]{1,0:T(8,128)(2,1)S(1)} %constant_dynamic-update-slice_fusion.5.refs_0_), channel_id=1, source_target_pairs={{0,4},{2,6},{4,0},{6,2},{1,5},{3,7},{5,1},{7,3},{8,12},{10,14},{12... | collective-permute-start | bytes 786440 | tf_op jit(solution)/shard_map/ppermute | solution.py:239
  54.2 0.8 collective-permute-start.12
  55.0 0.6 collective-permute-start.6
  55.7 2.4 %collective-permute-start.5 = (bf16[8,40,640]{2,1,0:T(8,128)(2,1)S(1)}, bf16[8,40,640]{2,1,0:T(8,128)(2,1)S(1)}, u32[]{:S(2)}, u32[]{:S(2)}) collective-permute-start(bf16[8,40,640]{2,1,0:T(8,128)(2,1)S(1)} %constant_dynamic-update-slice_fusion.refs_0_), channel_id=1, source_target_pairs={{0,32},{16,48},{32,0},{48,16},{1,33},{17,49},{33,1},{49,17},{2,34}... | collective-permute-start | bytes 1228808 | tf_op jit(solution)/shard_map/ppermute | solution.py:239
  58.1 1.7 collective-permute-start.4
  59.9 1.6 constant_dynamic-update-slice_fusion.8
  61.5 0.2 collective-permute-done.13.refs_2_
  61.6 0.7 copy-done.1
  62.3 1.6 constant_dynamic-update-slice_fusion.7.refs_4_
  63.9 2.0 %collective-permute-done.12.refs_1_ = bf16[256,512]{1,0:T(8,128)(2,1)S(1)} collective-permute-done((bf16[256,512]{1,0:T(8,128)(2,1)S(1)}, bf16[256,512]{1,0:T(8,128)(2,1)S(1)}, u32[]{:S(2)}, u32[]{:S(2)}) %collective-permute-start.12) | collective-permute-done | bytes 262176 | tf_op jit(solution)/shard_map/ppermute | solution.py:239
  65.9 0.7 copy-done.3
  66.6 0.6 collective-permute-start.21
  67.2 8.1 %collective-permute-done.5.refs_2_ = bf16[8,40,640]{2,1,0:T(8,128)(2,1)S(1)} collective-permute-done((bf16[8,40,640]{2,1,0:T(8,128)(2,1)S(1)}, bf16[8,40,640]{2,1,0:T(8,128)(2,1)S(1)}, u32[]{:S(2)}, u32[]{:S(2)}) %collective-permute-start.5) | collective-permute-done | bytes 409632 | tf_op jit(solution)/shard_map/ppermute | solution.py:239
  75.3 0.9 collective-permute-done.4.refs_1_
  76.2 0.4 collective-permute-done.21.refs_7_
  76.6 1.9 collective-permute-start.20
  78.4 1.2 collective-permute-start.19
  79.6 0.1 pad_add_fusion.2.place
  79.7 0.9 copy-done.2
  80.6 0.9 copy-done.4
  81.6 1.6 front.1
  83.2 2.1 %collective-permute-start.17 = (bf16[208,512]{1,0:T(8,128)(2,1)S(1)}, bf16[208,512]{1,0:T(8,128)(2,1)S(1)}, u32[]{:S(2)}, u32[]{:S(2)}) collective-permute-start(bf16[208,512]{1,0:T(8,128)(2,1)S(1)} %get-tuple-element.14.refs_0_), channel_id=1, source_target_pairs={{0,6},{2,0},{4,2},{6,4},{1,7},{3,1},{5,3},{7,5},{8,14},{10,8},{12,... | collective-permute-start | bytes 638984 | tf_op jit(solution)/shard_map/ppermute | solution.py:239
  85.3 0.5 collective-permute-start.16
  85.8 0.6 collective-permute-start.15
  86.3 0.1 pad_add_fusion.place
  86.4 0.1 pad_add_fusion.1.place
  86.5 7.9 %weights.1 = (bf16[1280,768]{1,0:T(8,128)(2,1)S(1)}, bf16[1280,768]{1,0:T(8,128)(2,1)}) custom-call(s32[4]{0:T(128)S(1)} %pad_add_fusion.1.place, bf16[8,40,640]{2,1,0:T(8,128)(2,1)S(1)} %constant_dynamic-update-slice_fusion.refs_0_, bf16[8,40,640]{2,1,0:T(8,128)(2,1)S(1)} %collective-permute-done.4.refs_1_, ...), custom_call_target="tpu_custom_call" | custom-call | flops 4194304 | bytes 8388608 | tf_op jit(solution)/shard_map/weights/pallas_call | solution.py:49
  94.4 1.3 copy-done.9
  95.7 0.4 collective-permute-done.19.refs_5_
  96.1 4.4 %collective-permute-done.16.refs_2_ = bf16[208,512]{1,0:T(8,128)(2,1)S(1)} collective-permute-done((bf16[208,512]{1,0:T(8,128)(2,1)S(1)}, bf16[208,512]{1,0:T(8,128)(2,1)S(1)}, u32[]{:S(2)}, u32[]{:S(2)}) %collective-permute-start.16) | collective-permute-done | bytes 213024 | tf_op jit(solution)/shard_map/ppermute | solution.py:239
  100.5 3.7 %collective-permute-done.15.refs_1_ = bf16[208,512]{1,0:T(8,128)(2,1)S(1)} collective-permute-done((bf16[208,512]{1,0:T(8,128)(2,1)S(1)}, bf16[208,512]{1,0:T(8,128)(2,1)S(1)}, u32[]{:S(2)}, u32[]{:S(2)}) %collective-permute-start.15) | collective-permute-done | bytes 213024 | tf_op jit(solution)/shard_map/ppermute | solution.py:239
  104.2 0.7 copy-done.12
  104.9 0.9 copy-done.11
  105.8 0.9 copy-done.13
  106.8 21.7 %ffn.1 = (f32[192,1280]{1,0:T(8,128)S(1)}, bf16[192,1280]{1,0:T(8,128)(2,1)S(1)}, bf16[192,1280]{1,0:T(8,128)(2,1)S(1)}, bf16[192,1280]{1,0:T(8,128)(2,1)S(1)}, ...) custom-call(s32[3]{0:T(128)S(1)} %pad_add_fusion.place, ...), custom_call_target="tpu_custom_call" | custom-call | flops 8556380160 | bytes 16777216 | tf_op jit(solution)/shard_map/ffn/pallas_call | solution.py:49
  128.4 3.7 %collective-permute-done.25 = bf16[4,8,40,640]{3,2,1,0:T(8,128)(2,1)S(1)} collective-permute-done((bf16[4,8,40,640]{3,2,1,0:T(8,128)(2,1)}, bf16[4,8,40,640]{3,2,1,0:T(8,128)(2,1)S(1)}, u32[]{:S(2)}, u32[]{:S(2)}) %collective-permute-start.25) | collective-permute-done | bytes 1638432 | tf_op jit(solution)/shard_map/ppermute | solution.py:239
  132.1 3.0 %add_convert_fusion = bf16[4,8,40,640]{3,2,1,0:T(8,128)(2,1)} fusion(bf16[4,8,40,640]{3,2,1,0:T(8,128)(2,1)S(1)} %collective-permute-done.25, bf16[4,8,40,640]{3,2,1,0:T(8,128)(2,1)} %get-tuple-element.20), kind=kLoop, calls=%fused_computation | loop fusion | flops 3276800 | bytes 4915200 | tf_op jit(solution)/shard_map/convert_element_type | solution.py:322
  135.1 7.0 %all-to-all-start.1 = ((bf16[4,8,40,640]{3,2,1,0:T(8,128)(2,1)}), bf16[4,8,40,640]{3,2,1,0:T(8,128)(2,1)}, u32[]{:S(2)}, u32[]{:S(2)}) async-start(bf16[4,8,40,640]{3,2,1,0:T(8,128)(2,1)} %add_convert_fusion), calls=%async_computation.1 | async-start | bytes 3276800 | tf_op jit(solution)/shard_map/all_to_all | solution.py:322
  142.1 0.7 collective-permute-start.22
  142.8 1.8 collective-permute-start.23
  144.6 0.8 collective-permute-start.24
  145.4 17.4 %all-to-all-done.1 = bf16[4,8,40,640]{3,2,1,0:T(8,128)(2,1)} async-done(((bf16[4,8,40,640]{3,2,1,0:T(8,128)(2,1)}), bf16[4,8,40,640]{3,2,1,0:T(8,128)(2,1)}, u32[]{:S(2)}, u32[]{:S(2)}) %all-to-all-start.1) | async-done | bytes 1638432 | tf_op jit(solution)/shard_map/all_to_all | solution.py:322
  162.8 2.5 %reduce_sum.12 = bf16[8,40,640]{2,1,0:T(8,128)(2,1)} reduce(bf16[4,8,40,640]{3,2,1,0:T(8,128)(2,1)} %all-to-all-done.1, bf16[]{:T(256)} %constant.23.clone.1), dimensions={0}, to_apply=%region_0.0 | reduce | flops 614400 | bytes 2048002 | tf_op jit(solution)/shard_map/reduce_sum | solution.py:323
  165.3 4.1 %all-to-all-start.2 = ((bf16[8,40,640]{2,1,0:T(8,128)(2,1)}), bf16[8,40,640]{2,1,0:T(8,128)(2,1)S(1)}, u32[]{:S(2)}, u32[]{:S(2)}) async-start(bf16[8,40,640]{2,1,0:T(8,128)(2,1)} %reduce_sum.12), calls=%async_computation.2 | async-start | bytes 819200 | tf_op jit(solution)/shard_map/all_to_all | solution.py:324
  169.4 0.1 convert_reduce_fusion
  169.5 2.2 %multiply_convert_fusion = bf16[192,1280]{1,0:T(8,128)(2,1)} fusion(bf16[192,1280]{1,0:T(8,128)(2,1)} %collective-permute-done.24, bf16[192,1280]{1,0:T(8,128)(2,1)} %collective-permute-done.23, f32[192,1280]{1,0:T(8,128)S(1)} %get-tuple-element.15, bf16[192,1280]{1,0:T(8,128)(2,1)S(1)} %collective-permute-done.22, f32[192]{0:T(256)S(1)} %convert_reduce_fusion), kind=kLoop, calls=%fused_computation.1 | loop fusion | flops 1966080 | bytes 2949888 | tf_op jit(solution)/shard_map/convert_element_type | solution.py:319
  171.7 12.2 %all-to-all-done.2.arrived = bf16[8,40,640]{2,1,0:T(8,128)(2,1)S(1)} async-done(((bf16[8,40,640]{2,1,0:T(8,128)(2,1)}), bf16[8,40,640]{2,1,0:T(8,128)(2,1)S(1)}, u32[]{:S(2)}, u32[]{:S(2)}) %all-to-all-start.2) | async-done | bytes 409632 | tf_op jit(solution)/shard_map/all_to_all | solution.py:324
  183.9 0.8 last.1
  (51 shorter events, 0.3 us)
Async XLA Ops:
  7.2 20.3 %copy-start.14 = (bf16[128,512]{1,0:T(8,128)(2,1)S(1)}, bf16[128,512]{1,0:T(8,128)(2,1)}, u32[]{:S(2)}) copy-start(bf16[128,512]{1,0:T(8,128)(2,1)} %param.8) | copy-start | bytes 393220
  7.2 97.7 %all-gather.2.cloned.1.call-start = ((), (), s32[]{:S(2)}) async-start(), calls=%async_computation.3 | async-start | bytes 2457600 | tf_op jit(solution)/shard_map/all_gather | solution.py:249
  7.9 0.8 copy-start.7
  8.8 18.7 %collective-permute-start = (bf16[40,640]{1,0:T(8,128)(2,1)S(1)}, bf16[40,640]{1,0:T(8,128)(2,1)S(1)}, u32[]{:S(2)}, u32[]{:S(2)}) collective-permute-start(bf16[40,640]{1,0:T(8,128)(2,1)S(1)} %pack.1), channel_id=1, source_target_pairs={{0,1},{1,0},{2,3},{3,2},{4,5},{5,4},{6,7},{7,6},{8,9},{9,8},{10,11... | collective-permute-start | bytes 153608 | tf_op jit(solution)/shard_map/ppermute | solution.py:239
  10.8 25.1 %collective-permute-start.11 = (bf16[128,512]{1,0:T(8,128)(2,1)}, bf16[128,512]{1,0:T(8,128)(2,1)S(1)}, u32[]{:S(2)}, u32[]{:S(2)}) collective-permute-start(bf16[128,512]{1,0:T(8,128)(2,1)} %param.8), channel_id=1, source_target_pairs={{0,1},{1,0},{2,3},{3,2},{4,5},{5,4},{6,7},{7,6},{8,9},{9,8},{10,11... | collective-permute-start | bytes 393224 | tf_op jit(solution)/shard_map/ppermute | solution.py:239
  10.9 44.7 %collective-permute-start.18 = (bf16[64,1280]{1,0:T(8,128)(2,1)}, bf16[64,1280]{1,0:T(8,128)(2,1)}, u32[]{:S(2)}, u32[]{:S(2)}) collective-permute-start(bf16[64,1280]{1,0:T(8,128)(2,1)} %param.9), channel_id=1, source_target_pairs={{0,1},{1,0},{2,3},{3,2},{4,5},{5,4},{6,7},{7,6},{8,9},{9,8},{10,11... | collective-permute-start | bytes 491528 | tf_op jit(solution)/shard_map/ppermute | solution.py:239
  13.6 0.9 copy-start
  14.6 0.7 copy-start.8
  16.7 63.0 %all-to-all-start = ((bf16[32,8,1024]{2,1,0:T(8,128)(2,1)}), bf16[32,8,1024]{2,1,0:T(8,128)(2,1)S(1)}, u32[]{:S(2)}, u32[]{:S(2)}) async-start(bf16[32,8,1024]{2,1,0:T(8,128)(2,1)} %bitcast.9), calls=%async_computation | async-start | bytes 1048576 | tf_op jit(solution)/shard_map/all_to_all | solution.py:273
  27.5 27.5 %collective-permute-start.3 = (bf16[2,40,640]{2,1,0:T(8,128)(2,1)S(1)}, bf16[2,40,640]{2,1,0:T(8,128)(2,1)S(1)}, u32[]{:S(2)}, u32[]{:S(2)}) collective-permute-start(bf16[2,40,640]{2,1,0:T(8,128)(2,1)S(1)} %pad_maximum_fusion), channel_id=1, source_target_pairs={{0,192},{64,0},{128,64},{192,128},{1,193},{65,1},{129,65},{193,129... | collective-permute-start | bytes 307208 | tf_op jit(solution)/shard_map/ppermute | solution.py:239
  31.2 23.0 %collective-permute-start.2 = (bf16[2,40,640]{2,1,0:T(8,128)(2,1)S(1)}, bf16[2,40,640]{2,1,0:T(8,128)(2,1)S(1)}, u32[]{:S(2)}, u32[]{:S(2)}) collective-permute-start(bf16[2,40,640]{2,1,0:T(8,128)(2,1)S(1)} %pad_maximum_fusion), channel_id=1, source_target_pairs={{0,128},{64,192},{128,0},{192,64},{1,129},{65,193},{129,1},{193,65... | collective-permute-start | bytes 307208 | tf_op jit(solution)/shard_map/ppermute | solution.py:239
  33.5 17.4 %collective-permute-start.1 = (bf16[2,40,640]{2,1,0:T(8,128)(2,1)S(1)}, bf16[2,40,640]{2,1,0:T(8,128)(2,1)S(1)}, u32[]{:S(2)}, u32[]{:S(2)}) collective-permute-start(bf16[2,40,640]{2,1,0:T(8,128)(2,1)S(1)} %pad_maximum_fusion), channel_id=1, source_target_pairs={{0,64},{64,128},{128,192},{192,0},{1,65},{65,129},{129,193},{193,1... | collective-permute-start | bytes 307208 | tf_op jit(solution)/shard_map/ppermute | solution.py:239
  35.9 22.2 %collective-permute-start.14 = (bf16[256,512]{1,0:T(8,128)(2,1)S(1)}, bf16[256,512]{1,0:T(8,128)(2,1)S(1)}, u32[]{:S(2)}, u32[]{:S(2)}) collective-permute-start(bf16[256,512]{1,0:T(8,128)(2,1)S(1)} %constant_dynamic-update-slice_fusion.5.refs_0_), channel_id=1, source_target_pairs={{0,6},{2,0},{4,2},{6,4},{1,7},{3,1},{5,3},{7,5},{8,14},{10,8},{12,... | collective-permute-start | bytes 786440 | tf_op jit(solution)/shard_map/ppermute | solution.py:239
  50.9 10.7 %collective-permute-start.13 = (bf16[256,512]{1,0:T(8,128)(2,1)S(1)}, bf16[256,512]{1,0:T(8,128)(2,1)S(1)}, u32[]{:S(2)}, u32[]{:S(2)}) collective-permute-start(bf16[256,512]{1,0:T(8,128)(2,1)S(1)} %constant_dynamic-update-slice_fusion.5.refs_0_), channel_id=1, source_target_pairs={{0,4},{2,6},{4,0},{6,2},{1,5},{3,7},{5,1},{7,3},{8,12},{10,14},{12... | collective-permute-start | bytes 786440 | tf_op jit(solution)/shard_map/ppermute | solution.py:239
  54.2 11.7 %collective-permute-start.12 = (bf16[256,512]{1,0:T(8,128)(2,1)S(1)}, bf16[256,512]{1,0:T(8,128)(2,1)S(1)}, u32[]{:S(2)}, u32[]{:S(2)}) collective-permute-start(bf16[256,512]{1,0:T(8,128)(2,1)S(1)} %constant_dynamic-update-slice_fusion.5.refs_0_), channel_id=1, source_target_pairs={{0,2},{2,4},{4,6},{6,0},{1,3},{3,5},{5,7},{7,1},{8,10},{10,12},{12... | collective-permute-start | bytes 786440 | tf_op jit(solution)/shard_map/ppermute | solution.py:239
  55.0 12.1 %collective-permute-start.6 = (bf16[8,40,640]{2,1,0:T(8,128)(2,1)S(1)}, bf16[8,40,640]{2,1,0:T(8,128)(2,1)S(1)}, u32[]{:S(2)}, u32[]{:S(2)}) collective-permute-start(bf16[8,40,640]{2,1,0:T(8,128)(2,1)S(1)} %constant_dynamic-update-slice_fusion.refs_0_), channel_id=1, source_target_pairs={{0,48},{16,0},{32,16},{48,32},{1,49},{17,1},{33,17},{49,33},{2,50}... | collective-permute-start | bytes 1228808 | tf_op jit(solution)/shard_map/ppermute | solution.py:239
  55.7 19.6 %collective-permute-start.5 = (bf16[8,40,640]{2,1,0:T(8,128)(2,1)S(1)}, bf16[8,40,640]{2,1,0:T(8,128)(2,1)S(1)}, u32[]{:S(2)}, u32[]{:S(2)}) collective-permute-start(bf16[8,40,640]{2,1,0:T(8,128)(2,1)S(1)} %constant_dynamic-update-slice_fusion.refs_0_), channel_id=1, source_target_pairs={{0,32},{16,48},{32,0},{48,16},{1,33},{17,49},{33,1},{49,17},{2,34}... | collective-permute-start | bytes 1228808 | tf_op jit(solution)/shard_map/ppermute | solution.py:239
  58.1 18.1 %collective-permute-start.4 = (bf16[8,40,640]{2,1,0:T(8,128)(2,1)S(1)}, bf16[8,40,640]{2,1,0:T(8,128)(2,1)S(1)}, u32[]{:S(2)}, u32[]{:S(2)}) collective-permute-start(bf16[8,40,640]{2,1,0:T(8,128)(2,1)S(1)} %constant_dynamic-update-slice_fusion.refs_0_), channel_id=1, source_target_pairs={{0,16},{16,32},{32,48},{48,0},{1,17},{17,33},{33,49},{49,1},{2,18}... | collective-permute-start | bytes 1228808 | tf_op jit(solution)/shard_map/ppermute | solution.py:239
  61.6 0.7 copy-start.1
  62.3 16.1 %collective-permute-start.7 = (bf16[8,40,640]{2,1,0:T(8,128)(2,1)S(1)}, bf16[8,40,640]{2,1,0:T(8,128)(2,1)S(1)}, u32[]{:S(2)}, u32[]{:S(2)}) collective-permute-start(bf16[8,40,640]{2,1,0:T(8,128)(2,1)S(1)} %constant_dynamic-update-slice_fusion.refs_0_), channel_id=1, source_target_pairs={{0,8},{8,0},{1,9},{9,1},{2,10},{10,2},{3,11},{11,3},{4,12},{12,4},... | collective-permute-start | bytes 1228808 | tf_op jit(solution)/shard_map/ppermute | solution.py:239
  65.9 0.7 copy-start.3
  66.6 9.9 %collective-permute-start.21 = (bf16[128,1280]{1,0:T(8,128)(2,1)}, bf16[128,1280]{1,0:T(8,128)(2,1)}, u32[]{:S(2)}, u32[]{:S(2)}) collective-permute-start(bf16[128,1280]{1,0:T(8,128)(2,1)} %constant_dynamic-update-slice_fusion.7.refs_4_), channel_id=1, source_target_pairs={{0,6},{2,0},{4,2},{6,4},{1,7},{3,1},{5,3},{7,5},{8,14},{10,8},{12,... | collective-permute-start | bytes 983048 | tf_op jit(solution)/shard_map/ppermute | solution.py:239
  67.2 16.0 %collective-permute-start.10 = (bf16[8,40,640]{2,1,0:T(8,128)(2,1)S(1)}, bf16[8,40,640]{2,1,0:T(8,128)(2,1)S(1)}, u32[]{:S(2)}, u32[]{:S(2)}) collective-permute-start(bf16[8,40,640]{2,1,0:T(8,128)(2,1)S(1)} %collective-permute-done.6.refs_3_), channel_id=1, source_target_pairs={{0,8},{8,0},{1,9},{9,1},{2,10},{10,2},{3,11},{11,3},{4,12},{12,4},... | collective-permute-start | bytes 1228808 | tf_op jit(solution)/shard_map/ppermute | solution.py:239
  75.3 10.0 %collective-permute-start.9 = (bf16[8,40,640]{2,1,0:T(8,128)(2,1)S(1)}, bf16[8,40,640]{2,1,0:T(8,128)(2,1)}, u32[]{:S(2)}, u32[]{:S(2)}) collective-permute-start(bf16[8,40,640]{2,1,0:T(8,128)(2,1)S(1)} %collective-permute-done.5.refs_2_), channel_id=1, source_target_pairs={{0,8},{8,0},{1,9},{9,1},{2,10},{10,2},{3,11},{11,3},{4,12},{12,4},... | collective-permute-start | bytes 1228808 | tf_op jit(solution)/shard_map/ppermute | solution.py:239
  76.2 9.6 %collective-permute-start.8 = (bf16[8,40,640]{2,1,0:T(8,128)(2,1)S(1)}, bf16[8,40,640]{2,1,0:T(8,128)(2,1)}, u32[]{:S(2)}, u32[]{:S(2)}) collective-permute-start(bf16[8,40,640]{2,1,0:T(8,128)(2,1)S(1)} %collective-permute-done.4.refs_1_), channel_id=1, source_target_pairs={{0,8},{8,0},{1,9},{9,1},{2,10},{10,2},{3,11},{11,3},{4,12},{12,4},... | collective-permute-start | bytes 1228808 | tf_op jit(solution)/shard_map/ppermute | solution.py:239
  76.6 19.1 %collective-permute-start.20 = (bf16[128,1280]{1,0:T(8,128)(2,1)}, bf16[128,1280]{1,0:T(8,128)(2,1)}, u32[]{:S(2)}, u32[]{:S(2)}) collective-permute-start(bf16[128,1280]{1,0:T(8,128)(2,1)} %constant_dynamic-update-slice_fusion.7.refs_4_), channel_id=1, source_target_pairs={{0,4},{2,6},{4,0},{6,2},{1,5},{3,7},{5,1},{7,3},{8,12},{10,14},{12... | collective-permute-start | bytes 983048 | tf_op jit(solution)/shard_map/ppermute | solution.py:239
  78.4 17.6 %collective-permute-start.19 = (bf16[128,1280]{1,0:T(8,128)(2,1)}, bf16[128,1280]{1,0:T(8,128)(2,1)}, u32[]{:S(2)}, u32[]{:S(2)}) collective-permute-start(bf16[128,1280]{1,0:T(8,128)(2,1)} %constant_dynamic-update-slice_fusion.7.refs_4_), channel_id=1, source_target_pairs={{0,2},{2,4},{4,6},{6,0},{1,3},{3,5},{5,7},{7,1},{8,10},{10,12},{12... | collective-permute-start | bytes 983048 | tf_op jit(solution)/shard_map/ppermute | solution.py:239
  79.7 1.0 copy-start.2
  80.6 0.9 copy-start.4
  83.2 11.2 %copy-start.5 = (f32[192,1]{1,0:T(8,128)}, f32[192,1]{1,0:T(8,128)S(1)}, u32[]{:S(2)}) copy-start(f32[192,1]{1,0:T(8,128)S(1)} %get-tuple-element.19) | copy-start | bytes 2308
  83.2 11.2 %copy-start.10 = (bf16[208,512]{1,0:T(8,128)(2,1)}, bf16[208,512]{1,0:T(8,128)(2,1)S(1)}, u32[]{:S(2)}) copy-start(bf16[208,512]{1,0:T(8,128)(2,1)S(1)} %get-tuple-element.14.refs_0_) | copy-start | bytes 638980
  83.2 12.9 %collective-permute-start.17 = (bf16[208,512]{1,0:T(8,128)(2,1)S(1)}, bf16[208,512]{1,0:T(8,128)(2,1)S(1)}, u32[]{:S(2)}, u32[]{:S(2)}) collective-permute-start(bf16[208,512]{1,0:T(8,128)(2,1)S(1)} %get-tuple-element.14.refs_0_), channel_id=1, source_target_pairs={{0,6},{2,0},{4,2},{6,4},{1,7},{3,1},{5,3},{7,5},{8,14},{10,8},{12,... | collective-permute-start | bytes 638984 | tf_op jit(solution)/shard_map/ppermute | solution.py:239
  85.3 15.2 %collective-permute-start.16 = (bf16[208,512]{1,0:T(8,128)(2,1)S(1)}, bf16[208,512]{1,0:T(8,128)(2,1)S(1)}, u32[]{:S(2)}, u32[]{:S(2)}) collective-permute-start(bf16[208,512]{1,0:T(8,128)(2,1)S(1)} %get-tuple-element.14.refs_0_), channel_id=1, source_target_pairs={{0,4},{2,6},{4,0},{6,2},{1,5},{3,7},{5,1},{7,3},{8,12},{10,14},{12... | collective-permute-start | bytes 638984 | tf_op jit(solution)/shard_map/ppermute | solution.py:239
  85.8 18.4 %collective-permute-start.15 = (bf16[208,512]{1,0:T(8,128)(2,1)S(1)}, bf16[208,512]{1,0:T(8,128)(2,1)S(1)}, u32[]{:S(2)}, u32[]{:S(2)}) collective-permute-start(bf16[208,512]{1,0:T(8,128)(2,1)S(1)} %get-tuple-element.14.refs_0_), channel_id=1, source_target_pairs={{0,2},{2,4},{4,6},{6,0},{1,3},{3,5},{5,7},{7,1},{8,10},{10,12},{12... | collective-permute-start | bytes 638984 | tf_op jit(solution)/shard_map/ppermute | solution.py:239
  94.4 1.3 copy-start.9
  104.2 0.7 copy-start.12
  104.9 0.9 copy-start.11
  105.8 0.9 copy-start.13
  128.4 3.7 %collective-permute-start.25 = (bf16[4,8,40,640]{3,2,1,0:T(8,128)(2,1)}, bf16[4,8,40,640]{3,2,1,0:T(8,128)(2,1)S(1)}, u32[]{:S(2)}, u32[]{:S(2)}) collective-permute-start(bf16[4,8,40,640]{3,2,1,0:T(8,128)(2,1)} %get-tuple-element.21), channel_id=1, source_target_pairs={{0,8},{8,0},{1,9},{9,1},{2,10},{10,2},{3,11},{11,3},{4,12},{12,4},... | collective-permute-start | bytes 4915208 | tf_op jit(solution)/shard_map/ppermute | solution.py:239
  135.1 27.6 %all-to-all-start.1 = ((bf16[4,8,40,640]{3,2,1,0:T(8,128)(2,1)}), bf16[4,8,40,640]{3,2,1,0:T(8,128)(2,1)}, u32[]{:S(2)}, u32[]{:S(2)}) async-start(bf16[4,8,40,640]{3,2,1,0:T(8,128)(2,1)} %add_convert_fusion), calls=%async_computation.1 | async-start | bytes 3276800 | tf_op jit(solution)/shard_map/all_to_all | solution.py:322
  142.1 27.3 %copy-start.6 = (f32[192,1]{1,0:T(8,128)S(1)}, f32[192,1]{1,0:T(8,128)}, u32[]{:S(2)}) copy-start(f32[192,1]{1,0:T(8,128)} %copy-done.5) | copy-start | bytes 2308
  142.1 27.4 %collective-permute-start.22 = (bf16[192,1280]{1,0:T(8,128)(2,1)S(1)}, bf16[192,1280]{1,0:T(8,128)(2,1)S(1)}, u32[]{:S(2)}, u32[]{:S(2)}) collective-permute-start(bf16[192,1280]{1,0:T(8,128)(2,1)S(1)} %get-tuple-element.16), channel_id=1, source_target_pairs={{0,6},{2,0},{4,2},{6,4},{1,7},{3,1},{5,3},{7,5},{8,14},{10,8},{12,... | collective-permute-start | bytes 1474568 | tf_op jit(solution)/shard_map/ppermute | solution.py:239
  142.8 26.7 %collective-permute-start.23 = (bf16[192,1280]{1,0:T(8,128)(2,1)S(1)}, bf16[192,1280]{1,0:T(8,128)(2,1)}, u32[]{:S(2)}, u32[]{:S(2)}) collective-permute-start(bf16[192,1280]{1,0:T(8,128)(2,1)S(1)} %get-tuple-element.17), channel_id=1, source_target_pairs={{0,4},{2,6},{4,0},{6,2},{1,5},{3,7},{5,1},{7,3},{8,12},{10,14},{12... | collective-permute-start | bytes 1474568 | tf_op jit(solution)/shard_map/ppermute | solution.py:239
  144.6 24.9 %collective-permute-start.24 = (bf16[192,1280]{1,0:T(8,128)(2,1)S(1)}, bf16[192,1280]{1,0:T(8,128)(2,1)}, u32[]{:S(2)}, u32[]{:S(2)}) collective-permute-start(bf16[192,1280]{1,0:T(8,128)(2,1)S(1)} %get-tuple-element.18), channel_id=1, source_target_pairs={{0,2},{2,4},{4,6},{6,0},{1,3},{3,5},{5,7},{7,1},{8,10},{10,12},{12... | collective-permute-start | bytes 1474568 | tf_op jit(solution)/shard_map/ppermute | solution.py:239
  165.3 18.6 %all-to-all-start.2 = ((bf16[8,40,640]{2,1,0:T(8,128)(2,1)}), bf16[8,40,640]{2,1,0:T(8,128)(2,1)S(1)}, u32[]{:S(2)}, u32[]{:S(2)}) async-start(bf16[8,40,640]{2,1,0:T(8,128)(2,1)} %reduce_sum.12), calls=%async_computation.2 | async-start | bytes 819200 | tf_op jit(solution)/shard_map/all_to_all | solution.py:324
Sparse Core Ops, SparseCore 0:
  9.8 39.5 all-gather.1

commit v3 on v2

--- a/solution.py
+++ b/solution.py
@@ -28,6 +28,7 @@
 
 VMEM = pl.BlockSpec(memory_space=pltpu.VMEM)
 SMEM = pl.BlockSpec(memory_space=pltpu.SMEM)
+HBM = pl.BlockSpec(memory_space=pltpu.HBM)
 
 
 def dot(a, b, dims=((1,), (0,))):
@@ -45,11 +46,11 @@
     return centered * lax.rsqrt(variance + epsilon)
 
 
-def call(kernel, out_shape, args, flops, bytes_accessed, scratch=(), vmem=48 << 20, smem=0, name=None):
+def call(kernel, out_shape, args, flops, bytes_accessed, scratch=(), vmem=12 << 20, smem=0, hbm=0, name=None):
     return pl.pallas_call(
         kernel,
         out_shape=out_shape,
-        in_specs=[SMEM] * smem + [VMEM] * (len(args) - smem),
+        in_specs=[SMEM] * smem + [VMEM] * (len(args) - smem - hbm) + [HBM] * hbm,
         out_specs=jax.tree.map(lambda _: VMEM, out_shape),
         scratch_shapes=list(scratch),
         compiler_params=pltpu.CompilerParams(vmem_limit_bytes=vmem),
@@ -85,12 +86,12 @@
 
 def route_kernel(owner, live, rows, outgoing):
     count = rows.shape[0]
-    target = owner[...]
+    diagonal = iota((count, count), 0) == iota((count, count), 1)
+    target = jnp.sum(jnp.where(diagonal, owner[...], 0), axis=1, keepdims=True)
     onehot = (target == iota((count, 128), 1)).astype(f32)
     earlier = (iota((count, count), 1) < iota((count, count), 0)).astype(bf16)
     before = dot(earlier, onehot.astype(bf16))
     position = jnp.sum(before * onehot, axis=1, keepdims=True).astype(i32)
-    diagonal = iota((count, count), 0) == iota((count, count), 1)
     state = 1.0 + jnp.sum(
         jnp.where(diagonal, live[...].astype(f32), 0.0), axis=1, keepdims=True
     )
@@ -105,14 +106,18 @@
 
 
 def front_kernel(place, incoming, *refs):
-    pieces, (block, flags_out, conv) = refs[:4], refs[4:]
+    pieces, (block, flags_out, conv, arrival) = refs[:8], refs[8:]
     y, zl = place[0], place[1]
+    copies = []
     for step in range(4):
         for other in range(2):
+            k = step * 2 + other
             start = lax.rem(y - step + 4, 4) * 256 + lax.rem(zl + other, 2) * 128
-            conv[pl.ds(pl.multiple_of(start, 128), 128), :] = pieces[step][
-                other * 128 : other * 128 + 128, :
-            ]
+            rows = pl.ds(pl.multiple_of(start, 128), 128)
+            copies.append(pltpu.make_async_copy(pieces[k], conv.at[rows, :], arrival.at[k]))
+            copies[-1].start()
+    for copy in copies:
+        copy.wait()
     raw = incoming[...]
     conv_out = dot(raw, conv[...])
     active = 0.5 * conv_out * (1.0 + lax.erf(conv_out * 0.7071067811865476))
@@ -135,53 +140,74 @@
 
 def weights_kernel(place, *refs):
     pieces, (up, down, wide_up, wide_down) = refs[:8], refs[8:]
-    zh, x, c, zl = place[0], place[1], place[2], place[3]
+    z, x, c = place[0], place[1], place[2]
     for core in range(2):
         for step in range(4):
             piece = pieces[core * 4 + step]
             base = lax.rem(x - step + 4, 4) * 80 + lax.rem(c + core, 2) * 40
 
             def one(k, carry):
-                row = lax.rem(zh - k // 2 + 4, 4) * 320 + base
-                half = lax.rem(zl + k, 2)
+                there = lax.rem(z - k + 8, 8)
+                row = (there // 2) * 320 + base
+                half = lax.rem(there, 2)
                 rows = pl.ds(pl.multiple_of(row, 8), BLOCK)
                 a, b = unpack_pair(piece[k].astype(f32))
                 wide_up[half, rows, :] = a
                 wide_down[half, rows, :] = b
                 return carry
 
-            lax.fori_loop(0, 8, one, 0)
+            lax.fori_loop(0, 8, one, 0, unroll=True)
     for half in range(2):
         up[:, half * LANES : (half + 1) * LANES] = wide_up[half].astype(bf16)
         down[:, half * LANES : (half + 1) * LANES] = wide_down[half].astype(bf16)
 
 
-def ffn_kernel(place, cot, up, down, *refs):
+def ffn_kernel(place, cot_in, up_in, down_in, *refs):
     blocks, protos, refs = refs[:4], refs[4:8], refs[8:]
     own, away1, away2, away3, kept, sent, refs = *refs[:6], refs[6:]
-    proj, feats, live, normed, hidden, grad_pre, grad_out, wide_up, wide_down = refs
+    proj, feats, live, normed, hidden, grad_pre, grad_out, wide_up, wide_down, *refs = refs
+    cot, up, down, arrival = refs
     y, zl, c = place[0], place[1], place[2]
+    copies = []
+
+    def fetch(source, target):
+        copy = pltpu.make_async_copy(source, target, arrival.at[len(copies)])
+        copy.start()
+        copies.append(copy)
+
+    for step in range(4):
+        fetch(blocks[step], feats.at[step])
     for step in range(4):
         for other in range(2):
             start = lax.rem(y - step + 4, 4) * 128 + lax.rem(zl + other, 2) * 64
-            proj[pl.ds(pl.multiple_of(start, 64), 64), :] = protos[step][
-                other * 64 : other * 64 + 64, :
-            ]
-        feats[step] = blocks[step][:SLOTS, :]
-        flags = blocks[step][SLOTS : SLOTS + 16, :].astype(f32)[:1, :]
+            rows = pl.ds(pl.multiple_of(start, 64), 64)
+            fetch(protos[step].at[pl.ds(other * 64, 64), :], proj.at[rows, :])
+    fetch(up_in, up)
+    fetch(down_in, down)
+    fetch(cot_in, cot)
+    for copy in copies[:13]:
+        copy.wait()
+    for step in range(4):
+        flags = feats[step, SLOTS : SLOTS + 16, :].astype(f32)[:1, :]
         wide = iota((SLOTS, CH), 1) == iota((SLOTS, CH), 0)
         flags = jnp.sum(jnp.where(wide, flags, 0.0), axis=1, keepdims=True)
         live[step] = (flags == 2.0).astype(f32)
 
     def forward(step, carry):
         rows = pl.ds(pl.multiple_of(step * SLOTS, SLOTS), SLOTS)
-        stream = dot(feats[step], proj[...]).astype(bf16).astype(f32)
+        stream = dot(feats[step, :SLOTS, :], proj[...]).astype(bf16).astype(f32)
         normed[rows, :] = normalize(stream).astype(bf16)
         pre = dot(normed[rows, :], up[...])
         cumulative = 0.5 * (1.0 + lax.erf(pre * 0.7071067811865476))
         density = jnp.exp(-0.5 * pre * pre) * 0.3989422804014327
         hidden[rows, :] = (pre * cumulative).astype(bf16)
         slope = cumulative + pre * density
+
+        @pl.when(step == 0)
+        def _():
+            copies[13].wait()
+            copies[14].wait()
+
         partial = dot(hidden[rows, :], down[...], ((1,), (1,)))
 
         @pl.when(step == 0)
@@ -226,6 +252,20 @@
     lax.fori_loop(0, 2, backward, 0)
 
 
+def core_sum_kernel(place, kept, arrived, *outs):
+    x = place[0]
+    for step, out in enumerate(outs):
+        there = lax.rem(x + step, 4)
+        out[...] = (kept[there].astype(f32) + arrived[there].astype(f32)).astype(bf16)
+
+
+def x_sum_kernel(*refs):
+    total = refs[0][...].astype(f32)
+    for ref in refs[1:-1]:
+        total = total + ref[...].astype(f32)
+    refs[-1][...] = total.astype(bf16)
+
+
 def last_kernel(arrived, out):
     total = arrived[0].astype(f32)
     for k in range(1, 8):
@@ -243,6 +283,15 @@
     return [values] + [ring(values, axis, size, step) for step in range(1, size)]
 
 
+def grid(values):
+    pieces = []
+    for step in range(8):
+        dy, dz = step // 2, step % 2
+        order = [(k, ((k // 2 + dy) % 4) * 2 + (k % 2 ^ dz)) for k in range(8)]
+        pieces.append(lax.ppermute(values, ("y", "zl"), order) if step else values)
+    return pieces
+
+
 def per_device(waveform_rows, conv_weight, proj_weight, ffn_pair, owner, frame_live, cotangent):
     dp = ("zh", "x", "c")
     zh, x, c, y, zl = (lax.axis_index(name).astype(i32) for name in ("zh", "x", "c", "y", "zl"))
@@ -254,20 +303,17 @@
         [jnp.transpose(ffn_pair, (1, 2, 0))],
         1 << 16, 1 << 17, name="pack",
     )
-    both = jnp.stack([packed, ring(packed, "zl", 2, 1)])
-    along_z = jnp.concatenate(around(both, "zh", 4), axis=0)
+    conv_pieces = grid(conv_weight)
+    along_z = jnp.stack(around(packed, ZX, 8))
     along_x = around(along_z, "x", 4)
-    pieces = along_x + [ring(piece, "c", 2, 1) for piece in along_x]
-
-    conv_pair = jnp.concatenate([conv_weight, ring(conv_weight, "zl", 2, 1)], axis=0)
-    conv_pieces = around(conv_pair, "y", 4)
+    proj_weight, _ = lax.optimization_barrier((proj_weight, conv_pieces[-1]))
     proj_pair = jnp.concatenate([proj_weight, ring(proj_weight, "zl", 2, 1)], axis=0)
     proj_pieces = around(proj_pair, "y", 4)
 
     outgoing = call(
         route_kernel,
         jax.ShapeDtypeStruct((N_DP * PAD, 1024), bf16),
-        [owner, frame_live.reshape(1, -1), waveform_rows],
+        [owner.reshape(1, -1), frame_live.reshape(1, -1), waveform_rows],
         2 * 256 * 128 * 1152, 1 << 20, name="route",
     )
     incoming = lax.all_to_all(
@@ -282,16 +328,19 @@
         ),
         [jnp.stack([y, zl]), incoming, *conv_pieces],
         2 * 256 * 1024 * 512, 2 << 20,
-        scratch=[pltpu.VMEM((1024, CH), bf16)], smem=1, name="front",
+        scratch=[pltpu.VMEM((1024, CH), bf16), pltpu.SemaphoreType.DMA((8,))],
+        smem=1, hbm=8, name="front",
     )
     blocks = around(block, "y", 4)
+    block, *along_x = lax.optimization_barrier((block, *along_x))
+    pieces = along_x + [ring(piece, "c", 2, 1) for piece in along_x]
 
     up, down = call(
         weights_kernel,
         (jax.ShapeDtypeStruct((D, WIDE), bf16),) * 2,
-        [jnp.stack([zh, x, c, zl]), *pieces],
+        [jnp.stack([zh * 2 + zl, x, c]), *pieces],
         1 << 22, 8 << 20,
-        scratch=[pltpu.VMEM((2, D, LANES), f32)] * 2, smem=1, name="weights",
+        scratch=[pltpu.VMEM((2, D, LANES), f32)] * 2, vmem=24 << 20, smem=1, name="weights",
     )
     rows = 4 * SLOTS
     piece = jax.ShapeDtypeStruct((SLOTS, D), bf16)
@@ -303,7 +352,7 @@
         2 * rows * D * (CH + 5 * WIDE), 16 << 20,
         scratch=[
             pltpu.VMEM((CH, D), bf16),
-            pltpu.VMEM((4, SLOTS, CH), bf16),
+            pltpu.VMEM((4, SLOTS + 16, CH), bf16),
             pltpu.VMEM((4, SLOTS, 1), f32),
             pltpu.VMEM((rows, D), bf16),
             pltpu.VMEM((rows, WIDE), bf16),
@@ -311,16 +360,30 @@
             pltpu.VMEM((rows, D), bf16),
             pltpu.VMEM((640, WIDE), f32),
             pltpu.VMEM((640, WIDE), f32),
+            pltpu.VMEM((rows, D), bf16),
+            pltpu.VMEM((D, WIDE), bf16),
+            pltpu.VMEM((D, WIDE), bf16),
+            pltpu.SemaphoreType.DMA((15,)),
         ],
-        smem=1, name="ffn",
-    )
+        vmem=36 << 20, smem=1, hbm=11, name="ffn",
+    )
+    tile = jax.ShapeDtypeStruct((8, BLOCK, 2 * UNITS), bf16)
+    parts = call(
+        core_sum_kernel,
+        (tile,) * 4,
+        [x[None], kept, ring(sent, "c", 2, 1)],
+        1 << 20, 5 << 20, smem=1, name="core_sum",
+    )
+    total = call(
+        x_sum_kernel,
+        tile,
+        [parts[0]] + [ring(parts[step], "x", 4, step) for step in range(1, 4)],
+        1 << 20, 2 << 20, name="x_sum",
+    )
+    away1, away2, away3, _ = lax.optimization_barrier((away1, away2, away3, parts[0]))
     for step, away in ((1, away1), (2, away2), (3, away3)):
         own = own + ring(away, "y", 4, 4 - step).astype(f32)
     encoded = (own * (flags > 0).astype(f32)).astype(bf16)
-
-    total = kept.astype(f32) + ring(sent, "c", 2, 1).astype(f32)
-    total = lax.all_to_all(total.astype(bf16), "x", split_axis=0, concat_axis=0, tiled=True)
-    total = jnp.sum(total.astype(f32), axis=0).astype(bf16)
     total = lax.all_to_all(total, ZX, split_axis=0, concat_axis=0, tiled=True)
     grad_pair = call(
         last_kernel,

time: 192 us -> 221 us (1.15)
  waiting for transfers between devices: 65.8 us -> 81.4 us
  starting transfers between devices: 56.3 us -> 70.7 us
  local copies, waits for them, and re-layouts: 13.6 us -> 21.2 us
  other arithmetic: 8.11 us -> 2.53 us
  Pallas kernels: 33.4 us -> 29.8 us
    ppermute x26 -> x28, waiting for transfers between devices: 35.6 us -> 59.6 us  [ring(): lax.ppermute(values, axis, [(k, (k + step) % size) for k in range(size)])]
    all_to_all x1 -> x0, waiting for transfers between devices: 17.4 us -> none  [per_device(): lax.all_to_all(total.astype(bf16), 'x', split_axis=0, concat_axis=0, tile...]
    ppermute x0 -> x7, starting transfers between devices: none -> 16.1 us  [grid(): pieces.append(lax.ppermute(values, ('y', 'zl'), order) if step else values)]
    ppermute x0 -> x7, waiting for transfers between devices: none -> 8.85 us  [grid(): pieces.append(lax.ppermute(values, ('y', 'zl'), order) if step else values)]
    unnamed x37 -> x52, local copies, waits for them, and re-layouts: 12 us -> 19.6 us
    ppermute x26 -> x28, starting transfers between devices: 34.5 us -> 41.7 us  [ring(): lax.ppermute(values, axis, [(k, (k + step) % size) for k in range(size)])]
    all_to_all x1 -> x0, starting transfers between devices: 6.98 us -> none  [per_device(): lax.all_to_all(total.astype(bf16), 'x', split_axis=0, concat_axis=0, tile...]
    all_to_all x1, starting transfers between devices: 10.7 us -> 5.87 us  [per_device(): lax.all_to_all(outgoing.reshape(N_DP, PAD, 1024), dp, split_axis=0, conca...]
  transfers between devices with their start and end apart: 30 -> 38, of which waited for: 12 -> 14; matrix products, arithmetic and copies ran while one was open for 5% -> 2% of each run, Pallas kernels for 6% -> 3%
where the time goes in v3:
time: 221 us; the launch traced here: 220 us
  waiting for transfers between devices  81.4 us (37%)
  starting transfers between devices  70.7 us (32%)
  Pallas kernels  29.8 us (13%)
  local copies, waits for them, and re-layouts  21.2 us (10%)
  between operations  14.3 us (6%)
  other arithmetic  2.53 us (1%)
    ppermute x28, waiting for transfers between devices, ring(): lax.ppermute(values, axis, [(k, (k + step) % size) for k in range(size)])  59.6 us
    ppermute x28, starting transfers between devices, ring(): lax.ppermute(values, axis, [(k, (k + step) % size) for k in range(size)])  41.7 us
    pallas_call x8, Pallas kernels, call(): pl.pallas_call(kernel, out_shape=out_shape, in_specs=[SMEM] * smem + [VME...  29.8 us
    unnamed x52, local copies, waits for them, and re-layouts  19.6 us
    ppermute x7, starting transfers between devices, grid(): pieces.append(lax.ppermute(values, ('y', 'zl'), order) if step else values)  16.1 us
    all_to_all x1, waiting for transfers between devices, per_device(): total = lax.all_to_all(total, ZX, split_axis=0, concat_axis=0, tiled=True)  12.9 us
    ppermute x7, waiting for transfers between devices, grid(): pieces.append(lax.ppermute(values, ('y', 'zl'), order) if step else values)  8.85 us
    all_to_all x1, starting transfers between devices, per_device(): total = lax.all_to_all(total, ZX, split_axis=0, concat_axis=0, tiled=True)  6.95 us
  transfers between devices with their start and end apart: 38, of which 14 were waited for; matrix products, arithmetic and copies ran while one was open for 2% of the time, Pallas kernels for 3%

profile of v3, /device:TPU:2, one launch (start us, length us, event | category | flops | bytes accessed | tf_op | source)
XLA Modules:
  0.0 219.9 jit_solution(9985887792674481852)
XLA Ops:
  7.2 0.8 copy-done.3
  8.2 5.9 %collective-permute-start.13 = (bf16[40,640]{1,0:T(8,128)(2,1)S(1)}, bf16[40,640]{1,0:T(8,128)(2,1)S(1)}, u32[]{:S(2)}, u32[]{:S(2)}) collective-permute-start(bf16[40,640]{1,0:T(8,128)(2,1)S(1)} %pack.1), channel_id=1, source_target_pairs={{0,193},{1,0},{64,1},{65,64},{128,65},{129,128},{192,129},{193,192... | collective-permute-start | bytes 153608 | tf_op jit(solution)/shard_map/ppermute | solution.py:279
  14.1 1.5 collective-permute-start.12
  16.0 5.0 %collective-permute-start.10 = (bf16[40,640]{1,0:T(8,128)(2,1)S(1)}, bf16[40,640]{1,0:T(8,128)(2,1)S(1)}, u32[]{:S(2)}, u32[]{:S(2)}) collective-permute-start(bf16[40,640]{1,0:T(8,128)(2,1)S(1)} %pack.1), channel_id=1, source_target_pairs={{0,128},{1,129},{64,192},{65,193},{128,0},{129,1},{192,64},{193,65... | collective-permute-start | bytes 153608 | tf_op jit(solution)/shard_map/ppermute | solution.py:279
  21.0 1.0 collective-permute-start.7
  22.1 0.9 copy-done
  24.3 1.5 route.1
  25.8 5.9 %all-to-all-start = ((bf16[32,8,1024]{2,1,0:T(8,128)(2,1)}), bf16[32,8,1024]{2,1,0:T(8,128)(2,1)S(1)}, u32[]{:S(2)}, u32[]{:S(2)}) async-start(bf16[32,8,1024]{2,1,0:T(8,128)(2,1)} %bitcast.7), calls=%async_computation | async-start | bytes 1048576 | tf_op jit(solution)/shard_map/all_to_all | solution.py:319
  31.7 2.4 %collective-permute-start.8 = (bf16[40,640]{1,0:T(8,128)(2,1)S(1)}, bf16[40,640]{1,0:T(8,128)(2,1)S(1)}, u32[]{:S(2)}, u32[]{:S(2)}) collective-permute-start(bf16[40,640]{1,0:T(8,128)(2,1)S(1)} %pack.1), channel_id=1, source_target_pairs={{0,64},{1,65},{64,128},{65,129},{128,192},{129,193},{192,0},{193,1... | collective-permute-start | bytes 153608 | tf_op jit(solution)/shard_map/ppermute | solution.py:279
  34.2 11.6 %collective-permute-done.8 = bf16[40,640]{1,0:T(8,128)(2,1)S(1)} collective-permute-done((bf16[40,640]{1,0:T(8,128)(2,1)S(1)}, bf16[40,640]{1,0:T(8,128)(2,1)S(1)}, u32[]{:S(2)}, u32[]{:S(2)}) %collective-permute-start.8) | collective-permute-done | bytes 51232 | tf_op jit(solution)/shard_map/ppermute | solution.py:279
  45.7 4.3 %collective-permute-start.9 = (bf16[40,640]{1,0:T(8,128)(2,1)S(1)}, bf16[40,640]{1,0:T(8,128)(2,1)S(1)}, u32[]{:S(2)}, u32[]{:S(2)}) collective-permute-start(bf16[40,640]{1,0:T(8,128)(2,1)S(1)} %pack.1), channel_id=1, source_target_pairs={{0,65},{1,128},{64,129},{65,192},{128,193},{129,0},{192,1},{193,64... | collective-permute-start | bytes 153608 | tf_op jit(solution)/shard_map/ppermute | solution.py:279
  50.1 4.7 %collective-permute-done.9 = bf16[40,640]{1,0:T(8,128)(2,1)S(1)} collective-permute-done((bf16[40,640]{1,0:T(8,128)(2,1)S(1)}, bf16[40,640]{1,0:T(8,128)(2,1)S(1)}, u32[]{:S(2)}, u32[]{:S(2)}) %collective-permute-start.9) | collective-permute-done | bytes 51232 | tf_op jit(solution)/shard_map/ppermute | solution.py:279
  54.8 3.0 %collective-permute-start.5 = (bf16[128,512]{1,0:T(8,128)(2,1)S(1)}, bf16[128,512]{1,0:T(8,128)(2,1)S(1)}, u32[]{:S(2)}, u32[]{:S(2)}) collective-permute-start(bf16[128,512]{1,0:T(8,128)(2,1)S(1)} %copy-done.1), channel_id=1, source_target_pairs={{0,6},{1,7},{2,0},{3,1},{4,2},{5,3},{6,4},{7,5},{8,14},{9,15},{10,... | collective-permute-start | bytes 393224 | tf_op jit(solution)/shard_map/ppermute | solution.py:291
  57.8 4.1 %collective-permute-start.4 = (bf16[128,512]{1,0:T(8,128)(2,1)S(1)}, bf16[128,512]{1,0:T(8,128)(2,1)S(1)}, u32[]{:S(2)}, u32[]{:S(2)}) collective-permute-start(bf16[128,512]{1,0:T(8,128)(2,1)S(1)} %copy-done.1), channel_id=1, source_target_pairs={{0,5},{1,4},{2,7},{3,6},{4,1},{5,0},{6,3},{7,2},{8,13},{9,12},{10,... | collective-permute-start | bytes 393224 | tf_op jit(solution)/shard_map/ppermute | solution.py:291
  61.9 3.1 %collective-permute-start.3 = (bf16[128,512]{1,0:T(8,128)(2,1)S(1)}, bf16[128,512]{1,0:T(8,128)(2,1)S(1)}, u32[]{:S(2)}, u32[]{:S(2)}) collective-permute-start(bf16[128,512]{1,0:T(8,128)(2,1)S(1)} %copy-done.1), channel_id=1, source_target_pairs={{0,4},{1,5},{2,6},{3,7},{4,0},{5,1},{6,2},{7,3},{8,12},{9,13},{10,... | collective-permute-start | bytes 393224 | tf_op jit(solution)/shard_map/ppermute | solution.py:291
  65.2 1.0 collective-permute-start.16
  66.1 2.5 %collective-permute-start.15 = (bf16[8,40,640]{2,1,0:T(8,128)(2,1)S(1)}, bf16[8,40,640]{2,1,0:T(8,128)(2,1)S(1)}, u32[]{:S(2)}, u32[]{:S(2)}) collective-permute-start(bf16[8,40,640]{2,1,0:T(8,128)(2,1)S(1)} %bitcast_dynamic-update-slice_fusion.refs_0_), channel_id=1, source_target_pairs={{0,32},{16,48},{32,0},{48,16},{1,33},{17,49},{33,1},{49,17},{2,34}... | collective-permute-start | bytes 1228808 | tf_op jit(solution)/shard_map/ppermute | solution.py:279
  68.6 1.8 collective-permute-start.14
  70.4 3.6 %collective-permute-start.2 = (bf16[128,512]{1,0:T(8,128)(2,1)S(1)}, bf16[128,512]{1,0:T(8,128)(2,1)S(1)}, u32[]{:S(2)}, u32[]{:S(2)}) collective-permute-start(bf16[128,512]{1,0:T(8,128)(2,1)S(1)} %copy-done.1), channel_id=1, source_target_pairs={{0,3},{1,2},{2,5},{3,4},{4,7},{5,6},{6,1},{7,0},{8,11},{9,10},{10,... | collective-permute-start | bytes 393224 | tf_op jit(solution)/shard_map/ppermute | solution.py:291
  74.0 1.4 collective-permute-start.1
  75.5 6.6 %collective-permute-done.2.refs_3_ = bf16[128,512]{1,0:T(8,128)(2,1)S(1)} collective-permute-done((bf16[128,512]{1,0:T(8,128)(2,1)S(1)}, bf16[128,512]{1,0:T(8,128)(2,1)S(1)}, u32[]{:S(2)}, u32[]{:S(2)}) %collective-permute-start.2) | collective-permute-done | bytes 131104 | tf_op jit(solution)/shard_map/ppermute | solution.py:291
  82.0 0.8 collective-permute-start
  82.8 1.2 collective-permute-start.24
  84.8 2.3 %collective-permute-done.refs_1_ = bf16[128,512]{1,0:T(8,128)(2,1)S(1)} collective-permute-done((bf16[128,512]{1,0:T(8,128)(2,1)S(1)}, bf16[128,512]{1,0:T(8,128)(2,1)S(1)}, u32[]{:S(2)}, u32[]{:S(2)}) %collective-permute-start) | collective-permute-done | bytes 131104 | tf_op jit(solution)/shard_map/ppermute | solution.py:291
  87.0 3.0 %front.1 = (bf16[208,512]{1,0:T(8,128)(2,1)S(1)}, f32[192,1]{1,0:T(8,128)S(1)}) custom-call(s32[2]{0:T(128)S(1)} %pad_add_fusion.place, bf16[256,1024]{1,0:T(8,128)(2,1)S(1)} %bitcast.27, bf16[128,512]{1,0:T(8,128)(2,1)S(1)} %copy-done.1, bf16[128,512]{1,0:T(8,128)(2,1)S(1)} %collective-permute-done.refs_1_, ...), custom_call_target="tpu_custom_call" | custom-call | flops 268435456 | bytes 2097152 | tf_op jit(solution)/shard_map/front/pallas_call | solution.py:50
  90.1 1.6 constant_dynamic-update-slice_fusion.refs_4_
  91.7 1.5 collective-permute-start.27
  93.9 8.1 %collective-permute-done.27.refs_7_ = bf16[128,1280]{1,0:T(8,128)(2,1)S(1)} collective-permute-done((bf16[128,1280]{1,0:T(8,128)(2,1)}, bf16[128,1280]{1,0:T(8,128)(2,1)S(1)}, u32[]{:S(2)}, u32[]{:S(2)}) %collective-permute-start.27) | collective-permute-done | bytes 327712 | tf_op jit(solution)/shard_map/ppermute | solution.py:279
  102.0 0.7 copy-done.11
  102.8 1.2 collective-permute-start.26
  104.0 2.3 %collective-permute-start.25 = (bf16[128,1280]{1,0:T(8,128)(2,1)}, bf16[128,1280]{1,0:T(8,128)(2,1)}, u32[]{:S(2)}, u32[]{:S(2)}) collective-permute-start(bf16[128,1280]{1,0:T(8,128)(2,1)} %constant_dynamic-update-slice_fusion.refs_4_), channel_id=1, source_target_pairs={{0,2},{2,4},{4,6},{6,0},{1,3},{3,5},{5,7},{7,1},{8,10},{10,12},{12... | collective-permute-start | bytes 983048 | tf_op jit(solution)/shard_map/ppermute | solution.py:279
  106.3 0.9 collective-permute-start.23
  107.2 1.3 collective-permute-start.22
  108.8 1.9 weights.1
  110.7 1.3 copy-done.7
  112.0 1.3 copy-done.9
  113.4 1.9 collective-permute-done.26.refs_6_
  115.2 7.1 %collective-permute-done.25.refs_5_ = bf16[128,1280]{1,0:T(8,128)(2,1)} collective-permute-done((bf16[128,1280]{1,0:T(8,128)(2,1)}, bf16[128,1280]{1,0:T(8,128)(2,1)}, u32[]{:S(2)}, u32[]{:S(2)}) %collective-permute-start.25) | collective-permute-done | bytes 327712 | tf_op jit(solution)/shard_map/ppermute | solution.py:279
  122.3 0.7 copy-done.15
  123.0 3.7 %collective-permute-done.22.refs_2_ = bf16[208,512]{1,0:T(8,128)(2,1)S(1)} collective-permute-done((bf16[208,512]{1,0:T(8,128)(2,1)}, bf16[208,512]{1,0:T(8,128)(2,1)S(1)}, u32[]{:S(2)}, u32[]{:S(2)}) %collective-permute-start.22) | collective-permute-done | bytes 213024 | tf_op jit(solution)/shard_map/ppermute | solution.py:279
  127.4 2.5 %collective-permute-done.21.refs_1_ = bf16[208,512]{1,0:T(8,128)(2,1)S(1)} collective-permute-done((bf16[208,512]{1,0:T(8,128)(2,1)}, bf16[208,512]{1,0:T(8,128)(2,1)S(1)}, u32[]{:S(2)}, u32[]{:S(2)}) %collective-permute-start.21) | collective-permute-done | bytes 213024 | tf_op jit(solution)/shard_map/ppermute | solution.py:279
  130.6 1.0 copy-done.2
  131.6 1.5 copy-done.6
  133.2 1.5 copy-done.8
  134.7 1.5 copy-done.10
  136.3 1.0 copy-done.12
  137.2 0.9 copy-done.14
  138.2 0.9 copy-done.16
  139.1 0.9 copy-done.18
  140.0 0.9 copy-done.20
  141.0 21.3 %ffn.1 = (f32[192,1280]{1,0:T(8,128)S(1)}, bf16[192,1280]{1,0:T(8,128)(2,1)S(1)}, bf16[192,1280]{1,0:T(8,128)(2,1)S(1)}, bf16[192,1280]{1,0:T(8,128)(2,1)S(1)}, ...) custom-call(s32[3]{0:T(128)S(1)} %add_add_fusion.place, bf16[768,1280]{1,0:T(8,128)(2,1)S(1)} %copy-done.6, ...), custom_call_target="tpu_custom_call" | custom-call | flops 8556380160 | bytes 16777216 | tf_op jit(solution)/shard_map/ffn/pallas_call | solution.py:50
  162.4 3.5 %collective-permute-done.28.arrived = bf16[4,8,40,640]{3,2,1,0:T(8,128)(2,1)S(1)} collective-permute-done((bf16[4,8,40,640]{3,2,1,0:T(8,128)(2,1)S(1)}, bf16[4,8,40,640]{3,2,1,0:T(8,128)(2,1)S(1)}, u32[]{:S(2)}, u32[]{:S(2)}) %collective-permute-start.28) | collective-permute-done | bytes 1638432 | tf_op jit(solution)/shard_map/ppermute | solution.py:279
  166.3 1.3 collective-permute-start.32
  167.6 2.1 collective-permute-start.33
  169.7 1.8 collective-permute-start.34
  171.5 0.9 collective-permute-start.29
  172.6 6.0 %collective-permute-done.32.refs_1_ = bf16[8,40,640]{2,1,0:T(8,128)(2,1)S(1)} collective-permute-done((bf16[8,40,640]{2,1,0:T(8,128)(2,1)S(1)}, bf16[8,40,640]{2,1,0:T(8,128)(2,1)S(1)}, u32[]{:S(2)}, u32[]{:S(2)}) %collective-permute-start.32) | collective-permute-done | bytes 409632 | tf_op jit(solution)/shard_map/ppermute | solution.py:279
  178.7 2.8 %collective-permute-done.33.refs_2_ = bf16[8,40,640]{2,1,0:T(8,128)(2,1)S(1)} collective-permute-done((bf16[8,40,640]{2,1,0:T(8,128)(2,1)S(1)}, bf16[8,40,640]{2,1,0:T(8,128)(2,1)S(1)}, u32[]{:S(2)}, u32[]{:S(2)}) %collective-permute-start.33) | collective-permute-done | bytes 409632 | tf_op jit(solution)/shard_map/ppermute | solution.py:279
  181.5 7.6 %collective-permute-done.34.refs_3_ = bf16[8,40,640]{2,1,0:T(8,128)(2,1)S(1)} collective-permute-done((bf16[8,40,640]{2,1,0:T(8,128)(2,1)S(1)}, bf16[8,40,640]{2,1,0:T(8,128)(2,1)S(1)}, u32[]{:S(2)}, u32[]{:S(2)}) %collective-permute-start.34) | collective-permute-done | bytes 409632 | tf_op jit(solution)/shard_map/ppermute | solution.py:279
  189.1 1.0 x_sum.1
  190.1 6.9 %all-to-all-start.1 = ((bf16[8,40,640]{2,1,0:T(8,128)(2,1)}), bf16[8,40,640]{2,1,0:T(8,128)(2,1)S(1)}, u32[]{:S(2)}, u32[]{:S(2)}) async-start(bf16[8,40,640]{2,1,0:T(8,128)(2,1)} %x_sum.1), calls=%async_computation.1 | async-start | bytes 819200 | tf_op jit(solution)/shard_map/all_to_all | solution.py:387
  197.2 2.2 %multiply_convert_fusion = bf16[192,1280]{1,0:T(8,128)(2,1)} fusion(bf16[192,1280]{1,0:T(8,128)(2,1)} %collective-permute-done.31, bf16[192,1280]{1,0:T(8,128)(2,1)} %collective-permute-done.30, f32[192,1280]{1,0:T(8,128)S(1)} %get-tuple-element.32, bf16[192,1280]{1,0:T(8,128)(2,1)S(1)} %collective-permute-done.29, f32[192]{0:T(256)S(1)} %convert_reduce_fusion), kind=kLoop, calls=%fused_computation | loop fusion | flops 1966080 | bytes 2949888 | tf_op jit(solution)/shard_map/convert_element_type | solution.py:386
  199.4 12.9 %all-to-all-done.1.arrived = bf16[8,40,640]{2,1,0:T(8,128)(2,1)S(1)} async-done(((bf16[8,40,640]{2,1,0:T(8,128)(2,1)}), bf16[8,40,640]{2,1,0:T(8,128)(2,1)S(1)}, u32[]{:S(2)}, u32[]{:S(2)}) %all-to-all-start.1) | async-done | bytes 409632 | tf_op jit(solution)/shard_map/all_to_all | solution.py:387
  212.3 0.8 last.1
  (80 shorter events, 6.3 us)
Async XLA Ops:
  7.2 47.6 %copy-start.1 = (bf16[128,512]{1,0:T(8,128)(2,1)S(1)}, bf16[128,512]{1,0:T(8,128)(2,1)}, u32[]{:S(2)}) copy-start(bf16[128,512]{1,0:T(8,128)(2,1)} %refs_0_.1) | copy-start | bytes 393220
  7.2 123.5 %all-gather.2.cloned.1.call-start = ((), (), s32[]{:S(2)}) async-start(), calls=%async_computation.2 | async-start | bytes 2457600 | tf_op jit(solution)/shard_map/all_gather | solution.py:298
  7.2 0.9 copy-start.3
  8.1 74.8 %copy-start.21 = (bf16[64,1280]{1,0:T(8,128)(2,1)S(1)}, bf16[64,1280]{1,0:T(8,128)(2,1)}, u32[]{:S(2)}) copy-start(bf16[64,1280]{1,0:T(8,128)(2,1)} %param.9) | copy-start | bytes 491524
  8.2 57.0 %collective-permute-start.13 = (bf16[40,640]{1,0:T(8,128)(2,1)S(1)}, bf16[40,640]{1,0:T(8,128)(2,1)S(1)}, u32[]{:S(2)}, u32[]{:S(2)}) collective-permute-start(bf16[40,640]{1,0:T(8,128)(2,1)S(1)} %pack.1), channel_id=1, source_target_pairs={{0,193},{1,0},{64,1},{65,64},{128,65},{129,128},{192,129},{193,192... | collective-permute-start | bytes 153608 | tf_op jit(solution)/shard_map/ppermute | solution.py:279
  14.1 50.9 %collective-permute-start.12 = (bf16[40,640]{1,0:T(8,128)(2,1)S(1)}, bf16[40,640]{1,0:T(8,128)(2,1)S(1)}, u32[]{:S(2)}, u32[]{:S(2)}) collective-permute-start(bf16[40,640]{1,0:T(8,128)(2,1)S(1)} %pack.1), channel_id=1, source_target_pairs={{0,192},{1,193},{64,0},{65,1},{128,64},{129,65},{192,128},{193,129... | collective-permute-start | bytes 153608 | tf_op jit(solution)/shard_map/ppermute | solution.py:279
  15.6 46.4 %collective-permute-start.11 = (bf16[40,640]{1,0:T(8,128)(2,1)S(1)}, bf16[40,640]{1,0:T(8,128)(2,1)S(1)}, u32[]{:S(2)}, u32[]{:S(2)}) collective-permute-start(bf16[40,640]{1,0:T(8,128)(2,1)S(1)} %pack.1), channel_id=1, source_target_pairs={{0,129},{1,192},{64,193},{65,0},{128,1},{129,64},{192,65},{193,128... | collective-permute-start | bytes 153608 | tf_op jit(solution)/shard_map/ppermute | solution.py:279
  16.0 41.8 %collective-permute-start.10 = (bf16[40,640]{1,0:T(8,128)(2,1)S(1)}, bf16[40,640]{1,0:T(8,128)(2,1)S(1)}, u32[]{:S(2)}, u32[]{:S(2)}) collective-permute-start(bf16[40,640]{1,0:T(8,128)(2,1)S(1)} %pack.1), channel_id=1, source_target_pairs={{0,128},{1,129},{64,192},{65,193},{128,0},{129,1},{192,64},{193,65... | collective-permute-start | bytes 153608 | tf_op jit(solution)/shard_map/ppermute | solution.py:279
  21.0 10.7 %collective-permute-start.7 = (bf16[40,640]{1,0:T(8,128)(2,1)S(1)}, bf16[40,640]{1,0:T(8,128)(2,1)S(1)}, u32[]{:S(2)}, u32[]{:S(2)}) collective-permute-start(bf16[40,640]{1,0:T(8,128)(2,1)S(1)} %pack.1), channel_id=1, source_target_pairs={{0,1},{1,64},{64,65},{65,128},{128,129},{129,192},{192,193},{193,0... | collective-permute-start | bytes 153608 | tf_op jit(solution)/shard_map/ppermute | solution.py:279
  22.1 1.0 copy-start
  23.0 0.7 copy-start.4
  23.7 0.7 copy-start.5
  25.8 61.2 %all-to-all-start = ((bf16[32,8,1024]{2,1,0:T(8,128)(2,1)}), bf16[32,8,1024]{2,1,0:T(8,128)(2,1)S(1)}, u32[]{:S(2)}, u32[]{:S(2)}) async-start(bf16[32,8,1024]{2,1,0:T(8,128)(2,1)} %bitcast.7), calls=%async_computation | async-start | bytes 1048576 | tf_op jit(solution)/shard_map/all_to_all | solution.py:319
  31.7 14.0 %collective-permute-start.8 = (bf16[40,640]{1,0:T(8,128)(2,1)S(1)}, bf16[40,640]{1,0:T(8,128)(2,1)S(1)}, u32[]{:S(2)}, u32[]{:S(2)}) collective-permute-start(bf16[40,640]{1,0:T(8,128)(2,1)S(1)} %pack.1), channel_id=1, source_target_pairs={{0,64},{1,65},{64,128},{65,129},{128,192},{129,193},{192,0},{193,1... | collective-permute-start | bytes 153608 | tf_op jit(solution)/shard_map/ppermute | solution.py:279
  45.7 9.1 %collective-permute-start.9 = (bf16[40,640]{1,0:T(8,128)(2,1)S(1)}, bf16[40,640]{1,0:T(8,128)(2,1)S(1)}, u32[]{:S(2)}, u32[]{:S(2)}) collective-permute-start(bf16[40,640]{1,0:T(8,128)(2,1)S(1)} %pack.1), channel_id=1, source_target_pairs={{0,65},{1,128},{64,129},{65,192},{128,193},{129,0},{192,1},{193,64... | collective-permute-start | bytes 153608 | tf_op jit(solution)/shard_map/ppermute | solution.py:279
  54.8 11.3 %collective-permute-start.5 = (bf16[128,512]{1,0:T(8,128)(2,1)S(1)}, bf16[128,512]{1,0:T(8,128)(2,1)S(1)}, u32[]{:S(2)}, u32[]{:S(2)}) collective-permute-start(bf16[128,512]{1,0:T(8,128)(2,1)S(1)} %copy-done.1), channel_id=1, source_target_pairs={{0,6},{1,7},{2,0},{3,1},{4,2},{5,3},{6,4},{7,5},{8,14},{9,15},{10,... | collective-permute-start | bytes 393224 | tf_op jit(solution)/shard_map/ppermute | solution.py:291
  57.8 10.8 %collective-permute-start.4 = (bf16[128,512]{1,0:T(8,128)(2,1)S(1)}, bf16[128,512]{1,0:T(8,128)(2,1)S(1)}, u32[]{:S(2)}, u32[]{:S(2)}) collective-permute-start(bf16[128,512]{1,0:T(8,128)(2,1)S(1)} %copy-done.1), channel_id=1, source_target_pairs={{0,5},{1,4},{2,7},{3,6},{4,1},{5,0},{6,3},{7,2},{8,13},{9,12},{10,... | collective-permute-start | bytes 393224 | tf_op jit(solution)/shard_map/ppermute | solution.py:291
  61.9 8.5 %collective-permute-start.3 = (bf16[128,512]{1,0:T(8,128)(2,1)S(1)}, bf16[128,512]{1,0:T(8,128)(2,1)S(1)}, u32[]{:S(2)}, u32[]{:S(2)}) collective-permute-start(bf16[128,512]{1,0:T(8,128)(2,1)S(1)} %copy-done.1), channel_id=1, source_target_pairs={{0,4},{1,5},{2,6},{3,7},{4,0},{5,1},{6,2},{7,3},{8,12},{9,13},{10,... | collective-permute-start | bytes 393224 | tf_op jit(solution)/shard_map/ppermute | solution.py:291
  65.0 9.0 %collective-permute-start.6 = (bf16[128,512]{1,0:T(8,128)(2,1)S(1)}, bf16[128,512]{1,0:T(8,128)(2,1)S(1)}, u32[]{:S(2)}, u32[]{:S(2)}) collective-permute-start(bf16[128,512]{1,0:T(8,128)(2,1)S(1)} %copy-done.1), channel_id=1, source_target_pairs={{0,7},{1,6},{2,1},{3,0},{4,3},{5,2},{6,5},{7,4},{8,15},{9,14},{10,... | collective-permute-start | bytes 393224 | tf_op jit(solution)/shard_map/ppermute | solution.py:291
  65.2 24.8 %collective-permute-start.16 = (bf16[8,40,640]{2,1,0:T(8,128)(2,1)S(1)}, bf16[8,40,640]{2,1,0:T(8,128)(2,1)S(1)}, u32[]{:S(2)}, u32[]{:S(2)}) collective-permute-start(bf16[8,40,640]{2,1,0:T(8,128)(2,1)S(1)} %bitcast_dynamic-update-slice_fusion.refs_0_), channel_id=1, source_target_pairs={{0,48},{16,0},{32,16},{48,32},{1,49},{17,1},{33,17},{49,33},{2,50}... | collective-permute-start | bytes 1228808 | tf_op jit(solution)/shard_map/ppermute | solution.py:279
  66.1 23.9 %collective-permute-start.15 = (bf16[8,40,640]{2,1,0:T(8,128)(2,1)S(1)}, bf16[8,40,640]{2,1,0:T(8,128)(2,1)S(1)}, u32[]{:S(2)}, u32[]{:S(2)}) collective-permute-start(bf16[8,40,640]{2,1,0:T(8,128)(2,1)S(1)} %bitcast_dynamic-update-slice_fusion.refs_0_), channel_id=1, source_target_pairs={{0,32},{16,48},{32,0},{48,16},{1,33},{17,49},{33,1},{49,17},{2,34}... | collective-permute-start | bytes 1228808 | tf_op jit(solution)/shard_map/ppermute | solution.py:279
  68.6 21.4 %collective-permute-start.14 = (bf16[8,40,640]{2,1,0:T(8,128)(2,1)S(1)}, bf16[8,40,640]{2,1,0:T(8,128)(2,1)S(1)}, u32[]{:S(2)}, u32[]{:S(2)}) collective-permute-start(bf16[8,40,640]{2,1,0:T(8,128)(2,1)S(1)} %bitcast_dynamic-update-slice_fusion.refs_0_), channel_id=1, source_target_pairs={{0,16},{16,32},{32,48},{48,0},{1,17},{17,33},{33,49},{49,1},{2,18}... | collective-permute-start | bytes 1228808 | tf_op jit(solution)/shard_map/ppermute | solution.py:279
  70.4 11.7 %collective-permute-start.2 = (bf16[128,512]{1,0:T(8,128)(2,1)S(1)}, bf16[128,512]{1,0:T(8,128)(2,1)S(1)}, u32[]{:S(2)}, u32[]{:S(2)}) collective-permute-start(bf16[128,512]{1,0:T(8,128)(2,1)S(1)} %copy-done.1), channel_id=1, source_target_pairs={{0,3},{1,2},{2,5},{3,4},{4,7},{5,6},{6,1},{7,0},{8,11},{9,10},{10,... | collective-permute-start | bytes 393224 | tf_op jit(solution)/shard_map/ppermute | solution.py:291
  74.0 8.8 %collective-permute-start.1 = (bf16[128,512]{1,0:T(8,128)(2,1)S(1)}, bf16[128,512]{1,0:T(8,128)(2,1)S(1)}, u32[]{:S(2)}, u32[]{:S(2)}) collective-permute-start(bf16[128,512]{1,0:T(8,128)(2,1)S(1)} %copy-done.1), channel_id=1, source_target_pairs={{0,2},{1,3},{2,4},{3,5},{4,6},{5,7},{6,0},{7,1},{8,10},{9,11},{10,... | collective-permute-start | bytes 393224 | tf_op jit(solution)/shard_map/ppermute | solution.py:291
  82.0 5.0 %collective-permute-start = (bf16[128,512]{1,0:T(8,128)(2,1)S(1)}, bf16[128,512]{1,0:T(8,128)(2,1)S(1)}, u32[]{:S(2)}, u32[]{:S(2)}) collective-permute-start(bf16[128,512]{1,0:T(8,128)(2,1)S(1)} %copy-done.1), channel_id=1, source_target_pairs={{0,1},{1,0},{2,3},{3,2},{4,5},{5,4},{6,7},{7,6},{8,9},{9,8},{10,11... | collective-permute-start | bytes 393224 | tf_op jit(solution)/shard_map/ppermute | solution.py:291
  82.8 7.3 %collective-permute-start.24 = (bf16[64,1280]{1,0:T(8,128)(2,1)S(1)}, bf16[64,1280]{1,0:T(8,128)(2,1)}, u32[]{:S(2)}, u32[]{:S(2)}) collective-permute-start(bf16[64,1280]{1,0:T(8,128)(2,1)S(1)} %copy-done.21), channel_id=1, source_target_pairs={{0,1},{1,0},{2,3},{3,2},{4,5},{5,4},{6,7},{7,6},{8,9},{9,8},{10,11... | collective-permute-start | bytes 491528 | tf_op jit(solution)/shard_map/ppermute | solution.py:279
  90.0 14.0 %copy-start.13 = (bf16[208,512]{1,0:T(8,128)(2,1)}, bf16[208,512]{1,0:T(8,128)(2,1)S(1)}, u32[]{:S(2)}) copy-start(bf16[208,512]{1,0:T(8,128)(2,1)S(1)} %get-tuple-element.24.refs_0_) | copy-start | bytes 638980
  90.0 13.9 %collective-permute-start.17 = (bf16[8,40,640]{2,1,0:T(8,128)(2,1)S(1)}, bf16[8,40,640]{2,1,0:T(8,128)(2,1)S(1)}, u32[]{:S(2)}, u32[]{:S(2)}) collective-permute-start(bf16[8,40,640]{2,1,0:T(8,128)(2,1)S(1)} %bitcast_dynamic-update-slice_fusion.refs_0_), channel_id=1, source_target_pairs={{0,8},{8,0},{1,9},{9,1},{2,10},{10,2},{3,11},{11,3},{4,12},{12,4},... | collective-permute-start | bytes 1228808 | tf_op jit(solution)/shard_map/ppermute | solution.py:279
  91.7 10.3 %collective-permute-start.27 = (bf16[128,1280]{1,0:T(8,128)(2,1)}, bf16[128,1280]{1,0:T(8,128)(2,1)S(1)}, u32[]{:S(2)}, u32[]{:S(2)}) collective-permute-start(bf16[128,1280]{1,0:T(8,128)(2,1)} %constant_dynamic-update-slice_fusion.refs_4_), channel_id=1, source_target_pairs={{0,6},{2,0},{4,2},{6,4},{1,7},{3,1},{5,3},{7,5},{8,14},{10,8},{12,... | collective-permute-start | bytes 983048 | tf_op jit(solution)/shard_map/ppermute | solution.py:279
  93.2 13.1 %collective-permute-start.18 = (bf16[8,40,640]{2,1,0:T(8,128)(2,1)S(1)}, bf16[8,40,640]{2,1,0:T(8,128)(2,1)S(1)}, u32[]{:S(2)}, u32[]{:S(2)}) collective-permute-start(bf16[8,40,640]{2,1,0:T(8,128)(2,1)S(1)} %collective-permute-done.14.refs_1_), channel_id=1, source_target_pairs={{0,8},{8,0},{1,9},{9,1},{2,10},{10,2},{3,11},{11,3},{4,12},{12,4},... | collective-permute-start | bytes 1228808 | tf_op jit(solution)/shard_map/ppermute | solution.py:279
  93.4 13.8 %collective-permute-start.19 = (bf16[8,40,640]{2,1,0:T(8,128)(2,1)S(1)}, bf16[8,40,640]{2,1,0:T(8,128)(2,1)S(1)}, u32[]{:S(2)}, u32[]{:S(2)}) collective-permute-start(bf16[8,40,640]{2,1,0:T(8,128)(2,1)S(1)} %collective-permute-done.15.refs_2_), channel_id=1, source_target_pairs={{0,8},{8,0},{1,9},{9,1},{2,10},{10,2},{3,11},{11,3},{4,12},{12,4},... | collective-permute-start | bytes 1228808 | tf_op jit(solution)/shard_map/ppermute | solution.py:279
  93.7 14.8 %collective-permute-start.20 = (bf16[8,40,640]{2,1,0:T(8,128)(2,1)S(1)}, bf16[8,40,640]{2,1,0:T(8,128)(2,1)S(1)}, u32[]{:S(2)}, u32[]{:S(2)}) collective-permute-start(bf16[8,40,640]{2,1,0:T(8,128)(2,1)S(1)} %collective-permute-done.16.refs_3_), channel_id=1, source_target_pairs={{0,8},{8,0},{1,9},{9,1},{2,10},{10,2},{3,11},{11,3},{4,12},{12,4},... | collective-permute-start | bytes 1228808 | tf_op jit(solution)/shard_map/ppermute | solution.py:279
  102.0 0.7 copy-start.11
  102.8 12.5 %collective-permute-start.26 = (bf16[128,1280]{1,0:T(8,128)(2,1)}, bf16[128,1280]{1,0:T(8,128)(2,1)}, u32[]{:S(2)}, u32[]{:S(2)}) collective-permute-start(bf16[128,1280]{1,0:T(8,128)(2,1)} %constant_dynamic-update-slice_fusion.refs_4_), channel_id=1, source_target_pairs={{0,4},{2,6},{4,0},{6,2},{1,5},{3,7},{5,1},{7,3},{8,12},{10,14},{12... | collective-permute-start | bytes 983048 | tf_op jit(solution)/shard_map/ppermute | solution.py:279
  104.0 18.3 %collective-permute-start.25 = (bf16[128,1280]{1,0:T(8,128)(2,1)}, bf16[128,1280]{1,0:T(8,128)(2,1)}, u32[]{:S(2)}, u32[]{:S(2)}) collective-permute-start(bf16[128,1280]{1,0:T(8,128)(2,1)} %constant_dynamic-update-slice_fusion.refs_4_), channel_id=1, source_target_pairs={{0,2},{2,4},{4,6},{6,0},{1,3},{3,5},{5,7},{7,1},{8,10},{10,12},{12... | collective-permute-start | bytes 983048 | tf_op jit(solution)/shard_map/ppermute | solution.py:279
  106.3 16.0 %collective-permute-start.23 = (bf16[208,512]{1,0:T(8,128)(2,1)}, bf16[208,512]{1,0:T(8,128)(2,1)S(1)}, u32[]{:S(2)}, u32[]{:S(2)}) collective-permute-start(bf16[208,512]{1,0:T(8,128)(2,1)} %copy-done.13), channel_id=1, source_target_pairs={{0,6},{2,0},{4,2},{6,4},{1,7},{3,1},{5,3},{7,5},{8,14},{10,8},{12,... | collective-permute-start | bytes 638984 | tf_op jit(solution)/shard_map/ppermute | solution.py:279
  107.2 19.5 %collective-permute-start.22 = (bf16[208,512]{1,0:T(8,128)(2,1)}, bf16[208,512]{1,0:T(8,128)(2,1)S(1)}, u32[]{:S(2)}, u32[]{:S(2)}) collective-permute-start(bf16[208,512]{1,0:T(8,128)(2,1)} %copy-done.13), channel_id=1, source_target_pairs={{0,4},{2,6},{4,0},{6,2},{1,5},{3,7},{5,1},{7,3},{8,12},{10,14},{12... | collective-permute-start | bytes 638984 | tf_op jit(solution)/shard_map/ppermute | solution.py:279
  108.5 21.4 %collective-permute-start.21 = (bf16[208,512]{1,0:T(8,128)(2,1)}, bf16[208,512]{1,0:T(8,128)(2,1)S(1)}, u32[]{:S(2)}, u32[]{:S(2)}) collective-permute-start(bf16[208,512]{1,0:T(8,128)(2,1)} %copy-done.13), channel_id=1, source_target_pairs={{0,2},{2,4},{4,6},{6,0},{1,3},{3,5},{5,7},{7,1},{8,10},{10,12},{12... | collective-permute-start | bytes 638984 | tf_op jit(solution)/shard_map/ppermute | solution.py:279
  110.7 1.3 copy-start.7
  112.0 1.3 copy-start.9
  122.3 0.7 copy-start.15
  126.8 0.7 copy-start.17
  129.9 0.7 copy-start.19
  130.6 1.0 copy-start.2
  131.6 1.5 copy-start.6
  133.2 1.5 copy-start.8
  134.7 1.5 copy-start.10
  136.3 1.0 copy-start.12
  137.2 0.9 copy-start.14
  138.2 0.9 copy-start.16
  139.1 0.9 copy-start.18
  140.0 0.9 copy-start.20
  162.3 3.6 %collective-permute-start.28 = (bf16[4,8,40,640]{3,2,1,0:T(8,128)(2,1)S(1)}, bf16[4,8,40,640]{3,2,1,0:T(8,128)(2,1)S(1)}, u32[]{:S(2)}, u32[]{:S(2)}) collective-permute-start(bf16[4,8,40,640]{3,2,1,0:T(8,128)(2,1)S(1)} %get-tuple-element.37), channel_id=1, source_target_pairs={{0,8},{8,0},{1,9},{9,1},{2,10},{10,2},{3,11},{11,3},{4,12},{12,4},... | collective-permute-start | bytes 4915208 | tf_op jit(solution)/shard_map/ppermute | solution.py:279
  166.3 12.4 %collective-permute-start.32 = (bf16[8,40,640]{2,1,0:T(8,128)(2,1)S(1)}, bf16[8,40,640]{2,1,0:T(8,128)(2,1)S(1)}, u32[]{:S(2)}, u32[]{:S(2)}) collective-permute-start(bf16[8,40,640]{2,1,0:T(8,128)(2,1)S(1)} %get-tuple-element.43), channel_id=1, source_target_pairs={{0,16},{16,32},{32,48},{48,0},{1,17},{17,33},{33,49},{49,1},{2,18}... | collective-permute-start | bytes 1228808 | tf_op jit(solution)/shard_map/ppermute | solution.py:279
  167.6 13.9 %collective-permute-start.33 = (bf16[8,40,640]{2,1,0:T(8,128)(2,1)S(1)}, bf16[8,40,640]{2,1,0:T(8,128)(2,1)S(1)}, u32[]{:S(2)}, u32[]{:S(2)}) collective-permute-start(bf16[8,40,640]{2,1,0:T(8,128)(2,1)S(1)} %get-tuple-element.44), channel_id=1, source_target_pairs={{0,32},{16,48},{32,0},{48,16},{1,33},{17,49},{33,1},{49,17},{2,34}... | collective-permute-start | bytes 1228808 | tf_op jit(solution)/shard_map/ppermute | solution.py:279
  169.7 19.4 %collective-permute-start.34 = (bf16[8,40,640]{2,1,0:T(8,128)(2,1)S(1)}, bf16[8,40,640]{2,1,0:T(8,128)(2,1)S(1)}, u32[]{:S(2)}, u32[]{:S(2)}) collective-permute-start(bf16[8,40,640]{2,1,0:T(8,128)(2,1)S(1)} %get-tuple-element.45), channel_id=1, source_target_pairs={{0,48},{16,0},{32,16},{48,32},{1,49},{17,1},{33,17},{49,33},{2,50}... | collective-permute-start | bytes 1228808 | tf_op jit(solution)/shard_map/ppermute | solution.py:279
  171.5 25.6 %collective-permute-start.29 = (bf16[192,1280]{1,0:T(8,128)(2,1)S(1)}, bf16[192,1280]{1,0:T(8,128)(2,1)S(1)}, u32[]{:S(2)}, u32[]{:S(2)}) collective-permute-start(bf16[192,1280]{1,0:T(8,128)(2,1)S(1)} %get-tuple-element.39), channel_id=1, source_target_pairs={{0,6},{2,0},{4,2},{6,4},{1,7},{3,1},{5,3},{7,5},{8,14},{10,8},{12,... | collective-permute-start | bytes 1474568 | tf_op jit(solution)/shard_map/ppermute | solution.py:279
  172.4 24.8 %collective-permute-start.30 = (bf16[192,1280]{1,0:T(8,128)(2,1)S(1)}, bf16[192,1280]{1,0:T(8,128)(2,1)}, u32[]{:S(2)}, u32[]{:S(2)}) collective-permute-start(bf16[192,1280]{1,0:T(8,128)(2,1)S(1)} %get-tuple-element.40), channel_id=1, source_target_pairs={{0,4},{2,6},{4,0},{6,2},{1,5},{3,7},{5,1},{7,3},{8,12},{10,14},{12... | collective-permute-start | bytes 1474568 | tf_op jit(solution)/shard_map/ppermute | solution.py:279
  178.6 18.5 %collective-permute-start.31 = (bf16[192,1280]{1,0:T(8,128)(2,1)S(1)}, bf16[192,1280]{1,0:T(8,128)(2,1)}, u32[]{:S(2)}, u32[]{:S(2)}) collective-permute-start(bf16[192,1280]{1,0:T(8,128)(2,1)S(1)} %get-tuple-element.41), channel_id=1, source_target_pairs={{0,2},{2,4},{4,6},{6,0},{1,3},{3,5},{5,7},{7,1},{8,10},{10,12},{12... | collective-permute-start | bytes 1474568 | tf_op jit(solution)/shard_map/ppermute | solution.py:279
  190.1 22.2 %all-to-all-start.1 = ((bf16[8,40,640]{2,1,0:T(8,128)(2,1)}), bf16[8,40,640]{2,1,0:T(8,128)(2,1)S(1)}, u32[]{:S(2)}, u32[]{:S(2)}) async-start(bf16[8,40,640]{2,1,0:T(8,128)(2,1)} %x_sum.1), calls=%async_computation.1 | async-start | bytes 819200 | tf_op jit(solution)/shard_map/all_to_all | solution.py:387
Sparse Core Ops, SparseCore 0:
  22.2 30.3 all-gather.1

commit v4 on v3

--- a/solution.py
+++ b/solution.py
@@ -47,6 +47,9 @@
 
 
 def call(kernel, out_shape, args, flops, bytes_accessed, scratch=(), vmem=12 << 20, smem=0, hbm=0, name=None):
+    args = list(args)
+    for k in range(len(args) - hbm, len(args)):
+        args[k] = pltpu.with_memory_space_constraint(args[k], pltpu.HBM)
     return pl.pallas_call(
         kernel,
         out_shape=out_shape,
@@ -106,7 +109,7 @@
 
 
 def front_kernel(place, incoming, *refs):
-    pieces, (block, flags_out, conv, arrival) = refs[:8], refs[8:]
+    pieces, (block, flags_out, conv, arrival) = refs[:4], refs[4:]
     y, zl = place[0], place[1]
     copies = []
     for step in range(4):
@@ -114,7 +117,8 @@
             k = step * 2 + other
             start = lax.rem(y - step + 4, 4) * 256 + lax.rem(zl + other, 2) * 128
             rows = pl.ds(pl.multiple_of(start, 128), 128)
-            copies.append(pltpu.make_async_copy(pieces[k], conv.at[rows, :], arrival.at[k]))
+            source = pieces[step].at[pl.ds(other * 128, 128), :]
+            copies.append(pltpu.make_async_copy(source, conv.at[rows, :], arrival.at[k]))
             copies[-1].start()
     for copy in copies:
         copy.wait()
@@ -140,16 +144,15 @@
 
 def weights_kernel(place, *refs):
     pieces, (up, down, wide_up, wide_down) = refs[:8], refs[8:]
-    z, x, c = place[0], place[1], place[2]
+    zh, x, c, zl = place[0], place[1], place[2], place[3]
     for core in range(2):
         for step in range(4):
             piece = pieces[core * 4 + step]
             base = lax.rem(x - step + 4, 4) * 80 + lax.rem(c + core, 2) * 40
 
             def one(k, carry):
-                there = lax.rem(z - k + 8, 8)
-                row = (there // 2) * 320 + base
-                half = lax.rem(there, 2)
+                row = lax.rem(zh - k // 2 + 4, 4) * 320 + base
+                half = lax.rem(zl + k, 2)
                 rows = pl.ds(pl.multiple_of(row, 8), BLOCK)
                 a, b = unpack_pair(piece[k].astype(f32))
                 wide_up[half, rows, :] = a
@@ -283,15 +286,6 @@
     return [values] + [ring(values, axis, size, step) for step in range(1, size)]
 
 
-def grid(values):
-    pieces = []
-    for step in range(8):
-        dy, dz = step // 2, step % 2
-        order = [(k, ((k // 2 + dy) % 4) * 2 + (k % 2 ^ dz)) for k in range(8)]
-        pieces.append(lax.ppermute(values, ("y", "zl"), order) if step else values)
-    return pieces
-
-
 def per_device(waveform_rows, conv_weight, proj_weight, ffn_pair, owner, frame_live, cotangent):
     dp = ("zh", "x", "c")
     zh, x, c, y, zl = (lax.axis_index(name).astype(i32) for name in ("zh", "x", "c", "y", "zl"))
@@ -303,12 +297,10 @@
         [jnp.transpose(ffn_pair, (1, 2, 0))],
         1 << 16, 1 << 17, name="pack",
     )
-    conv_pieces = grid(conv_weight)
-    along_z = jnp.stack(around(packed, ZX, 8))
-    along_x = around(along_z, "x", 4)
-    proj_weight, _ = lax.optimization_barrier((proj_weight, conv_pieces[-1]))
+    both = jnp.stack([packed, ring(packed, "zl", 2, 1)])
+    conv_pair = jnp.concatenate([conv_weight, ring(conv_weight, "zl", 2, 1)], axis=0)
     proj_pair = jnp.concatenate([proj_weight, ring(proj_weight, "zl", 2, 1)], axis=0)
-    proj_pieces = around(proj_pair, "y", 4)
+    along_z = jnp.concatenate(around(both, "zh", 4), axis=0)
 
     outgoing = call(
         route_kernel,
@@ -316,9 +308,17 @@
         [owner.reshape(1, -1), frame_live.reshape(1, -1), waveform_rows],
         2 * 256 * 128 * 1152, 1 << 20, name="route",
     )
+    outgoing, along_z, conv_pair, proj_pair = lax.optimization_barrier(
+        (outgoing, along_z, conv_pair, proj_pair)
+    )
+    along_x = around(along_z, "x", 4)
+    conv_pieces = around(conv_pair, "y", 4)
+    proj_pair, _ = lax.optimization_barrier((proj_pair, conv_pieces[1]))
+    proj_pieces = around(proj_pair, "y", 4)
     incoming = lax.all_to_all(
         outgoing.reshape(N_DP, PAD, 1024), dp, split_axis=0, concat_axis=0, tiled=True
     ).reshape(N_DP * PAD, 1024)
+    incoming, *proj_pieces = lax.optimization_barrier((incoming, *proj_pieces))
 
     block, flags = call(
         front_kernel,
@@ -329,16 +329,16 @@
         [jnp.stack([y, zl]), incoming, *conv_pieces],
         2 * 256 * 1024 * 512, 2 << 20,
         scratch=[pltpu.VMEM((1024, CH), bf16), pltpu.SemaphoreType.DMA((8,))],
-        smem=1, hbm=8, name="front",
+        smem=1, hbm=4, name="front",
     )
     blocks = around(block, "y", 4)
-    block, *along_x = lax.optimization_barrier((block, *along_x))
+    _, _, _, *along_x = lax.optimization_barrier((*blocks[1:], *along_x))
     pieces = along_x + [ring(piece, "c", 2, 1) for piece in along_x]
 
     up, down = call(
         weights_kernel,
         (jax.ShapeDtypeStruct((D, WIDE), bf16),) * 2,
-        [jnp.stack([zh * 2 + zl, x, c]), *pieces],
+        [jnp.stack([zh, x, c, zl]), *pieces],
         1 << 22, 8 << 20,
         scratch=[pltpu.VMEM((2, D, LANES), f32)] * 2, vmem=24 << 20, smem=1, name="weights",
     )

time: 221 us -> 184 us (0.83)
  starting transfers between devices: 70.7 us -> 52.8 us
  local copies, waits for them, and re-layouts: 21.2 us -> 7.15 us
  waiting for transfers between devices: 81.4 us -> 75.9 us
    ppermute x7 -> x0, starting transfers between devices: 16.1 us -> none  [grid(): pieces.append(lax.ppermute(values, ('y', 'zl'), order) if step else values)]
    unnamed x52 -> x40, local copies, waits for them, and re-layouts: 19.6 us -> 7.13 us
    ppermute x7 -> x0, waiting for transfers between devices: 8.85 us -> none  [grid(): pieces.append(lax.ppermute(values, ('y', 'zl'), order) if step else values)]
    ppermute x28 -> x29, starting transfers between devices: 41.7 us -> 37.9 us  [ring(): lax.ppermute(values, axis, [(k, (k + step) % size) for k in range(size)])]
    ppermute x28 -> x29, waiting for transfers between devices: 59.6 us -> 61.8 us  [ring(): lax.ppermute(values, axis, [(k, (k + step) % size) for k in range(size)])]
  transfers between devices with their start and end apart: 38 -> 32, of which waited for: 14 -> 20; matrix products, arithmetic and copies ran while one was open for 2% -> 1% of each run, Pallas kernels for 3% -> 4%
where the time goes in v4:
time: 184 us; the launch traced here: 183 us
  waiting for transfers between devices  75.9 us (41%)
  starting transfers between devices  52.8 us (29%)
  Pallas kernels  30.3 us (16%)
  between operations  14.3 us (8%)
  local copies, waits for them, and re-layouts  7.15 us (4%)
  other arithmetic  2.33 us (1%)
    ppermute x29, waiting for transfers between devices, ring(): lax.ppermute(values, axis, [(k, (k + step) % size) for k in range(size)])  61.8 us
    ppermute x29, starting transfers between devices, ring(): lax.ppermute(values, axis, [(k, (k + step) % size) for k in range(size)])  37.9 us
    pallas_call x8, Pallas kernels, call(): pl.pallas_call(kernel, out_shape=out_shape, in_specs=[SMEM] * smem + [VME...  30.3 us
    all_to_all x1, waiting for transfers between devices, per_device(): total = lax.all_to_all(total, ZX, split_axis=0, concat_axis=0, tiled=True)  13.4 us
    all_to_all x1, starting transfers between devices, per_device(): total = lax.all_to_all(total, ZX, split_axis=0, concat_axis=0, tiled=True)  7.64 us
    all_to_all x1, starting transfers between devices, per_device(): lax.all_to_all(outgoing.reshape(N_DP, PAD, 1024), dp, split_axis=0, conca...  7.21 us
    unnamed x40, local copies, waits for them, and re-layouts  7.13 us
  transfers between devices with their start and end apart: 32, of which 20 were waited for; matrix products, arithmetic and copies ran while one was open for 1% of the time, Pallas kernels for 4%

profile of v4, /device:TPU:2, one launch (start us, length us, event | category | flops | bytes accessed | tf_op | source)
XLA Modules:
  0.0 182.7 jit_solution(14979843344674070245)
XLA Ops:
  7.2 0.7 all-gather.2.cloned.1.call-update
  7.9 0.8 copy-done.1
  8.8 2.0 %collective-permute-start = (bf16[40,640]{1,0:T(8,128)(2,1)S(1)}, bf16[40,640]{1,0:T(8,128)(2,1)S(1)}, u32[]{:S(2)}, u32[]{:S(2)}) collective-permute-start(bf16[40,640]{1,0:T(8,128)(2,1)S(1)} %pack.1), channel_id=1, source_target_pairs={{0,1},{1,0},{2,3},{3,2},{4,5},{5,4},{6,7},{7,6},{8,9},{9,8},{10,11... | collective-permute-start | bytes 153608 | tf_op jit(solution)/shard_map/ppermute | solution.py:282
  10.8 0.1 collective-permute-start.4
  10.9 1.9 %collective-permute-start.5 = (bf16[64,1280]{1,0:T(8,128)(2,1)}, bf16[64,1280]{1,0:T(8,128)(2,1)S(1)}, u32[]{:S(2)}, u32[]{:S(2)}) collective-permute-start(bf16[64,1280]{1,0:T(8,128)(2,1)} %param.9), channel_id=1, source_target_pairs={{0,1},{1,0},{2,3},{3,2},{4,5},{5,4},{6,7},{7,6},{8,9},{9,8},{10,11... | collective-permute-start | bytes 491528 | tf_op jit(solution)/shard_map/ppermute | solution.py:282
  12.9 0.9 copy-done
  13.8 0.7 copy-done.2
  14.5 0.7 copy-done.3
  15.1 1.5 route.1
  16.6 5.5 %collective-permute-start.3 = (bf16[2,40,640]{2,1,0:T(8,128)(2,1)S(1)}, bf16[2,40,640]{2,1,0:T(8,128)(2,1)S(1)}, u32[]{:S(2)}, u32[]{:S(2)}) collective-permute-start(bf16[2,40,640]{2,1,0:T(8,128)(2,1)S(1)} %pad_maximum_fusion.2), channel_id=1, source_target_pairs={{0,192},{64,0},{128,64},{192,128},{1,193},{65,1},{129,65},{193,129... | collective-permute-start | bytes 307208 | tf_op jit(solution)/shard_map/ppermute | solution.py:282
  22.1 1.4 collective-permute-start.2
  23.5 2.4 %collective-permute-start.1 = (bf16[2,40,640]{2,1,0:T(8,128)(2,1)S(1)}, bf16[2,40,640]{2,1,0:T(8,128)(2,1)S(1)}, u32[]{:S(2)}, u32[]{:S(2)}) collective-permute-start(bf16[2,40,640]{2,1,0:T(8,128)(2,1)S(1)} %pad_maximum_fusion.2), channel_id=1, source_target_pairs={{0,64},{64,128},{128,192},{192,0},{1,65},{65,129},{129,193},{193,1... | collective-permute-start | bytes 307208 | tf_op jit(solution)/shard_map/ppermute | solution.py:282
  25.9 0.9 pad_maximum_fusion.1.refs_0_
  26.9 3.8 %collective-permute-done.1 = bf16[2,40,640]{2,1,0:T(8,128)(2,1)S(1)} collective-permute-done((bf16[2,40,640]{2,1,0:T(8,128)(2,1)S(1)}, bf16[2,40,640]{2,1,0:T(8,128)(2,1)S(1)}, u32[]{:S(2)}, u32[]{:S(2)}) %collective-permute-start.1) | collective-permute-done | bytes 102432 | tf_op jit(solution)/shard_map/ppermute | solution.py:282
  30.7 2.5 %collective-permute-done.2 = bf16[2,40,640]{2,1,0:T(8,128)(2,1)S(1)} collective-permute-done((bf16[2,40,640]{2,1,0:T(8,128)(2,1)S(1)}, bf16[2,40,640]{2,1,0:T(8,128)(2,1)S(1)}, u32[]{:S(2)}, u32[]{:S(2)}) %collective-permute-start.2) | collective-permute-done | bytes 102432 | tf_op jit(solution)/shard_map/ppermute | solution.py:282
  33.3 7.2 %all-to-all-start = ((bf16[32,8,1024]{2,1,0:T(8,128)(2,1)}), bf16[32,8,1024]{2,1,0:T(8,128)(2,1)S(1)}, u32[]{:S(2)}, u32[]{:S(2)}) async-start(bf16[32,8,1024]{2,1,0:T(8,128)(2,1)} %bitcast.10), calls=%async_computation | async-start | bytes 1048576 | tf_op jit(solution)/shard_map/all_to_all | solution.py:318
  40.6 1.7 collective-permute-start.6
  42.2 8.2 %collective-permute-done.6.refs_1_ = bf16[256,512]{1,0:T(8,128)(2,1)S(1)} collective-permute-done((bf16[256,512]{1,0:T(8,128)(2,1)S(1)}, bf16[256,512]{1,0:T(8,128)(2,1)S(1)}, u32[]{:S(2)}, u32[]{:S(2)}) %collective-permute-start.6) | collective-permute-done | bytes 262176 | tf_op jit(solution)/shard_map/ppermute | solution.py:282
  50.4 1.7 collective-permute-start.9
  52.0 0.6 collective-permute-start.8
  52.6 1.0 collective-permute-start.7
  53.6 0.4 collective-permute-start.17
  54.0 2.3 %collective-permute-start.11 = (bf16[256,512]{1,0:T(8,128)(2,1)S(1)}, bf16[256,512]{1,0:T(8,128)(2,1)S(1)}, u32[]{:S(2)}, u32[]{:S(2)}) collective-permute-start(bf16[256,512]{1,0:T(8,128)(2,1)S(1)} %pad_maximum_fusion.1.refs_0_), channel_id=1, source_target_pairs={{0,6},{2,0},{4,2},{6,4},{1,7},{3,1},{5,3},{7,5},{8,14},{10,8},{12,... | collective-permute-start | bytes 786440 | tf_op jit(solution)/shard_map/ppermute | solution.py:282
  56.2 10.6 %collective-permute-done.9.refs_7_ = bf16[128,1280]{1,0:T(8,128)(2,1)S(1)} collective-permute-done((bf16[128,1280]{1,0:T(8,128)(2,1)S(1)}, bf16[128,1280]{1,0:T(8,128)(2,1)S(1)}, u32[]{:S(2)}, u32[]{:S(2)}) %collective-permute-start.9) | collective-permute-done | bytes 327712 | tf_op jit(solution)/shard_map/ppermute | solution.py:282
  66.9 0.8 copy-done.12
  67.6 2.1 %collective-permute-start.16 = (bf16[8,40,640]{2,1,0:T(8,128)(2,1)S(1)}, bf16[8,40,640]{2,1,0:T(8,128)(2,1)S(1)}, u32[]{:S(2)}, u32[]{:S(2)}) collective-permute-start(bf16[8,40,640]{2,1,0:T(8,128)(2,1)S(1)} %constant_dynamic-update-slice_fusion.refs_0_), channel_id=1, source_target_pairs={{0,32},{16,48},{32,0},{48,16},{1,33},{17,49},{33,1},{49,17},{2,34}... | collective-permute-start | bytes 1228808 | tf_op jit(solution)/shard_map/ppermute | solution.py:282
  69.7 1.4 collective-permute-done.7.refs_5_
  71.1 1.5 collective-permute-start.15
  72.7 1.0 collective-permute-done.11.refs_3_
  73.7 1.3 collective-permute-done.10.refs_2_
  75.0 2.9 %front.1 = (bf16[208,512]{1,0:T(8,128)(2,1)S(1)}, f32[192,1]{1,0:T(8,128)S(1)}) custom-call(s32[2]{0:T(128)S(1)} %pad_add_fusion.2.place, bf16[256,1024]{1,0:T(8,128)(2,1)S(1)} %bitcast.15, bf16[256,512]{1,0:T(8,128)(2,1)} %copy-done.7, bf16[256,512]{1,0:T(8,128)(2,1)} %copy-done.9, bf16[256,512]{1,0:T(8,128)(2,1)} %collective-permute-done.10.refs_2_, ...), custom_call_target="tpu_custom_call" | custom-call | flops 268435456 | bytes 2097152 | tf_op jit(solution)/shard_map/front/pallas_call | solution.py:53
  77.9 5.8 %collective-permute-start.14 = (bf16[208,512]{1,0:T(8,128)(2,1)S(1)}, bf16[208,512]{1,0:T(8,128)(2,1)S(1)}, u32[]{:S(2)}, u32[]{:S(2)}) collective-permute-start(bf16[208,512]{1,0:T(8,128)(2,1)S(1)} %get-tuple-element.38.refs_0_), channel_id=1, source_target_pairs={{0,6},{2,0},{4,2},{6,4},{1,7},{3,1},{5,3},{7,5},{8,14},{10,8},{12,... | collective-permute-start | bytes 638984 | tf_op jit(solution)/shard_map/ppermute | solution.py:282
  83.7 0.5 collective-permute-start.13
  84.2 0.5 collective-permute-start.12
  84.7 1.2 collective-permute-done.15.refs_1_
  85.9 5.6 %collective-permute-done.14.refs_3_ = bf16[208,512]{1,0:T(8,128)(2,1)S(1)} collective-permute-done((bf16[208,512]{1,0:T(8,128)(2,1)S(1)}, bf16[208,512]{1,0:T(8,128)(2,1)S(1)}, u32[]{:S(2)}, u32[]{:S(2)}) %collective-permute-start.14) | collective-permute-done | bytes 213024 | tf_op jit(solution)/shard_map/ppermute | solution.py:282
  91.5 1.5 collective-permute-done.13.refs_2_
  93.0 1.9 %collective-permute-done.12.refs_1_ = bf16[208,512]{1,0:T(8,128)(2,1)S(1)} collective-permute-done((bf16[208,512]{1,0:T(8,128)(2,1)S(1)}, bf16[208,512]{1,0:T(8,128)(2,1)S(1)}, u32[]{:S(2)}, u32[]{:S(2)}) %collective-permute-start.12) | collective-permute-done | bytes 213024 | tf_op jit(solution)/shard_map/ppermute | solution.py:282
  95.0 0.6 copy-done.17
  95.6 0.5 collective-permute-start.20
  96.3 0.5 collective-permute-done.18.refs_4_
  96.8 0.6 collective-permute-done.19.refs_5_
  97.4 0.6 collective-permute-done.20.refs_6_
  98.0 0.6 collective-permute-done.21.refs_7_
  98.5 1.9 %weights.1 = (bf16[1280,768]{1,0:T(8,128)(2,1)S(1)}, bf16[1280,768]{1,0:T(8,128)(2,1)S(1)}) custom-call(s32[4]{0:T(128)S(1)} %pad_add_fusion.1.place, bf16[8,40,640]{2,1,0:T(8,128)(2,1)S(1)} %constant_dynamic-update-slice_fusion.refs_0_, bf16[8,40,640]{2,1,0:T(8,128)(2,1)S(1)} %collective-permute-done.15.refs_1_, ...), custom_call_target="tpu_custom_call" | custom-call | flops 4194304 | bytes 8388608 | tf_op jit(solution)/shard_map/weights/pallas_call | solution.py:53
  100.5 1.3 copy-done.4
  101.8 1.3 copy-done.5
  103.1 21.8 %ffn.1 = (f32[192,1280]{1,0:T(8,128)S(1)}, bf16[192,1280]{1,0:T(8,128)(2,1)}, bf16[192,1280]{1,0:T(8,128)(2,1)}, bf16[192,1280]{1,0:T(8,128)(2,1)}, bf16[4,8,40,...) custom-call(s32[3]{0:T(128)S(1)} %pad_add_fusion.place, ...), custom_call_target="tpu_custom_call" | custom-call | flops 8556380160 | bytes 16777216 | tf_op jit(solution)/shard_map/ffn/pallas_call | solution.py:53
  124.9 0.2 collective-permute-start.22
  125.2 3.4 %collective-permute-done.22.arrived = bf16[4,8,40,640]{3,2,1,0:T(8,128)(2,1)S(1)} collective-permute-done((bf16[4,8,40,640]{3,2,1,0:T(8,128)(2,1)S(1)}, bf16[4,8,40,640]{3,2,1,0:T(8,128)(2,1)S(1)}, u32[]{:S(2)}, u32[]{:S(2)}) %collective-permute-start.22) | collective-permute-done | bytes 1638432 | tf_op jit(solution)/shard_map/ppermute | solution.py:282
  128.5 0.4 core_sum.1
  128.9 1.5 collective-permute-start.26
  130.5 1.8 collective-permute-start.27
  132.2 1.5 collective-permute-start.28
  133.7 1.0 collective-permute-start.23
  134.7 0.2 collective-permute-start.24
  134.8 6.5 %collective-permute-done.26.refs_1_ = bf16[8,40,640]{2,1,0:T(8,128)(2,1)S(1)} collective-permute-done((bf16[8,40,640]{2,1,0:T(8,128)(2,1)S(1)}, bf16[8,40,640]{2,1,0:T(8,128)(2,1)S(1)}, u32[]{:S(2)}, u32[]{:S(2)}) %collective-permute-start.26) | collective-permute-done | bytes 409632 | tf_op jit(solution)/shard_map/ppermute | solution.py:282
  141.3 3.0 %collective-permute-done.27.refs_2_ = bf16[8,40,640]{2,1,0:T(8,128)(2,1)S(1)} collective-permute-done((bf16[8,40,640]{2,1,0:T(8,128)(2,1)S(1)}, bf16[8,40,640]{2,1,0:T(8,128)(2,1)S(1)}, u32[]{:S(2)}, u32[]{:S(2)}) %collective-permute-start.27) | collective-permute-done | bytes 409632 | tf_op jit(solution)/shard_map/ppermute | solution.py:282
  144.3 7.7 %collective-permute-done.28.refs_3_ = bf16[8,40,640]{2,1,0:T(8,128)(2,1)S(1)} collective-permute-done((bf16[8,40,640]{2,1,0:T(8,128)(2,1)S(1)}, bf16[8,40,640]{2,1,0:T(8,128)(2,1)S(1)}, u32[]{:S(2)}, u32[]{:S(2)}) %collective-permute-start.28) | collective-permute-done | bytes 409632 | tf_op jit(solution)/shard_map/ppermute | solution.py:282
  152.0 1.0 x_sum.1
  152.9 7.6 %all-to-all-start.1 = ((bf16[8,40,640]{2,1,0:T(8,128)(2,1)}), bf16[8,40,640]{2,1,0:T(8,128)(2,1)S(1)}, u32[]{:S(2)}, u32[]{:S(2)}) async-start(bf16[8,40,640]{2,1,0:T(8,128)(2,1)} %x_sum.1), calls=%async_computation.1 | async-start | bytes 819200 | tf_op jit(solution)/shard_map/all_to_all | solution.py:387
  160.7 1.0 multiply_convert_fusion
  161.8 13.4 %all-to-all-done.1.arrived = bf16[8,40,640]{2,1,0:T(8,128)(2,1)S(1)} async-done(((bf16[8,40,640]{2,1,0:T(8,128)(2,1)}), bf16[8,40,640]{2,1,0:T(8,128)(2,1)S(1)}, u32[]{:S(2)}, u32[]{:S(2)}) %all-to-all-start.1) | async-done | bytes 409632 | tf_op jit(solution)/shard_map/all_to_all | solution.py:387
  175.1 0.8 last.1
  (58 shorter events, 0.7 us)
Async XLA Ops:
  7.2 26.1 %copy-start.11 = (bf16[64,1280]{1,0:T(8,128)(2,1)S(1)}, bf16[64,1280]{1,0:T(8,128)(2,1)}, u32[]{:S(2)}) copy-start(bf16[64,1280]{1,0:T(8,128)(2,1)} %param.9) | copy-start | bytes 491524
  7.2 95.9 %all-gather.2.cloned.1.call-start = ((), (), s32[]{:S(2)}) async-start(), calls=%async_computation.2 | async-start | bytes 2457600 | tf_op jit(solution)/shard_map/all_gather | solution.py:292
  7.9 0.8 copy-start.1
  8.8 7.8 %collective-permute-start = (bf16[40,640]{1,0:T(8,128)(2,1)S(1)}, bf16[40,640]{1,0:T(8,128)(2,1)S(1)}, u32[]{:S(2)}, u32[]{:S(2)}) collective-permute-start(bf16[40,640]{1,0:T(8,128)(2,1)S(1)} %pack.1), channel_id=1, source_target_pairs={{0,1},{1,0},{2,3},{3,2},{4,5},{5,4},{6,7},{7,6},{8,9},{9,8},{10,11... | collective-permute-start | bytes 153608 | tf_op jit(solution)/shard_map/ppermute | solution.py:282
  10.8 15.1 %collective-permute-start.4 = (bf16[128,512]{1,0:T(8,128)(2,1)}, bf16[128,512]{1,0:T(8,128)(2,1)S(1)}, u32[]{:S(2)}, u32[]{:S(2)}) collective-permute-start(bf16[128,512]{1,0:T(8,128)(2,1)} %param.8), channel_id=1, source_target_pairs={{0,1},{1,0},{2,3},{3,2},{4,5},{5,4},{6,7},{7,6},{8,9},{9,8},{10,11... | collective-permute-start | bytes 393224 | tf_op jit(solution)/shard_map/ppermute | solution.py:282
  10.9 22.3 %collective-permute-start.5 = (bf16[64,1280]{1,0:T(8,128)(2,1)}, bf16[64,1280]{1,0:T(8,128)(2,1)S(1)}, u32[]{:S(2)}, u32[]{:S(2)}) collective-permute-start(bf16[64,1280]{1,0:T(8,128)(2,1)} %param.9), channel_id=1, source_target_pairs={{0,1},{1,0},{2,3},{3,2},{4,5},{5,4},{6,7},{7,6},{8,9},{9,8},{10,11... | collective-permute-start | bytes 491528 | tf_op jit(solution)/shard_map/ppermute | solution.py:282
  12.9 0.9 copy-start
  13.8 0.7 copy-start.2
  14.5 0.7 copy-start.3
  16.6 16.6 %collective-permute-start.3 = (bf16[2,40,640]{2,1,0:T(8,128)(2,1)S(1)}, bf16[2,40,640]{2,1,0:T(8,128)(2,1)S(1)}, u32[]{:S(2)}, u32[]{:S(2)}) collective-permute-start(bf16[2,40,640]{2,1,0:T(8,128)(2,1)S(1)} %pad_maximum_fusion.2), channel_id=1, source_target_pairs={{0,192},{64,0},{128,64},{192,128},{1,193},{65,1},{129,65},{193,129... | collective-permute-start | bytes 307208 | tf_op jit(solution)/shard_map/ppermute | solution.py:282
  22.1 11.1 %collective-permute-start.2 = (bf16[2,40,640]{2,1,0:T(8,128)(2,1)S(1)}, bf16[2,40,640]{2,1,0:T(8,128)(2,1)S(1)}, u32[]{:S(2)}, u32[]{:S(2)}) collective-permute-start(bf16[2,40,640]{2,1,0:T(8,128)(2,1)S(1)} %pad_maximum_fusion.2), channel_id=1, source_target_pairs={{0,128},{64,192},{128,0},{192,64},{1,129},{65,193},{129,1},{193,65... | collective-permute-start | bytes 307208 | tf_op jit(solution)/shard_map/ppermute | solution.py:282
  23.5 7.1 %collective-permute-start.1 = (bf16[2,40,640]{2,1,0:T(8,128)(2,1)S(1)}, bf16[2,40,640]{2,1,0:T(8,128)(2,1)S(1)}, u32[]{:S(2)}, u32[]{:S(2)}) collective-permute-start(bf16[2,40,640]{2,1,0:T(8,128)(2,1)S(1)} %pad_maximum_fusion.2), channel_id=1, source_target_pairs={{0,64},{64,128},{128,192},{192,0},{1,65},{65,129},{129,193},{193,1... | collective-permute-start | bytes 307208 | tf_op jit(solution)/shard_map/ppermute | solution.py:282
  26.9 48.1 %copy-start.7 = (bf16[256,512]{1,0:T(8,128)(2,1)}, bf16[256,512]{1,0:T(8,128)(2,1)S(1)}, u32[]{:S(2)}) copy-start(bf16[256,512]{1,0:T(8,128)(2,1)S(1)} %pad_maximum_fusion.1.refs_0_) | copy-start | bytes 786436
  33.3 36.4 %copy-start.8 = (bf16[128,1280]{1,0:T(8,128)(2,1)}, bf16[128,1280]{1,0:T(8,128)(2,1)S(1)}, u32[]{:S(2)}) copy-start(bf16[128,1280]{1,0:T(8,128)(2,1)S(1)} %pad_maximum_fusion.refs_4_) | copy-start | bytes 983044
  33.3 39.3 %all-to-all-start = ((bf16[32,8,1024]{2,1,0:T(8,128)(2,1)}), bf16[32,8,1024]{2,1,0:T(8,128)(2,1)S(1)}, u32[]{:S(2)}, u32[]{:S(2)}) async-start(bf16[32,8,1024]{2,1,0:T(8,128)(2,1)} %bitcast.10), calls=%async_computation | async-start | bytes 1048576 | tf_op jit(solution)/shard_map/all_to_all | solution.py:318
  40.6 9.8 %collective-permute-start.6 = (bf16[256,512]{1,0:T(8,128)(2,1)S(1)}, bf16[256,512]{1,0:T(8,128)(2,1)S(1)}, u32[]{:S(2)}, u32[]{:S(2)}) collective-permute-start(bf16[256,512]{1,0:T(8,128)(2,1)S(1)} %pad_maximum_fusion.1.refs_0_), channel_id=1, source_target_pairs={{0,2},{2,4},{4,6},{6,0},{1,3},{3,5},{5,7},{7,1},{8,10},{10,12},{12... | collective-permute-start | bytes 786440 | tf_op jit(solution)/shard_map/ppermute | solution.py:282
  50.4 24.6 %copy-start.9 = (bf16[256,512]{1,0:T(8,128)(2,1)}, bf16[256,512]{1,0:T(8,128)(2,1)S(1)}, u32[]{:S(2)}) copy-start(bf16[256,512]{1,0:T(8,128)(2,1)S(1)} %collective-permute-done.6.refs_1_) | copy-start | bytes 786436
  50.4 16.5 %collective-permute-start.9 = (bf16[128,1280]{1,0:T(8,128)(2,1)S(1)}, bf16[128,1280]{1,0:T(8,128)(2,1)S(1)}, u32[]{:S(2)}, u32[]{:S(2)}) collective-permute-start(bf16[128,1280]{1,0:T(8,128)(2,1)S(1)} %pad_maximum_fusion.refs_4_), channel_id=1, source_target_pairs={{0,6},{2,0},{4,2},{6,4},{1,7},{3,1},{5,3},{7,5},{8,14},{10,8},{12,... | collective-permute-start | bytes 983048 | tf_op jit(solution)/shard_map/ppermute | solution.py:282
  52.0 15.6 %collective-permute-start.8 = (bf16[128,1280]{1,0:T(8,128)(2,1)S(1)}, bf16[128,1280]{1,0:T(8,128)(2,1)S(1)}, u32[]{:S(2)}, u32[]{:S(2)}) collective-permute-start(bf16[128,1280]{1,0:T(8,128)(2,1)S(1)} %pad_maximum_fusion.refs_4_), channel_id=1, source_target_pairs={{0,4},{2,6},{4,0},{6,2},{1,5},{3,7},{5,1},{7,3},{8,12},{10,14},{12... | collective-permute-start | bytes 983048 | tf_op jit(solution)/shard_map/ppermute | solution.py:282
  52.6 18.5 %collective-permute-start.7 = (bf16[128,1280]{1,0:T(8,128)(2,1)S(1)}, bf16[128,1280]{1,0:T(8,128)(2,1)S(1)}, u32[]{:S(2)}, u32[]{:S(2)}) collective-permute-start(bf16[128,1280]{1,0:T(8,128)(2,1)S(1)} %pad_maximum_fusion.refs_4_), channel_id=1, source_target_pairs={{0,2},{2,4},{4,6},{6,0},{1,3},{3,5},{5,7},{7,1},{8,10},{10,12},{12... | collective-permute-start | bytes 983048 | tf_op jit(solution)/shard_map/ppermute | solution.py:282
  53.6 30.5 %collective-permute-start.17 = (bf16[8,40,640]{2,1,0:T(8,128)(2,1)S(1)}, bf16[8,40,640]{2,1,0:T(8,128)(2,1)S(1)}, u32[]{:S(2)}, u32[]{:S(2)}) collective-permute-start(bf16[8,40,640]{2,1,0:T(8,128)(2,1)S(1)} %constant_dynamic-update-slice_fusion.refs_0_), channel_id=1, source_target_pairs={{0,48},{16,0},{32,16},{48,32},{1,49},{17,1},{33,17},{49,33},{2,50}... | collective-permute-start | bytes 1228808 | tf_op jit(solution)/shard_map/ppermute | solution.py:282
  54.0 19.7 %collective-permute-start.11 = (bf16[256,512]{1,0:T(8,128)(2,1)S(1)}, bf16[256,512]{1,0:T(8,128)(2,1)S(1)}, u32[]{:S(2)}, u32[]{:S(2)}) collective-permute-start(bf16[256,512]{1,0:T(8,128)(2,1)S(1)} %pad_maximum_fusion.1.refs_0_), channel_id=1, source_target_pairs={{0,6},{2,0},{4,2},{6,4},{1,7},{3,1},{5,3},{7,5},{8,14},{10,8},{12,... | collective-permute-start | bytes 786440 | tf_op jit(solution)/shard_map/ppermute | solution.py:282
  66.9 0.8 copy-start.12
  66.9 8.1 %collective-permute-start.10 = (bf16[256,512]{1,0:T(8,128)(2,1)S(1)}, bf16[256,512]{1,0:T(8,128)(2,1)}, u32[]{:S(2)}, u32[]{:S(2)}) collective-permute-start(bf16[256,512]{1,0:T(8,128)(2,1)S(1)} %pad_maximum_fusion.1.refs_0_), channel_id=1, source_target_pairs={{0,4},{2,6},{4,0},{6,2},{1,5},{3,7},{5,1},{7,3},{8,12},{10,14},{12... | collective-permute-start | bytes 786440 | tf_op jit(solution)/shard_map/ppermute | solution.py:282
  67.6 3.5 %copy-start.13 = (bf16[128,1280]{1,0:T(8,128)(2,1)}, bf16[128,1280]{1,0:T(8,128)(2,1)S(1)}, u32[]{:S(2)}) copy-start(bf16[128,1280]{1,0:T(8,128)(2,1)S(1)} %collective-permute-done.8.refs_6_) | copy-start | bytes 983044
  67.6 17.0 %collective-permute-start.16 = (bf16[8,40,640]{2,1,0:T(8,128)(2,1)S(1)}, bf16[8,40,640]{2,1,0:T(8,128)(2,1)S(1)}, u32[]{:S(2)}, u32[]{:S(2)}) collective-permute-start(bf16[8,40,640]{2,1,0:T(8,128)(2,1)S(1)} %constant_dynamic-update-slice_fusion.refs_0_), channel_id=1, source_target_pairs={{0,32},{16,48},{32,0},{48,16},{1,33},{17,49},{33,1},{49,17},{2,34}... | collective-permute-start | bytes 1228808 | tf_op jit(solution)/shard_map/ppermute | solution.py:282
  71.1 1.5 copy-start.14
  71.1 14.7 %collective-permute-start.15 = (bf16[8,40,640]{2,1,0:T(8,128)(2,1)S(1)}, bf16[8,40,640]{2,1,0:T(8,128)(2,1)S(1)}, u32[]{:S(2)}, u32[]{:S(2)}) collective-permute-start(bf16[8,40,640]{2,1,0:T(8,128)(2,1)S(1)} %constant_dynamic-update-slice_fusion.refs_0_), channel_id=1, source_target_pairs={{0,16},{16,32},{32,48},{48,0},{1,17},{17,33},{33,49},{49,1},{2,18}... | collective-permute-start | bytes 1228808 | tf_op jit(solution)/shard_map/ppermute | solution.py:282
  73.7 1.3 copy-start.10
  77.8 17.1 %copy-start.6 = (bf16[208,512]{1,0:T(8,128)(2,1)}, bf16[208,512]{1,0:T(8,128)(2,1)S(1)}, u32[]{:S(2)}) copy-start(bf16[208,512]{1,0:T(8,128)(2,1)S(1)} %get-tuple-element.38.refs_0_) | copy-start | bytes 638980
  77.9 13.6 %collective-permute-start.14 = (bf16[208,512]{1,0:T(8,128)(2,1)S(1)}, bf16[208,512]{1,0:T(8,128)(2,1)S(1)}, u32[]{:S(2)}, u32[]{:S(2)}) collective-permute-start(bf16[208,512]{1,0:T(8,128)(2,1)S(1)} %get-tuple-element.38.refs_0_), channel_id=1, source_target_pairs={{0,6},{2,0},{4,2},{6,4},{1,7},{3,1},{5,3},{7,5},{8,14},{10,8},{12,... | collective-permute-start | bytes 638984 | tf_op jit(solution)/shard_map/ppermute | solution.py:282
  83.7 9.3 %collective-permute-start.13 = (bf16[208,512]{1,0:T(8,128)(2,1)S(1)}, bf16[208,512]{1,0:T(8,128)(2,1)S(1)}, u32[]{:S(2)}, u32[]{:S(2)}) collective-permute-start(bf16[208,512]{1,0:T(8,128)(2,1)S(1)} %get-tuple-element.38.refs_0_), channel_id=1, source_target_pairs={{0,4},{2,6},{4,0},{6,2},{1,5},{3,7},{5,1},{7,3},{8,12},{10,14},{12... | collective-permute-start | bytes 638984 | tf_op jit(solution)/shard_map/ppermute | solution.py:282
  84.2 10.8 %collective-permute-start.12 = (bf16[208,512]{1,0:T(8,128)(2,1)S(1)}, bf16[208,512]{1,0:T(8,128)(2,1)S(1)}, u32[]{:S(2)}, u32[]{:S(2)}) collective-permute-start(bf16[208,512]{1,0:T(8,128)(2,1)S(1)} %get-tuple-element.38.refs_0_), channel_id=1, source_target_pairs={{0,2},{2,4},{4,6},{6,0},{1,3},{3,5},{5,7},{7,1},{8,10},{10,12},{12... | collective-permute-start | bytes 638984 | tf_op jit(solution)/shard_map/ppermute | solution.py:282
  91.5 3.4 %copy-start.15 = (bf16[208,512]{1,0:T(8,128)(2,1)}, bf16[208,512]{1,0:T(8,128)(2,1)S(1)}, u32[]{:S(2)}) copy-start(bf16[208,512]{1,0:T(8,128)(2,1)S(1)} %collective-permute-done.14.refs_3_) | copy-start | bytes 638980
  93.0 2.0 %copy-start.16 = (bf16[208,512]{1,0:T(8,128)(2,1)}, bf16[208,512]{1,0:T(8,128)(2,1)S(1)}, u32[]{:S(2)}) copy-start(bf16[208,512]{1,0:T(8,128)(2,1)S(1)} %collective-permute-done.13.refs_2_) | copy-start | bytes 638980
  94.9 0.7 copy-start.17
  94.9 1.8 %collective-permute-start.18 = (bf16[8,40,640]{2,1,0:T(8,128)(2,1)S(1)}, bf16[8,40,640]{2,1,0:T(8,128)(2,1)S(1)}, u32[]{:S(2)}, u32[]{:S(2)}) collective-permute-start(bf16[8,40,640]{2,1,0:T(8,128)(2,1)S(1)} %constant_dynamic-update-slice_fusion.refs_0_), channel_id=1, source_target_pairs={{0,8},{8,0},{1,9},{9,1},{2,10},{10,2},{3,11},{11,3},{4,12},{12,4},... | collective-permute-start | bytes 1228808 | tf_op jit(solution)/shard_map/ppermute | solution.py:282
  95.6 1.7 collective-permute-start.19
  95.6 2.3 %collective-permute-start.20 = (bf16[8,40,640]{2,1,0:T(8,128)(2,1)S(1)}, bf16[8,40,640]{2,1,0:T(8,128)(2,1)S(1)}, u32[]{:S(2)}, u32[]{:S(2)}) collective-permute-start(bf16[8,40,640]{2,1,0:T(8,128)(2,1)S(1)} %collective-permute-done.16.refs_2_), channel_id=1, source_target_pairs={{0,8},{8,0},{1,9},{9,1},{2,10},{10,2},{3,11},{11,3},{4,12},{12,4},... | collective-permute-start | bytes 1228808 | tf_op jit(solution)/shard_map/ppermute | solution.py:282
  96.1 2.4 %collective-permute-start.21 = (bf16[8,40,640]{2,1,0:T(8,128)(2,1)S(1)}, bf16[8,40,640]{2,1,0:T(8,128)(2,1)S(1)}, u32[]{:S(2)}, u32[]{:S(2)}) collective-permute-start(bf16[8,40,640]{2,1,0:T(8,128)(2,1)S(1)} %collective-permute-done.17.refs_3_), channel_id=1, source_target_pairs={{0,8},{8,0},{1,9},{9,1},{2,10},{10,2},{3,11},{11,3},{4,12},{12,4},... | collective-permute-start | bytes 1228808 | tf_op jit(solution)/shard_map/ppermute | solution.py:282
  100.5 1.3 copy-start.4
  101.8 1.3 copy-start.5
  124.9 3.6 %collective-permute-start.22 = (bf16[4,8,40,640]{3,2,1,0:T(8,128)(2,1)S(1)}, bf16[4,8,40,640]{3,2,1,0:T(8,128)(2,1)S(1)}, u32[]{:S(2)}, u32[]{:S(2)}) collective-permute-start(bf16[4,8,40,640]{3,2,1,0:T(8,128)(2,1)S(1)} %get-tuple-element.55), channel_id=1, source_target_pairs={{0,8},{8,0},{1,9},{9,1},{2,10},{10,2},{3,11},{11,3},{4,12},{12,4},... | collective-permute-start | bytes 4915208 | tf_op jit(solution)/shard_map/ppermute | solution.py:282
  128.9 12.4 %collective-permute-start.26 = (bf16[8,40,640]{2,1,0:T(8,128)(2,1)S(1)}, bf16[8,40,640]{2,1,0:T(8,128)(2,1)S(1)}, u32[]{:S(2)}, u32[]{:S(2)}) collective-permute-start(bf16[8,40,640]{2,1,0:T(8,128)(2,1)S(1)} %get-tuple-element.61), channel_id=1, source_target_pairs={{0,16},{16,32},{32,48},{48,0},{1,17},{17,33},{33,49},{49,1},{2,18}... | collective-permute-start | bytes 1228808 | tf_op jit(solution)/shard_map/ppermute | solution.py:282
  130.5 13.9 %collective-permute-start.27 = (bf16[8,40,640]{2,1,0:T(8,128)(2,1)S(1)}, bf16[8,40,640]{2,1,0:T(8,128)(2,1)S(1)}, u32[]{:S(2)}, u32[]{:S(2)}) collective-permute-start(bf16[8,40,640]{2,1,0:T(8,128)(2,1)S(1)} %get-tuple-element.62), channel_id=1, source_target_pairs={{0,32},{16,48},{32,0},{48,16},{1,33},{17,49},{33,1},{49,17},{2,34}... | collective-permute-start | bytes 1228808 | tf_op jit(solution)/shard_map/ppermute | solution.py:282
  132.2 19.7 %collective-permute-start.28 = (bf16[8,40,640]{2,1,0:T(8,128)(2,1)S(1)}, bf16[8,40,640]{2,1,0:T(8,128)(2,1)S(1)}, u32[]{:S(2)}, u32[]{:S(2)}) collective-permute-start(bf16[8,40,640]{2,1,0:T(8,128)(2,1)S(1)} %get-tuple-element.63), channel_id=1, source_target_pairs={{0,48},{16,0},{32,16},{48,32},{1,49},{17,1},{33,17},{49,33},{2,50}... | collective-permute-start | bytes 1228808 | tf_op jit(solution)/shard_map/ppermute | solution.py:282
  133.7 27.0 %collective-permute-start.23 = (bf16[192,1280]{1,0:T(8,128)(2,1)}, bf16[192,1280]{1,0:T(8,128)(2,1)S(1)}, u32[]{:S(2)}, u32[]{:S(2)}) collective-permute-start(bf16[192,1280]{1,0:T(8,128)(2,1)} %get-tuple-element.57), channel_id=1, source_target_pairs={{0,6},{2,0},{4,2},{6,4},{1,7},{3,1},{5,3},{7,5},{8,14},{10,8},{12,... | collective-permute-start | bytes 1474568 | tf_op jit(solution)/shard_map/ppermute | solution.py:282
  134.7 26.0 %collective-permute-start.24 = (bf16[192,1280]{1,0:T(8,128)(2,1)}, bf16[192,1280]{1,0:T(8,128)(2,1)S(1)}, u32[]{:S(2)}, u32[]{:S(2)}) collective-permute-start(bf16[192,1280]{1,0:T(8,128)(2,1)} %get-tuple-element.58), channel_id=1, source_target_pairs={{0,4},{2,6},{4,0},{6,2},{1,5},{3,7},{5,1},{7,3},{8,12},{10,14},{12... | collective-permute-start | bytes 1474568 | tf_op jit(solution)/shard_map/ppermute | solution.py:282
  141.3 19.4 %collective-permute-start.25 = (bf16[192,1280]{1,0:T(8,128)(2,1)}, bf16[192,1280]{1,0:T(8,128)(2,1)S(1)}, u32[]{:S(2)}, u32[]{:S(2)}) collective-permute-start(bf16[192,1280]{1,0:T(8,128)(2,1)} %get-tuple-element.59), channel_id=1, source_target_pairs={{0,2},{2,4},{4,6},{6,0},{1,3},{3,5},{5,7},{7,1},{8,10},{10,12},{12... | collective-permute-start | bytes 1474568 | tf_op jit(solution)/shard_map/ppermute | solution.py:282
  152.9 22.2 %all-to-all-start.1 = ((bf16[8,40,640]{2,1,0:T(8,128)(2,1)}), bf16[8,40,640]{2,1,0:T(8,128)(2,1)S(1)}, u32[]{:S(2)}, u32[]{:S(2)}) async-start(bf16[8,40,640]{2,1,0:T(8,128)(2,1)} %x_sum.1), calls=%async_computation.1 | async-start | bytes 819200 | tf_op jit(solution)/shard_map/all_to_all | solution.py:387
Sparse Core Ops, SparseCore 0:
  9.8 35.3 all-gather.1

commit v5 on v4

--- a/solution.py
+++ b/solution.py
@@ -87,7 +87,16 @@
     return up, jnp.where(used, down, 0.0)
 
 
-def route_kernel(owner, live, rows, outgoing):
+def route_kernel(owner_in, live_in, rows_in, outgoing, owner, live, rows, arrival):
+    copies = [
+        pltpu.make_async_copy(owner_in, owner, arrival.at[0]),
+        pltpu.make_async_copy(live_in, live, arrival.at[1]),
+        pltpu.make_async_copy(rows_in, rows, arrival.at[2]),
+    ]
+    for copy in copies:
+        copy.start()
+    copies[0].wait()
+    copies[1].wait()
     count = rows.shape[0]
     diagonal = iota((count, count), 0) == iota((count, count), 1)
     target = jnp.sum(jnp.where(diagonal, owner[...], 0), axis=1, keepdims=True)
@@ -103,6 +112,7 @@
     flag_row = (target * PAD + CAP == slot).astype(bf16)
     flag_value = jnp.where(position == iota((count, 128), 1), state, 0.0).astype(bf16)
     first = ((0,), (0,))
+    copies[2].wait()
     outgoing[...] = dot(placement, rows[...], first).astype(bf16)
     flags = dot(flag_row, flag_value, first)
     outgoing[:, :128] = (outgoing[:, :128].astype(f32) + flags).astype(bf16)
@@ -142,34 +152,11 @@
     block[SLOTS:, :] = jnp.broadcast_to(as_row, (16, CH)).astype(bf16)
 
 
-def weights_kernel(place, *refs):
-    pieces, (up, down, wide_up, wide_down) = refs[:8], refs[8:]
-    zh, x, c, zl = place[0], place[1], place[2], place[3]
-    for core in range(2):
-        for step in range(4):
-            piece = pieces[core * 4 + step]
-            base = lax.rem(x - step + 4, 4) * 80 + lax.rem(c + core, 2) * 40
-
-            def one(k, carry):
-                row = lax.rem(zh - k // 2 + 4, 4) * 320 + base
-                half = lax.rem(zl + k, 2)
-                rows = pl.ds(pl.multiple_of(row, 8), BLOCK)
-                a, b = unpack_pair(piece[k].astype(f32))
-                wide_up[half, rows, :] = a
-                wide_down[half, rows, :] = b
-                return carry
-
-            lax.fori_loop(0, 8, one, 0, unroll=True)
-    for half in range(2):
-        up[:, half * LANES : (half + 1) * LANES] = wide_up[half].astype(bf16)
-        down[:, half * LANES : (half + 1) * LANES] = wide_down[half].astype(bf16)
-
-
-def ffn_kernel(place, cot_in, up_in, down_in, *refs):
-    blocks, protos, refs = refs[:4], refs[4:8], refs[8:]
+def ffn_kernel(place, blocks, own_pair, other_pair, *refs):
+    cots, protos, refs = refs[:4], refs[4:8], refs[8:]
     own, away1, away2, away3, kept, sent, refs = *refs[:6], refs[6:]
     proj, feats, live, normed, hidden, grad_pre, grad_out, wide_up, wide_down, *refs = refs
-    cot, up, down, arrival = refs
+    cot, up, down, raw, arrival = refs
     y, zl, c = place[0], place[1], place[2]
     copies = []
 
@@ -178,17 +165,33 @@
         copy.start()
         copies.append(copy)
 
+    for k, pair in enumerate((own_pair, other_pair)):
+        for other in range(2):
+            fetch(pair.at[:, other], raw.at[lax.rem(c + k, 2), lax.rem(zl + other, 2)])
     for step in range(4):
-        fetch(blocks[step], feats.at[step])
+        fetch(blocks.at[lax.rem(y - step + 4, 4)], feats.at[step])
     for step in range(4):
         for other in range(2):
             start = lax.rem(y - step + 4, 4) * 128 + lax.rem(zl + other, 2) * 64
             rows = pl.ds(pl.multiple_of(start, 64), 64)
             fetch(protos[step].at[pl.ds(other * 64, 64), :], proj.at[rows, :])
-    fetch(up_in, up)
-    fetch(down_in, down)
-    fetch(cot_in, cot)
-    for copy in copies[:13]:
+    for step in range(4):
+        fetch(cots[step], cot.at[pl.ds(step * SLOTS, SLOTS), :])
+    for copy in copies[:4]:
+        copy.wait()
+
+    def assemble(place, carry):
+        rows = pl.ds(pl.multiple_of(place * 2 * BLOCK, 16), 2 * BLOCK)
+        for half in range(2):
+            lanes = slice(half * LANES, (half + 1) * LANES)
+            up0, down0 = unpack_pair(raw[0, half, place].astype(f32))
+            up1, down1 = unpack_pair(raw[1, half, place].astype(f32))
+            up[rows, lanes] = jnp.concatenate([up0, up1], axis=0).astype(bf16)
+            down[rows, lanes] = jnp.concatenate([down0, down1], axis=0).astype(bf16)
+        return carry
+
+    lax.fori_loop(0, 16, assemble, 0, unroll=4)
+    for copy in copies[4:]:
         copy.wait()
     for step in range(4):
         flags = feats[step, SLOTS : SLOTS + 16, :].astype(f32)[:1, :]
@@ -205,12 +208,6 @@
         density = jnp.exp(-0.5 * pre * pre) * 0.3989422804014327
         hidden[rows, :] = (pre * cumulative).astype(bf16)
         slope = cumulative + pre * density
-
-        @pl.when(step == 0)
-        def _():
-            copies[13].wait()
-            copies[14].wait()
-
         partial = dot(hidden[rows, :], down[...], ((1,), (1,)))
 
         @pl.when(step == 0)
@@ -223,8 +220,7 @@
             def _():
                 away[...] = partial.astype(bf16)
 
-        there = lax.rem(y - step + 4, 4) * SLOTS
-        masked = cot[pl.ds(pl.multiple_of(there, SLOTS), SLOTS), :].astype(f32) * live[step]
+        masked = cot[rows, :].astype(f32) * live[step]
         grad_out[rows, :] = masked.astype(bf16)
         grad_hidden = dot(grad_out[rows, :], down[...])
         grad_pre[rows, :] = (grad_hidden * slope).astype(bf16)
@@ -289,8 +285,6 @@
 def per_device(waveform_rows, conv_weight, proj_weight, ffn_pair, owner, frame_live, cotangent):
     dp = ("zh", "x", "c")
     zh, x, c, y, zl = (lax.axis_index(name).astype(i32) for name in ("zh", "x", "c", "y", "zl"))
-    cot_all = lax.all_gather(cotangent, "y", axis=0, tiled=True)
-
     packed = call(
         pack_kernel,
         jax.ShapeDtypeStruct((BLOCK, 2 * UNITS), bf16),
@@ -300,25 +294,33 @@
     both = jnp.stack([packed, ring(packed, "zl", 2, 1)])
     conv_pair = jnp.concatenate([conv_weight, ring(conv_weight, "zl", 2, 1)], axis=0)
     proj_pair = jnp.concatenate([proj_weight, ring(proj_weight, "zl", 2, 1)], axis=0)
-    along_z = jnp.concatenate(around(both, "zh", 4), axis=0)
+    own_pair = lax.all_gather(both, ("zh", "x"), axis=0)
 
     outgoing = call(
         route_kernel,
         jax.ShapeDtypeStruct((N_DP * PAD, 1024), bf16),
         [owner.reshape(1, -1), frame_live.reshape(1, -1), waveform_rows],
-        2 * 256 * 128 * 1152, 1 << 20, name="route",
-    )
-    outgoing, along_z, conv_pair, proj_pair = lax.optimization_barrier(
-        (outgoing, along_z, conv_pair, proj_pair)
-    )
-    along_x = around(along_z, "x", 4)
+        2 * 256 * 128 * 1152, 1 << 20,
+        scratch=[
+            pltpu.VMEM((1, 128), i32),
+            pltpu.VMEM((1, 128), i32),
+            pltpu.VMEM((128, 1024), bf16),
+            pltpu.SemaphoreType.DMA((3,)),
+        ],
+        hbm=3, name="route",
+    )
+    cot_pieces = around(cotangent, "y", 4)
+    outgoing, both, conv_pair, proj_pair, cot_pieces[1], cot_pieces[3] = (
+        lax.optimization_barrier(
+            (outgoing, both, conv_pair, proj_pair, cot_pieces[1], cot_pieces[3])
+        )
+    )
     conv_pieces = around(conv_pair, "y", 4)
-    proj_pair, _ = lax.optimization_barrier((proj_pair, conv_pieces[1]))
+    proj_pair, *conv_pieces[1:] = lax.optimization_barrier((proj_pair, *conv_pieces[1:]))
     proj_pieces = around(proj_pair, "y", 4)
     incoming = lax.all_to_all(
         outgoing.reshape(N_DP, PAD, 1024), dp, split_axis=0, concat_axis=0, tiled=True
     ).reshape(N_DP * PAD, 1024)
-    incoming, *proj_pieces = lax.optimization_barrier((incoming, *proj_pieces))
 
     block, flags = call(
         front_kernel,
@@ -331,24 +333,22 @@
         scratch=[pltpu.VMEM((1024, CH), bf16), pltpu.SemaphoreType.DMA((8,))],
         smem=1, hbm=4, name="front",
     )
-    blocks = around(block, "y", 4)
-    _, _, _, *along_x = lax.optimization_barrier((*blocks[1:], *along_x))
-    pieces = along_x + [ring(piece, "c", 2, 1) for piece in along_x]
-
-    up, down = call(
-        weights_kernel,
-        (jax.ShapeDtypeStruct((D, WIDE), bf16),) * 2,
-        [jnp.stack([zh, x, c, zl]), *pieces],
-        1 << 22, 8 << 20,
-        scratch=[pltpu.VMEM((2, D, LANES), f32)] * 2, vmem=24 << 20, smem=1, name="weights",
-    )
+    block, cot_pieces[2], *proj_pieces = lax.optimization_barrier(
+        (block, cot_pieces[2], *proj_pieces)
+    )
+    blocks = lax.all_to_all(
+        jnp.broadcast_to(block[None], (4,) + block.shape), "y", split_axis=0, concat_axis=0
+    )
+    blocks, own_pair = lax.optimization_barrier((blocks, own_pair))
+    other_pair = ring(own_pair, "c", 2, 1)
+
     rows = 4 * SLOTS
     piece = jax.ShapeDtypeStruct((SLOTS, D), bf16)
     terms = jax.ShapeDtypeStruct((4, 8, BLOCK, 2 * UNITS), bf16)
     own, away1, away2, away3, kept, sent = call(
         ffn_kernel,
         (jax.ShapeDtypeStruct((SLOTS, D), f32), piece, piece, piece, terms, terms),
-        [jnp.stack([y, zl, c]), cot_all, up, down, *blocks, *proj_pieces],
+        [jnp.stack([y, zl, c]), blocks, own_pair, other_pair, *cot_pieces, *proj_pieces],
         2 * rows * D * (CH + 5 * WIDE), 16 << 20,
         scratch=[
             pltpu.VMEM((CH, D), bf16),
@@ -363,7 +363,8 @@
             pltpu.VMEM((rows, D), bf16),
             pltpu.VMEM((D, WIDE), bf16),
             pltpu.VMEM((D, WIDE), bf16),
-            pltpu.SemaphoreType.DMA((15,)),
+            pltpu.VMEM((2, 2, 16, BLOCK, 2 * UNITS), bf16),
+            pltpu.SemaphoreType.DMA((20,)),
         ],
         vmem=36 << 20, smem=1, hbm=11, name="ffn",
     )

time: 184 us -> 184 us (level)
  blocking collectives: 0 us -> 16.6 us
  starting transfers between devices: 52.8 us -> 42.1 us
  local copies, waits for them, and re-layouts: 7.15 us -> 3.06 us
    all_to_all x0 -> x1, blocking collectives: none -> 16.6 us  [per_device(): lax.all_to_all(jnp.broadcast_to(block[None], (4,) + block.shape), 'y', sp...]
    ppermute x29 -> x20, starting transfers between devices: 37.9 us -> 23.8 us  [ring(): lax.ppermute(values, axis, [(k, (k + step) % size) for k in range(size)])]
    all_to_all x1, starting transfers between devices: 7.21 us -> 11.4 us  [per_device(): lax.all_to_all(outgoing.reshape(N_DP, PAD, 1024), dp, split_axis=0, conca...]
    unnamed x40 -> x28, local copies, waits for them, and re-layouts: 7.13 us -> 3 us
    pallas_call x8 -> x7, Pallas kernels: 30.3 us -> 29.5 us  [call(): pl.pallas_call(kernel, out_shape=out_shape, in_specs=[SMEM] * smem + [VME...]
    ppermute x29 -> x20, waiting for transfers between devices: 61.8 us -> 61.6 us  [ring(): lax.ppermute(values, axis, [(k, (k + step) % size) for k in range(size)])]
  transfers between devices with their start and end apart: 32 -> 23, of which waited for: 20 -> 19; matrix products, arithmetic and copies ran while one was open for 1% -> 1% of each run, Pallas kernels for 4% -> 3%
where the time goes in v5:
time: 184 us; the launch traced here: 183 us
  waiting for transfers between devices  74.8 us (41%)
  starting transfers between devices  42.1 us (23%)
  Pallas kernels  29.5 us (16%)
  blocking collectives  16.6 us (9%)
  between operations  14.2 us (8%)
  local copies, waits for them, and re-layouts  3.06 us (2%)
  other arithmetic  2.88 us (2%)
    ppermute x20, waiting for transfers between devices, ring(): lax.ppermute(values, axis, [(k, (k + step) % size) for k in range(size)])  61.6 us
    pallas_call x7, Pallas kernels, call(): pl.pallas_call(kernel, out_shape=out_shape, in_specs=[SMEM] * smem + [VME...  29.5 us
    ppermute x20, starting transfers between devices, ring(): lax.ppermute(values, axis, [(k, (k + step) % size) for k in range(size)])  23.8 us
    all_to_all x1, blocking collectives, per_device(): lax.all_to_all(jnp.broadcast_to(block[None], (4,) + block.shape), 'y', sp...  16.6 us
    all_to_all x1, waiting for transfers between devices, per_device(): total = lax.all_to_all(total, ZX, split_axis=0, concat_axis=0, tiled=True)  13.2 us
    all_to_all x1, starting transfers between devices, per_device(): lax.all_to_all(outgoing.reshape(N_DP, PAD, 1024), dp, split_axis=0, conca...  11.4 us
    all_to_all x1, starting transfers between devices, per_device(): total = lax.all_to_all(total, ZX, split_axis=0, concat_axis=0, tiled=True)  6.86 us
  transfers between devices with their start and end apart: 23, of which 19 were waited for; matrix products, arithmetic and copies ran while one was open for 1% of the time, Pallas kernels for 3%

profile of v5, /device:TPU:2, one launch (start us, length us, event | category | flops | bytes accessed | tf_op | source)
XLA Modules:
  0.0 183.2 jit_solution(13217899742672307575)
XLA Ops:
  7.2 0.0 all-gather.3.cloned.1.call-start
  7.2 0.8 copy-done.2
  8.0 0.1 pack.1
  8.1 2.0 %collective-permute-start = (bf16[40,640]{1,0:T(8,128)(2,1)S(1)}, bf16[40,640]{1,0:T(8,128)(2,1)S(1)}, u32[]{:S(2)}, u32[]{:S(2)}) collective-permute-start(bf16[40,640]{1,0:T(8,128)(2,1)S(1)} %pack.1), channel_id=1, source_target_pairs={{0,1},{1,0},{2,3},{3,2},{4,5},{5,4},{6,7},{7,6},{8,9},{9,8},{10,11... | collective-permute-start | bytes 153608 | tf_op jit(solution)/shard_map/ppermute | solution.py:278
  10.1 2.2 %collective-permute-done = bf16[40,640]{1,0:T(8,128)(2,1)S(1)} collective-permute-done((bf16[40,640]{1,0:T(8,128)(2,1)S(1)}, bf16[40,640]{1,0:T(8,128)(2,1)S(1)}, u32[]{:S(2)}, u32[]{:S(2)}) %collective-permute-start) | collective-permute-done | bytes 51232 | tf_op jit(solution)/shard_map/ppermute | solution.py:278
  12.3 0.7 pad_maximum_fusion.2
  13.0 0.0 all-gather.3.cloned.1.call-update
  13.0 3.1 %collective-permute-start.4 = (bf16[192,1280]{1,0:T(8,128)(2,1)}, bf16[192,1280]{1,0:T(8,128)(2,1)S(1)}, u32[]{:S(2)}, u32[]{:S(2)}) collective-permute-start(bf16[192,1280]{1,0:T(8,128)(2,1)} %refs_0_.1), channel_id=1, source_target_pairs={{0,6},{2,0},{4,2},{6,4},{1,7},{3,1},{5,3},{7,5},{8,14},{10,8},{12,... | collective-permute-start | bytes 1474568 | tf_op jit(solution)/shard_map/ppermute | solution.py:278
  16.1 0.0 collective-permute-start.3
  16.1 1.9 %collective-permute-start.1 = (bf16[128,512]{1,0:T(8,128)(2,1)}, bf16[128,512]{1,0:T(8,128)(2,1)S(1)}, u32[]{:S(2)}, u32[]{:S(2)}) collective-permute-start(bf16[128,512]{1,0:T(8,128)(2,1)} %param.8), channel_id=1, source_target_pairs={{0,1},{1,0},{2,3},{3,2},{4,5},{5,4},{6,7},{7,6},{8,9},{9,8},{10,11... | collective-permute-start | bytes 393224 | tf_op jit(solution)/shard_map/ppermute | solution.py:278
  18.0 0.1 collective-permute-start.2
  18.1 2.2 %route.1 = bf16[256,1024]{1,0:T(8,128)(2,1)} custom-call(s32[1,128]{1,0:T(1,128)} %bitcast.18, s32[1,128]{1,0:T(1,128)} %bitcast.19, bf16[128,1024]{1,0:T(8,128)(2,1)} %rows_in.1), custom_call_target="tpu_custom_call" | custom-call | flops 75497472 | bytes 1048576 | tf_op jit(solution)/shard_map/route/pallas_call | solution.py:53
  20.3 1.8 collective-permute-done.1
  22.1 0.9 pad_maximum_fusion.1.refs_0_
  23.0 0.0 copy-start.3
  23.0 0.8 collective-permute-done.2
  23.9 2.0 %collective-permute-done.4.refs_3_ = bf16[192,1280]{1,0:T(8,128)(2,1)S(1)} collective-permute-done((bf16[192,1280]{1,0:T(8,128)(2,1)}, bf16[192,1280]{1,0:T(8,128)(2,1)S(1)}, u32[]{:S(2)}, u32[]{:S(2)}) %collective-permute-start.4) | collective-permute-done | bytes 491552 | tf_op jit(solution)/shard_map/ppermute | solution.py:278
  25.9 3.4 %collective-permute-done.3.refs_1_ = bf16[192,1280]{1,0:T(8,128)(2,1)} collective-permute-done((bf16[192,1280]{1,0:T(8,128)(2,1)}, bf16[192,1280]{1,0:T(8,128)(2,1)}, u32[]{:S(2)}, u32[]{:S(2)}) %collective-permute-start.3) | collective-permute-done | bytes 491552 | tf_op jit(solution)/shard_map/ppermute | solution.py:278
  29.3 11.4 %all-to-all-start = ((bf16[32,8,1024]{2,1,0:T(8,128)(2,1)}), bf16[32,8,1024]{2,1,0:T(8,128)(2,1)S(1)}, u32[]{:S(2)}, u32[]{:S(2)}) async-start(bf16[32,8,1024]{2,1,0:T(8,128)(2,1)} %bitcast.8), calls=%async_computation | async-start | bytes 1048576 | tf_op jit(solution)/shard_map/all_to_all | solution.py:321
  40.8 1.0 collective-permute-start.7
  41.8 0.2 collective-permute-start.6
  42.0 0.9 collective-permute-start.5
  42.9 4.1 %collective-permute-start.8 = (bf16[192,1280]{1,0:T(8,128)(2,1)S(1)}, bf16[192,1280]{1,0:T(8,128)(2,1)S(1)}, u32[]{:S(2)}, u32[]{:S(2)}) collective-permute-start(bf16[192,1280]{1,0:T(8,128)(2,1)S(1)} %copy-done.10), channel_id=1, source_target_pairs={{0,4},{2,6},{4,0},{6,2},{1,5},{3,7},{5,1},{7,3},{8,12},{10,14},{12... | collective-permute-start | bytes 1474568 | tf_op jit(solution)/shard_map/ppermute | solution.py:278
  47.0 3.0 %collective-permute-done.7.refs_3_ = bf16[256,512]{1,0:T(8,128)(2,1)S(1)} collective-permute-done((bf16[256,512]{1,0:T(8,128)(2,1)S(1)}, bf16[256,512]{1,0:T(8,128)(2,1)S(1)}, u32[]{:S(2)}, u32[]{:S(2)}) %collective-permute-start.7) | collective-permute-done | bytes 262176 | tf_op jit(solution)/shard_map/ppermute | solution.py:278
  50.0 2.5 %collective-permute-done.6.refs_2_ = bf16[256,512]{1,0:T(8,128)(2,1)S(1)} collective-permute-done((bf16[256,512]{1,0:T(8,128)(2,1)S(1)}, bf16[256,512]{1,0:T(8,128)(2,1)S(1)}, u32[]{:S(2)}, u32[]{:S(2)}) %collective-permute-start.6) | collective-permute-done | bytes 262176 | tf_op jit(solution)/shard_map/ppermute | solution.py:278
  52.6 5.5 %collective-permute-done.5.refs_1_ = bf16[256,512]{1,0:T(8,128)(2,1)S(1)} collective-permute-done((bf16[256,512]{1,0:T(8,128)(2,1)S(1)}, bf16[256,512]{1,0:T(8,128)(2,1)S(1)}, u32[]{:S(2)}, u32[]{:S(2)}) %collective-permute-start.5) | collective-permute-done | bytes 262176 | tf_op jit(solution)/shard_map/ppermute | solution.py:278
  58.1 0.7 collective-permute-start.11
  58.7 0.2 collective-permute-start.10
  58.9 1.2 collective-permute-start.9
  60.1 0.1 pad_add_fusion.1.place
  60.2 0.0 all-to-all-done
  60.2 2.9 %front.1 = (bf16[208,512]{1,0:T(8,128)(2,1)S(1)}, f32[192,1]{1,0:T(8,128)S(1)}) custom-call(s32[2]{0:T(128)S(1)} %pad_add_fusion.1.place, bf16[256,1024]{1,0:T(8,128)(2,1)S(1)} %bitcast.13, bf16[256,512]{1,0:T(8,128)(2,1)} %copy-done.3, bf16[256,512]{1,0:T(8,128)(2,1)} %copy-done.7, bf16[256,512]{1,0:T(8,128)(2,1)} %copy-done.6, bf16[256,512]{1,0:T(8,128)(2,1)} %copy-done.5), custom_call_target="tpu_custom_call" | custom-call | flops 268435456 | bytes 2097152 | tf_op jit(solution)/shard_map/front/pallas_call | solution.py:53
  63.1 5.7 %collective-permute-done.8.refs_2_ = bf16[192,1280]{1,0:T(8,128)(2,1)S(1)} collective-permute-done((bf16[192,1280]{1,0:T(8,128)(2,1)S(1)}, bf16[192,1280]{1,0:T(8,128)(2,1)S(1)}, u32[]{:S(2)}, u32[]{:S(2)}) %collective-permute-start.8) | collective-permute-done | bytes 491552 | tf_op jit(solution)/shard_map/ppermute | solution.py:278
  68.8 4.4 %collective-permute-done.11.refs_7_ = bf16[128,1280]{1,0:T(8,128)(2,1)S(1)} collective-permute-done((bf16[128,1280]{1,0:T(8,128)(2,1)S(1)}, bf16[128,1280]{1,0:T(8,128)(2,1)S(1)}, u32[]{:S(2)}, u32[]{:S(2)}) %collective-permute-start.11) | collective-permute-done | bytes 327712 | tf_op jit(solution)/shard_map/ppermute | solution.py:278
  73.2 2.7 %collective-permute-done.10.refs_6_ = bf16[128,1280]{1,0:T(8,128)(2,1)} collective-permute-done((bf16[128,1280]{1,0:T(8,128)(2,1)S(1)}, bf16[128,1280]{1,0:T(8,128)(2,1)}, u32[]{:S(2)}, u32[]{:S(2)}) %collective-permute-start.10) | collective-permute-done | bytes 327712 | tf_op jit(solution)/shard_map/ppermute | solution.py:278
  75.9 5.9 %collective-permute-done.9.refs_5_ = bf16[128,1280]{1,0:T(8,128)(2,1)} collective-permute-done((bf16[128,1280]{1,0:T(8,128)(2,1)S(1)}, bf16[128,1280]{1,0:T(8,128)(2,1)}, u32[]{:S(2)}, u32[]{:S(2)}) %collective-permute-start.9) | collective-permute-done | bytes 327712 | tf_op jit(solution)/shard_map/ppermute | solution.py:278
  81.8 0.1 broadcast_in_dim.4
  81.8 16.6 %all_to_all.15.blocks = bf16[4,208,512]{2,1,0:T(8,128)(2,1)} all-to-all(bf16[4,208,512]{2,1,0:T(8,128)(2,1)S(1)} %broadcast_in_dim.4), channel_id=1, replica_groups=mesh['zh'=4,'x'=4,'c'=2,'y'=4,'zl'=2] {'y'}, dimensions={0} | all-to-all | bytes 1703936 | tf_op jit(solution)/shard_map/all_to_all | solution.py:339
  98.4 0.3 collective-permute-start.12
  98.7 0.1 pad_add_fusion.place
  98.8 3.6 %collective-permute-done.12.other_pair = bf16[16,2,40,640]{3,2,1,0:T(8,128)(2,1)S(1)} collective-permute-done((bf16[16,2,40,640]{3,2,1,0:T(8,128)(2,1)}, bf16[16,2,40,640]{3,2,1,0:T(8,128)(2,1)S(1)}, u32[]{:S(2)}, u32[]{:S(2)}) %collective-permute-start.12) | collective-permute-done | bytes 1638432 | tf_op jit(solution)/shard_map/ppermute | solution.py:278
  102.4 1.2 copy-done.9
  103.6 22.3 %ffn.1 = (f32[192,1280]{1,0:T(8,128)S(1)}, bf16[192,1280]{1,0:T(8,128)(2,1)}, bf16[192,1280]{1,0:T(8,128)(2,1)}, bf16[192,1280]{1,0:T(8,128)(2,1)}, bf16[4,8,40,...) custom-call(s32[3]{0:T(128)S(1)} %pad_add_fusion.place, bf16[4,208,512]{2,1,0:T(8,128)(2,1)} %all_to_all.15.blocks, ...), custom_call_target="tpu_custom_call" | custom-call | flops 8556380160 | bytes 16777216 | tf_op jit(solution)/shard_map/ffn/pallas_call | solution.py:53
  125.9 0.9 copy-done
  126.8 0.2 collective-permute-start.13
  127.0 3.6 %collective-permute-done.13.arrived = bf16[4,8,40,640]{3,2,1,0:T(8,128)(2,1)S(1)} collective-permute-done((bf16[4,8,40,640]{3,2,1,0:T(8,128)(2,1)}, bf16[4,8,40,640]{3,2,1,0:T(8,128)(2,1)S(1)}, u32[]{:S(2)}, u32[]{:S(2)}) %collective-permute-start.13) | collective-permute-done | bytes 1638432 | tf_op jit(solution)/shard_map/ppermute | solution.py:278
  130.6 0.4 core_sum.1
  131.0 1.5 collective-permute-start.17
  132.5 1.0 collective-permute-start.18
  133.5 2.2 %collective-permute-start.19 = (bf16[8,40,640]{2,1,0:T(8,128)(2,1)S(1)}, bf16[8,40,640]{2,1,0:T(8,128)(2,1)S(1)}, u32[]{:S(2)}, u32[]{:S(2)}) collective-permute-start(bf16[8,40,640]{2,1,0:T(8,128)(2,1)S(1)} %get-tuple-element.65), channel_id=1, source_target_pairs={{0,48},{16,0},{32,16},{48,32},{1,49},{17,1},{33,17},{49,33},{2,50}... | collective-permute-start | bytes 1228808 | tf_op jit(solution)/shard_map/ppermute | solution.py:278
  135.7 1.2 collective-permute-start.14
  136.9 1.4 collective-permute-start.15
  138.3 5.0 %collective-permute-done.17.refs_1_ = bf16[8,40,640]{2,1,0:T(8,128)(2,1)S(1)} collective-permute-done((bf16[8,40,640]{2,1,0:T(8,128)(2,1)S(1)}, bf16[8,40,640]{2,1,0:T(8,128)(2,1)S(1)}, u32[]{:S(2)}, u32[]{:S(2)}) %collective-permute-start.17) | collective-permute-done | bytes 409632 | tf_op jit(solution)/shard_map/ppermute | solution.py:278
  143.3 0.6 collective-permute-start.16
  143.9 2.4 %collective-permute-done.18.refs_2_ = bf16[8,40,640]{2,1,0:T(8,128)(2,1)S(1)} collective-permute-done((bf16[8,40,640]{2,1,0:T(8,128)(2,1)S(1)}, bf16[8,40,640]{2,1,0:T(8,128)(2,1)S(1)}, u32[]{:S(2)}, u32[]{:S(2)}) %collective-permute-start.18) | collective-permute-done | bytes 409632 | tf_op jit(solution)/shard_map/ppermute | solution.py:278
  146.4 6.9 %collective-permute-done.19.refs_3_ = bf16[8,40,640]{2,1,0:T(8,128)(2,1)S(1)} collective-permute-done((bf16[8,40,640]{2,1,0:T(8,128)(2,1)S(1)}, bf16[8,40,640]{2,1,0:T(8,128)(2,1)S(1)}, u32[]{:S(2)}, u32[]{:S(2)}) %collective-permute-start.19) | collective-permute-done | bytes 409632 | tf_op jit(solution)/shard_map/ppermute | solution.py:278
  153.2 1.0 x_sum.1
  154.2 6.9 %all-to-all-start.2 = ((bf16[8,40,640]{2,1,0:T(8,128)(2,1)}), bf16[8,40,640]{2,1,0:T(8,128)(2,1)S(1)}, u32[]{:S(2)}, u32[]{:S(2)}) async-start(bf16[8,40,640]{2,1,0:T(8,128)(2,1)} %x_sum.1), calls=%async_computation.2 | async-start | bytes 819200 | tf_op jit(solution)/shard_map/all_to_all | solution.py:388
  161.0 0.1 convert_reduce_fusion
  161.1 0.0 collective-permute-done.14
  161.2 0.1 collective-permute-done.16
  161.3 1.0 multiply_convert_fusion
  162.3 13.2 %all-to-all-done.2.arrived = bf16[8,40,640]{2,1,0:T(8,128)(2,1)S(1)} async-done(((bf16[8,40,640]{2,1,0:T(8,128)(2,1)}), bf16[8,40,640]{2,1,0:T(8,128)(2,1)S(1)}, u32[]{:S(2)}, u32[]{:S(2)}) %all-to-all-start.2) | async-done | bytes 409632 | tf_op jit(solution)/shard_map/all_to_all | solution.py:388
  175.6 0.8 last.1
  (27 shorter events, 0.1 us)
Async XLA Ops:
  7.2 91.3 %all-gather.3.cloned.1.call-start = ((), (), s32[]{:S(2)}) async-start(), calls=%async_computation.3 | async-start | bytes 1740800 | tf_op jit(solution)/shard_map/all_gather | solution.py:297
  7.2 0.8 copy-start.2
  8.0 15.8 %copy-start.8 = (bf16[64,1280]{1,0:T(8,128)(2,1)S(1)}, bf16[64,1280]{1,0:T(8,128)(2,1)}, u32[]{:S(2)}) copy-start(bf16[64,1280]{1,0:T(8,128)(2,1)} %param.9) | copy-start | bytes 491524
  8.1 4.2 %collective-permute-start = (bf16[40,640]{1,0:T(8,128)(2,1)S(1)}, bf16[40,640]{1,0:T(8,128)(2,1)S(1)}, u32[]{:S(2)}, u32[]{:S(2)}) collective-permute-start(bf16[40,640]{1,0:T(8,128)(2,1)S(1)} %pack.1), channel_id=1, source_target_pairs={{0,1},{1,0},{2,3},{3,2},{4,5},{5,4},{6,7},{7,6},{8,9},{9,8},{10,11... | collective-permute-start | bytes 153608 | tf_op jit(solution)/shard_map/ppermute | solution.py:278
  12.3 30.6 %copy-start.10 = (bf16[192,1280]{1,0:T(8,128)(2,1)S(1)}, bf16[192,1280]{1,0:T(8,128)(2,1)}, u32[]{:S(2)}) copy-start(bf16[192,1280]{1,0:T(8,128)(2,1)} %refs_0_.1) | copy-start | bytes 1474564
  13.0 12.9 %collective-permute-start.4 = (bf16[192,1280]{1,0:T(8,128)(2,1)}, bf16[192,1280]{1,0:T(8,128)(2,1)S(1)}, u32[]{:S(2)}, u32[]{:S(2)}) collective-permute-start(bf16[192,1280]{1,0:T(8,128)(2,1)} %refs_0_.1), channel_id=1, source_target_pairs={{0,6},{2,0},{4,2},{6,4},{1,7},{3,1},{5,3},{7,5},{8,14},{10,8},{12,... | collective-permute-start | bytes 1474568 | tf_op jit(solution)/shard_map/ppermute | solution.py:278
  16.1 13.2 %collective-permute-start.3 = (bf16[192,1280]{1,0:T(8,128)(2,1)}, bf16[192,1280]{1,0:T(8,128)(2,1)}, u32[]{:S(2)}, u32[]{:S(2)}) collective-permute-start(bf16[192,1280]{1,0:T(8,128)(2,1)} %refs_0_.1), channel_id=1, source_target_pairs={{0,2},{2,4},{4,6},{6,0},{1,3},{3,5},{5,7},{7,1},{8,10},{10,12},{12... | collective-permute-start | bytes 1474568 | tf_op jit(solution)/shard_map/ppermute | solution.py:278
  16.1 6.0 %collective-permute-start.1 = (bf16[128,512]{1,0:T(8,128)(2,1)}, bf16[128,512]{1,0:T(8,128)(2,1)S(1)}, u32[]{:S(2)}, u32[]{:S(2)}) collective-permute-start(bf16[128,512]{1,0:T(8,128)(2,1)} %param.8), channel_id=1, source_target_pairs={{0,1},{1,0},{2,3},{3,2},{4,5},{5,4},{6,7},{7,6},{8,9},{9,8},{10,11... | collective-permute-start | bytes 393224 | tf_op jit(solution)/shard_map/ppermute | solution.py:278
  18.0 5.8 %collective-permute-start.2 = (bf16[64,1280]{1,0:T(8,128)(2,1)}, bf16[64,1280]{1,0:T(8,128)(2,1)S(1)}, u32[]{:S(2)}, u32[]{:S(2)}) collective-permute-start(bf16[64,1280]{1,0:T(8,128)(2,1)} %param.9), channel_id=1, source_target_pairs={{0,1},{1,0},{2,3},{3,2},{4,5},{5,4},{6,7},{7,6},{8,9},{9,8},{10,11... | collective-permute-start | bytes 491528 | tf_op jit(solution)/shard_map/ppermute | solution.py:278
  23.0 37.2 %copy-start.3 = (bf16[256,512]{1,0:T(8,128)(2,1)}, bf16[256,512]{1,0:T(8,128)(2,1)S(1)}, u32[]{:S(2)}) copy-start(bf16[256,512]{1,0:T(8,128)(2,1)S(1)} %pad_maximum_fusion.1.refs_0_) | copy-start | bytes 786436
  23.9 57.9 %copy-start.4 = (bf16[128,1280]{1,0:T(8,128)(2,1)}, bf16[128,1280]{1,0:T(8,128)(2,1)S(1)}, u32[]{:S(2)}) copy-start(bf16[128,1280]{1,0:T(8,128)(2,1)S(1)} %pad_maximum_fusion.refs_4_) | copy-start | bytes 983044
  25.9 3.4 %copy-start.11 = (bf16[192,1280]{1,0:T(8,128)(2,1)}, bf16[192,1280]{1,0:T(8,128)(2,1)S(1)}, u32[]{:S(2)}) copy-start(bf16[192,1280]{1,0:T(8,128)(2,1)S(1)} %collective-permute-done.4.refs_3_) | copy-start | bytes 1474564
  29.3 30.9 %all-to-all-start = ((bf16[32,8,1024]{2,1,0:T(8,128)(2,1)}), bf16[32,8,1024]{2,1,0:T(8,128)(2,1)S(1)}, u32[]{:S(2)}, u32[]{:S(2)}) async-start(bf16[32,8,1024]{2,1,0:T(8,128)(2,1)} %bitcast.8), calls=%async_computation | async-start | bytes 1048576 | tf_op jit(solution)/shard_map/all_to_all | solution.py:321
  40.8 9.2 %collective-permute-start.7 = (bf16[256,512]{1,0:T(8,128)(2,1)S(1)}, bf16[256,512]{1,0:T(8,128)(2,1)S(1)}, u32[]{:S(2)}, u32[]{:S(2)}) collective-permute-start(bf16[256,512]{1,0:T(8,128)(2,1)S(1)} %pad_maximum_fusion.1.refs_0_), channel_id=1, source_target_pairs={{0,6},{2,0},{4,2},{6,4},{1,7},{3,1},{5,3},{7,5},{8,14},{10,8},{12,... | collective-permute-start | bytes 786440 | tf_op jit(solution)/shard_map/ppermute | solution.py:278
  41.8 10.7 %collective-permute-start.6 = (bf16[256,512]{1,0:T(8,128)(2,1)S(1)}, bf16[256,512]{1,0:T(8,128)(2,1)S(1)}, u32[]{:S(2)}, u32[]{:S(2)}) collective-permute-start(bf16[256,512]{1,0:T(8,128)(2,1)S(1)} %pad_maximum_fusion.1.refs_0_), channel_id=1, source_target_pairs={{0,4},{2,6},{4,0},{6,2},{1,5},{3,7},{5,1},{7,3},{8,12},{10,14},{12... | collective-permute-start | bytes 786440 | tf_op jit(solution)/shard_map/ppermute | solution.py:278
  42.0 16.1 %collective-permute-start.5 = (bf16[256,512]{1,0:T(8,128)(2,1)S(1)}, bf16[256,512]{1,0:T(8,128)(2,1)S(1)}, u32[]{:S(2)}, u32[]{:S(2)}) collective-permute-start(bf16[256,512]{1,0:T(8,128)(2,1)S(1)} %pad_maximum_fusion.1.refs_0_), channel_id=1, source_target_pairs={{0,2},{2,4},{4,6},{6,0},{1,3},{3,5},{5,7},{7,1},{8,10},{10,12},{12... | collective-permute-start | bytes 786440 | tf_op jit(solution)/shard_map/ppermute | solution.py:278
  42.9 25.9 %collective-permute-start.8 = (bf16[192,1280]{1,0:T(8,128)(2,1)S(1)}, bf16[192,1280]{1,0:T(8,128)(2,1)S(1)}, u32[]{:S(2)}, u32[]{:S(2)}) collective-permute-start(bf16[192,1280]{1,0:T(8,128)(2,1)S(1)} %copy-done.10), channel_id=1, source_target_pairs={{0,4},{2,6},{4,0},{6,2},{1,5},{3,7},{5,1},{7,3},{8,12},{10,14},{12... | collective-permute-start | bytes 1474568 | tf_op jit(solution)/shard_map/ppermute | solution.py:278
  50.0 10.2 %copy-start.5 = (bf16[256,512]{1,0:T(8,128)(2,1)}, bf16[256,512]{1,0:T(8,128)(2,1)S(1)}, u32[]{:S(2)}) copy-start(bf16[256,512]{1,0:T(8,128)(2,1)S(1)} %collective-permute-done.7.refs_3_) | copy-start | bytes 786436
  52.6 7.7 %copy-start.6 = (bf16[256,512]{1,0:T(8,128)(2,1)}, bf16[256,512]{1,0:T(8,128)(2,1)S(1)}, u32[]{:S(2)}) copy-start(bf16[256,512]{1,0:T(8,128)(2,1)S(1)} %collective-permute-done.6.refs_2_) | copy-start | bytes 786436
  58.1 2.1 %copy-start.7 = (bf16[256,512]{1,0:T(8,128)(2,1)}, bf16[256,512]{1,0:T(8,128)(2,1)S(1)}, u32[]{:S(2)}) copy-start(bf16[256,512]{1,0:T(8,128)(2,1)S(1)} %collective-permute-done.5.refs_1_) | copy-start | bytes 786436
  58.1 15.1 %collective-permute-start.11 = (bf16[128,1280]{1,0:T(8,128)(2,1)S(1)}, bf16[128,1280]{1,0:T(8,128)(2,1)S(1)}, u32[]{:S(2)}, u32[]{:S(2)}) collective-permute-start(bf16[128,1280]{1,0:T(8,128)(2,1)S(1)} %pad_maximum_fusion.refs_4_), channel_id=1, source_target_pairs={{0,6},{2,0},{4,2},{6,4},{1,7},{3,1},{5,3},{7,5},{8,14},{10,8},{12,... | collective-permute-start | bytes 983048 | tf_op jit(solution)/shard_map/ppermute | solution.py:278
  58.7 17.1 %collective-permute-start.10 = (bf16[128,1280]{1,0:T(8,128)(2,1)S(1)}, bf16[128,1280]{1,0:T(8,128)(2,1)}, u32[]{:S(2)}, u32[]{:S(2)}) collective-permute-start(bf16[128,1280]{1,0:T(8,128)(2,1)S(1)} %pad_maximum_fusion.refs_4_), channel_id=1, source_target_pairs={{0,4},{2,6},{4,0},{6,2},{1,5},{3,7},{5,1},{7,3},{8,12},{10,14},{12... | collective-permute-start | bytes 983048 | tf_op jit(solution)/shard_map/ppermute | solution.py:278
  58.9 22.8 %collective-permute-start.9 = (bf16[128,1280]{1,0:T(8,128)(2,1)S(1)}, bf16[128,1280]{1,0:T(8,128)(2,1)}, u32[]{:S(2)}, u32[]{:S(2)}) collective-permute-start(bf16[128,1280]{1,0:T(8,128)(2,1)S(1)} %pad_maximum_fusion.refs_4_), channel_id=1, source_target_pairs={{0,2},{2,4},{4,6},{6,0},{1,3},{3,5},{5,7},{7,1},{8,10},{10,12},{12... | collective-permute-start | bytes 983048 | tf_op jit(solution)/shard_map/ppermute | solution.py:278
  68.8 29.6 %copy-start.12 = (bf16[192,1280]{1,0:T(8,128)(2,1)}, bf16[192,1280]{1,0:T(8,128)(2,1)S(1)}, u32[]{:S(2)}) copy-start(bf16[192,1280]{1,0:T(8,128)(2,1)S(1)} %collective-permute-done.8.refs_2_) | copy-start | bytes 1474564
  73.2 25.2 %copy-start.13 = (bf16[128,1280]{1,0:T(8,128)(2,1)}, bf16[128,1280]{1,0:T(8,128)(2,1)S(1)}, u32[]{:S(2)}) copy-start(bf16[128,1280]{1,0:T(8,128)(2,1)S(1)} %collective-permute-done.11.refs_7_) | copy-start | bytes 983044
  98.4 4.0 %collective-permute-start.12 = (bf16[16,2,40,640]{3,2,1,0:T(8,128)(2,1)}, bf16[16,2,40,640]{3,2,1,0:T(8,128)(2,1)S(1)}, u32[]{:S(2)}, u32[]{:S(2)}) collective-permute-start(bf16[16,2,40,640]{3,2,1,0:T(8,128)(2,1)} %bitcast.20), channel_id=1, source_target_pairs={{0,8},{8,0},{1,9},{9,1},{2,10},{10,2},{3,11},{11,3},{4,12},{12,4},... | collective-permute-start | bytes 4915208 | tf_op jit(solution)/shard_map/ppermute | solution.py:278
  102.4 1.2 copy-start.9
  125.9 1.0 copy-start
  126.8 3.7 %collective-permute-start.13 = (bf16[4,8,40,640]{3,2,1,0:T(8,128)(2,1)}, bf16[4,8,40,640]{3,2,1,0:T(8,128)(2,1)S(1)}, u32[]{:S(2)}, u32[]{:S(2)}) collective-permute-start(bf16[4,8,40,640]{3,2,1,0:T(8,128)(2,1)} %get-tuple-element.57), channel_id=1, source_target_pairs={{0,8},{8,0},{1,9},{9,1},{2,10},{10,2},{3,11},{11,3},{4,12},{12,4},... | collective-permute-start | bytes 4915208 | tf_op jit(solution)/shard_map/ppermute | solution.py:278
  130.9 30.4 %copy-start.1 = (f32[192,1280]{1,0:T(8,128)S(1)}, f32[192,1280]{1,0:T(8,128)}, u32[]{:S(2)}) copy-start(f32[192,1280]{1,0:T(8,128)} %copy-done) | copy-start | bytes 2949124
  131.0 12.4 %collective-permute-start.17 = (bf16[8,40,640]{2,1,0:T(8,128)(2,1)S(1)}, bf16[8,40,640]{2,1,0:T(8,128)(2,1)S(1)}, u32[]{:S(2)}, u32[]{:S(2)}) collective-permute-start(bf16[8,40,640]{2,1,0:T(8,128)(2,1)S(1)} %get-tuple-element.63), channel_id=1, source_target_pairs={{0,16},{16,32},{32,48},{48,0},{1,17},{17,33},{33,49},{49,1},{2,18}... | collective-permute-start | bytes 1228808 | tf_op jit(solution)/shard_map/ppermute | solution.py:278
  132.5 13.9 %collective-permute-start.18 = (bf16[8,40,640]{2,1,0:T(8,128)(2,1)S(1)}, bf16[8,40,640]{2,1,0:T(8,128)(2,1)S(1)}, u32[]{:S(2)}, u32[]{:S(2)}) collective-permute-start(bf16[8,40,640]{2,1,0:T(8,128)(2,1)S(1)} %get-tuple-element.64), channel_id=1, source_target_pairs={{0,32},{16,48},{32,0},{48,16},{1,33},{17,49},{33,1},{49,17},{2,34}... | collective-permute-start | bytes 1228808 | tf_op jit(solution)/shard_map/ppermute | solution.py:278
  133.5 19.7 %collective-permute-start.19 = (bf16[8,40,640]{2,1,0:T(8,128)(2,1)S(1)}, bf16[8,40,640]{2,1,0:T(8,128)(2,1)S(1)}, u32[]{:S(2)}, u32[]{:S(2)}) collective-permute-start(bf16[8,40,640]{2,1,0:T(8,128)(2,1)S(1)} %get-tuple-element.65), channel_id=1, source_target_pairs={{0,48},{16,0},{32,16},{48,32},{1,49},{17,1},{33,17},{49,33},{2,50}... | collective-permute-start | bytes 1228808 | tf_op jit(solution)/shard_map/ppermute | solution.py:278
  135.7 25.4 %collective-permute-start.14 = (bf16[192,1280]{1,0:T(8,128)(2,1)}, bf16[192,1280]{1,0:T(8,128)(2,1)S(1)}, u32[]{:S(2)}, u32[]{:S(2)}) collective-permute-start(bf16[192,1280]{1,0:T(8,128)(2,1)} %get-tuple-element.59), channel_id=1, source_target_pairs={{0,6},{2,0},{4,2},{6,4},{1,7},{3,1},{5,3},{7,5},{8,14},{10,8},{12,... | collective-permute-start | bytes 1474568 | tf_op jit(solution)/shard_map/ppermute | solution.py:278
  136.9 24.2 %collective-permute-start.15 = (bf16[192,1280]{1,0:T(8,128)(2,1)}, bf16[192,1280]{1,0:T(8,128)(2,1)S(1)}, u32[]{:S(2)}, u32[]{:S(2)}) collective-permute-start(bf16[192,1280]{1,0:T(8,128)(2,1)} %get-tuple-element.60), channel_id=1, source_target_pairs={{0,4},{2,6},{4,0},{6,2},{1,5},{3,7},{5,1},{7,3},{8,12},{10,14},{12... | collective-permute-start | bytes 1474568 | tf_op jit(solution)/shard_map/ppermute | solution.py:278
  143.3 18.0 %collective-permute-start.16 = (bf16[192,1280]{1,0:T(8,128)(2,1)}, bf16[192,1280]{1,0:T(8,128)(2,1)S(1)}, u32[]{:S(2)}, u32[]{:S(2)}) collective-permute-start(bf16[192,1280]{1,0:T(8,128)(2,1)} %get-tuple-element.61), channel_id=1, source_target_pairs={{0,2},{2,4},{4,6},{6,0},{1,3},{3,5},{5,7},{7,1},{8,10},{10,12},{12... | collective-permute-start | bytes 1474568 | tf_op jit(solution)/shard_map/ppermute | solution.py:278
  154.2 21.4 %all-to-all-start.2 = ((bf16[8,40,640]{2,1,0:T(8,128)(2,1)}), bf16[8,40,640]{2,1,0:T(8,128)(2,1)S(1)}, u32[]{:S(2)}, u32[]{:S(2)}) async-start(bf16[8,40,640]{2,1,0:T(8,128)(2,1)} %x_sum.1), calls=%async_computation.2 | async-start | bytes 819200 | tf_op jit(solution)/shard_map/all_to_all | solution.py:388
Sparse Core Ops, SparseCore 0:
  13.1 61.4 all-gather.2

commit v6 on v5

--- a/solution.py
+++ b/solution.py
@@ -64,7 +64,28 @@
     )(*args)
 
 
-def pack_kernel(pair, packed):
+def pack_kernel(place, pair_in, conv_in, proj_in, packed, wire, pair, arrival):
+    c = place[0]
+    conv_rows = pl.ds(pl.multiple_of(c * 64, 64), 64)
+    proj_rows = pl.ds(pl.multiple_of(c * 32, 32), 32)
+    low = pl.ds(pl.multiple_of(c * 32, 16), 16)
+    high = pl.ds(pl.multiple_of(c * 32 + 16, 16), 16)
+    routes = (
+        (pair_in, pair),
+        (conv_in.at[conv_rows, :], wire.at[pl.ds(0, 64), :]),
+        (proj_in.at[proj_rows, pl.ds(0, 512)], wire.at[pl.ds(64, 32), :]),
+        (proj_in.at[proj_rows, pl.ds(512, 512)], wire.at[pl.ds(96, 32), :]),
+        (proj_in.at[low, pl.ds(1024, 256)], wire.at[pl.ds(128, 16), pl.ds(0, 256)]),
+        (proj_in.at[high, pl.ds(1024, 256)], wire.at[pl.ds(128, 16), pl.ds(256, 256)]),
+    )
+    copies = [
+        pltpu.make_async_copy(source, target, arrival.at[k])
+        for k, (source, target) in enumerate(routes)
+    ]
+    for copy in copies:
+        copy.start()
+    for copy in copies:
+        copy.wait()
     up = pair[0].astype(f32)
     down = pair[1].astype(f32)
     blank = jnp.zeros((BLOCK, LANES - UNITS), f32)
@@ -118,18 +139,33 @@
     outgoing[:, :128] = (outgoing[:, :128].astype(f32) + flags).astype(bf16)
 
 
+def wire_places(place, rows_each):
+    y, zl, c = place[0], place[1], place[2]
+    for step in range(4):
+        for k in range(4):
+            source = lax.rem(y - step + 4, 4) * 4 + lax.rem(zl + k // 2, 2) * 2
+            source = source + lax.rem(c + k % 2, 2)
+            yield step, k, pl.multiple_of(source * rows_each, rows_each)
+
+
+def proj_kernel(place, *refs):
+    wires, proj = refs[:4], refs[4]
+    for step, k, row in wire_places(place, 32):
+        rows = pl.ds(row, 32)
+        proj[rows, :512] = wires[k][step, 64:96, :]
+        proj[rows, 512:1024] = wires[k][step, 96:128, :]
+        proj[pl.ds(row, 16), 1024:] = wires[k][step, 128:144, :256]
+        proj[pl.ds(pl.multiple_of(row + 16, 16), 16), 1024:] = wires[k][step, 128:144, 256:]
+
+
 def front_kernel(place, incoming, *refs):
-    pieces, (block, flags_out, conv, arrival) = refs[:4], refs[4:]
-    y, zl = place[0], place[1]
+    wires, (block, flags_out, conv, arrival) = refs[:4], refs[4:]
     copies = []
-    for step in range(4):
-        for other in range(2):
-            k = step * 2 + other
-            start = lax.rem(y - step + 4, 4) * 256 + lax.rem(zl + other, 2) * 128
-            rows = pl.ds(pl.multiple_of(start, 128), 128)
-            source = pieces[step].at[pl.ds(other * 128, 128), :]
-            copies.append(pltpu.make_async_copy(source, conv.at[rows, :], arrival.at[k]))
-            copies[-1].start()
+    for step, k, row in wire_places(place, 64):
+        source = wires[k].at[step, pl.ds(0, 64), :]
+        target = conv.at[pl.ds(row, 64), :]
+        copies.append(pltpu.make_async_copy(source, target, arrival.at[step * 4 + k]))
+        copies[-1].start()
     for copy in copies:
         copy.wait()
     raw = incoming[...]
@@ -153,11 +189,11 @@
 
 
 def ffn_kernel(place, blocks, own_pair, other_pair, *refs):
-    cots, protos, refs = refs[:4], refs[4:8], refs[8:]
+    cots, proj_in, refs = refs[:4], refs[4], refs[5:]
     own, away1, away2, away3, kept, sent, refs = *refs[:6], refs[6:]
     proj, feats, live, normed, hidden, grad_pre, grad_out, wide_up, wide_down, *refs = refs
     cot, up, down, raw, arrival = refs
-    y, zl, c = place[0], place[1], place[2]
+    y, zl, c, zh = place[0], place[1], place[2], place[3]
     copies = []
 
     def fetch(source, target):
@@ -166,32 +202,33 @@
         copies.append(copy)
 
     for k, pair in enumerate((own_pair, other_pair)):
-        for other in range(2):
-            fetch(pair.at[:, other], raw.at[lax.rem(c + k, 2), lax.rem(zl + other, 2)])
+        for step in range(4):
+            for other in range(2):
+                target = raw.at[
+                    lax.rem(c + k, 2), lax.rem(zl + other, 2), lax.rem(zh - step + 4, 4)
+                ]
+                fetch(pair.at[:, step, other], target)
     for step in range(4):
         fetch(blocks.at[lax.rem(y - step + 4, 4)], feats.at[step])
-    for step in range(4):
-        for other in range(2):
-            start = lax.rem(y - step + 4, 4) * 128 + lax.rem(zl + other, 2) * 64
-            rows = pl.ds(pl.multiple_of(start, 64), 64)
-            fetch(protos[step].at[pl.ds(other * 64, 64), :], proj.at[rows, :])
+    fetch(proj_in, proj)
     for step in range(4):
         fetch(cots[step], cot.at[pl.ds(step * SLOTS, SLOTS), :])
-    for copy in copies[:4]:
+    for copy in copies[:16]:
         copy.wait()
 
-    def assemble(place, carry):
-        rows = pl.ds(pl.multiple_of(place * 2 * BLOCK, 16), 2 * BLOCK)
+    def assemble(spot, carry):
+        rows = pl.ds(pl.multiple_of(spot * 2 * BLOCK, 16), 2 * BLOCK)
+        high, x = spot // 4, lax.rem(spot, 4)
         for half in range(2):
             lanes = slice(half * LANES, (half + 1) * LANES)
-            up0, down0 = unpack_pair(raw[0, half, place].astype(f32))
-            up1, down1 = unpack_pair(raw[1, half, place].astype(f32))
+            up0, down0 = unpack_pair(raw[0, half, high, x].astype(f32))
+            up1, down1 = unpack_pair(raw[1, half, high, x].astype(f32))
             up[rows, lanes] = jnp.concatenate([up0, up1], axis=0).astype(bf16)
             down[rows, lanes] = jnp.concatenate([down0, down1], axis=0).astype(bf16)
         return carry
 
     lax.fori_loop(0, 16, assemble, 0, unroll=4)
-    for copy in copies[4:]:
+    for copy in copies[16:]:
         copy.wait()
     for step in range(4):
         flags = feats[step, SLOTS : SLOTS + 16, :].astype(f32)[:1, :]
@@ -285,16 +322,22 @@
 def per_device(waveform_rows, conv_weight, proj_weight, ffn_pair, owner, frame_live, cotangent):
     dp = ("zh", "x", "c")
     zh, x, c, y, zl = (lax.axis_index(name).astype(i32) for name in ("zh", "x", "c", "y", "zl"))
-    packed = call(
+    packed, wire = call(
         pack_kernel,
-        jax.ShapeDtypeStruct((BLOCK, 2 * UNITS), bf16),
-        [jnp.transpose(ffn_pair, (1, 2, 0))],
-        1 << 16, 1 << 17, name="pack",
+        (
+            jax.ShapeDtypeStruct((BLOCK, 2 * UNITS), bf16),
+            jax.ShapeDtypeStruct((144, CH), bf16),
+        ),
+        [c[None], jnp.transpose(ffn_pair, (1, 2, 0)), conv_weight, proj_weight],
+        1 << 16, 1 << 19,
+        scratch=[pltpu.VMEM((2, BLOCK, UNITS), bf16), pltpu.SemaphoreType.DMA((6,))],
+        smem=1, hbm=3, name="pack",
     )
     both = jnp.stack([packed, ring(packed, "zl", 2, 1)])
-    conv_pair = jnp.concatenate([conv_weight, ring(conv_weight, "zl", 2, 1)], axis=0)
-    proj_pair = jnp.concatenate([proj_weight, ring(proj_weight, "zl", 2, 1)], axis=0)
-    own_pair = lax.all_gather(both, ("zh", "x"), axis=0)
+    wire_y = jnp.stack(around(wire, "y", 4))
+    along_z = jnp.stack(around(both, "zh", 4))
+    own_pair = lax.all_gather(along_z, "x", axis=0)
+    cot_pieces = around(cotangent, "y", 4)
 
     outgoing = call(
         route_kernel,
@@ -309,18 +352,22 @@
         ],
         hbm=3, name="route",
     )
-    cot_pieces = around(cotangent, "y", 4)
-    outgoing, both, conv_pair, proj_pair, cot_pieces[1], cot_pieces[3] = (
-        lax.optimization_barrier(
-            (outgoing, both, conv_pair, proj_pair, cot_pieces[1], cot_pieces[3])
-        )
-    )
-    conv_pieces = around(conv_pair, "y", 4)
-    proj_pair, *conv_pieces[1:] = lax.optimization_barrier((proj_pair, *conv_pieces[1:]))
-    proj_pieces = around(proj_pair, "y", 4)
+    outgoing, wire_y, along_z = lax.optimization_barrier((outgoing, wire_y, along_z))
+    wire_z = ring(wire_y, "zl", 2, 1)
+    wires = [wire_y, ring(wire_y, "c", 2, 1), wire_z, ring(wire_z, "c", 2, 1)]
     incoming = lax.all_to_all(
         outgoing.reshape(N_DP, PAD, 1024), dp, split_axis=0, concat_axis=0, tiled=True
     ).reshape(N_DP * PAD, 1024)
+    incoming, cot_pieces[1], cot_pieces[3] = lax.optimization_barrier(
+        (incoming, cot_pieces[1], cot_pieces[3])
+    )
+    where = jnp.stack([y, zl, c])
+    proj_full = call(
+        proj_kernel,
+        jax.ShapeDtypeStruct((CH, D), bf16),
+        [where, *wires],
+        1 << 18, 3 << 20, smem=1, name="proj",
+    )
 
     block, flags = call(
         front_kernel,
@@ -328,18 +375,18 @@
             jax.ShapeDtypeStruct((SLOTS + 16, CH), bf16),
             jax.ShapeDtypeStruct((SLOTS, 1), f32),
         ),
-        [jnp.stack([y, zl]), incoming, *conv_pieces],
+        [where, incoming, *wires],
         2 * 256 * 1024 * 512, 2 << 20,
-        scratch=[pltpu.VMEM((1024, CH), bf16), pltpu.SemaphoreType.DMA((8,))],
+        scratch=[pltpu.VMEM((1024, CH), bf16), pltpu.SemaphoreType.DMA((16,))],
         smem=1, hbm=4, name="front",
     )
-    block, cot_pieces[2], *proj_pieces = lax.optimization_barrier(
-        (block, cot_pieces[2], *proj_pieces)
-    )
+    block, proj_full = lax.optimization_barrier((block, proj_full))
     blocks = lax.all_to_all(
         jnp.broadcast_to(block[None], (4,) + block.shape), "y", split_axis=0, concat_axis=0
     )
-    blocks, own_pair = lax.optimization_barrier((blocks, own_pair))
+    blocks, own_pair, cot_pieces[2] = lax.optimization_barrier(
+        (blocks, own_pair, cot_pieces[2])
+    )
     other_pair = ring(own_pair, "c", 2, 1)
 
     rows = 4 * SLOTS
@@ -348,7 +395,7 @@
     own, away1, away2, away3, kept, sent = call(
         ffn_kernel,
         (jax.ShapeDtypeStruct((SLOTS, D), f32), piece, piece, piece, terms, terms),
-        [jnp.stack([y, zl, c]), blocks, own_pair, other_pair, *cot_pieces, *proj_pieces],
+        [jnp.stack([y, zl, c, zh]), blocks, own_pair, other_pair, *cot_pieces, proj_full],
         2 * rows * D * (CH + 5 * WIDE), 16 << 20,
         scratch=[
             pltpu.VMEM((CH, D), bf16),
@@ -363,10 +410,10 @@
             pltpu.VMEM((rows, D), bf16),
             pltpu.VMEM((D, WIDE), bf16),
             pltpu.VMEM((D, WIDE), bf16),
-            pltpu.VMEM((2, 2, 16, BLOCK, 2 * UNITS), bf16),
-            pltpu.SemaphoreType.DMA((20,)),
+            pltpu.VMEM((2, 2, 4, 4, BLOCK, 2 * UNITS), bf16),
+            pltpu.SemaphoreType.DMA((25,)),
         ],
-        vmem=36 << 20, smem=1, hbm=11, name="ffn",
+        vmem=40 << 20, smem=1, hbm=8, name="ffn",
     )
     tile = jax.ShapeDtypeStruct((8, BLOCK, 2 * UNITS), bf16)
     parts = call(

time: 184 us -> 194 us (1.054)
  waiting for transfers between devices: 74.8 us -> 93 us
  blocking collectives: 16.6 us -> 0 us
  starting transfers between devices: 42.1 us -> 49 us
    ppermute x20 -> x21, waiting for transfers between devices: 61.6 us -> 82.1 us  [ring(): lax.ppermute(values, axis, [(k, (k + step) % size) for k in range(size)])]
    all_to_all x1 -> x0, blocking collectives: 16.6 us -> none  [per_device(): lax.all_to_all(jnp.broadcast_to(block[None], (4,) + block.shape), 'y', sp...]
    ppermute x20 -> x21, starting transfers between devices: 23.8 us -> 32.8 us  [ring(): lax.ppermute(values, axis, [(k, (k + step) % size) for k in range(size)])]
    all_to_all x0 -> x1, starting transfers between devices: none -> 3.5 us  [per_device(): lax.all_to_all(jnp.broadcast_to(block[None], (4,) + block.shape), 'y', sp...]
    all_to_all x1, starting transfers between devices: 11.4 us -> 8.05 us  [per_device(): lax.all_to_all(outgoing.reshape(N_DP, PAD, 1024), dp, split_axis=0, conca...]
    all_to_all x1, waiting for transfers between devices: 13.2 us -> 10.8 us  [per_device(): total = lax.all_to_all(total, ZX, split_axis=0, concat_axis=0, tiled=True)]
    all_to_all x1, starting transfers between devices: 6.86 us -> 4.6 us  [per_device(): total = lax.all_to_all(total, ZX, split_axis=0, concat_axis=0, tiled=True)]
    pallas_call x7 -> x8, Pallas kernels: 29.5 us -> 31.3 us  [call(): pl.pallas_call(kernel, out_shape=out_shape, in_specs=[SMEM] * smem + [VME...]
  transfers between devices with their start and end apart: 23 -> 25, of which waited for: 19 -> 18; matrix products, arithmetic and copies ran while one was open for 1% -> 1% of each run, Pallas kernels for 3% -> 3%
where the time goes in v6:
time: 194 us; the launch traced here: 193 us
  waiting for transfers between devices  93 us (48%)
  starting transfers between devices  49 us (25%)
  Pallas kernels  31.3 us (16%)
  between operations  14.2 us (7%)
  local copies, waits for them, and re-layouts  3.38 us (2%)
  other arithmetic  2.19 us (1%)
    ppermute x21, waiting for transfers between devices, ring(): lax.ppermute(values, axis, [(k, (k + step) % size) for k in range(size)])  82.1 us
    ppermute x21, starting transfers between devices, ring(): lax.ppermute(values, axis, [(k, (k + step) % size) for k in range(size)])  32.8 us
    pallas_call x8, Pallas kernels, call(): pl.pallas_call(kernel, out_shape=out_shape, in_specs=[SMEM] * smem + [VME...  31.3 us
    all_to_all x1, waiting for transfers between devices, per_device(): total = lax.all_to_all(total, ZX, split_axis=0, concat_axis=0, tiled=True)  10.8 us
    all_to_all x1, starting transfers between devices, per_device(): lax.all_to_all(outgoing.reshape(N_DP, PAD, 1024), dp, split_axis=0, conca...  8.05 us
    all_to_all x1, starting transfers between devices, per_device(): total = lax.all_to_all(total, ZX, split_axis=0, concat_axis=0, tiled=True)  4.6 us
  transfers between devices with their start and end apart: 25, of which 18 were waited for; matrix products, arithmetic and copies ran while one was open for 1% of the time, Pallas kernels for 3%

profile of v6, /device:TPU:2, one launch (start us, length us, event | category | flops | bytes accessed | tf_op | source)
XLA Modules:
  0.0 193.1 jit_solution(10778087492574831880)
XLA Ops:
  7.2 0.0 all-gather.3.cloned.1.call-start
  7.2 1.0 pack.1
  8.2 2.0 %collective-permute-start.3 = (bf16[40,640]{1,0:T(8,128)(2,1)S(1)}, bf16[40,640]{1,0:T(8,128)(2,1)S(1)}, u32[]{:S(2)}, u32[]{:S(2)}) collective-permute-start(bf16[40,640]{1,0:T(8,128)(2,1)S(1)} %get-tuple-element.30), channel_id=1, source_target_pairs={{0,1},{1,0},{2,3},{3,2},{4,5},{5,4},{6,7},{7,6},{8,9},{9,8},{10,11... | collective-permute-start | bytes 153608 | tf_op jit(solution)/shard_map/ppermute | solution.py:315
  10.2 2.2 %collective-permute-done.3 = bf16[40,640]{1,0:T(8,128)(2,1)S(1)} collective-permute-done((bf16[40,640]{1,0:T(8,128)(2,1)S(1)}, bf16[40,640]{1,0:T(8,128)(2,1)S(1)}, u32[]{:S(2)}, u32[]{:S(2)}) %collective-permute-start.3) | collective-permute-done | bytes 51232 | tf_op jit(solution)/shard_map/ppermute | solution.py:315
  12.5 7.3 %collective-permute-start.5 = (bf16[2,40,640]{2,1,0:T(8,128)(2,1)S(1)}, bf16[2,40,640]{2,1,0:T(8,128)(2,1)S(1)}, u32[]{:S(2)}, u32[]{:S(2)}) collective-permute-start(bf16[2,40,640]{2,1,0:T(8,128)(2,1)S(1)} %get-tuple-element.57), channel_id=1, source_target_pairs={{0,128},{64,192},{128,0},{192,64},{1,129},{65,193},{129,1},{193,65... | collective-permute-start | bytes 307208 | tf_op jit(solution)/shard_map/ppermute | solution.py:315
  19.7 1.5 collective-permute-start.4
  21.2 2.7 %collective-permute-start.6 = (bf16[2,40,640]{2,1,0:T(8,128)(2,1)S(1)}, bf16[2,40,640]{2,1,0:T(8,128)(2,1)S(1)}, u32[]{:S(2)}, u32[]{:S(2)}) collective-permute-start(bf16[2,40,640]{2,1,0:T(8,128)(2,1)S(1)} %get-tuple-element.57), channel_id=1, source_target_pairs={{0,192},{64,0},{128,64},{192,128},{1,193},{65,1},{129,65},{193,129... | collective-permute-start | bytes 307208 | tf_op jit(solution)/shard_map/ppermute | solution.py:315
  23.9 0.8 collective-permute-done.5
  24.7 2.6 %collective-permute-done.4 = bf16[2,40,640]{2,1,0:T(8,128)(2,1)S(1)} collective-permute-done((bf16[2,40,640]{2,1,0:T(8,128)(2,1)S(1)}, bf16[2,40,640]{2,1,0:T(8,128)(2,1)S(1)}, u32[]{:S(2)}, u32[]{:S(2)}) %collective-permute-start.4) | collective-permute-done | bytes 102432 | tf_op jit(solution)/shard_map/ppermute | solution.py:315
  27.3 1.9 %collective-permute-done.6 = bf16[2,40,640]{2,1,0:T(8,128)(2,1)S(1)} collective-permute-done((bf16[2,40,640]{2,1,0:T(8,128)(2,1)S(1)}, bf16[2,40,640]{2,1,0:T(8,128)(2,1)S(1)}, u32[]{:S(2)}, u32[]{:S(2)}) %collective-permute-start.6) | collective-permute-done | bytes 102432 | tf_op jit(solution)/shard_map/ppermute | solution.py:315
  29.2 0.8 pad_maximum_fusion.1
  30.1 0.0 all-gather.3.cloned.1.call-update
  30.1 3.1 %collective-permute-start.2 = (bf16[144,512]{1,0:T(8,128)(2,1)S(1)}, bf16[144,512]{1,0:T(8,128)(2,1)S(1)}, u32[]{:S(2)}, u32[]{:S(2)}) collective-permute-start(bf16[144,512]{1,0:T(8,128)(2,1)S(1)} %get-tuple-element.29), channel_id=1, source_target_pairs={{0,6},{2,0},{4,2},{6,4},{1,7},{3,1},{5,3},{7,5},{8,14},{10,8},{12,... | collective-permute-start | bytes 442376 | tf_op jit(solution)/shard_map/ppermute | solution.py:315
  33.2 0.6 collective-permute-start.1
  33.8 1.0 collective-permute-start
  34.8 2.2 %route.1 = bf16[256,1024]{1,0:T(8,128)(2,1)} custom-call(s32[1,128]{1,0:T(1,128)} %bitcast.35, s32[1,128]{1,0:T(1,128)} %bitcast.36, bf16[128,1024]{1,0:T(8,128)(2,1)} %rows_in.1), custom_call_target="tpu_custom_call" | custom-call | flops 75497472 | bytes 1048576 | tf_op jit(solution)/shard_map/route/pallas_call | solution.py:53
  37.0 2.3 %collective-permute-done.2 = bf16[144,512]{1,0:T(8,128)(2,1)S(1)} collective-permute-done((bf16[144,512]{1,0:T(8,128)(2,1)S(1)}, bf16[144,512]{1,0:T(8,128)(2,1)S(1)}, u32[]{:S(2)}, u32[]{:S(2)}) %collective-permute-start.2) | collective-permute-done | bytes 147488 | tf_op jit(solution)/shard_map/ppermute | solution.py:315
  39.2 2.1 %collective-permute-done.1 = bf16[144,512]{1,0:T(8,128)(2,1)S(1)} collective-permute-done((bf16[144,512]{1,0:T(8,128)(2,1)S(1)}, bf16[144,512]{1,0:T(8,128)(2,1)S(1)}, u32[]{:S(2)}, u32[]{:S(2)}) %collective-permute-start.1) | collective-permute-done | bytes 147488 | tf_op jit(solution)/shard_map/ppermute | solution.py:315
  41.4 1.6 collective-permute-done
  43.0 0.1 pad_maximum_fusion.refs_0_
  43.0 0.1 collective-permute-start.10
  43.1 8.1 %all-to-all-start = ((bf16[32,8,1024]{2,1,0:T(8,128)(2,1)}), bf16[32,8,1024]{2,1,0:T(8,128)(2,1)S(1)}, u32[]{:S(2)}, u32[]{:S(2)}) async-start(bf16[32,8,1024]{2,1,0:T(8,128)(2,1)} %bitcast.17), calls=%async_computation | async-start | bytes 1048576 | tf_op jit(solution)/shard_map/all_to_all | solution.py:358
  51.2 0.2 collective-permute-start.9
  51.4 11.2 %collective-permute-done.10.refs_2_ = bf16[4,144,512]{2,1,0:T(8,128)(2,1)S(1)} collective-permute-done((bf16[4,144,512]{2,1,0:T(8,128)(2,1)S(1)}, bf16[4,144,512]{2,1,0:T(8,128)(2,1)S(1)}, u32[]{:S(2)}, u32[]{:S(2)}) %collective-permute-start.10) | collective-permute-done | bytes 589856 | tf_op jit(solution)/shard_map/ppermute | solution.py:315
  62.7 1.1 collective-permute-start.8
  63.7 1.0 collective-permute-start.7
  64.8 0.1 pad_add_fusion.1.place
  64.9 11.6 %collective-permute-done.8.refs_3_ = bf16[192,1280]{1,0:T(8,128)(2,1)} collective-permute-done((bf16[192,1280]{1,0:T(8,128)(2,1)S(1)}, bf16[192,1280]{1,0:T(8,128)(2,1)}, u32[]{:S(2)}, u32[]{:S(2)}) %collective-permute-start.8) | collective-permute-done | bytes 491552 | tf_op jit(solution)/shard_map/ppermute | solution.py:315
  76.4 1.9 collective-permute-done.7.refs_1_
  78.4 0.0 collective-permute-done.9.refs_1_
  78.4 0.6 proj.1.refs_4_
  79.1 0.1 copy-done.2
  79.2 0.2 copy-done.3
  79.4 1.1 copy-done.4
  80.5 2.9 %front.1 = (bf16[208,512]{1,0:T(8,128)(2,1)S(1)}, f32[192,1]{1,0:T(8,128)S(1)}) custom-call(s32[3]{0:T(128)S(1)} %pad_add_fusion.1.place, bf16[256,1024]{1,0:T(8,128)(2,1)S(1)} %bitcast.23, bf16[4,144,512]{2,1,0:T(8,128)(2,1)} %copy-done, bf16[4,144,512]{2,1,0:T(8,128)(2,1)} %copy-done.2, bf16[4,144,512]{2,1,0:T(8,128)(2,1)} %copy-done.1, ...), custom_call_target="tpu_custom_call" | custom-call | flops 268435456 | bytes 2097152 | tf_op jit(solution)/shard_map/front/pallas_call | solution.py:53
  83.3 0.0 copy-start.9
  83.4 1.0 broadcast_in_dim.4
  84.4 3.5 %all-to-all-start.1 = ((bf16[4,208,512]{2,1,0:T(8,128)(2,1)}), bf16[4,208,512]{2,1,0:T(8,128)(2,1)S(1)}, u32[]{:S(2)}, u32[]{:S(2)}) async-start(bf16[4,208,512]{2,1,0:T(8,128)(2,1)} %broadcast_in_dim.4), calls=%async_computation.1 | async-start | bytes 1703936 | tf_op jit(solution)/shard_map/all_to_all | solution.py:384
  87.9 3.5 %collective-permute-start.12 = (bf16[192,1280]{1,0:T(8,128)(2,1)S(1)}, bf16[192,1280]{1,0:T(8,128)(2,1)}, u32[]{:S(2)}, u32[]{:S(2)}) collective-permute-start(bf16[192,1280]{1,0:T(8,128)(2,1)S(1)} %copy-done.9), channel_id=1, source_target_pairs={{0,4},{2,6},{4,0},{6,2},{1,5},{3,7},{5,1},{7,3},{8,12},{10,14},{12... | collective-permute-start | bytes 1474568 | tf_op jit(solution)/shard_map/ppermute | solution.py:315
  91.4 19.9 %collective-permute-done.12.refs_2_ = bf16[192,1280]{1,0:T(8,128)(2,1)} collective-permute-done((bf16[192,1280]{1,0:T(8,128)(2,1)S(1)}, bf16[192,1280]{1,0:T(8,128)(2,1)}, u32[]{:S(2)}, u32[]{:S(2)}) %collective-permute-start.12) | collective-permute-done | bytes 491552 | tf_op jit(solution)/shard_map/ppermute | solution.py:315
  111.2 0.3 collective-permute-start.13
  111.5 0.1 pad_add_fusion.place
  111.6 3.7 %collective-permute-done.13.other_pair = bf16[4,4,2,40,640]{4,3,2,1,0:T(8,128)(2,1)} collective-permute-done((bf16[4,4,2,40,640]{4,3,2,1,0:T(8,128)(2,1)}, bf16[4,4,2,40,640]{4,3,2,1,0:T(8,128)(2,1)}, u32[]{:S(2)}, u32[]{:S(2)}) %collective-permute-start.13) | collective-permute-done | bytes 1638432 | tf_op jit(solution)/shard_map/ppermute | solution.py:315
  115.4 22.5 %ffn.1 = (f32[192,1280]{1,0:T(8,128)S(1)}, bf16[192,1280]{1,0:T(8,128)(2,1)}, bf16[192,1280]{1,0:T(8,128)(2,1)}, bf16[192,1280]{1,0:T(8,128)(2,1)}, bf16[4,8,40,...) custom-call(s32[4]{0:T(128)S(1)} %pad_add_fusion.place, bf16[4,208,512]{2,1,0:T(8,128)(2,1)} %copy-done.7, ...), custom_call_target="tpu_custom_call" | custom-call | flops 8556380160 | bytes 16777216 | tf_op jit(solution)/shard_map/ffn/pallas_call | solution.py:53
  137.9 0.9 copy-done.5
  138.8 0.1 collective-permute-start.14
  138.9 3.6 %collective-permute-done.14.arrived = bf16[4,8,40,640]{3,2,1,0:T(8,128)(2,1)S(1)} collective-permute-done((bf16[4,8,40,640]{3,2,1,0:T(8,128)(2,1)}, bf16[4,8,40,640]{3,2,1,0:T(8,128)(2,1)S(1)}, u32[]{:S(2)}, u32[]{:S(2)}) %collective-permute-start.14) | collective-permute-done | bytes 1638432 | tf_op jit(solution)/shard_map/ppermute | solution.py:315
  142.5 0.4 core_sum.1
  142.9 1.7 collective-permute-start.18
  144.6 1.0 collective-permute-start.19
  145.6 2.5 %collective-permute-start.20 = (bf16[8,40,640]{2,1,0:T(8,128)(2,1)S(1)}, bf16[8,40,640]{2,1,0:T(8,128)(2,1)S(1)}, u32[]{:S(2)}, u32[]{:S(2)}) collective-permute-start(bf16[8,40,640]{2,1,0:T(8,128)(2,1)S(1)} %get-tuple-element.55), channel_id=1, source_target_pairs={{0,48},{16,0},{32,16},{48,32},{1,49},{17,1},{33,17},{49,33},{2,50}... | collective-permute-start | bytes 1228808 | tf_op jit(solution)/shard_map/ppermute | solution.py:315
  148.1 1.1 collective-permute-start.15
  149.2 1.5 collective-permute-start.16
  150.7 4.6 %collective-permute-done.18.refs_1_ = bf16[8,40,640]{2,1,0:T(8,128)(2,1)S(1)} collective-permute-done((bf16[8,40,640]{2,1,0:T(8,128)(2,1)S(1)}, bf16[8,40,640]{2,1,0:T(8,128)(2,1)S(1)}, u32[]{:S(2)}, u32[]{:S(2)}) %collective-permute-start.18) | collective-permute-done | bytes 409632 | tf_op jit(solution)/shard_map/ppermute | solution.py:315
  155.3 0.6 collective-permute-start.17
  155.9 2.6 %collective-permute-done.19.refs_2_ = bf16[8,40,640]{2,1,0:T(8,128)(2,1)S(1)} collective-permute-done((bf16[8,40,640]{2,1,0:T(8,128)(2,1)S(1)}, bf16[8,40,640]{2,1,0:T(8,128)(2,1)S(1)}, u32[]{:S(2)}, u32[]{:S(2)}) %collective-permute-start.19) | collective-permute-done | bytes 409632 | tf_op jit(solution)/shard_map/ppermute | solution.py:315
  158.4 7.1 %collective-permute-done.20.refs_3_ = bf16[8,40,640]{2,1,0:T(8,128)(2,1)S(1)} collective-permute-done((bf16[8,40,640]{2,1,0:T(8,128)(2,1)S(1)}, bf16[8,40,640]{2,1,0:T(8,128)(2,1)S(1)}, u32[]{:S(2)}, u32[]{:S(2)}) %collective-permute-start.20) | collective-permute-done | bytes 409632 | tf_op jit(solution)/shard_map/ppermute | solution.py:315
  165.6 1.0 x_sum.1
  166.5 4.6 %all-to-all-start.2 = ((bf16[8,40,640]{2,1,0:T(8,128)(2,1)}), bf16[8,40,640]{2,1,0:T(8,128)(2,1)S(1)}, u32[]{:S(2)}, u32[]{:S(2)}) async-start(bf16[8,40,640]{2,1,0:T(8,128)(2,1)} %x_sum.1), calls=%async_computation.2 | async-start | bytes 819200 | tf_op jit(solution)/shard_map/all_to_all | solution.py:435
  171.2 0.1 convert_reduce_fusion
  171.3 2.4 %collective-permute-done.17 = bf16[192,1280]{1,0:T(8,128)(2,1)S(1)} collective-permute-done((bf16[192,1280]{1,0:T(8,128)(2,1)}, bf16[192,1280]{1,0:T(8,128)(2,1)S(1)}, u32[]{:S(2)}, u32[]{:S(2)}) %collective-permute-start.17) | collective-permute-done | bytes 491552 | tf_op jit(solution)/shard_map/ppermute | solution.py:315
  173.6 1.0 multiply_convert_fusion
  174.7 10.8 %all-to-all-done.2.arrived = bf16[8,40,640]{2,1,0:T(8,128)(2,1)S(1)} async-done(((bf16[8,40,640]{2,1,0:T(8,128)(2,1)}), bf16[8,40,640]{2,1,0:T(8,128)(2,1)S(1)}, u32[]{:S(2)}, u32[]{:S(2)}) %all-to-all-start.2) | async-done | bytes 409632 | tf_op jit(solution)/shard_map/all_to_all | solution.py:435
  185.5 0.8 last.1
  (23 shorter events, 0.1 us)
Async XLA Ops:
  7.2 104.1 %all-gather.3.cloned.1.call-start = ((), (), s32[]{:S(2)}) async-start(), calls=%async_computation.3 | async-start | bytes 2048000 | tf_op jit(solution)/shard_map/all_gather | solution.py:339
  8.2 4.2 %collective-permute-start.3 = (bf16[40,640]{1,0:T(8,128)(2,1)S(1)}, bf16[40,640]{1,0:T(8,128)(2,1)S(1)}, u32[]{:S(2)}, u32[]{:S(2)}) collective-permute-start(bf16[40,640]{1,0:T(8,128)(2,1)S(1)} %get-tuple-element.30), channel_id=1, source_target_pairs={{0,1},{1,0},{2,3},{3,2},{4,5},{5,4},{6,7},{7,6},{8,9},{9,8},{10,11... | collective-permute-start | bytes 153608 | tf_op jit(solution)/shard_map/ppermute | solution.py:315
  12.5 12.2 %collective-permute-start.5 = (bf16[2,40,640]{2,1,0:T(8,128)(2,1)S(1)}, bf16[2,40,640]{2,1,0:T(8,128)(2,1)S(1)}, u32[]{:S(2)}, u32[]{:S(2)}) collective-permute-start(bf16[2,40,640]{2,1,0:T(8,128)(2,1)S(1)} %get-tuple-element.57), channel_id=1, source_target_pairs={{0,128},{64,192},{128,0},{192,64},{1,129},{65,193},{129,1},{193,65... | collective-permute-start | bytes 307208 | tf_op jit(solution)/shard_map/ppermute | solution.py:315
  19.7 7.6 %collective-permute-start.4 = (bf16[2,40,640]{2,1,0:T(8,128)(2,1)S(1)}, bf16[2,40,640]{2,1,0:T(8,128)(2,1)S(1)}, u32[]{:S(2)}, u32[]{:S(2)}) collective-permute-start(bf16[2,40,640]{2,1,0:T(8,128)(2,1)S(1)} %get-tuple-element.57), channel_id=1, source_target_pairs={{0,64},{64,128},{128,192},{192,0},{1,65},{65,129},{129,193},{193,1... | collective-permute-start | bytes 307208 | tf_op jit(solution)/shard_map/ppermute | solution.py:315
  21.2 8.0 %collective-permute-start.6 = (bf16[2,40,640]{2,1,0:T(8,128)(2,1)S(1)}, bf16[2,40,640]{2,1,0:T(8,128)(2,1)S(1)}, u32[]{:S(2)}, u32[]{:S(2)}) collective-permute-start(bf16[2,40,640]{2,1,0:T(8,128)(2,1)S(1)} %get-tuple-element.57), channel_id=1, source_target_pairs={{0,192},{64,0},{128,64},{192,128},{1,193},{65,1},{129,65},{193,129... | collective-permute-start | bytes 307208 | tf_op jit(solution)/shard_map/ppermute | solution.py:315
  30.1 32.6 %copy-start.8 = (bf16[192,1280]{1,0:T(8,128)(2,1)S(1)}, bf16[192,1280]{1,0:T(8,128)(2,1)}, u32[]{:S(2)}) copy-start(bf16[192,1280]{1,0:T(8,128)(2,1)} %refs_0_.1) | copy-start | bytes 1474564
  30.1 9.2 %collective-permute-start.2 = (bf16[144,512]{1,0:T(8,128)(2,1)S(1)}, bf16[144,512]{1,0:T(8,128)(2,1)S(1)}, u32[]{:S(2)}, u32[]{:S(2)}) collective-permute-start(bf16[144,512]{1,0:T(8,128)(2,1)S(1)} %get-tuple-element.29), channel_id=1, source_target_pairs={{0,6},{2,0},{4,2},{6,4},{1,7},{3,1},{5,3},{7,5},{8,14},{10,8},{12,... | collective-permute-start | bytes 442376 | tf_op jit(solution)/shard_map/ppermute | solution.py:315
  33.2 8.2 %collective-permute-start.1 = (bf16[144,512]{1,0:T(8,128)(2,1)S(1)}, bf16[144,512]{1,0:T(8,128)(2,1)S(1)}, u32[]{:S(2)}, u32[]{:S(2)}) collective-permute-start(bf16[144,512]{1,0:T(8,128)(2,1)S(1)} %get-tuple-element.29), channel_id=1, source_target_pairs={{0,4},{2,6},{4,0},{6,2},{1,5},{3,7},{5,1},{7,3},{8,12},{10,14},{12... | collective-permute-start | bytes 442376 | tf_op jit(solution)/shard_map/ppermute | solution.py:315
  33.8 9.1 %collective-permute-start = (bf16[144,512]{1,0:T(8,128)(2,1)S(1)}, bf16[144,512]{1,0:T(8,128)(2,1)S(1)}, u32[]{:S(2)}, u32[]{:S(2)}) collective-permute-start(bf16[144,512]{1,0:T(8,128)(2,1)S(1)} %get-tuple-element.29), channel_id=1, source_target_pairs={{0,2},{2,4},{4,6},{6,0},{1,3},{3,5},{5,7},{7,1},{8,10},{10,12},{12... | collective-permute-start | bytes 442376 | tf_op jit(solution)/shard_map/ppermute | solution.py:315
  43.0 36.0 %copy-start = (bf16[4,144,512]{2,1,0:T(8,128)(2,1)}, bf16[4,144,512]{2,1,0:T(8,128)(2,1)S(1)}, u32[]{:S(2)}) copy-start(bf16[4,144,512]{2,1,0:T(8,128)(2,1)S(1)} %pad_maximum_fusion.refs_0_) | copy-start | bytes 1769476
  43.0 19.6 %collective-permute-start.10 = (bf16[4,144,512]{2,1,0:T(8,128)(2,1)S(1)}, bf16[4,144,512]{2,1,0:T(8,128)(2,1)S(1)}, u32[]{:S(2)}, u32[]{:S(2)}) collective-permute-start(bf16[4,144,512]{2,1,0:T(8,128)(2,1)S(1)} %pad_maximum_fusion.refs_0_), channel_id=1, source_target_pairs={{0,1},{1,0},{2,3},{3,2},{4,5},{5,4},{6,7},{7,6},{8,9},{9,8},{10,11... | collective-permute-start | bytes 1769480 | tf_op jit(solution)/shard_map/ppermute | solution.py:315
  43.1 35.2 %all-to-all-start = ((bf16[32,8,1024]{2,1,0:T(8,128)(2,1)}), bf16[32,8,1024]{2,1,0:T(8,128)(2,1)S(1)}, u32[]{:S(2)}, u32[]{:S(2)}) async-start(bf16[32,8,1024]{2,1,0:T(8,128)(2,1)} %bitcast.17), calls=%async_computation | async-start | bytes 1048576 | tf_op jit(solution)/shard_map/all_to_all | solution.py:358
  51.2 27.1 %collective-permute-start.9 = (bf16[4,144,512]{2,1,0:T(8,128)(2,1)S(1)}, bf16[4,144,512]{2,1,0:T(8,128)(2,1)S(1)}, u32[]{:S(2)}, u32[]{:S(2)}) collective-permute-start(bf16[4,144,512]{2,1,0:T(8,128)(2,1)S(1)} %pad_maximum_fusion.refs_0_), channel_id=1, source_target_pairs={{0,8},{8,0},{1,9},{9,1},{2,10},{10,2},{3,11},{11,3},{4,12},{12,4},... | collective-permute-start | bytes 1769480 | tf_op jit(solution)/shard_map/ppermute | solution.py:315
  62.7 16.4 %copy-start.1 = (bf16[4,144,512]{2,1,0:T(8,128)(2,1)}, bf16[4,144,512]{2,1,0:T(8,128)(2,1)S(1)}, u32[]{:S(2)}) copy-start(bf16[4,144,512]{2,1,0:T(8,128)(2,1)S(1)} %collective-permute-done.10.refs_2_) | copy-start | bytes 1769476
  62.7 15.7 %collective-permute-start.11 = (bf16[4,144,512]{2,1,0:T(8,128)(2,1)S(1)}, bf16[4,144,512]{2,1,0:T(8,128)(2,1)S(1)}, u32[]{:S(2)}, u32[]{:S(2)}) collective-permute-start(bf16[4,144,512]{2,1,0:T(8,128)(2,1)S(1)} %collective-permute-done.10.refs_2_), channel_id=1, source_target_pairs={{0,8},{8,0},{1,9},{9,1},{2,10},{10,2},{3,11},{11,3},{4,12},{12,4},... | collective-permute-start | bytes 1769480 | tf_op jit(solution)/shard_map/ppermute | solution.py:315
  62.7 13.8 %collective-permute-start.8 = (bf16[192,1280]{1,0:T(8,128)(2,1)S(1)}, bf16[192,1280]{1,0:T(8,128)(2,1)}, u32[]{:S(2)}, u32[]{:S(2)}) collective-permute-start(bf16[192,1280]{1,0:T(8,128)(2,1)S(1)} %copy-done.8), channel_id=1, source_target_pairs={{0,6},{2,0},{4,2},{6,4},{1,7},{3,1},{5,3},{7,5},{8,14},{10,8},{12,... | collective-permute-start | bytes 1474568 | tf_op jit(solution)/shard_map/ppermute | solution.py:315
  63.7 14.6 %collective-permute-start.7 = (bf16[192,1280]{1,0:T(8,128)(2,1)S(1)}, bf16[192,1280]{1,0:T(8,128)(2,1)}, u32[]{:S(2)}, u32[]{:S(2)}) collective-permute-start(bf16[192,1280]{1,0:T(8,128)(2,1)S(1)} %copy-done.8), channel_id=1, source_target_pairs={{0,2},{2,4},{4,6},{6,0},{1,3},{3,5},{5,7},{7,1},{8,10},{10,12},{12... | collective-permute-start | bytes 1474568 | tf_op jit(solution)/shard_map/ppermute | solution.py:315
  78.4 0.8 copy-start.2
  78.4 1.0 copy-start.3
  79.4 1.1 copy-start.4
  83.3 4.5 %copy-start.9 = (bf16[192,1280]{1,0:T(8,128)(2,1)S(1)}, bf16[192,1280]{1,0:T(8,128)(2,1)}, u32[]{:S(2)}) copy-start(bf16[192,1280]{1,0:T(8,128)(2,1)} %refs_0_.1) | copy-start | bytes 1474564
  84.4 26.9 %all-to-all-start.1 = ((bf16[4,208,512]{2,1,0:T(8,128)(2,1)}), bf16[4,208,512]{2,1,0:T(8,128)(2,1)S(1)}, u32[]{:S(2)}, u32[]{:S(2)}) async-start(bf16[4,208,512]{2,1,0:T(8,128)(2,1)} %broadcast_in_dim.4), calls=%async_computation.1 | async-start | bytes 1703936 | tf_op jit(solution)/shard_map/all_to_all | solution.py:384
  87.9 23.4 %collective-permute-start.12 = (bf16[192,1280]{1,0:T(8,128)(2,1)S(1)}, bf16[192,1280]{1,0:T(8,128)(2,1)}, u32[]{:S(2)}, u32[]{:S(2)}) collective-permute-start(bf16[192,1280]{1,0:T(8,128)(2,1)S(1)} %copy-done.9), channel_id=1, source_target_pairs={{0,4},{2,6},{4,0},{6,2},{1,5},{3,7},{5,1},{7,3},{8,12},{10,14},{12... | collective-permute-start | bytes 1474568 | tf_op jit(solution)/shard_map/ppermute | solution.py:315
  111.2 4.1 %copy-start.7 = (bf16[4,208,512]{2,1,0:T(8,128)(2,1)}, bf16[4,208,512]{2,1,0:T(8,128)(2,1)S(1)}, u32[]{:S(2)}) copy-start(bf16[4,208,512]{2,1,0:T(8,128)(2,1)S(1)} %all-to-all-done.1.blocks) | copy-start | bytes 2555908
  111.2 4.1 %collective-permute-start.13 = (bf16[4,4,2,40,640]{4,3,2,1,0:T(8,128)(2,1)}, bf16[4,4,2,40,640]{4,3,2,1,0:T(8,128)(2,1)}, u32[]{:S(2)}, u32[]{:S(2)}) collective-permute-start(bf16[4,4,2,40,640]{4,3,2,1,0:T(8,128)(2,1)} %bitcast.37), channel_id=1, source_target_pairs={{0,8},{8,0},{1,9},{9,1},{2,10},{10,2},{3,11},{11,3},{4,12},{12,4},... | collective-permute-start | bytes 4915208 | tf_op jit(solution)/shard_map/ppermute | solution.py:315
  137.8 0.9 copy-start.5
  138.8 3.7 %collective-permute-start.14 = (bf16[4,8,40,640]{3,2,1,0:T(8,128)(2,1)}, bf16[4,8,40,640]{3,2,1,0:T(8,128)(2,1)S(1)}, u32[]{:S(2)}, u32[]{:S(2)}) collective-permute-start(bf16[4,8,40,640]{3,2,1,0:T(8,128)(2,1)} %get-tuple-element.47), channel_id=1, source_target_pairs={{0,8},{8,0},{1,9},{9,1},{2,10},{10,2},{3,11},{11,3},{4,12},{12,4},... | collective-permute-start | bytes 4915208 | tf_op jit(solution)/shard_map/ppermute | solution.py:315
  142.9 30.7 %copy-start.6 = (f32[192,1280]{1,0:T(8,128)S(1)}, f32[192,1280]{1,0:T(8,128)}, u32[]{:S(2)}) copy-start(f32[192,1280]{1,0:T(8,128)} %copy-done.5) | copy-start | bytes 2949124
  142.9 12.4 %collective-permute-start.18 = (bf16[8,40,640]{2,1,0:T(8,128)(2,1)S(1)}, bf16[8,40,640]{2,1,0:T(8,128)(2,1)S(1)}, u32[]{:S(2)}, u32[]{:S(2)}) collective-permute-start(bf16[8,40,640]{2,1,0:T(8,128)(2,1)S(1)} %get-tuple-element.53), channel_id=1, source_target_pairs={{0,16},{16,32},{32,48},{48,0},{1,17},{17,33},{33,49},{49,1},{2,18}... | collective-permute-start | bytes 1228808 | tf_op jit(solution)/shard_map/ppermute | solution.py:315
  144.6 13.9 %collective-permute-start.19 = (bf16[8,40,640]{2,1,0:T(8,128)(2,1)S(1)}, bf16[8,40,640]{2,1,0:T(8,128)(2,1)S(1)}, u32[]{:S(2)}, u32[]{:S(2)}) collective-permute-start(bf16[8,40,640]{2,1,0:T(8,128)(2,1)S(1)} %get-tuple-element.54), channel_id=1, source_target_pairs={{0,32},{16,48},{32,0},{48,16},{1,33},{17,49},{33,1},{49,17},{2,34}... | collective-permute-start | bytes 1228808 | tf_op jit(solution)/shard_map/ppermute | solution.py:315
  145.6 20.0 %collective-permute-start.20 = (bf16[8,40,640]{2,1,0:T(8,128)(2,1)S(1)}, bf16[8,40,640]{2,1,0:T(8,128)(2,1)S(1)}, u32[]{:S(2)}, u32[]{:S(2)}) collective-permute-start(bf16[8,40,640]{2,1,0:T(8,128)(2,1)S(1)} %get-tuple-element.55), channel_id=1, source_target_pairs={{0,48},{16,0},{32,16},{48,32},{1,49},{17,1},{33,17},{49,33},{2,50}... | collective-permute-start | bytes 1228808 | tf_op jit(solution)/shard_map/ppermute | solution.py:315
  148.1 23.2 %collective-permute-start.15 = (bf16[192,1280]{1,0:T(8,128)(2,1)}, bf16[192,1280]{1,0:T(8,128)(2,1)S(1)}, u32[]{:S(2)}, u32[]{:S(2)}) collective-permute-start(bf16[192,1280]{1,0:T(8,128)(2,1)} %get-tuple-element.49), channel_id=1, source_target_pairs={{0,6},{2,0},{4,2},{6,4},{1,7},{3,1},{5,3},{7,5},{8,14},{10,8},{12,... | collective-permute-start | bytes 1474568 | tf_op jit(solution)/shard_map/ppermute | solution.py:315
  149.2 22.0 %collective-permute-start.16 = (bf16[192,1280]{1,0:T(8,128)(2,1)}, bf16[192,1280]{1,0:T(8,128)(2,1)S(1)}, u32[]{:S(2)}, u32[]{:S(2)}) collective-permute-start(bf16[192,1280]{1,0:T(8,128)(2,1)} %get-tuple-element.50), channel_id=1, source_target_pairs={{0,4},{2,6},{4,0},{6,2},{1,5},{3,7},{5,1},{7,3},{8,12},{10,14},{12... | collective-permute-start | bytes 1474568 | tf_op jit(solution)/shard_map/ppermute | solution.py:315
  155.3 18.3 %collective-permute-start.17 = (bf16[192,1280]{1,0:T(8,128)(2,1)}, bf16[192,1280]{1,0:T(8,128)(2,1)S(1)}, u32[]{:S(2)}, u32[]{:S(2)}) collective-permute-start(bf16[192,1280]{1,0:T(8,128)(2,1)} %get-tuple-element.51), channel_id=1, source_target_pairs={{0,2},{2,4},{4,6},{6,0},{1,3},{3,5},{5,7},{7,1},{8,10},{10,12},{12... | collective-permute-start | bytes 1474568 | tf_op jit(solution)/shard_map/ppermute | solution.py:315
  166.5 18.9 %all-to-all-start.2 = ((bf16[8,40,640]{2,1,0:T(8,128)(2,1)}), bf16[8,40,640]{2,1,0:T(8,128)(2,1)S(1)}, u32[]{:S(2)}, u32[]{:S(2)}) async-start(bf16[8,40,640]{2,1,0:T(8,128)(2,1)} %x_sum.1), calls=%async_computation.2 | async-start | bytes 819200 | tf_op jit(solution)/shard_map/all_to_all | solution.py:435
Sparse Core Ops, SparseCore 0:
  30.2 30.5 all-gather.2

commit v7 on v6

--- a/solution.py
+++ b/solution.py
@@ -145,26 +145,26 @@
         for k in range(4):
             source = lax.rem(y - step + 4, 4) * 4 + lax.rem(zl + k // 2, 2) * 2
             source = source + lax.rem(c + k % 2, 2)
-            yield step, k, pl.multiple_of(source * rows_each, rows_each)
-
-
-def proj_kernel(place, *refs):
-    wires, proj = refs[:4], refs[4]
-    for step, k, row in wire_places(place, 32):
+            yield step, k // 2, k % 2, pl.multiple_of(source * rows_each, rows_each)
+
+
+def proj_kernel(place, own, other, proj):
+    for step, half, core, row in wire_places(place, 32):
+        wire = (own, other)[core]
         rows = pl.ds(row, 32)
-        proj[rows, :512] = wires[k][step, 64:96, :]
-        proj[rows, 512:1024] = wires[k][step, 96:128, :]
-        proj[pl.ds(row, 16), 1024:] = wires[k][step, 128:144, :256]
-        proj[pl.ds(pl.multiple_of(row + 16, 16), 16), 1024:] = wires[k][step, 128:144, 256:]
+        proj[rows, :512] = wire[step, half, 64:96, :]
+        proj[rows, 512:1024] = wire[step, half, 96:128, :]
+        proj[pl.ds(row, 16), 1024:] = wire[step, half, 128:144, :256]
+        proj[pl.ds(pl.multiple_of(row + 16, 16), 16), 1024:] = wire[step, half, 128:144, 256:]
 
 
 def front_kernel(place, incoming, *refs):
-    wires, (block, flags_out, conv, arrival) = refs[:4], refs[4:]
+    wires, (block, flags_out, conv, arrival) = refs[:2], refs[2:]
     copies = []
-    for step, k, row in wire_places(place, 64):
-        source = wires[k].at[step, pl.ds(0, 64), :]
+    for step, half, core, row in wire_places(place, 64):
+        source = wires[core].at[step, half, pl.ds(0, 64), :]
         target = conv.at[pl.ds(row, 64), :]
-        copies.append(pltpu.make_async_copy(source, target, arrival.at[step * 4 + k]))
+        copies.append(pltpu.make_async_copy(source, target, arrival.at[len(copies)]))
         copies[-1].start()
     for copy in copies:
         copy.wait()
@@ -189,11 +189,11 @@
 
 
 def ffn_kernel(place, blocks, own_pair, other_pair, *refs):
-    cots, proj_in, refs = refs[:4], refs[4], refs[5:]
+    cots, proj_in, refs = refs[0], refs[1], refs[2:]
     own, away1, away2, away3, kept, sent, refs = *refs[:6], refs[6:]
     proj, feats, live, normed, hidden, grad_pre, grad_out, wide_up, wide_down, *refs = refs
     cot, up, down, raw, arrival = refs
-    y, zl, c, zh = place[0], place[1], place[2], place[3]
+    y, zl, c, zh, x = place[0], place[1], place[2], place[3], place[4]
     copies = []
 
     def fetch(source, target):
@@ -212,17 +212,18 @@
         fetch(blocks.at[lax.rem(y - step + 4, 4)], feats.at[step])
     fetch(proj_in, proj)
     for step in range(4):
-        fetch(cots[step], cot.at[pl.ds(step * SLOTS, SLOTS), :])
+        fetch(cots.at[lax.rem(y - step + 4, 4)], cot.at[pl.ds(step * SLOTS, SLOTS), :])
     for copy in copies[:16]:
         copy.wait()
 
     def assemble(spot, carry):
-        rows = pl.ds(pl.multiple_of(spot * 2 * BLOCK, 16), 2 * BLOCK)
-        high, x = spot // 4, lax.rem(spot, 4)
+        high, behind = spot // 4, lax.rem(spot, 4)
+        row = high * 320 + lax.rem(x - behind + 4, 4) * 2 * BLOCK
+        rows = pl.ds(pl.multiple_of(row, 16), 2 * BLOCK)
         for half in range(2):
             lanes = slice(half * LANES, (half + 1) * LANES)
-            up0, down0 = unpack_pair(raw[0, half, high, x].astype(f32))
-            up1, down1 = unpack_pair(raw[1, half, high, x].astype(f32))
+            up0, down0 = unpack_pair(raw[0, half, high, behind].astype(f32))
+            up1, down1 = unpack_pair(raw[1, half, high, behind].astype(f32))
             up[rows, lanes] = jnp.concatenate([up0, up1], axis=0).astype(bf16)
             down[rows, lanes] = jnp.concatenate([down0, down1], axis=0).astype(bf16)
         return carry
@@ -333,11 +334,9 @@
         scratch=[pltpu.VMEM((2, BLOCK, UNITS), bf16), pltpu.SemaphoreType.DMA((6,))],
         smem=1, hbm=3, name="pack",
     )
+    cot_all = lax.all_gather(cotangent, "y", axis=0)
     both = jnp.stack([packed, ring(packed, "zl", 2, 1)])
-    wire_y = jnp.stack(around(wire, "y", 4))
-    along_z = jnp.stack(around(both, "zh", 4))
-    own_pair = lax.all_gather(along_z, "x", axis=0)
-    cot_pieces = around(cotangent, "y", 4)
+    wire_pair = jnp.stack([wire, ring(wire, "zl", 2, 1)])
 
     outgoing = call(
         route_kernel,
@@ -352,15 +351,15 @@
         ],
         hbm=3, name="route",
     )
-    outgoing, wire_y, along_z = lax.optimization_barrier((outgoing, wire_y, along_z))
-    wire_z = ring(wire_y, "zl", 2, 1)
-    wires = [wire_y, ring(wire_y, "c", 2, 1), wire_z, ring(wire_z, "c", 2, 1)]
+    along_z = jnp.stack(around(both, "zh", 4))
+    outgoing, along_z, wire_pair = lax.optimization_barrier((outgoing, along_z, wire_pair))
+    wire_own = jnp.stack(around(wire_pair, "y", 4))
+    wires = [wire_own, ring(wire_own, "c", 2, 1)]
+    along_x = around(along_z, "x", 4)
     incoming = lax.all_to_all(
         outgoing.reshape(N_DP, PAD, 1024), dp, split_axis=0, concat_axis=0, tiled=True
     ).reshape(N_DP * PAD, 1024)
-    incoming, cot_pieces[1], cot_pieces[3] = lax.optimization_barrier(
-        (incoming, cot_pieces[1], cot_pieces[3])
-    )
+    incoming, *along_x = lax.optimization_barrier((incoming, *along_x))
     where = jnp.stack([y, zl, c])
     proj_full = call(
         proj_kernel,
@@ -378,15 +377,13 @@
         [where, incoming, *wires],
         2 * 256 * 1024 * 512, 2 << 20,
         scratch=[pltpu.VMEM((1024, CH), bf16), pltpu.SemaphoreType.DMA((16,))],
-        smem=1, hbm=4, name="front",
+        smem=1, hbm=2, name="front",
     )
     block, proj_full = lax.optimization_barrier((block, proj_full))
     blocks = lax.all_to_all(
         jnp.broadcast_to(block[None], (4,) + block.shape), "y", split_axis=0, concat_axis=0
     )
-    blocks, own_pair, cot_pieces[2] = lax.optimization_barrier(
-        (blocks, own_pair, cot_pieces[2])
-    )
+    own_pair = jnp.stack(along_x)
     other_pair = ring(own_pair, "c", 2, 1)
 
     rows = 4 * SLOTS
@@ -395,7 +392,7 @@
     own, away1, away2, away3, kept, sent = call(
         ffn_kernel,
         (jax.ShapeDtypeStruct((SLOTS, D), f32), piece, piece, piece, terms, terms),
-        [jnp.stack([y, zl, c, zh]), blocks, own_pair, other_pair, *cot_pieces, proj_full],
+        [jnp.stack([y, zl, c, zh, x]), blocks, own_pair, other_pair, cot_all, proj_full],
         2 * rows * D * (CH + 5 * WIDE), 16 << 20,
         scratch=[
             pltpu.VMEM((CH, D), bf16),
@@ -413,7 +410,7 @@
             pltpu.VMEM((2, 2, 4, 4, BLOCK, 2 * UNITS), bf16),
             pltpu.SemaphoreType.DMA((25,)),
         ],
-        vmem=40 << 20, smem=1, hbm=8, name="ffn",
+        vmem=40 << 20, smem=1, hbm=5, name="ffn",
     )
     tile = jax.ShapeDtypeStruct((8, BLOCK, 2 * UNITS), bf16)
     parts = call(

time: 194 us -> 173 us (0.89)
  waiting for transfers between devices: 93 us -> 70.7 us
  other arithmetic: 2.19 us -> 5.29 us
    ppermute x21 -> x20, waiting for transfers between devices: 82.1 us -> 45.1 us  [ring(): lax.ppermute(values, axis, [(k, (k + step) % size) for k in range(size)])]
    all_to_all x1, waiting for transfers between devices: 0.01 us -> 13.6 us  [per_device(): lax.all_to_all(jnp.broadcast_to(block[None], (4,) + block.shape), 'y', sp...]
    another operation x2 -> x3, other arithmetic: 0.15 us -> 2.83 us  [the longest x1 2.65 us: per_device(): own_pair = jnp.stack(along_x)]
    ppermute x21 -> x20, starting transfers between devices: 32.8 us -> 31.4 us  [ring(): lax.ppermute(values, axis, [(k, (k + step) % size) for k in range(size)])]
  transfers between devices with their start and end apart: 25 -> 24, of which waited for: 18 -> 15; matrix products, arithmetic and copies ran while one was open for 1% -> 4% of each run, Pallas kernels for 3% -> 4%
where the time goes in v7:
time: 173 us; the launch traced here: 172 us
  waiting for transfers between devices  70.7 us (41%)
  starting transfers between devices  48.4 us (28%)
  Pallas kernels  29.6 us (17%)
  between operations  14.2 us (8%)
  other arithmetic  5.29 us (3%)
  local copies, waits for them, and re-layouts  3.46 us (2%)
    ppermute x20, waiting for transfers between devices, ring(): lax.ppermute(values, axis, [(k, (k + step) % size) for k in range(size)])  45.1 us
    ppermute x20, starting transfers between devices, ring(): lax.ppermute(values, axis, [(k, (k + step) % size) for k in range(size)])  31.4 us
    pallas_call x8, Pallas kernels, call(): pl.pallas_call(kernel, out_shape=out_shape, in_specs=[SMEM] * smem + [VME...  29.6 us
    all_to_all x1, waiting for transfers between devices, per_device(): lax.all_to_all(jnp.broadcast_to(block[None], (4,) + block.shape), 'y', sp...  13.6 us
    all_to_all x1, waiting for transfers between devices, per_device(): total = lax.all_to_all(total, ZX, split_axis=0, concat_axis=0, tiled=True)  11.9 us
    all_to_all x1, starting transfers between devices, per_device(): lax.all_to_all(outgoing.reshape(N_DP, PAD, 1024), dp, split_axis=0, conca...  7.82 us
    all_to_all x1, starting transfers between devices, per_device(): total = lax.all_to_all(total, ZX, split_axis=0, concat_axis=0, tiled=True)  5.43 us
    all_to_all x1, starting transfers between devices, per_device(): lax.all_to_all(jnp.broadcast_to(block[None], (4,) + block.shape), 'y', sp...  3.71 us
  transfers between devices with their start and end apart: 24, of which 15 were waited for; matrix products, arithmetic and copies ran while one was open for 4% of the time, Pallas kernels for 4%

profile of v7, /device:TPU:2, one launch (start us, length us, event | category | flops | bytes accessed | tf_op | source)
XLA Modules:
  0.0 171.7 jit_solution(17810841737943069420)
XLA Ops:
  7.2 0.0 all-gather.3.cloned.1.call-start
  7.2 1.0 pack.1
  8.2 2.0 %collective-permute-start = (bf16[40,640]{1,0:T(8,128)(2,1)S(1)}, bf16[40,640]{1,0:T(8,128)(2,1)S(1)}, u32[]{:S(2)}, u32[]{:S(2)}) collective-permute-start(bf16[40,640]{1,0:T(8,128)(2,1)S(1)} %get-tuple-element.29), channel_id=1, source_target_pairs={{0,1},{1,0},{2,3},{3,2},{4,5},{5,4},{6,7},{7,6},{8,9},{9,8},{10,11... | collective-permute-start | bytes 153608 | tf_op jit(solution)/shard_map/ppermute | solution.py:316
  10.2 0.1 collective-permute-start.4
  10.3 0.0 all-gather.3.cloned.1.call-update
  10.4 2.2 %route.1 = bf16[256,1024]{1,0:T(8,128)(2,1)} custom-call(s32[1,128]{1,0:T(1,128)} %bitcast.44, s32[1,128]{1,0:T(1,128)} %bitcast.45, bf16[128,1024]{1,0:T(8,128)(2,1)} %rows_in.1), custom_call_target="tpu_custom_call" | custom-call | flops 75497472 | bytes 1048576 | tf_op jit(solution)/shard_map/route/pallas_call | solution.py:53
  12.6 0.0 collective-permute-done
  12.6 7.6 %collective-permute-start.2 = (bf16[2,40,640]{2,1,0:T(8,128)(2,1)S(1)}, bf16[2,40,640]{2,1,0:T(8,128)(2,1)S(1)}, u32[]{:S(2)}, u32[]{:S(2)}) collective-permute-start(bf16[2,40,640]{2,1,0:T(8,128)(2,1)S(1)} %get-tuple-element.57), channel_id=1, source_target_pairs={{0,128},{64,192},{128,0},{192,64},{1,129},{65,193},{129,1},{193,65... | collective-permute-start | bytes 307208 | tf_op jit(solution)/shard_map/ppermute | solution.py:316
  20.2 1.5 collective-permute-start.1
  21.7 2.7 %collective-permute-start.3 = (bf16[2,40,640]{2,1,0:T(8,128)(2,1)S(1)}, bf16[2,40,640]{2,1,0:T(8,128)(2,1)S(1)}, u32[]{:S(2)}, u32[]{:S(2)}) collective-permute-start(bf16[2,40,640]{2,1,0:T(8,128)(2,1)S(1)} %get-tuple-element.57), channel_id=1, source_target_pairs={{0,192},{64,0},{128,64},{192,128},{1,193},{65,1},{129,65},{193,129... | collective-permute-start | bytes 307208 | tf_op jit(solution)/shard_map/ppermute | solution.py:316
  24.3 0.0 collective-permute-done.4
  24.4 1.8 %collective-permute-done.2 = bf16[2,40,640]{2,1,0:T(8,128)(2,1)S(1)} collective-permute-done((bf16[2,40,640]{2,1,0:T(8,128)(2,1)S(1)}, bf16[2,40,640]{2,1,0:T(8,128)(2,1)S(1)}, u32[]{:S(2)}, u32[]{:S(2)}) %collective-permute-start.2) | collective-permute-done | bytes 102432 | tf_op jit(solution)/shard_map/ppermute | solution.py:316
  26.1 1.7 %collective-permute-done.1 = bf16[2,40,640]{2,1,0:T(8,128)(2,1)S(1)} collective-permute-done((bf16[2,40,640]{2,1,0:T(8,128)(2,1)S(1)}, bf16[2,40,640]{2,1,0:T(8,128)(2,1)S(1)}, u32[]{:S(2)}, u32[]{:S(2)}) %collective-permute-start.1) | collective-permute-done | bytes 102432 | tf_op jit(solution)/shard_map/ppermute | solution.py:316
  27.9 2.4 %collective-permute-done.3 = bf16[2,40,640]{2,1,0:T(8,128)(2,1)S(1)} collective-permute-done((bf16[2,40,640]{2,1,0:T(8,128)(2,1)S(1)}, bf16[2,40,640]{2,1,0:T(8,128)(2,1)S(1)}, u32[]{:S(2)}, u32[]{:S(2)}) %collective-permute-start.3) | collective-permute-done | bytes 102432 | tf_op jit(solution)/shard_map/ppermute | solution.py:316
  30.2 0.1 pad_maximum_fusion.2
  30.3 7.8 %all-to-all-start = ((bf16[32,8,1024]{2,1,0:T(8,128)(2,1)}), bf16[32,8,1024]{2,1,0:T(8,128)(2,1)S(1)}, u32[]{:S(2)}, u32[]{:S(2)}) async-start(bf16[32,8,1024]{2,1,0:T(8,128)(2,1)} %bitcast.16), calls=%async_computation | async-start | bytes 1048576 | tf_op jit(solution)/shard_map/all_to_all | solution.py:359
  38.1 3.1 %collective-permute-start.10 = (bf16[2,144,512]{2,1,0:T(8,128)(2,1)S(1)}, bf16[2,144,512]{2,1,0:T(8,128)(2,1)S(1)}, u32[]{:S(2)}, u32[]{:S(2)}) collective-permute-start(bf16[2,144,512]{2,1,0:T(8,128)(2,1)S(1)} %pad_maximum_fusion.3), channel_id=1, source_target_pairs={{0,6},{2,0},{4,2},{6,4},{1,7},{3,1},{5,3},{7,5},{8,14},{10,8},{12,... | collective-permute-start | bytes 884744 | tf_op jit(solution)/shard_map/ppermute | solution.py:316
  41.2 0.6 collective-permute-start.9
  41.8 1.0 collective-permute-start.8
  42.8 0.2 collective-permute-start.7
  43.1 2.7 %collective-permute-start.6 = (bf16[4,2,40,640]{3,2,1,0:T(8,128)(2,1)S(1)}, bf16[4,2,40,640]{3,2,1,0:T(8,128)(2,1)}, u32[]{:S(2)}, u32[]{:S(2)}) collective-permute-start(bf16[4,2,40,640]{3,2,1,0:T(8,128)(2,1)S(1)} %pad_maximum_fusion.2), channel_id=1, source_target_pairs={{0,32},{16,48},{32,0},{48,16},{1,33},{17,49},{33,1},{49,17},{2,34}... | collective-permute-start | bytes 1228808 | tf_op jit(solution)/shard_map/ppermute | solution.py:316
  45.7 5.3 %collective-permute-done.10 = bf16[2,144,512]{2,1,0:T(8,128)(2,1)S(1)} collective-permute-done((bf16[2,144,512]{2,1,0:T(8,128)(2,1)S(1)}, bf16[2,144,512]{2,1,0:T(8,128)(2,1)S(1)}, u32[]{:S(2)}, u32[]{:S(2)}) %collective-permute-start.10) | collective-permute-done | bytes 294944 | tf_op jit(solution)/shard_map/ppermute | solution.py:316
  51.1 1.5 collective-permute-start.5
  52.6 0.1 collective-permute-done.9
  52.6 5.5 %collective-permute-done.8 = bf16[2,144,512]{2,1,0:T(8,128)(2,1)S(1)} collective-permute-done((bf16[2,144,512]{2,1,0:T(8,128)(2,1)S(1)}, bf16[2,144,512]{2,1,0:T(8,128)(2,1)S(1)}, u32[]{:S(2)}, u32[]{:S(2)}) %collective-permute-start.8) | collective-permute-done | bytes 294944 | tf_op jit(solution)/shard_map/ppermute | solution.py:316
  58.1 0.1 pad_maximum_fusion.1.refs_0_.own
  58.3 0.1 collective-permute-start.11
  58.4 0.0 collective-permute-done.7
  58.4 8.5 %collective-permute-done.6 = bf16[4,2,40,640]{3,2,1,0:T(8,128)(2,1)} collective-permute-done((bf16[4,2,40,640]{3,2,1,0:T(8,128)(2,1)S(1)}, bf16[4,2,40,640]{3,2,1,0:T(8,128)(2,1)}, u32[]{:S(2)}, u32[]{:S(2)}) %collective-permute-start.6) | collective-permute-done | bytes 409632 | tf_op jit(solution)/shard_map/ppermute | solution.py:316
  66.9 0.2 collective-permute-done.5
  67.1 0.0 all-to-all-done
  67.1 2.6 %pad_maximum_fusion.own_pair = bf16[4,4,2,40,640]{4,3,2,1,0:T(8,128)(2,1)} fusion(bf16[1,4,2,40,640]{4,3,2,1,0:T(8,128)(2,1)} %bitcast.25, bf16[1,4,2,40,640]{4,3,2,1,0:T(8,128)(2,1)} %bitcast.24, bf16[1,4,2,40,640]{4,3,2,1,0:T(8,128)(2,1)} %bitcast.23, bf16[1,4,2,40,640]{4,3,2,1,0:T(8,128)(2,1)S(1)} %bitcast.32), kind=kLoop, calls=%fused_computation | loop fusion | flops 2457600 | bytes 3276800 | tf_op jit(solution)/shard_map/stack | solution.py:386
  69.7 0.1 pad_add_fusion.place
  69.8 0.0 collective-permute-done.11.refs_1_.other
  69.8 0.6 proj.1.refs_1_
  70.5 0.5 copy-done.1
  70.9 1.1 copy-done.2
  72.0 2.9 %front.1 = (bf16[208,512]{1,0:T(8,128)(2,1)S(1)}, f32[192,1]{1,0:T(8,128)S(1)}) custom-call(s32[3]{0:T(128)S(1)} %pad_add_fusion.place, bf16[256,1024]{1,0:T(8,128)(2,1)S(1)} %bitcast.29, bf16[4,2,144,512]{3,2,1,0:T(8,128)(2,1)} %copy-done, bf16[4,2,144,512]{3,2,1,0:T(8,128)(2,1)} %copy-done.1), custom_call_target="tpu_custom_call" | custom-call | flops 268435456 | bytes 2097152 | tf_op jit(solution)/shard_map/front/pallas_call | solution.py:53
  74.9 1.0 broadcast_in_dim.2
  75.9 3.7 %all-to-all-start.1 = ((bf16[4,208,512]{2,1,0:T(8,128)(2,1)}), bf16[4,208,512]{2,1,0:T(8,128)(2,1)S(1)}, u32[]{:S(2)}, u32[]{:S(2)}) async-start(bf16[4,208,512]{2,1,0:T(8,128)(2,1)} %broadcast_in_dim.2), calls=%async_computation.1 | async-start | bytes 1703936 | tf_op jit(solution)/shard_map/all_to_all | solution.py:383
  79.6 0.1 stack.92.place
  79.7 13.6 %all-to-all-done.1.blocks = bf16[4,208,512]{2,1,0:T(8,128)(2,1)S(1)} async-done(((bf16[4,208,512]{2,1,0:T(8,128)(2,1)}), bf16[4,208,512]{2,1,0:T(8,128)(2,1)S(1)}, u32[]{:S(2)}, u32[]{:S(2)}) %all-to-all-start.1) | async-done | bytes 852000 | tf_op jit(solution)/shard_map/all_to_all | solution.py:383
  93.3 0.0 collective-permute-done.12.other_pair
  93.3 0.9 copy-done.3
  94.2 20.8 %ffn.1 = (f32[192,1280]{1,0:T(8,128)S(1)}, bf16[192,1280]{1,0:T(8,128)(2,1)S(1)}, bf16[192,1280]{1,0:T(8,128)(2,1)S(1)}, bf16[192,1280]{1,0:T(8,128)(2,1)S(1)}, ...) custom-call(s32[5]{0:T(128)S(1)} %stack.92.place, bf16[4,208,512]{2,1,0:T(8,128)(2,1)} %copy-done.3, ...), custom_call_target="tpu_custom_call" | custom-call | flops 8556380160 | bytes 16777216 | tf_op jit(solution)/shard_map/ffn/pallas_call | solution.py:53
  115.0 0.1 collective-permute-start.13
  115.1 3.5 %collective-permute-done.13.arrived = bf16[4,8,40,640]{3,2,1,0:T(8,128)(2,1)S(1)} collective-permute-done((bf16[4,8,40,640]{3,2,1,0:T(8,128)(2,1)S(1)}, bf16[4,8,40,640]{3,2,1,0:T(8,128)(2,1)S(1)}, u32[]{:S(2)}, u32[]{:S(2)}) %collective-permute-start.13) | collective-permute-done | bytes 1638432 | tf_op jit(solution)/shard_map/ppermute | solution.py:316
  118.6 0.4 core_sum.1
  119.0 1.5 collective-permute-start.17
  120.5 3.6 %collective-permute-start.18 = (bf16[8,40,640]{2,1,0:T(8,128)(2,1)S(1)}, bf16[8,40,640]{2,1,0:T(8,128)(2,1)S(1)}, u32[]{:S(2)}, u32[]{:S(2)}) collective-permute-start(bf16[8,40,640]{2,1,0:T(8,128)(2,1)S(1)} %get-tuple-element.54), channel_id=1, source_target_pairs={{0,32},{16,48},{32,0},{48,16},{1,33},{17,49},{33,1},{49,17},{2,34}... | collective-permute-start | bytes 1228808 | tf_op jit(solution)/shard_map/ppermute | solution.py:316
  124.1 1.3 collective-permute-start.14
  125.4 1.3 collective-permute-start.15
  126.7 5.5 %collective-permute-done.17.refs_1_ = bf16[8,40,640]{2,1,0:T(8,128)(2,1)S(1)} collective-permute-done((bf16[8,40,640]{2,1,0:T(8,128)(2,1)S(1)}, bf16[8,40,640]{2,1,0:T(8,128)(2,1)S(1)}, u32[]{:S(2)}, u32[]{:S(2)}) %collective-permute-start.17) | collective-permute-done | bytes 409632 | tf_op jit(solution)/shard_map/ppermute | solution.py:316
  132.3 0.6 collective-permute-start.16
  132.8 1.6 collective-permute-done.18.refs_2_
  134.4 7.9 %collective-permute-done.19.refs_3_ = bf16[8,40,640]{2,1,0:T(8,128)(2,1)S(1)} collective-permute-done((bf16[8,40,640]{2,1,0:T(8,128)(2,1)S(1)}, bf16[8,40,640]{2,1,0:T(8,128)(2,1)S(1)}, u32[]{:S(2)}, u32[]{:S(2)}) %collective-permute-start.19) | collective-permute-done | bytes 409632 | tf_op jit(solution)/shard_map/ppermute | solution.py:316
  142.3 0.9 x_sum.1
  143.3 5.4 %all-to-all-start.2 = ((bf16[8,40,640]{2,1,0:T(8,128)(2,1)}), bf16[8,40,640]{2,1,0:T(8,128)(2,1)S(1)}, u32[]{:S(2)}, u32[]{:S(2)}) async-start(bf16[8,40,640]{2,1,0:T(8,128)(2,1)} %x_sum.1), calls=%async_computation.2 | async-start | bytes 819200 | tf_op jit(solution)/shard_map/all_to_all | solution.py:432
  148.7 0.1 convert_reduce_fusion
  148.8 0.0 collective-permute-done.15
  148.9 1.1 collective-permute-done.16
  150.0 2.2 %multiply_convert_fusion = bf16[192,1280]{1,0:T(8,128)(2,1)} fusion(bf16[192,1280]{1,0:T(8,128)(2,1)} %collective-permute-done.16, bf16[192,1280]{1,0:T(8,128)(2,1)} %collective-permute-done.15, f32[192,1280]{1,0:T(8,128)S(1)} %get-tuple-element.42, bf16[192,1280]{1,0:T(8,128)(2,1)S(1)} %collective-permute-done.14, f32[192]{0:T(256)S(1)} %convert_reduce_fusion), kind=kLoop, calls=%fused_computation.2 | loop fusion | flops 1966080 | bytes 2949888 | tf_op jit(solution)/shard_map/convert_element_type | solution.py:431
  152.2 11.9 %all-to-all-done.2.arrived = bf16[8,40,640]{2,1,0:T(8,128)(2,1)S(1)} async-done(((bf16[8,40,640]{2,1,0:T(8,128)(2,1)}), bf16[8,40,640]{2,1,0:T(8,128)(2,1)S(1)}, u32[]{:S(2)}, u32[]{:S(2)}) %all-to-all-start.2) | async-done | bytes 409632 | tf_op jit(solution)/shard_map/all_to_all | solution.py:432
  164.0 0.8 last.1
  (11 shorter events, 0.1 us)
Async XLA Ops:
  7.2 86.1 %all-gather.3.cloned.1.call-start = ((), (), s32[]{:S(2)}) async-start(), calls=%async_computation.3 | async-start | bytes 2457600 | tf_op jit(solution)/shard_map/all_gather | solution.py:337
  8.2 4.3 %collective-permute-start = (bf16[40,640]{1,0:T(8,128)(2,1)S(1)}, bf16[40,640]{1,0:T(8,128)(2,1)S(1)}, u32[]{:S(2)}, u32[]{:S(2)}) collective-permute-start(bf16[40,640]{1,0:T(8,128)(2,1)S(1)} %get-tuple-element.29), channel_id=1, source_target_pairs={{0,1},{1,0},{2,3},{3,2},{4,5},{5,4},{6,7},{7,6},{8,9},{9,8},{10,11... | collective-permute-start | bytes 153608 | tf_op jit(solution)/shard_map/ppermute | solution.py:316
  10.2 14.1 %collective-permute-start.4 = (bf16[144,512]{1,0:T(8,128)(2,1)S(1)}, bf16[144,512]{1,0:T(8,128)(2,1)S(1)}, u32[]{:S(2)}, u32[]{:S(2)}) collective-permute-start(bf16[144,512]{1,0:T(8,128)(2,1)S(1)} %get-tuple-element.30), channel_id=1, source_target_pairs={{0,1},{1,0},{2,3},{3,2},{4,5},{5,4},{6,7},{7,6},{8,9},{9,8},{10,11... | collective-permute-start | bytes 442376 | tf_op jit(solution)/shard_map/ppermute | solution.py:316
  12.6 13.5 %collective-permute-start.2 = (bf16[2,40,640]{2,1,0:T(8,128)(2,1)S(1)}, bf16[2,40,640]{2,1,0:T(8,128)(2,1)S(1)}, u32[]{:S(2)}, u32[]{:S(2)}) collective-permute-start(bf16[2,40,640]{2,1,0:T(8,128)(2,1)S(1)} %get-tuple-element.57), channel_id=1, source_target_pairs={{0,128},{64,192},{128,0},{192,64},{1,129},{65,193},{129,1},{193,65... | collective-permute-start | bytes 307208 | tf_op jit(solution)/shard_map/ppermute | solution.py:316
  20.2 7.7 %collective-permute-start.1 = (bf16[2,40,640]{2,1,0:T(8,128)(2,1)S(1)}, bf16[2,40,640]{2,1,0:T(8,128)(2,1)S(1)}, u32[]{:S(2)}, u32[]{:S(2)}) collective-permute-start(bf16[2,40,640]{2,1,0:T(8,128)(2,1)S(1)} %get-tuple-element.57), channel_id=1, source_target_pairs={{0,64},{64,128},{128,192},{192,0},{1,65},{65,129},{129,193},{193,1... | collective-permute-start | bytes 307208 | tf_op jit(solution)/shard_map/ppermute | solution.py:316
  21.7 8.6 %collective-permute-start.3 = (bf16[2,40,640]{2,1,0:T(8,128)(2,1)S(1)}, bf16[2,40,640]{2,1,0:T(8,128)(2,1)S(1)}, u32[]{:S(2)}, u32[]{:S(2)}) collective-permute-start(bf16[2,40,640]{2,1,0:T(8,128)(2,1)S(1)} %get-tuple-element.57), channel_id=1, source_target_pairs={{0,192},{64,0},{128,64},{192,128},{1,193},{65,1},{129,65},{193,129... | collective-permute-start | bytes 307208 | tf_op jit(solution)/shard_map/ppermute | solution.py:316
  30.3 36.8 %all-to-all-start = ((bf16[32,8,1024]{2,1,0:T(8,128)(2,1)}), bf16[32,8,1024]{2,1,0:T(8,128)(2,1)S(1)}, u32[]{:S(2)}, u32[]{:S(2)}) async-start(bf16[32,8,1024]{2,1,0:T(8,128)(2,1)} %bitcast.16), calls=%async_computation | async-start | bytes 1048576 | tf_op jit(solution)/shard_map/all_to_all | solution.py:359
  38.1 13.0 %collective-permute-start.10 = (bf16[2,144,512]{2,1,0:T(8,128)(2,1)S(1)}, bf16[2,144,512]{2,1,0:T(8,128)(2,1)S(1)}, u32[]{:S(2)}, u32[]{:S(2)}) collective-permute-start(bf16[2,144,512]{2,1,0:T(8,128)(2,1)S(1)} %pad_maximum_fusion.3), channel_id=1, source_target_pairs={{0,6},{2,0},{4,2},{6,4},{1,7},{3,1},{5,3},{7,5},{8,14},{10,8},{12,... | collective-permute-start | bytes 884744 | tf_op jit(solution)/shard_map/ppermute | solution.py:316
  41.2 11.4 %collective-permute-start.9 = (bf16[2,144,512]{2,1,0:T(8,128)(2,1)S(1)}, bf16[2,144,512]{2,1,0:T(8,128)(2,1)S(1)}, u32[]{:S(2)}, u32[]{:S(2)}) collective-permute-start(bf16[2,144,512]{2,1,0:T(8,128)(2,1)S(1)} %pad_maximum_fusion.3), channel_id=1, source_target_pairs={{0,4},{2,6},{4,0},{6,2},{1,5},{3,7},{5,1},{7,3},{8,12},{10,14},{12... | collective-permute-start | bytes 884744 | tf_op jit(solution)/shard_map/ppermute | solution.py:316
  41.8 16.3 %collective-permute-start.8 = (bf16[2,144,512]{2,1,0:T(8,128)(2,1)S(1)}, bf16[2,144,512]{2,1,0:T(8,128)(2,1)S(1)}, u32[]{:S(2)}, u32[]{:S(2)}) collective-permute-start(bf16[2,144,512]{2,1,0:T(8,128)(2,1)S(1)} %pad_maximum_fusion.3), channel_id=1, source_target_pairs={{0,2},{2,4},{4,6},{6,0},{1,3},{3,5},{5,7},{7,1},{8,10},{10,12},{12... | collective-permute-start | bytes 884744 | tf_op jit(solution)/shard_map/ppermute | solution.py:316
  42.8 15.6 %collective-permute-start.7 = (bf16[4,2,40,640]{3,2,1,0:T(8,128)(2,1)S(1)}, bf16[4,2,40,640]{3,2,1,0:T(8,128)(2,1)}, u32[]{:S(2)}, u32[]{:S(2)}) collective-permute-start(bf16[4,2,40,640]{3,2,1,0:T(8,128)(2,1)S(1)} %pad_maximum_fusion.2), channel_id=1, source_target_pairs={{0,48},{16,0},{32,16},{48,32},{1,49},{17,1},{33,17},{49,33},{2,50}... | collective-permute-start | bytes 1228808 | tf_op jit(solution)/shard_map/ppermute | solution.py:316
  43.1 23.8 %collective-permute-start.6 = (bf16[4,2,40,640]{3,2,1,0:T(8,128)(2,1)S(1)}, bf16[4,2,40,640]{3,2,1,0:T(8,128)(2,1)}, u32[]{:S(2)}, u32[]{:S(2)}) collective-permute-start(bf16[4,2,40,640]{3,2,1,0:T(8,128)(2,1)S(1)} %pad_maximum_fusion.2), channel_id=1, source_target_pairs={{0,32},{16,48},{32,0},{48,16},{1,33},{17,49},{33,1},{49,17},{2,34}... | collective-permute-start | bytes 1228808 | tf_op jit(solution)/shard_map/ppermute | solution.py:316
  51.1 16.0 %collective-permute-start.5 = (bf16[4,2,40,640]{3,2,1,0:T(8,128)(2,1)S(1)}, bf16[4,2,40,640]{3,2,1,0:T(8,128)(2,1)}, u32[]{:S(2)}, u32[]{:S(2)}) collective-permute-start(bf16[4,2,40,640]{3,2,1,0:T(8,128)(2,1)S(1)} %pad_maximum_fusion.2), channel_id=1, source_target_pairs={{0,16},{16,32},{32,48},{48,0},{1,17},{17,33},{33,49},{49,1},{2,18}... | collective-permute-start | bytes 1228808 | tf_op jit(solution)/shard_map/ppermute | solution.py:316
  58.3 11.6 %copy-start = (bf16[4,2,144,512]{3,2,1,0:T(8,128)(2,1)}, bf16[4,2,144,512]{3,2,1,0:T(8,128)(2,1)S(1)}, u32[]{:S(2)}) copy-start(bf16[4,2,144,512]{3,2,1,0:T(8,128)(2,1)S(1)} %pad_maximum_fusion.1.refs_0_.own) | copy-start | bytes 3538948
  58.3 11.5 %collective-permute-start.11 = (bf16[4,2,144,512]{3,2,1,0:T(8,128)(2,1)S(1)}, bf16[4,2,144,512]{3,2,1,0:T(8,128)(2,1)S(1)}, u32[]{:S(2)}, u32[]{:S(2)}) collective-permute-start(bf16[4,2,144,512]{3,2,1,0:T(8,128)(2,1)S(1)} %pad_maximum_fusion.1.refs_0_.own), channel_id=1, source_target_pairs={{0,8},{8,0},{1,9},{9,1},{2,10},{10,2},{3,11},{11,3},{4,12},{12,4},... | collective-permute-start | bytes 3538952 | tf_op jit(solution)/shard_map/ppermute | solution.py:316
  69.7 23.5 %collective-permute-start.12 = (bf16[4,4,2,40,640]{4,3,2,1,0:T(8,128)(2,1)}, bf16[4,4,2,40,640]{4,3,2,1,0:T(8,128)(2,1)}, u32[]{:S(2)}, u32[]{:S(2)}) collective-permute-start(bf16[4,4,2,40,640]{4,3,2,1,0:T(8,128)(2,1)} %pad_maximum_fusion.own_pair), channel_id=1, source_target_pairs={{0,8},{8,0},{1,9},{9,1},{2,10},{10,2},{3,11},{11,3},{4,12},{12,4},... | collective-permute-start | bytes 4915208 | tf_op jit(solution)/shard_map/ppermute | solution.py:316
  69.8 1.1 copy-start.1
  70.9 1.1 copy-start.2
  75.9 17.4 %all-to-all-start.1 = ((bf16[4,208,512]{2,1,0:T(8,128)(2,1)}), bf16[4,208,512]{2,1,0:T(8,128)(2,1)S(1)}, u32[]{:S(2)}, u32[]{:S(2)}) async-start(bf16[4,208,512]{2,1,0:T(8,128)(2,1)} %broadcast_in_dim.2), calls=%async_computation.1 | async-start | bytes 1703936 | tf_op jit(solution)/shard_map/all_to_all | solution.py:383
  93.3 0.9 copy-start.3
  115.0 3.6 %collective-permute-start.13 = (bf16[4,8,40,640]{3,2,1,0:T(8,128)(2,1)S(1)}, bf16[4,8,40,640]{3,2,1,0:T(8,128)(2,1)S(1)}, u32[]{:S(2)}, u32[]{:S(2)}) collective-permute-start(bf16[4,8,40,640]{3,2,1,0:T(8,128)(2,1)S(1)} %get-tuple-element.47), channel_id=1, source_target_pairs={{0,8},{8,0},{1,9},{9,1},{2,10},{10,2},{3,11},{11,3},{4,12},{12,4},... | collective-permute-start | bytes 4915208 | tf_op jit(solution)/shard_map/ppermute | solution.py:316
  119.0 13.3 %collective-permute-start.17 = (bf16[8,40,640]{2,1,0:T(8,128)(2,1)S(1)}, bf16[8,40,640]{2,1,0:T(8,128)(2,1)S(1)}, u32[]{:S(2)}, u32[]{:S(2)}) collective-permute-start(bf16[8,40,640]{2,1,0:T(8,128)(2,1)S(1)} %get-tuple-element.53), channel_id=1, source_target_pairs={{0,16},{16,32},{32,48},{48,0},{1,17},{17,33},{33,49},{49,1},{2,18}... | collective-permute-start | bytes 1228808 | tf_op jit(solution)/shard_map/ppermute | solution.py:316
  120.5 13.9 %collective-permute-start.18 = (bf16[8,40,640]{2,1,0:T(8,128)(2,1)S(1)}, bf16[8,40,640]{2,1,0:T(8,128)(2,1)S(1)}, u32[]{:S(2)}, u32[]{:S(2)}) collective-permute-start(bf16[8,40,640]{2,1,0:T(8,128)(2,1)S(1)} %get-tuple-element.54), channel_id=1, source_target_pairs={{0,32},{16,48},{32,0},{48,16},{1,33},{17,49},{33,1},{49,17},{2,34}... | collective-permute-start | bytes 1228808 | tf_op jit(solution)/shard_map/ppermute | solution.py:316
  124.1 18.3 %collective-permute-start.19 = (bf16[8,40,640]{2,1,0:T(8,128)(2,1)S(1)}, bf16[8,40,640]{2,1,0:T(8,128)(2,1)S(1)}, u32[]{:S(2)}, u32[]{:S(2)}) collective-permute-start(bf16[8,40,640]{2,1,0:T(8,128)(2,1)S(1)} %get-tuple-element.55), channel_id=1, source_target_pairs={{0,48},{16,0},{32,16},{48,32},{1,49},{17,1},{33,17},{49,33},{2,50}... | collective-permute-start | bytes 1228808 | tf_op jit(solution)/shard_map/ppermute | solution.py:316
  124.1 24.7 %collective-permute-start.14 = (bf16[192,1280]{1,0:T(8,128)(2,1)S(1)}, bf16[192,1280]{1,0:T(8,128)(2,1)S(1)}, u32[]{:S(2)}, u32[]{:S(2)}) collective-permute-start(bf16[192,1280]{1,0:T(8,128)(2,1)S(1)} %get-tuple-element.49), channel_id=1, source_target_pairs={{0,6},{2,0},{4,2},{6,4},{1,7},{3,1},{5,3},{7,5},{8,14},{10,8},{12,... | collective-permute-start | bytes 1474568 | tf_op jit(solution)/shard_map/ppermute | solution.py:316
  125.4 23.5 %collective-permute-start.15 = (bf16[192,1280]{1,0:T(8,128)(2,1)S(1)}, bf16[192,1280]{1,0:T(8,128)(2,1)}, u32[]{:S(2)}, u32[]{:S(2)}) collective-permute-start(bf16[192,1280]{1,0:T(8,128)(2,1)S(1)} %get-tuple-element.50), channel_id=1, source_target_pairs={{0,4},{2,6},{4,0},{6,2},{1,5},{3,7},{5,1},{7,3},{8,12},{10,14},{12... | collective-permute-start | bytes 1474568 | tf_op jit(solution)/shard_map/ppermute | solution.py:316
  132.3 17.7 %collective-permute-start.16 = (bf16[192,1280]{1,0:T(8,128)(2,1)S(1)}, bf16[192,1280]{1,0:T(8,128)(2,1)}, u32[]{:S(2)}, u32[]{:S(2)}) collective-permute-start(bf16[192,1280]{1,0:T(8,128)(2,1)S(1)} %get-tuple-element.51), channel_id=1, source_target_pairs={{0,2},{2,4},{4,6},{6,0},{1,3},{3,5},{5,7},{7,1},{8,10},{10,12},{12... | collective-permute-start | bytes 1474568 | tf_op jit(solution)/shard_map/ppermute | solution.py:316
  143.3 20.8 %all-to-all-start.2 = ((bf16[8,40,640]{2,1,0:T(8,128)(2,1)}), bf16[8,40,640]{2,1,0:T(8,128)(2,1)S(1)}, u32[]{:S(2)}, u32[]{:S(2)}) async-start(bf16[8,40,640]{2,1,0:T(8,128)(2,1)} %x_sum.1), calls=%async_computation.2 | async-start | bytes 819200 | tf_op jit(solution)/shard_map/all_to_all | solution.py:432
Sparse Core Ops, SparseCore 0:
  10.5 37.8 all-gather.2

commit v8 on v7

--- a/solution.py
+++ b/solution.py
@@ -29,6 +29,7 @@
 VMEM = pl.BlockSpec(memory_space=pltpu.VMEM)
 SMEM = pl.BlockSpec(memory_space=pltpu.SMEM)
 HBM = pl.BlockSpec(memory_space=pltpu.HBM)
+ANY = pl.BlockSpec(memory_space=pl.ANY)
 
 
 def dot(a, b, dims=((1,), (0,))):
@@ -46,14 +47,14 @@
     return centered * lax.rsqrt(variance + epsilon)
 
 
-def call(kernel, out_shape, args, flops, bytes_accessed, scratch=(), vmem=12 << 20, smem=0, hbm=0, name=None):
+def call(kernel, out_shape, args, flops, bytes_accessed, scratch=(), vmem=12 << 20, smem=0, hbm=0, free=0, name=None):
     args = list(args)
     for k in range(len(args) - hbm, len(args)):
         args[k] = pltpu.with_memory_space_constraint(args[k], pltpu.HBM)
     return pl.pallas_call(
         kernel,
         out_shape=out_shape,
-        in_specs=[SMEM] * smem + [VMEM] * (len(args) - smem - hbm) + [HBM] * hbm,
+        in_specs=[SMEM] * smem + [VMEM] * (len(args) - smem - free - hbm) + [ANY] * free + [HBM] * hbm,
         out_specs=jax.tree.map(lambda _: VMEM, out_shape),
         scratch_shapes=list(scratch),
         compiler_params=pltpu.CompilerParams(vmem_limit_bytes=vmem),
@@ -176,7 +177,9 @@
     row = iota((SLOTS, N_DP * PAD), 1)
     owner, rank = slot // CAP, slot % CAP
     compact = (row == owner * PAD + rank).astype(bf16)
-    block[:SLOTS, :] = dot(compact, features).astype(bf16)
+    compacted = dot(compact, features).astype(bf16)
+    for copy in range(4):
+        block[copy, :SLOTS, :] = compacted
     flag_rows = dot((row == owner * PAD + CAP).astype(bf16), raw[:, :128])
     lane = iota((SLOTS, 128), 1)
     flags = jnp.sum(
@@ -185,11 +188,12 @@
     flags_out[...] = flags
     wide = iota((SLOTS, CH), 1) == iota((SLOTS, CH), 0)
     as_row = jnp.sum(jnp.where(wide, flags, 0.0), axis=0, keepdims=True)
-    block[SLOTS:, :] = jnp.broadcast_to(as_row, (16, CH)).astype(bf16)
-
-
-def ffn_kernel(place, blocks, own_pair, other_pair, *refs):
-    cots, proj_in, refs = refs[0], refs[1], refs[2:]
+    for copy in range(4):
+        block[copy, SLOTS:, :] = jnp.broadcast_to(as_row, (16, CH)).astype(bf16)
+
+
+def ffn_kernel(place, blocks, *refs):
+    pieces, cots, proj_in, refs = refs[:8], refs[8], refs[9], refs[10:]
     own, away1, away2, away3, kept, sent, refs = *refs[:6], refs[6:]
     proj, feats, live, normed, hidden, grad_pre, grad_out, wide_up, wide_down, *refs = refs
     cot, up, down, raw, arrival = refs
@@ -201,35 +205,31 @@
         copy.start()
         copies.append(copy)
 
-    for k, pair in enumerate((own_pair, other_pair)):
-        for step in range(4):
-            for other in range(2):
-                target = raw.at[
-                    lax.rem(c + k, 2), lax.rem(zl + other, 2), lax.rem(zh - step + 4, 4)
-                ]
-                fetch(pair.at[:, step, other], target)
+    for k, piece in enumerate(pieces):
+        fetch(piece, raw.at[k // 4, k % 4])
     for step in range(4):
         fetch(blocks.at[lax.rem(y - step + 4, 4)], feats.at[step])
     fetch(proj_in, proj)
     for step in range(4):
         fetch(cots.at[lax.rem(y - step + 4, 4)], cot.at[pl.ds(step * SLOTS, SLOTS), :])
-    for copy in copies[:16]:
+    for copy in copies[:8]:
         copy.wait()
 
     def assemble(spot, carry):
-        high, behind = spot // 4, lax.rem(spot, 4)
-        row = high * 320 + lax.rem(x - behind + 4, 4) * 2 * BLOCK
+        above, behind = spot // 4, lax.rem(spot, 4)
+        row = lax.rem(zh - above + 4, 4) * 320 + lax.rem(x - behind + 4, 4) * 2 * BLOCK
         rows = pl.ds(pl.multiple_of(row, 16), 2 * BLOCK)
         for half in range(2):
             lanes = slice(half * LANES, (half + 1) * LANES)
-            up0, down0 = unpack_pair(raw[0, half, high, behind].astype(f32))
-            up1, down1 = unpack_pair(raw[1, half, high, behind].astype(f32))
+            other = lax.rem(zl + half, 2)
+            up0, down0 = unpack_pair(raw[c, behind, above, other].astype(f32))
+            up1, down1 = unpack_pair(raw[1 - c, behind, above, other].astype(f32))
             up[rows, lanes] = jnp.concatenate([up0, up1], axis=0).astype(bf16)
             down[rows, lanes] = jnp.concatenate([down0, down1], axis=0).astype(bf16)
         return carry
 
     lax.fori_loop(0, 16, assemble, 0, unroll=4)
-    for copy in copies[16:]:
+    for copy in copies[8:]:
         copy.wait()
     for step in range(4):
         flags = feats[step, SLOTS : SLOTS + 16, :].astype(f32)[:1, :]
@@ -352,14 +352,13 @@
         hbm=3, name="route",
     )
     along_z = jnp.stack(around(both, "zh", 4))
-    outgoing, along_z, wire_pair = lax.optimization_barrier((outgoing, along_z, wire_pair))
     wire_own = jnp.stack(around(wire_pair, "y", 4))
+    outgoing, along_z, wire_own = lax.optimization_barrier((outgoing, along_z, wire_own))
     wires = [wire_own, ring(wire_own, "c", 2, 1)]
     along_x = around(along_z, "x", 4)
     incoming = lax.all_to_all(
         outgoing.reshape(N_DP, PAD, 1024), dp, split_axis=0, concat_axis=0, tiled=True
     ).reshape(N_DP * PAD, 1024)
-    incoming, *along_x = lax.optimization_barrier((incoming, *along_x))
     where = jnp.stack([y, zl, c])
     proj_full = call(
         proj_kernel,
@@ -371,20 +370,17 @@
     block, flags = call(
         front_kernel,
         (
-            jax.ShapeDtypeStruct((SLOTS + 16, CH), bf16),
+            jax.ShapeDtypeStruct((4, SLOTS + 16, CH), bf16),
             jax.ShapeDtypeStruct((SLOTS, 1), f32),
         ),
         [where, incoming, *wires],
         2 * 256 * 1024 * 512, 2 << 20,
         scratch=[pltpu.VMEM((1024, CH), bf16), pltpu.SemaphoreType.DMA((16,))],
-        smem=1, hbm=2, name="front",
-    )
-    block, proj_full = lax.optimization_barrier((block, proj_full))
-    blocks = lax.all_to_all(
-        jnp.broadcast_to(block[None], (4,) + block.shape), "y", split_axis=0, concat_axis=0
-    )
-    own_pair = jnp.stack(along_x)
-    other_pair = ring(own_pair, "c", 2, 1)
+        smem=1, free=2, name="front",
+    )
+    block, proj_full, *along_x = lax.optimization_barrier((block, proj_full, *along_x))
+    blocks = lax.all_to_all(block, "y", split_axis=0, concat_axis=0, tiled=True)
+    pieces = along_x + [ring(piece, "c", 2, 1) for piece in along_x]
 
     rows = 4 * SLOTS
     piece = jax.ShapeDtypeStruct((SLOTS, D), bf16)
@@ -392,7 +388,7 @@
     own, away1, away2, away3, kept, sent = call(
         ffn_kernel,
         (jax.ShapeDtypeStruct((SLOTS, D), f32), piece, piece, piece, terms, terms),
-        [jnp.stack([y, zl, c, zh, x]), blocks, own_pair, other_pair, cot_all, proj_full],
+        [jnp.stack([y, zl, c, zh, x]), blocks, *pieces, cot_all, proj_full],
         2 * rows * D * (CH + 5 * WIDE), 16 << 20,
         scratch=[
             pltpu.VMEM((CH, D), bf16),
@@ -407,10 +403,10 @@
             pltpu.VMEM((rows, D), bf16),
             pltpu.VMEM((D, WIDE), bf16),
             pltpu.VMEM((D, WIDE), bf16),
-            pltpu.VMEM((2, 2, 4, 4, BLOCK, 2 * UNITS), bf16),
-            pltpu.SemaphoreType.DMA((25,)),
+            pltpu.VMEM((2, 4, 4, 2, BLOCK, 2 * UNITS), bf16),
+            pltpu.SemaphoreType.DMA((17,)),
         ],
-        vmem=40 << 20, smem=1, hbm=5, name="ffn",
+        vmem=40 << 20, smem=1, hbm=10, free=1, name="ffn",
     )
     tile = jax.ShapeDtypeStruct((8, BLOCK, 2 * UNITS), bf16)
     parts = call(

time: 173 us -> 175 us (1.012)
  waiting for transfers between devices: 70.7 us -> 75.2 us
  other arithmetic: 5.29 us -> 2.8 us
  starting transfers between devices: 48.4 us -> 50.2 us
    all_to_all x1, waiting for transfers between devices: 0.01 us -> 10.4 us  [per_device(): lax.all_to_all(outgoing.reshape(N_DP, PAD, 1024), dp, split_axis=0, conca...]
    all_to_all x1, waiting for transfers between devices: 13.6 us -> 9.07 us  [per_device(): blocks = lax.all_to_all(block, 'y', split_axis=0, concat_axis=0, tiled=True)]
    ppermute x20 -> x23, starting transfers between devices: 31.4 us -> 34.5 us  [ring(): lax.ppermute(values, axis, [(k, (k + step) % size) for k in range(size)])]
    another operation x2 -> x0, other arithmetic: 2.68 us -> none  [the longest x1 2.65 us: per_device(): own_pair = jnp.stack(along_x)]
    ppermute x20 -> x23, waiting for transfers between devices: 45.1 us -> 43.6 us  [ring(): lax.ppermute(values, axis, [(k, (k + step) % size) for k in range(size)])]
  transfers between devices with their start and end apart: 24 -> 27, of which waited for: 15 -> 18; matrix products, arithmetic and copies ran while one was open for 4% -> 2% of each run, Pallas kernels for 4% -> 4%
where the time goes in v8:
time: 175 us; the launch traced here: 174 us
  waiting for transfers between devices  75.2 us (43%)
  starting transfers between devices  50.2 us (29%)
  Pallas kernels  29.7 us (17%)
  between operations  14.2 us (8%)
  other arithmetic  2.8 us (2%)
  local copies, waits for them, and re-layouts  2.07 us (1%)
    ppermute x23, waiting for transfers between devices, ring(): lax.ppermute(values, axis, [(k, (k + step) % size) for k in range(size)])  43.6 us
    ppermute x23, starting transfers between devices, ring(): lax.ppermute(values, axis, [(k, (k + step) % size) for k in range(size)])  34.5 us
    pallas_call x8, Pallas kernels, call(): pl.pallas_call(kernel, out_shape=out_shape, in_specs=[SMEM] * smem + [VME...  29.7 us
    all_to_all x1, waiting for transfers between devices, per_device(): total = lax.all_to_all(total, ZX, split_axis=0, concat_axis=0, tiled=True)  11.5 us
    all_to_all x1, waiting for transfers between devices, per_device(): lax.all_to_all(outgoing.reshape(N_DP, PAD, 1024), dp, split_axis=0, conca...  10.4 us
    all_to_all x1, waiting for transfers between devices, per_device(): blocks = lax.all_to_all(block, 'y', split_axis=0, concat_axis=0, tiled=True)  9.07 us
    all_to_all x1, starting transfers between devices, per_device(): lax.all_to_all(outgoing.reshape(N_DP, PAD, 1024), dp, split_axis=0, conca...  6.17 us
    all_to_all x1, starting transfers between devices, per_device(): total = lax.all_to_all(total, ZX, split_axis=0, concat_axis=0, tiled=True)  5.76 us
  transfers between devices with their start and end apart: 27, of which 18 were waited for; matrix products, arithmetic and copies ran while one was open for 2% of the time, Pallas kernels for 4%

profile of v8, /device:TPU:2, one launch (start us, length us, event | category | flops | bytes accessed | tf_op | source)
XLA Modules:
  0.0 174.1 jit_solution(1124474769273831210)
XLA Ops:
  7.2 0.0 all-gather.3.cloned.1.call-start
  7.2 0.7 all-gather.3.cloned.1.call-update
  7.9 1.0 pack.1
  8.9 2.0 %collective-permute-start = (bf16[40,640]{1,0:T(8,128)(2,1)S(1)}, bf16[40,640]{1,0:T(8,128)(2,1)S(1)}, u32[]{:S(2)}, u32[]{:S(2)}) collective-permute-start(bf16[40,640]{1,0:T(8,128)(2,1)S(1)} %get-tuple-element.28), channel_id=1, source_target_pairs={{0,1},{1,0},{2,3},{3,2},{4,5},{5,4},{6,7},{7,6},{8,9},{9,8},{10,11... | collective-permute-start | bytes 153608 | tf_op jit(solution)/shard_map/ppermute | solution.py:316
  10.9 0.1 collective-permute-start.4
  11.0 2.2 %collective-permute-done = bf16[40,640]{1,0:T(8,128)(2,1)S(1)} collective-permute-done((bf16[40,640]{1,0:T(8,128)(2,1)S(1)}, bf16[40,640]{1,0:T(8,128)(2,1)S(1)}, u32[]{:S(2)}, u32[]{:S(2)}) %collective-permute-start) | collective-permute-done | bytes 51232 | tf_op jit(solution)/shard_map/ppermute | solution.py:316
  13.3 7.6 %collective-permute-start.2 = (bf16[2,40,640]{2,1,0:T(8,128)(2,1)S(1)}, bf16[2,40,640]{2,1,0:T(8,128)(2,1)S(1)}, u32[]{:S(2)}, u32[]{:S(2)}) collective-permute-start(bf16[2,40,640]{2,1,0:T(8,128)(2,1)S(1)} %get-tuple-element.57), channel_id=1, source_target_pairs={{0,128},{64,192},{128,0},{192,64},{1,129},{65,193},{129,1},{193,65... | collective-permute-start | bytes 307208 | tf_op jit(solution)/shard_map/ppermute | solution.py:316
  20.9 0.0 collective-permute-done.4
  20.9 3.3 %collective-permute-start.6 = (bf16[2,144,512]{2,1,0:T(8,128)(2,1)S(1)}, bf16[2,144,512]{2,1,0:T(8,128)(2,1)S(1)}, u32[]{:S(2)}, u32[]{:S(2)}) collective-permute-start(bf16[2,144,512]{2,1,0:T(8,128)(2,1)S(1)} %get-tuple-element.55), channel_id=1, source_target_pairs={{0,4},{2,6},{4,0},{6,2},{1,5},{3,7},{5,1},{7,3},{8,12},{10,14},{12... | collective-permute-start | bytes 884744 | tf_op jit(solution)/shard_map/ppermute | solution.py:316
  24.2 0.7 collective-permute-start.5
  24.9 2.6 %collective-permute-start.7 = (bf16[2,144,512]{2,1,0:T(8,128)(2,1)S(1)}, bf16[2,144,512]{2,1,0:T(8,128)(2,1)S(1)}, u32[]{:S(2)}, u32[]{:S(2)}) collective-permute-start(bf16[2,144,512]{2,1,0:T(8,128)(2,1)S(1)} %get-tuple-element.55), channel_id=1, source_target_pairs={{0,6},{2,0},{4,2},{6,4},{1,7},{3,1},{5,3},{7,5},{8,14},{10,8},{12,... | collective-permute-start | bytes 884744 | tf_op jit(solution)/shard_map/ppermute | solution.py:316
  27.4 1.5 collective-permute-start.1
  28.9 0.0 collective-permute-done.2
  28.9 2.7 %collective-permute-start.3 = (bf16[2,40,640]{2,1,0:T(8,128)(2,1)S(1)}, bf16[2,40,640]{2,1,0:T(8,128)(2,1)S(1)}, u32[]{:S(2)}, u32[]{:S(2)}) collective-permute-start(bf16[2,40,640]{2,1,0:T(8,128)(2,1)S(1)} %get-tuple-element.57), channel_id=1, source_target_pairs={{0,192},{64,0},{128,64},{192,128},{1,193},{65,1},{129,65},{193,129... | collective-permute-start | bytes 307208 | tf_op jit(solution)/shard_map/ppermute | solution.py:316
  31.6 2.2 %route.1 = bf16[256,1024]{1,0:T(8,128)(2,1)} custom-call(s32[1,128]{1,0:T(1,128)} %bitcast.39, s32[1,128]{1,0:T(1,128)} %bitcast.40, bf16[128,1024]{1,0:T(8,128)(2,1)} %rows_in.1), custom_call_target="tpu_custom_call" | custom-call | flops 75497472 | bytes 1048576 | tf_op jit(solution)/shard_map/route/pallas_call | solution.py:54
  33.8 0.6 collective-permute-done.1
  34.4 1.5 collective-permute-done.3
  35.9 0.1 pad_maximum_fusion.1.refs_0_
  36.0 0.0 copy-start.2
  36.0 1.6 collective-permute-done.6
  37.6 9.6 %collective-permute-done.5 = bf16[2,144,512]{2,1,0:T(8,128)(2,1)S(1)} collective-permute-done((bf16[2,144,512]{2,1,0:T(8,128)(2,1)S(1)}, bf16[2,144,512]{2,1,0:T(8,128)(2,1)S(1)}, u32[]{:S(2)}, u32[]{:S(2)}) %collective-permute-start.5) | collective-permute-done | bytes 294944 | tf_op jit(solution)/shard_map/ppermute | solution.py:316
  47.2 0.0 collective-permute-done.7
  47.2 0.1 pad_maximum_fusion.refs_0_.own
  47.4 0.1 collective-permute-start.8
  47.5 6.2 %all-to-all-start = ((bf16[32,8,1024]{2,1,0:T(8,128)(2,1)}), bf16[32,8,1024]{2,1,0:T(8,128)(2,1)S(1)}, u32[]{:S(2)}, u32[]{:S(2)}) async-start(bf16[32,8,1024]{2,1,0:T(8,128)(2,1)} %bitcast.20), calls=%async_computation | async-start | bytes 1048576 | tf_op jit(solution)/shard_map/all_to_all | solution.py:359
  53.6 0.3 collective-permute-start.11
  53.9 2.7 %collective-permute-start.10 = (bf16[4,2,40,640]{3,2,1,0:T(8,128)(2,1)S(1)}, bf16[4,2,40,640]{3,2,1,0:T(8,128)(2,1)}, u32[]{:S(2)}, u32[]{:S(2)}) collective-permute-start(bf16[4,2,40,640]{3,2,1,0:T(8,128)(2,1)S(1)} %pad_maximum_fusion.1.refs_0_), channel_id=1, source_target_pairs={{0,32},{16,48},{32,0},{48,16},{1,33},{17,49},{33,1},{49,17},{2,34}... | collective-permute-start | bytes 1228808 | tf_op jit(solution)/shard_map/ppermute | solution.py:316
  56.6 1.8 %collective-permute-start.9 = (bf16[4,2,40,640]{3,2,1,0:T(8,128)(2,1)S(1)}, bf16[4,2,40,640]{3,2,1,0:T(8,128)(2,1)}, u32[]{:S(2)}, u32[]{:S(2)}) collective-permute-start(bf16[4,2,40,640]{3,2,1,0:T(8,128)(2,1)S(1)} %pad_maximum_fusion.1.refs_0_), channel_id=1, source_target_pairs={{0,16},{16,32},{32,48},{48,0},{1,17},{17,33},{33,49},{49,1},{2,18}... | collective-permute-start | bytes 1228808 | tf_op jit(solution)/shard_map/ppermute | solution.py:316
  58.4 0.1 pad_add_fusion.place
  58.5 0.6 proj.1.refs_9_
  59.2 1.1 copy-done
  60.2 10.4 %all-to-all-done = bf16[32,8,1024]{2,1,0:T(8,128)(2,1)S(1)} async-done(((bf16[32,8,1024]{2,1,0:T(8,128)(2,1)}), bf16[32,8,1024]{2,1,0:T(8,128)(2,1)S(1)}, u32[]{:S(2)}, u32[]{:S(2)}) %all-to-all-start) | async-done | bytes 524320 | tf_op jit(solution)/shard_map/all_to_all | solution.py:359
  70.6 3.1 %front.1 = (bf16[4,208,512]{2,1,0:T(8,128)(2,1)S(1)}, f32[192,1]{1,0:T(8,128)S(1)}) custom-call(s32[3]{0:T(128)S(1)} %pad_add_fusion.place, bf16[256,1024]{1,0:T(8,128)(2,1)S(1)} %bitcast.26, bf16[4,2,144,512]{3,2,1,0:T(8,128)(2,1)S(1)} %pad_maximum_fusion.refs_0_.own, bf16[4,2,144,512]{3,2,1,0:T(8,128)(2,1)S(1)} %collective-permute-done.8.refs_1_.other), custom_call_target="tpu_custom_call" | custom-call | flops 268435456 | bytes 2097152 | tf_op jit(solution)/shard_map/front/pallas_call | solution.py:54
  73.7 0.9 copy-done.1
  74.6 5.4 %collective-permute-done.10.refs_2_ = bf16[4,2,40,640]{3,2,1,0:T(8,128)(2,1)} collective-permute-done((bf16[4,2,40,640]{3,2,1,0:T(8,128)(2,1)S(1)}, bf16[4,2,40,640]{3,2,1,0:T(8,128)(2,1)}, u32[]{:S(2)}, u32[]{:S(2)}) %collective-permute-start.10) | collective-permute-done | bytes 409632 | tf_op jit(solution)/shard_map/ppermute | solution.py:316
  80.1 3.8 %all-to-all-start.1 = ((bf16[4,208,512]{2,1,0:T(8,128)(2,1)}), bf16[4,208,512]{2,1,0:T(8,128)(2,1)S(1)}, u32[]{:S(2)}, u32[]{:S(2)}) async-start(bf16[4,208,512]{2,1,0:T(8,128)(2,1)} %copy-done.1), calls=%async_computation.1 | async-start | bytes 1703936 | tf_op jit(solution)/shard_map/all_to_all | solution.py:382
  83.8 0.5 collective-permute-start.13
  84.3 0.1 collective-permute-start.14
  84.4 0.4 collective-permute-start.15
  84.9 0.1 stack.77.place
  84.9 0.6 collective-permute-done.12.refs_4_
  85.6 0.8 collective-permute-done.13.refs_5_
  86.4 0.6 collective-permute-done.14.refs_6_
  87.0 0.6 collective-permute-done.15.refs_7_
  87.6 9.1 %all-to-all-done.1.blocks = bf16[4,208,512]{2,1,0:T(8,128)(2,1)S(1)} async-done(((bf16[4,208,512]{2,1,0:T(8,128)(2,1)}), bf16[4,208,512]{2,1,0:T(8,128)(2,1)S(1)}, u32[]{:S(2)}, u32[]{:S(2)}) %all-to-all-start.1) | async-done | bytes 852000 | tf_op jit(solution)/shard_map/all_to_all | solution.py:382
  96.6 20.7 %ffn.1 = (f32[192,1280]{1,0:T(8,128)S(1)}, bf16[192,1280]{1,0:T(8,128)(2,1)S(1)}, bf16[192,1280]{1,0:T(8,128)(2,1)S(1)}, bf16[192,1280]{1,0:T(8,128)(2,1)S(1)}, ...) custom-call(s32[5]{0:T(128)S(1)} %stack.77.place, ...), custom_call_target="tpu_custom_call" | custom-call | flops 8556380160 | bytes 16777216 | tf_op jit(solution)/shard_map/ffn/pallas_call | solution.py:54
  117.4 0.1 collective-permute-start.16
  117.5 3.5 %collective-permute-done.16.arrived = bf16[4,8,40,640]{3,2,1,0:T(8,128)(2,1)S(1)} collective-permute-done((bf16[4,8,40,640]{3,2,1,0:T(8,128)(2,1)S(1)}, bf16[4,8,40,640]{3,2,1,0:T(8,128)(2,1)S(1)}, u32[]{:S(2)}, u32[]{:S(2)}) %collective-permute-start.16) | collective-permute-done | bytes 1638432 | tf_op jit(solution)/shard_map/ppermute | solution.py:316
  121.0 0.4 core_sum.1
  121.4 1.6 collective-permute-start.20
  122.9 3.3 %collective-permute-start.21 = (bf16[8,40,640]{2,1,0:T(8,128)(2,1)S(1)}, bf16[8,40,640]{2,1,0:T(8,128)(2,1)S(1)}, u32[]{:S(2)}, u32[]{:S(2)}) collective-permute-start(bf16[8,40,640]{2,1,0:T(8,128)(2,1)S(1)} %get-tuple-element.52), channel_id=1, source_target_pairs={{0,32},{16,48},{32,0},{48,16},{1,33},{17,49},{33,1},{49,17},{2,34}... | collective-permute-start | bytes 1228808 | tf_op jit(solution)/shard_map/ppermute | solution.py:316
  126.2 1.9 %collective-permute-start.17 = (bf16[192,1280]{1,0:T(8,128)(2,1)S(1)}, bf16[192,1280]{1,0:T(8,128)(2,1)}, u32[]{:S(2)}, u32[]{:S(2)}) collective-permute-start(bf16[192,1280]{1,0:T(8,128)(2,1)S(1)} %get-tuple-element.47), channel_id=1, source_target_pairs={{0,6},{2,0},{4,2},{6,4},{1,7},{3,1},{5,3},{7,5},{8,14},{10,8},{12,... | collective-permute-start | bytes 1474568 | tf_op jit(solution)/shard_map/ppermute | solution.py:316
  128.2 0.7 collective-permute-start.18
  128.9 5.5 %collective-permute-done.20.refs_1_ = bf16[8,40,640]{2,1,0:T(8,128)(2,1)S(1)} collective-permute-done((bf16[8,40,640]{2,1,0:T(8,128)(2,1)S(1)}, bf16[8,40,640]{2,1,0:T(8,128)(2,1)S(1)}, u32[]{:S(2)}, u32[]{:S(2)}) %collective-permute-start.20) | collective-permute-done | bytes 409632 | tf_op jit(solution)/shard_map/ppermute | solution.py:316
  134.4 0.6 collective-permute-start.19
  135.0 1.8 %collective-permute-done.21.refs_2_ = bf16[8,40,640]{2,1,0:T(8,128)(2,1)S(1)} collective-permute-done((bf16[8,40,640]{2,1,0:T(8,128)(2,1)S(1)}, bf16[8,40,640]{2,1,0:T(8,128)(2,1)S(1)}, u32[]{:S(2)}, u32[]{:S(2)}) %collective-permute-start.21) | collective-permute-done | bytes 409632 | tf_op jit(solution)/shard_map/ppermute | solution.py:316
  136.8 7.7 %collective-permute-done.22.refs_3_ = bf16[8,40,640]{2,1,0:T(8,128)(2,1)S(1)} collective-permute-done((bf16[8,40,640]{2,1,0:T(8,128)(2,1)S(1)}, bf16[8,40,640]{2,1,0:T(8,128)(2,1)S(1)}, u32[]{:S(2)}, u32[]{:S(2)}) %collective-permute-start.22) | collective-permute-done | bytes 409632 | tf_op jit(solution)/shard_map/ppermute | solution.py:316
  144.5 0.9 x_sum.1
  145.5 5.8 %all-to-all-start.2 = ((bf16[8,40,640]{2,1,0:T(8,128)(2,1)}), bf16[8,40,640]{2,1,0:T(8,128)(2,1)S(1)}, u32[]{:S(2)}, u32[]{:S(2)}) async-start(bf16[8,40,640]{2,1,0:T(8,128)(2,1)} %x_sum.1), calls=%async_computation.2 | async-start | bytes 819200 | tf_op jit(solution)/shard_map/all_to_all | solution.py:428
  151.2 0.1 convert_reduce_fusion
  151.3 1.4 collective-permute-done.19
  152.7 2.3 %multiply_convert_fusion = bf16[192,1280]{1,0:T(8,128)(2,1)} fusion(bf16[192,1280]{1,0:T(8,128)(2,1)} %collective-permute-done.19, bf16[192,1280]{1,0:T(8,128)(2,1)} %collective-permute-done.18, f32[192,1280]{1,0:T(8,128)S(1)} %get-tuple-element.40, bf16[192,1280]{1,0:T(8,128)(2,1)} %collective-permute-done.17, f32[192]{0:T(256)S(1)} %convert_reduce_fusion), kind=kLoop, calls=%fused_computation.1 | loop fusion | flops 1966080 | bytes 2949888 | tf_op jit(solution)/shard_map/convert_element_type | solution.py:427
  155.1 11.5 %all-to-all-done.2.arrived = bf16[8,40,640]{2,1,0:T(8,128)(2,1)S(1)} async-done(((bf16[8,40,640]{2,1,0:T(8,128)(2,1)}), bf16[8,40,640]{2,1,0:T(8,128)(2,1)S(1)}, u32[]{:S(2)}, u32[]{:S(2)}) %all-to-all-start.2) | async-done | bytes 409632 | tf_op jit(solution)/shard_map/all_to_all | solution.py:428
  166.5 0.8 last.1
  (21 shorter events, 0.1 us)
Async XLA Ops:
  7.2 89.5 %all-gather.3.cloned.1.call-start = ((), (), s32[]{:S(2)}) async-start(), calls=%async_computation.3 | async-start | bytes 2457600 | tf_op jit(solution)/shard_map/all_gather | solution.py:337
  8.9 4.3 %collective-permute-start = (bf16[40,640]{1,0:T(8,128)(2,1)S(1)}, bf16[40,640]{1,0:T(8,128)(2,1)S(1)}, u32[]{:S(2)}, u32[]{:S(2)}) collective-permute-start(bf16[40,640]{1,0:T(8,128)(2,1)S(1)} %get-tuple-element.28), channel_id=1, source_target_pairs={{0,1},{1,0},{2,3},{3,2},{4,5},{5,4},{6,7},{7,6},{8,9},{9,8},{10,11... | collective-permute-start | bytes 153608 | tf_op jit(solution)/shard_map/ppermute | solution.py:316
  10.9 10.0 %collective-permute-start.4 = (bf16[144,512]{1,0:T(8,128)(2,1)S(1)}, bf16[144,512]{1,0:T(8,128)(2,1)S(1)}, u32[]{:S(2)}, u32[]{:S(2)}) collective-permute-start(bf16[144,512]{1,0:T(8,128)(2,1)S(1)} %get-tuple-element.29), channel_id=1, source_target_pairs={{0,1},{1,0},{2,3},{3,2},{4,5},{5,4},{6,7},{7,6},{8,9},{9,8},{10,11... | collective-permute-start | bytes 442376 | tf_op jit(solution)/shard_map/ppermute | solution.py:316
  13.3 15.7 %collective-permute-start.2 = (bf16[2,40,640]{2,1,0:T(8,128)(2,1)S(1)}, bf16[2,40,640]{2,1,0:T(8,128)(2,1)S(1)}, u32[]{:S(2)}, u32[]{:S(2)}) collective-permute-start(bf16[2,40,640]{2,1,0:T(8,128)(2,1)S(1)} %get-tuple-element.57), channel_id=1, source_target_pairs={{0,128},{64,192},{128,0},{192,64},{1,129},{65,193},{129,1},{193,65... | collective-permute-start | bytes 307208 | tf_op jit(solution)/shard_map/ppermute | solution.py:316
  20.9 16.7 %collective-permute-start.6 = (bf16[2,144,512]{2,1,0:T(8,128)(2,1)S(1)}, bf16[2,144,512]{2,1,0:T(8,128)(2,1)S(1)}, u32[]{:S(2)}, u32[]{:S(2)}) collective-permute-start(bf16[2,144,512]{2,1,0:T(8,128)(2,1)S(1)} %get-tuple-element.55), channel_id=1, source_target_pairs={{0,4},{2,6},{4,0},{6,2},{1,5},{3,7},{5,1},{7,3},{8,12},{10,14},{12... | collective-permute-start | bytes 884744 | tf_op jit(solution)/shard_map/ppermute | solution.py:316
  24.2 23.0 %collective-permute-start.5 = (bf16[2,144,512]{2,1,0:T(8,128)(2,1)S(1)}, bf16[2,144,512]{2,1,0:T(8,128)(2,1)S(1)}, u32[]{:S(2)}, u32[]{:S(2)}) collective-permute-start(bf16[2,144,512]{2,1,0:T(8,128)(2,1)S(1)} %get-tuple-element.55), channel_id=1, source_target_pairs={{0,2},{2,4},{4,6},{6,0},{1,3},{3,5},{5,7},{7,1},{8,10},{10,12},{12... | collective-permute-start | bytes 884744 | tf_op jit(solution)/shard_map/ppermute | solution.py:316
  24.9 22.3 %collective-permute-start.7 = (bf16[2,144,512]{2,1,0:T(8,128)(2,1)S(1)}, bf16[2,144,512]{2,1,0:T(8,128)(2,1)S(1)}, u32[]{:S(2)}, u32[]{:S(2)}) collective-permute-start(bf16[2,144,512]{2,1,0:T(8,128)(2,1)S(1)} %get-tuple-element.55), channel_id=1, source_target_pairs={{0,6},{2,0},{4,2},{6,4},{1,7},{3,1},{5,3},{7,5},{8,14},{10,8},{12,... | collective-permute-start | bytes 884744 | tf_op jit(solution)/shard_map/ppermute | solution.py:316
  27.4 6.9 %collective-permute-start.1 = (bf16[2,40,640]{2,1,0:T(8,128)(2,1)S(1)}, bf16[2,40,640]{2,1,0:T(8,128)(2,1)S(1)}, u32[]{:S(2)}, u32[]{:S(2)}) collective-permute-start(bf16[2,40,640]{2,1,0:T(8,128)(2,1)S(1)} %get-tuple-element.57), channel_id=1, source_target_pairs={{0,64},{64,128},{128,192},{192,0},{1,65},{65,129},{129,193},{193,1... | collective-permute-start | bytes 307208 | tf_op jit(solution)/shard_map/ppermute | solution.py:316
  28.9 7.0 %collective-permute-start.3 = (bf16[2,40,640]{2,1,0:T(8,128)(2,1)S(1)}, bf16[2,40,640]{2,1,0:T(8,128)(2,1)S(1)}, u32[]{:S(2)}, u32[]{:S(2)}) collective-permute-start(bf16[2,40,640]{2,1,0:T(8,128)(2,1)S(1)} %get-tuple-element.57), channel_id=1, source_target_pairs={{0,192},{64,0},{128,64},{192,128},{1,193},{65,1},{129,65},{193,129... | collective-permute-start | bytes 307208 | tf_op jit(solution)/shard_map/ppermute | solution.py:316
  36.0 47.9 %copy-start.2 = (bf16[4,2,40,640]{3,2,1,0:T(8,128)(2,1)}, bf16[4,2,40,640]{3,2,1,0:T(8,128)(2,1)S(1)}, u32[]{:S(2)}) copy-start(bf16[4,2,40,640]{3,2,1,0:T(8,128)(2,1)S(1)} %pad_maximum_fusion.1.refs_0_) | copy-start | bytes 1228804
  47.4 11.1 %collective-permute-start.8 = (bf16[4,2,144,512]{3,2,1,0:T(8,128)(2,1)S(1)}, bf16[4,2,144,512]{3,2,1,0:T(8,128)(2,1)S(1)}, u32[]{:S(2)}, u32[]{:S(2)}) collective-permute-start(bf16[4,2,144,512]{3,2,1,0:T(8,128)(2,1)S(1)} %pad_maximum_fusion.refs_0_.own), channel_id=1, source_target_pairs={{0,8},{8,0},{1,9},{9,1},{2,10},{10,2},{3,11},{11,3},{4,12},{12,4},... | collective-permute-start | bytes 3538952 | tf_op jit(solution)/shard_map/ppermute | solution.py:316
  47.5 23.2 %all-to-all-start = ((bf16[32,8,1024]{2,1,0:T(8,128)(2,1)}), bf16[32,8,1024]{2,1,0:T(8,128)(2,1)S(1)}, u32[]{:S(2)}, u32[]{:S(2)}) async-start(bf16[32,8,1024]{2,1,0:T(8,128)(2,1)} %bitcast.20), calls=%async_computation | async-start | bytes 1048576 | tf_op jit(solution)/shard_map/all_to_all | solution.py:359
  53.6 21.0 %collective-permute-start.11 = (bf16[4,2,40,640]{3,2,1,0:T(8,128)(2,1)S(1)}, bf16[4,2,40,640]{3,2,1,0:T(8,128)(2,1)}, u32[]{:S(2)}, u32[]{:S(2)}) collective-permute-start(bf16[4,2,40,640]{3,2,1,0:T(8,128)(2,1)S(1)} %pad_maximum_fusion.1.refs_0_), channel_id=1, source_target_pairs={{0,48},{16,0},{32,16},{48,32},{1,49},{17,1},{33,17},{49,33},{2,50}... | collective-permute-start | bytes 1228808 | tf_op jit(solution)/shard_map/ppermute | solution.py:316
  53.9 26.1 %collective-permute-start.10 = (bf16[4,2,40,640]{3,2,1,0:T(8,128)(2,1)S(1)}, bf16[4,2,40,640]{3,2,1,0:T(8,128)(2,1)}, u32[]{:S(2)}, u32[]{:S(2)}) collective-permute-start(bf16[4,2,40,640]{3,2,1,0:T(8,128)(2,1)S(1)} %pad_maximum_fusion.1.refs_0_), channel_id=1, source_target_pairs={{0,32},{16,48},{32,0},{48,16},{1,33},{17,49},{33,1},{49,17},{2,34}... | collective-permute-start | bytes 1228808 | tf_op jit(solution)/shard_map/ppermute | solution.py:316
  56.6 23.4 %collective-permute-start.9 = (bf16[4,2,40,640]{3,2,1,0:T(8,128)(2,1)S(1)}, bf16[4,2,40,640]{3,2,1,0:T(8,128)(2,1)}, u32[]{:S(2)}, u32[]{:S(2)}) collective-permute-start(bf16[4,2,40,640]{3,2,1,0:T(8,128)(2,1)S(1)} %pad_maximum_fusion.1.refs_0_), channel_id=1, source_target_pairs={{0,16},{16,32},{32,48},{48,0},{1,17},{17,33},{33,49},{49,1},{2,18}... | collective-permute-start | bytes 1228808 | tf_op jit(solution)/shard_map/ppermute | solution.py:316
  59.1 1.1 copy-start
  73.7 0.9 copy-start.1
  80.1 16.5 %all-to-all-start.1 = ((bf16[4,208,512]{2,1,0:T(8,128)(2,1)}), bf16[4,208,512]{2,1,0:T(8,128)(2,1)S(1)}, u32[]{:S(2)}, u32[]{:S(2)}) async-start(bf16[4,208,512]{2,1,0:T(8,128)(2,1)} %copy-done.1), calls=%async_computation.1 | async-start | bytes 1703936 | tf_op jit(solution)/shard_map/all_to_all | solution.py:382
  83.8 1.7 %collective-permute-start.12 = (bf16[4,2,40,640]{3,2,1,0:T(8,128)(2,1)S(1)}, bf16[4,2,40,640]{3,2,1,0:T(8,128)(2,1)S(1)}, u32[]{:S(2)}, u32[]{:S(2)}) collective-permute-start(bf16[4,2,40,640]{3,2,1,0:T(8,128)(2,1)S(1)} %pad_maximum_fusion.1.refs_0_), channel_id=1, source_target_pairs={{0,8},{8,0},{1,9},{9,1},{2,10},{10,2},{3,11},{11,3},{4,12},{12,4},... | collective-permute-start | bytes 1228808 | tf_op jit(solution)/shard_map/ppermute | solution.py:316
  83.8 2.5 %collective-permute-start.13 = (bf16[4,2,40,640]{3,2,1,0:T(8,128)(2,1)}, bf16[4,2,40,640]{3,2,1,0:T(8,128)(2,1)S(1)}, u32[]{:S(2)}, u32[]{:S(2)}) collective-permute-start(bf16[4,2,40,640]{3,2,1,0:T(8,128)(2,1)} %collective-permute-done.9.refs_1_), channel_id=1, source_target_pairs={{0,8},{8,0},{1,9},{9,1},{2,10},{10,2},{3,11},{11,3},{4,12},{12,4},... | collective-permute-start | bytes 1228808 | tf_op jit(solution)/shard_map/ppermute | solution.py:316
  84.3 2.6 %collective-permute-start.14 = (bf16[4,2,40,640]{3,2,1,0:T(8,128)(2,1)}, bf16[4,2,40,640]{3,2,1,0:T(8,128)(2,1)S(1)}, u32[]{:S(2)}, u32[]{:S(2)}) collective-permute-start(bf16[4,2,40,640]{3,2,1,0:T(8,128)(2,1)} %collective-permute-done.10.refs_2_), channel_id=1, source_target_pairs={{0,8},{8,0},{1,9},{9,1},{2,10},{10,2},{3,11},{11,3},{4,12},{12,4},... | collective-permute-start | bytes 1228808 | tf_op jit(solution)/shard_map/ppermute | solution.py:316
  84.4 3.1 %collective-permute-start.15 = (bf16[4,2,40,640]{3,2,1,0:T(8,128)(2,1)}, bf16[4,2,40,640]{3,2,1,0:T(8,128)(2,1)S(1)}, u32[]{:S(2)}, u32[]{:S(2)}) collective-permute-start(bf16[4,2,40,640]{3,2,1,0:T(8,128)(2,1)} %collective-permute-done.11.refs_3_), channel_id=1, source_target_pairs={{0,8},{8,0},{1,9},{9,1},{2,10},{10,2},{3,11},{11,3},{4,12},{12,4},... | collective-permute-start | bytes 1228808 | tf_op jit(solution)/shard_map/ppermute | solution.py:316
  85.6 11.0 %copy-start.3 = (bf16[4,2,40,640]{3,2,1,0:T(8,128)(2,1)}, bf16[4,2,40,640]{3,2,1,0:T(8,128)(2,1)S(1)}, u32[]{:S(2)}) copy-start(bf16[4,2,40,640]{3,2,1,0:T(8,128)(2,1)S(1)} %collective-permute-done.12.refs_4_) | copy-start | bytes 1228804
  86.4 10.3 %copy-start.4 = (bf16[4,2,40,640]{3,2,1,0:T(8,128)(2,1)}, bf16[4,2,40,640]{3,2,1,0:T(8,128)(2,1)S(1)}, u32[]{:S(2)}) copy-start(bf16[4,2,40,640]{3,2,1,0:T(8,128)(2,1)S(1)} %collective-permute-done.13.refs_5_) | copy-start | bytes 1228804
  87.0 9.7 %copy-start.5 = (bf16[4,2,40,640]{3,2,1,0:T(8,128)(2,1)}, bf16[4,2,40,640]{3,2,1,0:T(8,128)(2,1)S(1)}, u32[]{:S(2)}) copy-start(bf16[4,2,40,640]{3,2,1,0:T(8,128)(2,1)S(1)} %collective-permute-done.14.refs_6_) | copy-start | bytes 1228804
  87.5 9.1 %copy-start.6 = (bf16[4,2,40,640]{3,2,1,0:T(8,128)(2,1)}, bf16[4,2,40,640]{3,2,1,0:T(8,128)(2,1)S(1)}, u32[]{:S(2)}) copy-start(bf16[4,2,40,640]{3,2,1,0:T(8,128)(2,1)S(1)} %collective-permute-done.15.refs_7_) | copy-start | bytes 1228804
  117.4 3.6 %collective-permute-start.16 = (bf16[4,8,40,640]{3,2,1,0:T(8,128)(2,1)S(1)}, bf16[4,8,40,640]{3,2,1,0:T(8,128)(2,1)S(1)}, u32[]{:S(2)}, u32[]{:S(2)}) collective-permute-start(bf16[4,8,40,640]{3,2,1,0:T(8,128)(2,1)S(1)} %get-tuple-element.45), channel_id=1, source_target_pairs={{0,8},{8,0},{1,9},{9,1},{2,10},{10,2},{3,11},{11,3},{4,12},{12,4},... | collective-permute-start | bytes 4915208 | tf_op jit(solution)/shard_map/ppermute | solution.py:316
  121.4 13.1 %collective-permute-start.20 = (bf16[8,40,640]{2,1,0:T(8,128)(2,1)S(1)}, bf16[8,40,640]{2,1,0:T(8,128)(2,1)S(1)}, u32[]{:S(2)}, u32[]{:S(2)}) collective-permute-start(bf16[8,40,640]{2,1,0:T(8,128)(2,1)S(1)} %get-tuple-element.51), channel_id=1, source_target_pairs={{0,16},{16,32},{32,48},{48,0},{1,17},{17,33},{33,49},{49,1},{2,18}... | collective-permute-start | bytes 1228808 | tf_op jit(solution)/shard_map/ppermute | solution.py:316
  122.9 13.9 %collective-permute-start.21 = (bf16[8,40,640]{2,1,0:T(8,128)(2,1)S(1)}, bf16[8,40,640]{2,1,0:T(8,128)(2,1)S(1)}, u32[]{:S(2)}, u32[]{:S(2)}) collective-permute-start(bf16[8,40,640]{2,1,0:T(8,128)(2,1)S(1)} %get-tuple-element.52), channel_id=1, source_target_pairs={{0,32},{16,48},{32,0},{48,16},{1,33},{17,49},{33,1},{49,17},{2,34}... | collective-permute-start | bytes 1228808 | tf_op jit(solution)/shard_map/ppermute | solution.py:316
  126.2 18.3 %collective-permute-start.22 = (bf16[8,40,640]{2,1,0:T(8,128)(2,1)S(1)}, bf16[8,40,640]{2,1,0:T(8,128)(2,1)S(1)}, u32[]{:S(2)}, u32[]{:S(2)}) collective-permute-start(bf16[8,40,640]{2,1,0:T(8,128)(2,1)S(1)} %get-tuple-element.53), channel_id=1, source_target_pairs={{0,48},{16,0},{32,16},{48,32},{1,49},{17,1},{33,17},{49,33},{2,50}... | collective-permute-start | bytes 1228808 | tf_op jit(solution)/shard_map/ppermute | solution.py:316
  126.2 25.1 %collective-permute-start.17 = (bf16[192,1280]{1,0:T(8,128)(2,1)S(1)}, bf16[192,1280]{1,0:T(8,128)(2,1)}, u32[]{:S(2)}, u32[]{:S(2)}) collective-permute-start(bf16[192,1280]{1,0:T(8,128)(2,1)S(1)} %get-tuple-element.47), channel_id=1, source_target_pairs={{0,6},{2,0},{4,2},{6,4},{1,7},{3,1},{5,3},{7,5},{8,14},{10,8},{12,... | collective-permute-start | bytes 1474568 | tf_op jit(solution)/shard_map/ppermute | solution.py:316
  128.2 23.2 %collective-permute-start.18 = (bf16[192,1280]{1,0:T(8,128)(2,1)S(1)}, bf16[192,1280]{1,0:T(8,128)(2,1)}, u32[]{:S(2)}, u32[]{:S(2)}) collective-permute-start(bf16[192,1280]{1,0:T(8,128)(2,1)S(1)} %get-tuple-element.48), channel_id=1, source_target_pairs={{0,4},{2,6},{4,0},{6,2},{1,5},{3,7},{5,1},{7,3},{8,12},{10,14},{12... | collective-permute-start | bytes 1474568 | tf_op jit(solution)/shard_map/ppermute | solution.py:316
  134.4 18.3 %collective-permute-start.19 = (bf16[192,1280]{1,0:T(8,128)(2,1)S(1)}, bf16[192,1280]{1,0:T(8,128)(2,1)}, u32[]{:S(2)}, u32[]{:S(2)}) collective-permute-start(bf16[192,1280]{1,0:T(8,128)(2,1)S(1)} %get-tuple-element.49), channel_id=1, source_target_pairs={{0,2},{2,4},{4,6},{6,0},{1,3},{3,5},{5,7},{7,1},{8,10},{10,12},{12... | collective-permute-start | bytes 1474568 | tf_op jit(solution)/shard_map/ppermute | solution.py:316
  145.5 21.1 %all-to-all-start.2 = ((bf16[8,40,640]{2,1,0:T(8,128)(2,1)}), bf16[8,40,640]{2,1,0:T(8,128)(2,1)S(1)}, u32[]{:S(2)}, u32[]{:S(2)}) async-start(bf16[8,40,640]{2,1,0:T(8,128)(2,1)} %x_sum.1), calls=%async_computation.2 | async-start | bytes 819200 | tf_op jit(solution)/shard_map/all_to_all | solution.py:428
Sparse Core Ops, SparseCore 0:
  9.8 42.3 all-gather.2

commit v9 on v8

--- a/solution.py
+++ b/solution.py
@@ -334,7 +334,6 @@
         scratch=[pltpu.VMEM((2, BLOCK, UNITS), bf16), pltpu.SemaphoreType.DMA((6,))],
         smem=1, hbm=3, name="pack",
     )
-    cot_all = lax.all_gather(cotangent, "y", axis=0)
     both = jnp.stack([packed, ring(packed, "zl", 2, 1)])
     wire_pair = jnp.stack([wire, ring(wire, "zl", 2, 1)])
 
@@ -354,6 +353,8 @@
     along_z = jnp.stack(around(both, "zh", 4))
     wire_own = jnp.stack(around(wire_pair, "y", 4))
     outgoing, along_z, wire_own = lax.optimization_barrier((outgoing, along_z, wire_own))
+    cotangent, wire_own = lax.optimization_barrier((cotangent, wire_own))
+    cot_all = lax.all_gather(cotangent, "y", axis=0)
     wires = [wire_own, ring(wire_own, "c", 2, 1)]
     along_x = around(along_z, "x", 4)
     incoming = lax.all_to_all(

time: 175 us -> 166 us (0.949)
  waiting for transfers between devices: 75.2 us -> 63.7 us
  starting transfers between devices: 50.2 us -> 52.4 us
    ppermute x23, waiting for transfers between devices: 43.6 us -> 32.3 us  [ring(): lax.ppermute(values, axis, [(k, (k + step) % size) for k in range(size)])]
    all_to_all x1, starting transfers between devices: 6.17 us -> 8.39 us  [per_device(): lax.all_to_all(outgoing.reshape(N_DP, PAD, 1024), dp, split_axis=0, conca...]
where the time goes in v9:
time: 166 us; the launch traced here: 165 us
  waiting for transfers between devices  63.7 us (38%)
  starting transfers between devices  52.4 us (32%)
  Pallas kernels  29.7 us (18%)
  between operations  14.2 us (9%)
  other arithmetic  2.8 us (2%)
  local copies, waits for them, and re-layouts  2.07 us (1%)
    ppermute x23, starting transfers between devices, ring(): lax.ppermute(values, axis, [(k, (k + step) % size) for k in range(size)])  34.6 us
    ppermute x23, waiting for transfers between devices, ring(): lax.ppermute(values, axis, [(k, (k + step) % size) for k in range(size)])  32.3 us
    pallas_call x8, Pallas kernels, call(): pl.pallas_call(kernel, out_shape=out_shape, in_specs=[SMEM] * smem + [VME...  29.7 us
    all_to_all x1, waiting for transfers between devices, per_device(): total = lax.all_to_all(total, ZX, split_axis=0, concat_axis=0, tiled=True)  12.4 us
    all_to_all x1, waiting for transfers between devices, per_device(): lax.all_to_all(outgoing.reshape(N_DP, PAD, 1024), dp, split_axis=0, conca...  9.91 us
    all_to_all x1, waiting for transfers between devices, per_device(): blocks = lax.all_to_all(block, 'y', split_axis=0, concat_axis=0, tiled=True)  9.09 us
    all_to_all x1, starting transfers between devices, per_device(): lax.all_to_all(outgoing.reshape(N_DP, PAD, 1024), dp, split_axis=0, conca...  8.39 us
    all_to_all x1, starting transfers between devices, per_device(): total = lax.all_to_all(total, ZX, split_axis=0, concat_axis=0, tiled=True)  5.89 us
  transfers between devices with their start and end apart: 27, of which 18 were waited for; matrix products, arithmetic and copies ran while one was open for 2% of the time, Pallas kernels for 4%

profile of v9, /device:TPU:2, one launch (start us, length us, event | category | flops | bytes accessed | tf_op | source)
XLA Modules:
  0.0 165.0 jit_solution(11183032199599581050)
XLA Ops:
  7.2 0.0 all-gather.3.cloned.1.call-start
  7.2 1.0 pack.1
  8.2 2.0 %collective-permute-start = (bf16[40,640]{1,0:T(8,128)(2,1)S(1)}, bf16[40,640]{1,0:T(8,128)(2,1)S(1)}, u32[]{:S(2)}, u32[]{:S(2)}) collective-permute-start(bf16[40,640]{1,0:T(8,128)(2,1)S(1)} %get-tuple-element.30), channel_id=1, source_target_pairs={{0,1},{1,0},{2,3},{3,2},{4,5},{5,4},{6,7},{7,6},{8,9},{9,8},{10,11... | collective-permute-start | bytes 153608 | tf_op jit(solution)/shard_map/ppermute | solution.py:316
  10.2 0.1 collective-permute-start.4
  10.3 2.2 %collective-permute-done = bf16[40,640]{1,0:T(8,128)(2,1)S(1)} collective-permute-done((bf16[40,640]{1,0:T(8,128)(2,1)S(1)}, bf16[40,640]{1,0:T(8,128)(2,1)S(1)}, u32[]{:S(2)}, u32[]{:S(2)}) %collective-permute-start) | collective-permute-done | bytes 51232 | tf_op jit(solution)/shard_map/ppermute | solution.py:316
  12.6 7.6 %collective-permute-start.2 = (bf16[2,40,640]{2,1,0:T(8,128)(2,1)S(1)}, bf16[2,40,640]{2,1,0:T(8,128)(2,1)S(1)}, u32[]{:S(2)}, u32[]{:S(2)}) collective-permute-start(bf16[2,40,640]{2,1,0:T(8,128)(2,1)S(1)} %get-tuple-element.61), channel_id=1, source_target_pairs={{0,128},{64,192},{128,0},{192,64},{1,129},{65,193},{129,1},{193,65... | collective-permute-start | bytes 307208 | tf_op jit(solution)/shard_map/ppermute | solution.py:316
  20.2 0.0 collective-permute-done.4
  20.2 3.3 %collective-permute-start.6 = (bf16[2,144,512]{2,1,0:T(8,128)(2,1)S(1)}, bf16[2,144,512]{2,1,0:T(8,128)(2,1)S(1)}, u32[]{:S(2)}, u32[]{:S(2)}) collective-permute-start(bf16[2,144,512]{2,1,0:T(8,128)(2,1)S(1)} %get-tuple-element.59), channel_id=1, source_target_pairs={{0,4},{2,6},{4,0},{6,2},{1,5},{3,7},{5,1},{7,3},{8,12},{10,14},{12... | collective-permute-start | bytes 884744 | tf_op jit(solution)/shard_map/ppermute | solution.py:316
  23.5 0.7 collective-permute-start.5
  24.2 2.6 %collective-permute-start.7 = (bf16[2,144,512]{2,1,0:T(8,128)(2,1)S(1)}, bf16[2,144,512]{2,1,0:T(8,128)(2,1)S(1)}, u32[]{:S(2)}, u32[]{:S(2)}) collective-permute-start(bf16[2,144,512]{2,1,0:T(8,128)(2,1)S(1)} %get-tuple-element.59), channel_id=1, source_target_pairs={{0,6},{2,0},{4,2},{6,4},{1,7},{3,1},{5,3},{7,5},{8,14},{10,8},{12,... | collective-permute-start | bytes 884744 | tf_op jit(solution)/shard_map/ppermute | solution.py:316
  26.8 1.5 collective-permute-start.1
  28.2 0.0 collective-permute-done.2
  28.2 2.7 %collective-permute-start.3 = (bf16[2,40,640]{2,1,0:T(8,128)(2,1)S(1)}, bf16[2,40,640]{2,1,0:T(8,128)(2,1)S(1)}, u32[]{:S(2)}, u32[]{:S(2)}) collective-permute-start(bf16[2,40,640]{2,1,0:T(8,128)(2,1)S(1)} %get-tuple-element.61), channel_id=1, source_target_pairs={{0,192},{64,0},{128,64},{192,128},{1,193},{65,1},{129,65},{193,129... | collective-permute-start | bytes 307208 | tf_op jit(solution)/shard_map/ppermute | solution.py:316
  30.9 2.2 %route.1 = bf16[256,1024]{1,0:T(8,128)(2,1)} custom-call(s32[1,128]{1,0:T(1,128)} %bitcast.39, s32[1,128]{1,0:T(1,128)} %bitcast.40, bf16[128,1024]{1,0:T(8,128)(2,1)} %rows_in.1), custom_call_target="tpu_custom_call" | custom-call | flops 75497472 | bytes 1048576 | tf_op jit(solution)/shard_map/route/pallas_call | solution.py:54
  33.1 0.6 collective-permute-done.1
  33.7 1.5 collective-permute-done.3
  35.2 0.1 pad_maximum_fusion.1.refs_0_
  35.3 0.0 copy-start.2
  35.3 0.1 collective-permute-done.7
  35.4 0.1 pad_maximum_fusion.refs_0_.own
  35.5 0.0 all-gather.3.cloned.1.call-update
  35.5 0.1 collective-permute-start.8
  35.6 8.4 %all-to-all-start = ((bf16[32,8,1024]{2,1,0:T(8,128)(2,1)}), bf16[32,8,1024]{2,1,0:T(8,128)(2,1)S(1)}, u32[]{:S(2)}, u32[]{:S(2)}) async-start(bf16[32,8,1024]{2,1,0:T(8,128)(2,1)} %bitcast.20), calls=%async_computation | async-start | bytes 1048576 | tf_op jit(solution)/shard_map/all_to_all | solution.py:360
  44.0 0.3 collective-permute-start.11
  44.3 2.7 %collective-permute-start.10 = (bf16[4,2,40,640]{3,2,1,0:T(8,128)(2,1)S(1)}, bf16[4,2,40,640]{3,2,1,0:T(8,128)(2,1)}, u32[]{:S(2)}, u32[]{:S(2)}) collective-permute-start(bf16[4,2,40,640]{3,2,1,0:T(8,128)(2,1)S(1)} %pad_maximum_fusion.1.refs_0_), channel_id=1, source_target_pairs={{0,32},{16,48},{32,0},{48,16},{1,33},{17,49},{33,1},{49,17},{2,34}... | collective-permute-start | bytes 1228808 | tf_op jit(solution)/shard_map/ppermute | solution.py:316
  47.0 1.8 %collective-permute-start.9 = (bf16[4,2,40,640]{3,2,1,0:T(8,128)(2,1)S(1)}, bf16[4,2,40,640]{3,2,1,0:T(8,128)(2,1)}, u32[]{:S(2)}, u32[]{:S(2)}) collective-permute-start(bf16[4,2,40,640]{3,2,1,0:T(8,128)(2,1)S(1)} %pad_maximum_fusion.1.refs_0_), channel_id=1, source_target_pairs={{0,16},{16,32},{32,48},{48,0},{1,17},{17,33},{33,49},{49,1},{2,18}... | collective-permute-start | bytes 1228808 | tf_op jit(solution)/shard_map/ppermute | solution.py:316
  48.8 0.1 pad_add_fusion.place
  48.9 0.6 proj.1.refs_9_
  49.5 1.1 copy-done
  50.6 9.9 %all-to-all-done = bf16[32,8,1024]{2,1,0:T(8,128)(2,1)S(1)} async-done(((bf16[32,8,1024]{2,1,0:T(8,128)(2,1)}), bf16[32,8,1024]{2,1,0:T(8,128)(2,1)S(1)}, u32[]{:S(2)}, u32[]{:S(2)}) %all-to-all-start) | async-done | bytes 524320 | tf_op jit(solution)/shard_map/all_to_all | solution.py:360
  60.5 3.1 %front.1 = (bf16[4,208,512]{2,1,0:T(8,128)(2,1)S(1)}, f32[192,1]{1,0:T(8,128)S(1)}) custom-call(s32[3]{0:T(128)S(1)} %pad_add_fusion.place, bf16[256,1024]{1,0:T(8,128)(2,1)S(1)} %bitcast.26, bf16[4,2,144,512]{3,2,1,0:T(8,128)(2,1)S(1)} %pad_maximum_fusion.refs_0_.own, bf16[4,2,144,512]{3,2,1,0:T(8,128)(2,1)S(1)} %collective-permute-done.8.refs_1_.other), custom_call_target="tpu_custom_call" | custom-call | flops 268435456 | bytes 2097152 | tf_op jit(solution)/shard_map/front/pallas_call | solution.py:54
  63.6 0.9 copy-done.1
  64.5 6.0 %collective-permute-done.10.refs_2_ = bf16[4,2,40,640]{3,2,1,0:T(8,128)(2,1)} collective-permute-done((bf16[4,2,40,640]{3,2,1,0:T(8,128)(2,1)S(1)}, bf16[4,2,40,640]{3,2,1,0:T(8,128)(2,1)}, u32[]{:S(2)}, u32[]{:S(2)}) %collective-permute-start.10) | collective-permute-done | bytes 409632 | tf_op jit(solution)/shard_map/ppermute | solution.py:316
  70.5 0.3 collective-permute-done.9.refs_1_
  70.8 3.5 %all-to-all-start.1 = ((bf16[4,208,512]{2,1,0:T(8,128)(2,1)}), bf16[4,208,512]{2,1,0:T(8,128)(2,1)S(1)}, u32[]{:S(2)}, u32[]{:S(2)}) async-start(bf16[4,208,512]{2,1,0:T(8,128)(2,1)} %copy-done.1), calls=%async_computation.1 | async-start | bytes 1703936 | tf_op jit(solution)/shard_map/all_to_all | solution.py:383
  74.3 0.1 collective-permute-start.12
  74.4 0.5 collective-permute-start.13
  74.9 0.1 collective-permute-start.14
  75.0 0.4 collective-permute-start.15
  75.4 0.1 stack.77.place
  75.5 0.6 collective-permute-done.12.refs_4_
  76.1 0.8 collective-permute-done.13.refs_5_
  76.9 0.6 collective-permute-done.14.refs_6_
  77.5 0.6 collective-permute-done.15.refs_7_
  78.1 9.1 %all-to-all-done.1.blocks = bf16[4,208,512]{2,1,0:T(8,128)(2,1)S(1)} async-done(((bf16[4,208,512]{2,1,0:T(8,128)(2,1)}), bf16[4,208,512]{2,1,0:T(8,128)(2,1)S(1)}, u32[]{:S(2)}, u32[]{:S(2)}) %all-to-all-start.1) | async-done | bytes 852000 | tf_op jit(solution)/shard_map/all_to_all | solution.py:383
  87.2 20.7 %ffn.1 = (f32[192,1280]{1,0:T(8,128)S(1)}, bf16[192,1280]{1,0:T(8,128)(2,1)S(1)}, bf16[192,1280]{1,0:T(8,128)(2,1)S(1)}, bf16[192,1280]{1,0:T(8,128)(2,1)S(1)}, ...) custom-call(s32[5]{0:T(128)S(1)} %stack.77.place, ...), custom_call_target="tpu_custom_call" | custom-call | flops 8556380160 | bytes 16777216 | tf_op jit(solution)/shard_map/ffn/pallas_call | solution.py:54
  108.0 0.1 collective-permute-start.16
  108.1 3.5 %collective-permute-done.16.arrived = bf16[4,8,40,640]{3,2,1,0:T(8,128)(2,1)S(1)} collective-permute-done((bf16[4,8,40,640]{3,2,1,0:T(8,128)(2,1)S(1)}, bf16[4,8,40,640]{3,2,1,0:T(8,128)(2,1)S(1)}, u32[]{:S(2)}, u32[]{:S(2)}) %collective-permute-start.16) | collective-permute-done | bytes 1638432 | tf_op jit(solution)/shard_map/ppermute | solution.py:316
  111.5 0.4 core_sum.1
  111.9 1.8 %collective-permute-start.20 = (bf16[8,40,640]{2,1,0:T(8,128)(2,1)S(1)}, bf16[8,40,640]{2,1,0:T(8,128)(2,1)S(1)}, u32[]{:S(2)}, u32[]{:S(2)}) collective-permute-start(bf16[8,40,640]{2,1,0:T(8,128)(2,1)S(1)} %get-tuple-element.55), channel_id=1, source_target_pairs={{0,16},{16,32},{32,48},{48,0},{1,17},{17,33},{33,49},{49,1},{2,18}... | collective-permute-start | bytes 1228808 | tf_op jit(solution)/shard_map/ppermute | solution.py:316
  113.7 3.2 %collective-permute-start.21 = (bf16[8,40,640]{2,1,0:T(8,128)(2,1)S(1)}, bf16[8,40,640]{2,1,0:T(8,128)(2,1)S(1)}, u32[]{:S(2)}, u32[]{:S(2)}) collective-permute-start(bf16[8,40,640]{2,1,0:T(8,128)(2,1)S(1)} %get-tuple-element.56), channel_id=1, source_target_pairs={{0,32},{16,48},{32,0},{48,16},{1,33},{17,49},{33,1},{49,17},{2,34}... | collective-permute-start | bytes 1228808 | tf_op jit(solution)/shard_map/ppermute | solution.py:316
  116.9 1.2 collective-permute-start.17
  118.0 1.5 collective-permute-start.18
  119.5 5.5 %collective-permute-done.20.refs_1_ = bf16[8,40,640]{2,1,0:T(8,128)(2,1)S(1)} collective-permute-done((bf16[8,40,640]{2,1,0:T(8,128)(2,1)S(1)}, bf16[8,40,640]{2,1,0:T(8,128)(2,1)S(1)}, u32[]{:S(2)}, u32[]{:S(2)}) %collective-permute-start.20) | collective-permute-done | bytes 409632 | tf_op jit(solution)/shard_map/ppermute | solution.py:316
  125.1 0.6 collective-permute-start.19
  125.6 1.9 %collective-permute-done.21.refs_2_ = bf16[8,40,640]{2,1,0:T(8,128)(2,1)S(1)} collective-permute-done((bf16[8,40,640]{2,1,0:T(8,128)(2,1)S(1)}, bf16[8,40,640]{2,1,0:T(8,128)(2,1)S(1)}, u32[]{:S(2)}, u32[]{:S(2)}) %collective-permute-start.21) | collective-permute-done | bytes 409632 | tf_op jit(solution)/shard_map/ppermute | solution.py:316
  127.6 7.6 %collective-permute-done.22.refs_3_ = bf16[8,40,640]{2,1,0:T(8,128)(2,1)S(1)} collective-permute-done((bf16[8,40,640]{2,1,0:T(8,128)(2,1)S(1)}, bf16[8,40,640]{2,1,0:T(8,128)(2,1)S(1)}, u32[]{:S(2)}, u32[]{:S(2)}) %collective-permute-start.22) | collective-permute-done | bytes 409632 | tf_op jit(solution)/shard_map/ppermute | solution.py:316
  135.2 0.9 x_sum.1
  136.1 5.9 %all-to-all-start.2 = ((bf16[8,40,640]{2,1,0:T(8,128)(2,1)}), bf16[8,40,640]{2,1,0:T(8,128)(2,1)S(1)}, u32[]{:S(2)}, u32[]{:S(2)}) async-start(bf16[8,40,640]{2,1,0:T(8,128)(2,1)} %x_sum.1), calls=%async_computation.2 | async-start | bytes 819200 | tf_op jit(solution)/shard_map/all_to_all | solution.py:429
  142.0 0.1 convert_reduce_fusion
  142.2 0.5 collective-permute-done.19
  142.6 2.3 %multiply_convert_fusion = bf16[192,1280]{1,0:T(8,128)(2,1)} fusion(bf16[192,1280]{1,0:T(8,128)(2,1)} %collective-permute-done.19, bf16[192,1280]{1,0:T(8,128)(2,1)} %collective-permute-done.18, f32[192,1280]{1,0:T(8,128)S(1)} %get-tuple-element.44, bf16[192,1280]{1,0:T(8,128)(2,1)} %collective-permute-done.17, f32[192]{0:T(256)S(1)} %convert_reduce_fusion), kind=kLoop, calls=%fused_computation.1 | loop fusion | flops 1966080 | bytes 2949888 | tf_op jit(solution)/shard_map/convert_element_type | solution.py:428
  145.0 12.4 %all-to-all-done.2.arrived = bf16[8,40,640]{2,1,0:T(8,128)(2,1)S(1)} async-done(((bf16[8,40,640]{2,1,0:T(8,128)(2,1)}), bf16[8,40,640]{2,1,0:T(8,128)(2,1)S(1)}, u32[]{:S(2)}, u32[]{:S(2)}) %all-to-all-start.2) | async-done | bytes 409632 | tf_op jit(solution)/shard_map/all_to_all | solution.py:429
  157.4 0.8 last.1
  (21 shorter events, 0.1 us)
Async XLA Ops:
  7.2 80.0 %all-gather.3.cloned.1.call-start = ((), (), s32[]{:S(2)}) async-start(), calls=%async_computation.3 | async-start | bytes 2457600 | tf_op jit(solution)/shard_map/all_gather | solution.py:357
  8.2 4.3 %collective-permute-start = (bf16[40,640]{1,0:T(8,128)(2,1)S(1)}, bf16[40,640]{1,0:T(8,128)(2,1)S(1)}, u32[]{:S(2)}, u32[]{:S(2)}) collective-permute-start(bf16[40,640]{1,0:T(8,128)(2,1)S(1)} %get-tuple-element.30), channel_id=1, source_target_pairs={{0,1},{1,0},{2,3},{3,2},{4,5},{5,4},{6,7},{7,6},{8,9},{9,8},{10,11... | collective-permute-start | bytes 153608 | tf_op jit(solution)/shard_map/ppermute | solution.py:316
  10.2 10.0 %collective-permute-start.4 = (bf16[144,512]{1,0:T(8,128)(2,1)S(1)}, bf16[144,512]{1,0:T(8,128)(2,1)S(1)}, u32[]{:S(2)}, u32[]{:S(2)}) collective-permute-start(bf16[144,512]{1,0:T(8,128)(2,1)S(1)} %get-tuple-element.31), channel_id=1, source_target_pairs={{0,1},{1,0},{2,3},{3,2},{4,5},{5,4},{6,7},{7,6},{8,9},{9,8},{10,11... | collective-permute-start | bytes 442376 | tf_op jit(solution)/shard_map/ppermute | solution.py:316
  12.6 15.7 %collective-permute-start.2 = (bf16[2,40,640]{2,1,0:T(8,128)(2,1)S(1)}, bf16[2,40,640]{2,1,0:T(8,128)(2,1)S(1)}, u32[]{:S(2)}, u32[]{:S(2)}) collective-permute-start(bf16[2,40,640]{2,1,0:T(8,128)(2,1)S(1)} %get-tuple-element.61), channel_id=1, source_target_pairs={{0,128},{64,192},{128,0},{192,64},{1,129},{65,193},{129,1},{193,65... | collective-permute-start | bytes 307208 | tf_op jit(solution)/shard_map/ppermute | solution.py:316
  20.2 15.0 %collective-permute-start.6 = (bf16[2,144,512]{2,1,0:T(8,128)(2,1)S(1)}, bf16[2,144,512]{2,1,0:T(8,128)(2,1)S(1)}, u32[]{:S(2)}, u32[]{:S(2)}) collective-permute-start(bf16[2,144,512]{2,1,0:T(8,128)(2,1)S(1)} %get-tuple-element.59), channel_id=1, source_target_pairs={{0,4},{2,6},{4,0},{6,2},{1,5},{3,7},{5,1},{7,3},{8,12},{10,14},{12... | collective-permute-start | bytes 884744 | tf_op jit(solution)/shard_map/ppermute | solution.py:316
  23.5 11.8 %collective-permute-start.5 = (bf16[2,144,512]{2,1,0:T(8,128)(2,1)S(1)}, bf16[2,144,512]{2,1,0:T(8,128)(2,1)S(1)}, u32[]{:S(2)}, u32[]{:S(2)}) collective-permute-start(bf16[2,144,512]{2,1,0:T(8,128)(2,1)S(1)} %get-tuple-element.59), channel_id=1, source_target_pairs={{0,2},{2,4},{4,6},{6,0},{1,3},{3,5},{5,7},{7,1},{8,10},{10,12},{12... | collective-permute-start | bytes 884744 | tf_op jit(solution)/shard_map/ppermute | solution.py:316
  24.2 11.2 %collective-permute-start.7 = (bf16[2,144,512]{2,1,0:T(8,128)(2,1)S(1)}, bf16[2,144,512]{2,1,0:T(8,128)(2,1)S(1)}, u32[]{:S(2)}, u32[]{:S(2)}) collective-permute-start(bf16[2,144,512]{2,1,0:T(8,128)(2,1)S(1)} %get-tuple-element.59), channel_id=1, source_target_pairs={{0,6},{2,0},{4,2},{6,4},{1,7},{3,1},{5,3},{7,5},{8,14},{10,8},{12,... | collective-permute-start | bytes 884744 | tf_op jit(solution)/shard_map/ppermute | solution.py:316
  26.8 6.9 %collective-permute-start.1 = (bf16[2,40,640]{2,1,0:T(8,128)(2,1)S(1)}, bf16[2,40,640]{2,1,0:T(8,128)(2,1)S(1)}, u32[]{:S(2)}, u32[]{:S(2)}) collective-permute-start(bf16[2,40,640]{2,1,0:T(8,128)(2,1)S(1)} %get-tuple-element.61), channel_id=1, source_target_pairs={{0,64},{64,128},{128,192},{192,0},{1,65},{65,129},{129,193},{193,1... | collective-permute-start | bytes 307208 | tf_op jit(solution)/shard_map/ppermute | solution.py:316
  28.2 7.0 %collective-permute-start.3 = (bf16[2,40,640]{2,1,0:T(8,128)(2,1)S(1)}, bf16[2,40,640]{2,1,0:T(8,128)(2,1)S(1)}, u32[]{:S(2)}, u32[]{:S(2)}) collective-permute-start(bf16[2,40,640]{2,1,0:T(8,128)(2,1)S(1)} %get-tuple-element.61), channel_id=1, source_target_pairs={{0,192},{64,0},{128,64},{192,128},{1,193},{65,1},{129,65},{193,129... | collective-permute-start | bytes 307208 | tf_op jit(solution)/shard_map/ppermute | solution.py:316
  35.3 39.0 %copy-start.2 = (bf16[4,2,40,640]{3,2,1,0:T(8,128)(2,1)}, bf16[4,2,40,640]{3,2,1,0:T(8,128)(2,1)S(1)}, u32[]{:S(2)}) copy-start(bf16[4,2,40,640]{3,2,1,0:T(8,128)(2,1)S(1)} %pad_maximum_fusion.1.refs_0_) | copy-start | bytes 1228804
  35.5 13.4 %collective-permute-start.8 = (bf16[4,2,144,512]{3,2,1,0:T(8,128)(2,1)S(1)}, bf16[4,2,144,512]{3,2,1,0:T(8,128)(2,1)S(1)}, u32[]{:S(2)}, u32[]{:S(2)}) collective-permute-start(bf16[4,2,144,512]{3,2,1,0:T(8,128)(2,1)S(1)} %pad_maximum_fusion.refs_0_.own), channel_id=1, source_target_pairs={{0,8},{8,0},{1,9},{9,1},{2,10},{10,2},{3,11},{11,3},{4,12},{12,4},... | collective-permute-start | bytes 3538952 | tf_op jit(solution)/shard_map/ppermute | solution.py:316
  35.6 24.9 %all-to-all-start = ((bf16[32,8,1024]{2,1,0:T(8,128)(2,1)}), bf16[32,8,1024]{2,1,0:T(8,128)(2,1)S(1)}, u32[]{:S(2)}, u32[]{:S(2)}) async-start(bf16[32,8,1024]{2,1,0:T(8,128)(2,1)} %bitcast.20), calls=%async_computation | async-start | bytes 1048576 | tf_op jit(solution)/shard_map/all_to_all | solution.py:360
  44.0 20.5 %collective-permute-start.11 = (bf16[4,2,40,640]{3,2,1,0:T(8,128)(2,1)S(1)}, bf16[4,2,40,640]{3,2,1,0:T(8,128)(2,1)}, u32[]{:S(2)}, u32[]{:S(2)}) collective-permute-start(bf16[4,2,40,640]{3,2,1,0:T(8,128)(2,1)S(1)} %pad_maximum_fusion.1.refs_0_), channel_id=1, source_target_pairs={{0,48},{16,0},{32,16},{48,32},{1,49},{17,1},{33,17},{49,33},{2,50}... | collective-permute-start | bytes 1228808 | tf_op jit(solution)/shard_map/ppermute | solution.py:316
  44.3 26.1 %collective-permute-start.10 = (bf16[4,2,40,640]{3,2,1,0:T(8,128)(2,1)S(1)}, bf16[4,2,40,640]{3,2,1,0:T(8,128)(2,1)}, u32[]{:S(2)}, u32[]{:S(2)}) collective-permute-start(bf16[4,2,40,640]{3,2,1,0:T(8,128)(2,1)S(1)} %pad_maximum_fusion.1.refs_0_), channel_id=1, source_target_pairs={{0,32},{16,48},{32,0},{48,16},{1,33},{17,49},{33,1},{49,17},{2,34}... | collective-permute-start | bytes 1228808 | tf_op jit(solution)/shard_map/ppermute | solution.py:316
  47.0 23.8 %collective-permute-start.9 = (bf16[4,2,40,640]{3,2,1,0:T(8,128)(2,1)S(1)}, bf16[4,2,40,640]{3,2,1,0:T(8,128)(2,1)}, u32[]{:S(2)}, u32[]{:S(2)}) collective-permute-start(bf16[4,2,40,640]{3,2,1,0:T(8,128)(2,1)S(1)} %pad_maximum_fusion.1.refs_0_), channel_id=1, source_target_pairs={{0,16},{16,32},{32,48},{48,0},{1,17},{17,33},{33,49},{49,1},{2,18}... | collective-permute-start | bytes 1228808 | tf_op jit(solution)/shard_map/ppermute | solution.py:316
  49.5 1.1 copy-start
  63.6 0.9 copy-start.1
  70.8 16.4 %all-to-all-start.1 = ((bf16[4,208,512]{2,1,0:T(8,128)(2,1)}), bf16[4,208,512]{2,1,0:T(8,128)(2,1)S(1)}, u32[]{:S(2)}, u32[]{:S(2)}) async-start(bf16[4,208,512]{2,1,0:T(8,128)(2,1)} %copy-done.1), calls=%async_computation.1 | async-start | bytes 1703936 | tf_op jit(solution)/shard_map/all_to_all | solution.py:383
  74.3 1.8 %collective-permute-start.12 = (bf16[4,2,40,640]{3,2,1,0:T(8,128)(2,1)S(1)}, bf16[4,2,40,640]{3,2,1,0:T(8,128)(2,1)S(1)}, u32[]{:S(2)}, u32[]{:S(2)}) collective-permute-start(bf16[4,2,40,640]{3,2,1,0:T(8,128)(2,1)S(1)} %pad_maximum_fusion.1.refs_0_), channel_id=1, source_target_pairs={{0,8},{8,0},{1,9},{9,1},{2,10},{10,2},{3,11},{11,3},{4,12},{12,4},... | collective-permute-start | bytes 1228808 | tf_op jit(solution)/shard_map/ppermute | solution.py:316
  74.4 2.5 %collective-permute-start.13 = (bf16[4,2,40,640]{3,2,1,0:T(8,128)(2,1)}, bf16[4,2,40,640]{3,2,1,0:T(8,128)(2,1)S(1)}, u32[]{:S(2)}, u32[]{:S(2)}) collective-permute-start(bf16[4,2,40,640]{3,2,1,0:T(8,128)(2,1)} %collective-permute-done.9.refs_1_), channel_id=1, source_target_pairs={{0,8},{8,0},{1,9},{9,1},{2,10},{10,2},{3,11},{11,3},{4,12},{12,4},... | collective-permute-start | bytes 1228808 | tf_op jit(solution)/shard_map/ppermute | solution.py:316
  74.9 2.6 %collective-permute-start.14 = (bf16[4,2,40,640]{3,2,1,0:T(8,128)(2,1)}, bf16[4,2,40,640]{3,2,1,0:T(8,128)(2,1)S(1)}, u32[]{:S(2)}, u32[]{:S(2)}) collective-permute-start(bf16[4,2,40,640]{3,2,1,0:T(8,128)(2,1)} %collective-permute-done.10.refs_2_), channel_id=1, source_target_pairs={{0,8},{8,0},{1,9},{9,1},{2,10},{10,2},{3,11},{11,3},{4,12},{12,4},... | collective-permute-start | bytes 1228808 | tf_op jit(solution)/shard_map/ppermute | solution.py:316
  75.0 3.1 %collective-permute-start.15 = (bf16[4,2,40,640]{3,2,1,0:T(8,128)(2,1)}, bf16[4,2,40,640]{3,2,1,0:T(8,128)(2,1)S(1)}, u32[]{:S(2)}, u32[]{:S(2)}) collective-permute-start(bf16[4,2,40,640]{3,2,1,0:T(8,128)(2,1)} %collective-permute-done.11.refs_3_), channel_id=1, source_target_pairs={{0,8},{8,0},{1,9},{9,1},{2,10},{10,2},{3,11},{11,3},{4,12},{12,4},... | collective-permute-start | bytes 1228808 | tf_op jit(solution)/shard_map/ppermute | solution.py:316
  76.1 11.1 %copy-start.3 = (bf16[4,2,40,640]{3,2,1,0:T(8,128)(2,1)}, bf16[4,2,40,640]{3,2,1,0:T(8,128)(2,1)S(1)}, u32[]{:S(2)}) copy-start(bf16[4,2,40,640]{3,2,1,0:T(8,128)(2,1)S(1)} %collective-permute-done.12.refs_4_) | copy-start | bytes 1228804
  76.9 10.3 %copy-start.4 = (bf16[4,2,40,640]{3,2,1,0:T(8,128)(2,1)}, bf16[4,2,40,640]{3,2,1,0:T(8,128)(2,1)S(1)}, u32[]{:S(2)}) copy-start(bf16[4,2,40,640]{3,2,1,0:T(8,128)(2,1)S(1)} %collective-permute-done.13.refs_5_) | copy-start | bytes 1228804
  77.5 9.7 %copy-start.5 = (bf16[4,2,40,640]{3,2,1,0:T(8,128)(2,1)}, bf16[4,2,40,640]{3,2,1,0:T(8,128)(2,1)S(1)}, u32[]{:S(2)}) copy-start(bf16[4,2,40,640]{3,2,1,0:T(8,128)(2,1)S(1)} %collective-permute-done.14.refs_6_) | copy-start | bytes 1228804
  78.1 9.1 %copy-start.6 = (bf16[4,2,40,640]{3,2,1,0:T(8,128)(2,1)}, bf16[4,2,40,640]{3,2,1,0:T(8,128)(2,1)S(1)}, u32[]{:S(2)}) copy-start(bf16[4,2,40,640]{3,2,1,0:T(8,128)(2,1)S(1)} %collective-permute-done.15.refs_7_) | copy-start | bytes 1228804
  108.0 3.6 %collective-permute-start.16 = (bf16[4,8,40,640]{3,2,1,0:T(8,128)(2,1)S(1)}, bf16[4,8,40,640]{3,2,1,0:T(8,128)(2,1)S(1)}, u32[]{:S(2)}, u32[]{:S(2)}) collective-permute-start(bf16[4,8,40,640]{3,2,1,0:T(8,128)(2,1)S(1)} %get-tuple-element.49), channel_id=1, source_target_pairs={{0,8},{8,0},{1,9},{9,1},{2,10},{10,2},{3,11},{11,3},{4,12},{12,4},... | collective-permute-start | bytes 4915208 | tf_op jit(solution)/shard_map/ppermute | solution.py:316
  111.9 13.1 %collective-permute-start.20 = (bf16[8,40,640]{2,1,0:T(8,128)(2,1)S(1)}, bf16[8,40,640]{2,1,0:T(8,128)(2,1)S(1)}, u32[]{:S(2)}, u32[]{:S(2)}) collective-permute-start(bf16[8,40,640]{2,1,0:T(8,128)(2,1)S(1)} %get-tuple-element.55), channel_id=1, source_target_pairs={{0,16},{16,32},{32,48},{48,0},{1,17},{17,33},{33,49},{49,1},{2,18}... | collective-permute-start | bytes 1228808 | tf_op jit(solution)/shard_map/ppermute | solution.py:316
  113.7 13.9 %collective-permute-start.21 = (bf16[8,40,640]{2,1,0:T(8,128)(2,1)S(1)}, bf16[8,40,640]{2,1,0:T(8,128)(2,1)S(1)}, u32[]{:S(2)}, u32[]{:S(2)}) collective-permute-start(bf16[8,40,640]{2,1,0:T(8,128)(2,1)S(1)} %get-tuple-element.56), channel_id=1, source_target_pairs={{0,32},{16,48},{32,0},{48,16},{1,33},{17,49},{33,1},{49,17},{2,34}... | collective-permute-start | bytes 1228808 | tf_op jit(solution)/shard_map/ppermute | solution.py:316
  116.9 18.3 %collective-permute-start.22 = (bf16[8,40,640]{2,1,0:T(8,128)(2,1)S(1)}, bf16[8,40,640]{2,1,0:T(8,128)(2,1)S(1)}, u32[]{:S(2)}, u32[]{:S(2)}) collective-permute-start(bf16[8,40,640]{2,1,0:T(8,128)(2,1)S(1)} %get-tuple-element.57), channel_id=1, source_target_pairs={{0,48},{16,0},{32,16},{48,32},{1,49},{17,1},{33,17},{49,33},{2,50}... | collective-permute-start | bytes 1228808 | tf_op jit(solution)/shard_map/ppermute | solution.py:316
  116.9 25.2 %collective-permute-start.17 = (bf16[192,1280]{1,0:T(8,128)(2,1)S(1)}, bf16[192,1280]{1,0:T(8,128)(2,1)}, u32[]{:S(2)}, u32[]{:S(2)}) collective-permute-start(bf16[192,1280]{1,0:T(8,128)(2,1)S(1)} %get-tuple-element.51), channel_id=1, source_target_pairs={{0,6},{2,0},{4,2},{6,4},{1,7},{3,1},{5,3},{7,5},{8,14},{10,8},{12,... | collective-permute-start | bytes 1474568 | tf_op jit(solution)/shard_map/ppermute | solution.py:316
  118.0 24.1 %collective-permute-start.18 = (bf16[192,1280]{1,0:T(8,128)(2,1)S(1)}, bf16[192,1280]{1,0:T(8,128)(2,1)}, u32[]{:S(2)}, u32[]{:S(2)}) collective-permute-start(bf16[192,1280]{1,0:T(8,128)(2,1)S(1)} %get-tuple-element.52), channel_id=1, source_target_pairs={{0,4},{2,6},{4,0},{6,2},{1,5},{3,7},{5,1},{7,3},{8,12},{10,14},{12... | collective-permute-start | bytes 1474568 | tf_op jit(solution)/shard_map/ppermute | solution.py:316
  125.1 17.5 %collective-permute-start.19 = (bf16[192,1280]{1,0:T(8,128)(2,1)S(1)}, bf16[192,1280]{1,0:T(8,128)(2,1)}, u32[]{:S(2)}, u32[]{:S(2)}) collective-permute-start(bf16[192,1280]{1,0:T(8,128)(2,1)S(1)} %get-tuple-element.53), channel_id=1, source_target_pairs={{0,2},{2,4},{4,6},{6,0},{1,3},{3,5},{5,7},{7,1},{8,10},{10,12},{12... | collective-permute-start | bytes 1474568 | tf_op jit(solution)/shard_map/ppermute | solution.py:316
  136.1 21.2 %all-to-all-start.2 = ((bf16[8,40,640]{2,1,0:T(8,128)(2,1)}), bf16[8,40,640]{2,1,0:T(8,128)(2,1)S(1)}, u32[]{:S(2)}, u32[]{:S(2)}) async-start(bf16[8,40,640]{2,1,0:T(8,128)(2,1)} %x_sum.1), calls=%async_computation.2 | async-start | bytes 819200 | tf_op jit(solution)/shard_map/all_to_all | solution.py:429
Sparse Core Ops, SparseCore 0:
  35.7 31.0 all-gather.2

commit v10 on v9

--- a/solution.py
+++ b/solution.py
@@ -24,7 +24,6 @@
 LANES = 384
 WIDE = 2 * LANES
 BLOCK = 40
-ZX = ("zh", "zl")
 
 VMEM = pl.BlockSpec(memory_space=pltpu.VMEM)
 SMEM = pl.BlockSpec(memory_space=pltpu.SMEM)
@@ -296,17 +295,22 @@
         out[...] = (kept[there].astype(f32) + arrived[there].astype(f32)).astype(bf16)
 
 
-def x_sum_kernel(*refs):
-    total = refs[0][...].astype(f32)
-    for ref in refs[1:-1]:
+def x_sum_kernel(place, *refs):
+    zl, arrived, (kept, sent) = place[0], refs[:4], refs[4:]
+    for high in range(4):
+        for other, out in enumerate((kept, sent)):
+            there = high * 2 + lax.rem(zl + other, 2)
+            total = arrived[0][there].astype(f32)
+            for ref in arrived[1:]:
+                total = total + ref[there].astype(f32)
+            out[high] = total.astype(bf16)
+
+
+def last_kernel(*refs):
+    arrived, out = refs[:4], refs[4]
+    total = arrived[0][...].astype(f32)
+    for ref in arrived[1:]:
         total = total + ref[...].astype(f32)
-    refs[-1][...] = total.astype(bf16)
-
-
-def last_kernel(arrived, out):
-    total = arrived[0].astype(f32)
-    for k in range(1, 8):
-        total = total + arrived[k].astype(f32)
     up, down = unpack_pair(total)
     out[0] = up[:, :UNITS]
     out[1] = down[:, :UNITS]
@@ -379,7 +383,9 @@
         scratch=[pltpu.VMEM((1024, CH), bf16), pltpu.SemaphoreType.DMA((16,))],
         smem=1, free=2, name="front",
     )
-    block, proj_full, *along_x = lax.optimization_barrier((block, proj_full, *along_x))
+    block, proj_full, along_x[1], along_x[3] = lax.optimization_barrier(
+        (block, proj_full, along_x[1], along_x[3])
+    )
     blocks = lax.all_to_all(block, "y", split_axis=0, concat_axis=0, tiled=True)
     pieces = along_x + [ring(piece, "c", 2, 1) for piece in along_x]
 
@@ -416,21 +422,27 @@
         [x[None], kept, ring(sent, "c", 2, 1)],
         1 << 20, 5 << 20, smem=1, name="core_sum",
     )
-    total = call(
+    half = jax.ShapeDtypeStruct((4, BLOCK, 2 * UNITS), bf16)
+    kept, sent = call(
         x_sum_kernel,
-        tile,
-        [parts[0]] + [ring(parts[step], "x", 4, step) for step in range(1, 4)],
-        1 << 20, 2 << 20, name="x_sum",
+        (half, half),
+        [zl[None], parts[0]] + [ring(parts[step], "x", 4, step) for step in range(1, 4)],
+        1 << 20, 2 << 20, smem=1, name="x_sum",
+    )
+    quarters = call(
+        core_sum_kernel,
+        (jax.ShapeDtypeStruct((BLOCK, 2 * UNITS), bf16),) * 4,
+        [zh[None], kept, ring(sent, "zl", 2, 1)],
+        1 << 18, 1 << 19, smem=1, name="z_sum",
     )
     away1, away2, away3, _ = lax.optimization_barrier((away1, away2, away3, parts[0]))
     for step, away in ((1, away1), (2, away2), (3, away3)):
         own = own + ring(away, "y", 4, 4 - step).astype(f32)
     encoded = (own * (flags > 0).astype(f32)).astype(bf16)
-    total = lax.all_to_all(total, ZX, split_axis=0, concat_axis=0, tiled=True)
     grad_pair = call(
         last_kernel,
         jax.ShapeDtypeStruct((2, BLOCK, UNITS), f32),
-        [total],
+        [quarters[0]] + [ring(quarters[step], "zh", 4, step) for step in range(1, 4)],
         1 << 18, 1 << 19, name="last",
     )
     return (encoded, jnp.transpose(grad_pair, (2, 0, 1)))

time: 166 us -> 159 us (0.958)
  waiting for transfers between devices: 63.7 us -> 52.9 us
  starting transfers between devices: 52.4 us -> 59.2 us
    all_to_all x1 -> x0, waiting for transfers between devices: 12.4 us -> none  [per_device(): total = lax.all_to_all(total, ZX, split_axis=0, concat_axis=0, tiled=True)]
    ppermute x23 -> x27, starting transfers between devices: 34.6 us -> 46.8 us  [ring(): lax.ppermute(values, axis, [(k, (k + step) % size) for k in range(size)])]
    all_to_all x1 -> x0, starting transfers between devices: 5.89 us -> none  [per_device(): total = lax.all_to_all(total, ZX, split_axis=0, concat_axis=0, tiled=True)]
    ppermute x23 -> x27, waiting for transfers between devices: 32.3 us -> 35.2 us  [ring(): lax.ppermute(values, axis, [(k, (k + step) % size) for k in range(size)])]
    pallas_call x8 -> x9, Pallas kernels: 29.7 us -> 29 us  [call(): pl.pallas_call(kernel, out_shape=out_shape, in_specs=[SMEM] * smem + [VME...]
  transfers between devices with their start and end apart: 27 -> 30, of which waited for: 18 -> 17; matrix products, arithmetic and copies ran while one was open for 2% -> 1% of each run, Pallas kernels for 4% -> 4%
where the time goes in v10:
time: 159 us
  starting transfers between devices  59.2 us (37%)
  waiting for transfers between devices  52.9 us (33%)
  Pallas kernels  29 us (18%)
  between operations  14.2 us (9%)
  local copies, waits for them, and re-layouts  2.06 us (1%)
    ppermute x27, starting transfers between devices, ring(): lax.ppermute(values, axis, [(k, (k + step) % size) for k in range(size)])  46.8 us
    ppermute x27, waiting for transfers between devices, ring(): lax.ppermute(values, axis, [(k, (k + step) % size) for k in range(size)])  35.2 us
    pallas_call x9, Pallas kernels, call(): pl.pallas_call(kernel, out_shape=out_shape, in_specs=[SMEM] * smem + [VME...  29 us
    all_to_all x1, waiting for transfers between devices, per_device(): lax.all_to_all(outgoing.reshape(N_DP, PAD, 1024), dp, split_axis=0, conca...  9.32 us
    all_to_all x1, waiting for transfers between devices, per_device(): blocks = lax.all_to_all(block, 'y', split_axis=0, concat_axis=0, tiled=True)  8.43 us
    all_to_all x1, starting transfers between devices, per_device(): lax.all_to_all(outgoing.reshape(N_DP, PAD, 1024), dp, split_axis=0, conca...  8.39 us
    all_to_all x1, starting transfers between devices, per_device(): blocks = lax.all_to_all(block, 'y', split_axis=0, concat_axis=0, tiled=True)  3.91 us
  transfers between devices with their start and end apart: 30, of which 17 were waited for; matrix products, arithmetic and copies ran while one was open for 1% of the time, Pallas kernels for 4%

profile of v10, /device:TPU:2, one launch (start us, length us, event | category | flops | bytes accessed | tf_op | source)
XLA Modules:
  0.0 158.9 jit_solution(6641835104437880)
XLA Ops:
  7.2 0.0 all-gather.3.cloned.1.call-start
  7.2 1.0 pack.1
  8.2 2.0 %collective-permute-start = (bf16[40,640]{1,0:T(8,128)(2,1)S(1)}, bf16[40,640]{1,0:T(8,128)(2,1)S(1)}, u32[]{:S(2)}, u32[]{:S(2)}) collective-permute-start(bf16[40,640]{1,0:T(8,128)(2,1)S(1)} %get-tuple-element.34), channel_id=1, source_target_pairs={{0,1},{1,0},{2,3},{3,2},{4,5},{5,4},{6,7},{7,6},{8,9},{9,8},{10,11... | collective-permute-start | bytes 153608 | tf_op jit(solution)/shard_map/ppermute | solution.py:320
  10.2 0.1 collective-permute-start.4
  10.3 2.2 %collective-permute-done = bf16[40,640]{1,0:T(8,128)(2,1)S(1)} collective-permute-done((bf16[40,640]{1,0:T(8,128)(2,1)S(1)}, bf16[40,640]{1,0:T(8,128)(2,1)S(1)}, u32[]{:S(2)}, u32[]{:S(2)}) %collective-permute-start) | collective-permute-done | bytes 51232 | tf_op jit(solution)/shard_map/ppermute | solution.py:320
  12.6 7.6 %collective-permute-start.2 = (bf16[2,40,640]{2,1,0:T(8,128)(2,1)S(1)}, bf16[2,40,640]{2,1,0:T(8,128)(2,1)S(1)}, u32[]{:S(2)}, u32[]{:S(2)}) collective-permute-start(bf16[2,40,640]{2,1,0:T(8,128)(2,1)S(1)} %get-tuple-element.69), channel_id=1, source_target_pairs={{0,128},{64,192},{128,0},{192,64},{1,129},{65,193},{129,1},{193,65... | collective-permute-start | bytes 307208 | tf_op jit(solution)/shard_map/ppermute | solution.py:320
  20.2 3.3 %collective-permute-start.6 = (bf16[2,144,512]{2,1,0:T(8,128)(2,1)S(1)}, bf16[2,144,512]{2,1,0:T(8,128)(2,1)S(1)}, u32[]{:S(2)}, u32[]{:S(2)}) collective-permute-start(bf16[2,144,512]{2,1,0:T(8,128)(2,1)S(1)} %get-tuple-element.67), channel_id=1, source_target_pairs={{0,4},{2,6},{4,0},{6,2},{1,5},{3,7},{5,1},{7,3},{8,12},{10,14},{12... | collective-permute-start | bytes 884744 | tf_op jit(solution)/shard_map/ppermute | solution.py:320
  23.5 0.7 collective-permute-start.5
  24.2 2.6 %collective-permute-start.7 = (bf16[2,144,512]{2,1,0:T(8,128)(2,1)S(1)}, bf16[2,144,512]{2,1,0:T(8,128)(2,1)S(1)}, u32[]{:S(2)}, u32[]{:S(2)}) collective-permute-start(bf16[2,144,512]{2,1,0:T(8,128)(2,1)S(1)} %get-tuple-element.67), channel_id=1, source_target_pairs={{0,6},{2,0},{4,2},{6,4},{1,7},{3,1},{5,3},{7,5},{8,14},{10,8},{12,... | collective-permute-start | bytes 884744 | tf_op jit(solution)/shard_map/ppermute | solution.py:320
  26.8 1.5 collective-permute-start.1
  28.2 2.7 %collective-permute-start.3 = (bf16[2,40,640]{2,1,0:T(8,128)(2,1)S(1)}, bf16[2,40,640]{2,1,0:T(8,128)(2,1)S(1)}, u32[]{:S(2)}, u32[]{:S(2)}) collective-permute-start(bf16[2,40,640]{2,1,0:T(8,128)(2,1)S(1)} %get-tuple-element.69), channel_id=1, source_target_pairs={{0,192},{64,0},{128,64},{192,128},{1,193},{65,1},{129,65},{193,129... | collective-permute-start | bytes 307208 | tf_op jit(solution)/shard_map/ppermute | solution.py:320
  30.9 2.2 %route.1 = bf16[256,1024]{1,0:T(8,128)(2,1)} custom-call(s32[1,128]{1,0:T(1,128)} %bitcast.39, s32[1,128]{1,0:T(1,128)} %bitcast.40, bf16[128,1024]{1,0:T(8,128)(2,1)} %rows_in.1), custom_call_target="tpu_custom_call" | custom-call | flops 75497472 | bytes 1048576 | tf_op jit(solution)/shard_map/route/pallas_call | solution.py:53
  33.1 0.6 collective-permute-done.1
  33.7 1.5 collective-permute-done.3
  35.2 0.1 pad_maximum_fusion.1.refs_0_
  35.3 0.0 copy-start.2
  35.3 0.1 collective-permute-done.7
  35.4 0.1 pad_maximum_fusion.refs_0_.own
  35.5 0.0 all-gather.3.cloned.1.call-update
  35.5 0.1 collective-permute-start.8
  35.6 8.4 %all-to-all-start = ((bf16[32,8,1024]{2,1,0:T(8,128)(2,1)}), bf16[32,8,1024]{2,1,0:T(8,128)(2,1)S(1)}, u32[]{:S(2)}, u32[]{:S(2)}) async-start(bf16[32,8,1024]{2,1,0:T(8,128)(2,1)} %bitcast.20), calls=%async_computation | async-start | bytes 1048576 | tf_op jit(solution)/shard_map/all_to_all | solution.py:364
  44.0 0.3 collective-permute-start.10
  44.3 1.8 %collective-permute-start.9 = (bf16[4,2,40,640]{3,2,1,0:T(8,128)(2,1)S(1)}, bf16[4,2,40,640]{3,2,1,0:T(8,128)(2,1)}, u32[]{:S(2)}, u32[]{:S(2)}) collective-permute-start(bf16[4,2,40,640]{3,2,1,0:T(8,128)(2,1)S(1)} %pad_maximum_fusion.1.refs_0_), channel_id=1, source_target_pairs={{0,16},{16,32},{32,48},{48,0},{1,17},{17,33},{33,49},{49,1},{2,18}... | collective-permute-start | bytes 1228808 | tf_op jit(solution)/shard_map/ppermute | solution.py:320
  46.1 3.3 %collective-permute-start.11 = (bf16[4,2,40,640]{3,2,1,0:T(8,128)(2,1)S(1)}, bf16[4,2,40,640]{3,2,1,0:T(8,128)(2,1)}, u32[]{:S(2)}, u32[]{:S(2)}) collective-permute-start(bf16[4,2,40,640]{3,2,1,0:T(8,128)(2,1)S(1)} %pad_maximum_fusion.1.refs_0_), channel_id=1, source_target_pairs={{0,32},{16,48},{32,0},{48,16},{1,33},{17,49},{33,1},{49,17},{2,34}... | collective-permute-start | bytes 1228808 | tf_op jit(solution)/shard_map/ppermute | solution.py:320
  49.4 0.1 pad_add_fusion.place
  49.5 0.6 proj.1.refs_9_
  50.1 1.0 copy-done
  51.2 9.3 %all-to-all-done = bf16[32,8,1024]{2,1,0:T(8,128)(2,1)S(1)} async-done(((bf16[32,8,1024]{2,1,0:T(8,128)(2,1)}), bf16[32,8,1024]{2,1,0:T(8,128)(2,1)S(1)}, u32[]{:S(2)}, u32[]{:S(2)}) %all-to-all-start) | async-done | bytes 524320 | tf_op jit(solution)/shard_map/all_to_all | solution.py:364
  60.5 3.1 %front.1 = (bf16[4,208,512]{2,1,0:T(8,128)(2,1)S(1)}, f32[192,1]{1,0:T(8,128)S(1)}) custom-call(s32[3]{0:T(128)S(1)} %pad_add_fusion.place, bf16[256,1024]{1,0:T(8,128)(2,1)S(1)} %bitcast.26, bf16[4,2,144,512]{3,2,1,0:T(8,128)(2,1)S(1)} %pad_maximum_fusion.refs_0_.own, bf16[4,2,144,512]{3,2,1,0:T(8,128)(2,1)S(1)} %collective-permute-done.8.refs_1_.other), custom_call_target="tpu_custom_call" | custom-call | flops 268435456 | bytes 2097152 | tf_op jit(solution)/shard_map/front/pallas_call | solution.py:53
  63.6 0.9 copy-done.1
  64.5 3.9 %all-to-all-start.1 = ((bf16[4,208,512]{2,1,0:T(8,128)(2,1)}), bf16[4,208,512]{2,1,0:T(8,128)(2,1)S(1)}, u32[]{:S(2)}, u32[]{:S(2)}) async-start(bf16[4,208,512]{2,1,0:T(8,128)(2,1)} %copy-done.1), calls=%async_computation.1 | async-start | bytes 1703936 | tf_op jit(solution)/shard_map/all_to_all | solution.py:389
  68.4 0.3 collective-permute-start.12
  68.7 1.7 %collective-permute-done.11.refs_2_ = bf16[4,2,40,640]{3,2,1,0:T(8,128)(2,1)} collective-permute-done((bf16[4,2,40,640]{3,2,1,0:T(8,128)(2,1)S(1)}, bf16[4,2,40,640]{3,2,1,0:T(8,128)(2,1)}, u32[]{:S(2)}, u32[]{:S(2)}) %collective-permute-start.11) | collective-permute-done | bytes 409632 | tf_op jit(solution)/shard_map/ppermute | solution.py:320
  70.5 0.5 collective-permute-start.13
  71.0 0.0 collective-permute-start.15
  71.0 0.1 stack.77.place
  71.1 1.4 collective-permute-done.14.refs_6_
  72.4 0.6 collective-permute-done.13.refs_5_
  73.0 0.6 collective-permute-done.15.refs_7_
  73.6 8.4 %all-to-all-done.1.blocks = bf16[4,208,512]{2,1,0:T(8,128)(2,1)S(1)} async-done(((bf16[4,208,512]{2,1,0:T(8,128)(2,1)}), bf16[4,208,512]{2,1,0:T(8,128)(2,1)S(1)}, u32[]{:S(2)}, u32[]{:S(2)}) %all-to-all-start.1) | async-done | bytes 852000 | tf_op jit(solution)/shard_map/all_to_all | solution.py:389
  82.1 20.7 %ffn.1 = (f32[192,1280]{1,0:T(8,128)S(1)}, bf16[192,1280]{1,0:T(8,128)(2,1)S(1)}, bf16[192,1280]{1,0:T(8,128)(2,1)S(1)}, bf16[192,1280]{1,0:T(8,128)(2,1)S(1)}, ...) custom-call(s32[5]{0:T(128)S(1)} %stack.77.place, ...), custom_call_target="tpu_custom_call" | custom-call | flops 8556380160 | bytes 16777216 | tf_op jit(solution)/shard_map/ffn/pallas_call | solution.py:53
  102.8 0.1 collective-permute-start.16
  102.9 3.5 %collective-permute-done.16.arrived = bf16[4,8,40,640]{3,2,1,0:T(8,128)(2,1)S(1)} collective-permute-done((bf16[4,8,40,640]{3,2,1,0:T(8,128)(2,1)S(1)}, bf16[4,8,40,640]{3,2,1,0:T(8,128)(2,1)S(1)}, u32[]{:S(2)}, u32[]{:S(2)}) %collective-permute-start.16) | collective-permute-done | bytes 1638432 | tf_op jit(solution)/shard_map/ppermute | solution.py:320
  106.4 0.4 core_sum.1
  106.8 0.7 collective-permute-start.20
  107.4 5.6 %collective-permute-start.21 = (bf16[8,40,640]{2,1,0:T(8,128)(2,1)S(1)}, bf16[8,40,640]{2,1,0:T(8,128)(2,1)S(1)}, u32[]{:S(2)}, u32[]{:S(2)}) collective-permute-start(bf16[8,40,640]{2,1,0:T(8,128)(2,1)S(1)} %get-tuple-element.58), channel_id=1, source_target_pairs={{0,32},{16,48},{32,0},{48,16},{1,33},{17,49},{33,1},{49,17},{2,34}... | collective-permute-start | bytes 1228808 | tf_op jit(solution)/shard_map/ppermute | solution.py:320
  113.1 1.2 collective-permute-start.17
  114.2 1.4 collective-permute-start.18
  115.7 5.5 %collective-permute-done.20.refs_1_ = bf16[8,40,640]{2,1,0:T(8,128)(2,1)S(1)} collective-permute-done((bf16[8,40,640]{2,1,0:T(8,128)(2,1)S(1)}, bf16[8,40,640]{2,1,0:T(8,128)(2,1)S(1)}, u32[]{:S(2)}, u32[]{:S(2)}) %collective-permute-start.20) | collective-permute-done | bytes 409632 | tf_op jit(solution)/shard_map/ppermute | solution.py:320
  121.2 0.6 collective-permute-start.19
  121.8 1.6 collective-permute-done.21.refs_2_
  123.4 7.9 %collective-permute-done.22.refs_3_ = bf16[8,40,640]{2,1,0:T(8,128)(2,1)S(1)} collective-permute-done((bf16[8,40,640]{2,1,0:T(8,128)(2,1)S(1)}, bf16[8,40,640]{2,1,0:T(8,128)(2,1)S(1)}, u32[]{:S(2)}, u32[]{:S(2)}) %collective-permute-start.22) | collective-permute-done | bytes 409632 | tf_op jit(solution)/shard_map/ppermute | solution.py:320
  131.3 0.2 x_sum.1
  131.5 4.1 %collective-permute-start.23 = (bf16[4,40,640]{2,1,0:T(8,128)(2,1)S(1)}, bf16[4,40,640]{2,1,0:T(8,128)(2,1)S(1)}, u32[]{:S(2)}, u32[]{:S(2)}) collective-permute-start(bf16[4,40,640]{2,1,0:T(8,128)(2,1)S(1)} %get-tuple-element.61), channel_id=1, source_target_pairs={{0,1},{1,0},{2,3},{3,2},{4,5},{5,4},{6,7},{7,6},{8,9},{9,8},{10,11... | collective-permute-start | bytes 614408 | tf_op jit(solution)/shard_map/ppermute | solution.py:320
  135.7 0.1 convert_reduce_fusion
  135.8 5.2 %collective-permute-done.23.arrived = bf16[4,40,640]{2,1,0:T(8,128)(2,1)S(1)} collective-permute-done((bf16[4,40,640]{2,1,0:T(8,128)(2,1)S(1)}, bf16[4,40,640]{2,1,0:T(8,128)(2,1)S(1)}, u32[]{:S(2)}, u32[]{:S(2)}) %collective-permute-start.23) | collective-permute-done | bytes 204832 | tf_op jit(solution)/shard_map/ppermute | solution.py:320
  140.9 0.1 z_sum.1
  141.0 0.1 collective-permute-start.24
  141.1 3.4 %collective-permute-start.25 = (bf16[40,640]{1,0:T(8,128)(2,1)S(1)}, bf16[40,640]{1,0:T(8,128)(2,1)S(1)}, u32[]{:S(2)}, u32[]{:S(2)}) collective-permute-start(bf16[40,640]{1,0:T(8,128)(2,1)S(1)} %get-tuple-element.64), channel_id=1, source_target_pairs={{0,128},{64,192},{128,0},{192,64},{1,129},{65,193},{129,1},{193,65... | collective-permute-start | bytes 153608 | tf_op jit(solution)/shard_map/ppermute | solution.py:320
  144.5 2.9 %collective-permute-start.26 = (bf16[40,640]{1,0:T(8,128)(2,1)S(1)}, bf16[40,640]{1,0:T(8,128)(2,1)S(1)}, u32[]{:S(2)}, u32[]{:S(2)}) collective-permute-start(bf16[40,640]{1,0:T(8,128)(2,1)S(1)} %get-tuple-element.65), channel_id=1, source_target_pairs={{0,192},{64,0},{128,64},{192,128},{1,193},{65,1},{129,65},{193,129... | collective-permute-start | bytes 153608 | tf_op jit(solution)/shard_map/ppermute | solution.py:320
  147.4 1.1 multiply_convert_fusion
  148.5 0.7 collective-permute-done.25.refs_2_
  149.2 2.1 %collective-permute-done.26.refs_3_ = bf16[40,640]{1,0:T(8,128)(2,1)S(1)} collective-permute-done((bf16[40,640]{1,0:T(8,128)(2,1)S(1)}, bf16[40,640]{1,0:T(8,128)(2,1)S(1)}, u32[]{:S(2)}, u32[]{:S(2)}) %collective-permute-start.26) | collective-permute-done | bytes 51232 | tf_op jit(solution)/shard_map/ppermute | solution.py:320
  151.3 0.7 last.1
  (28 shorter events, 0.1 us)
Async XLA Ops:
  7.2 74.9 %all-gather.3.cloned.1.call-start = ((), (), s32[]{:S(2)}) async-start(), calls=%async_computation.2 | async-start | bytes 2457600 | tf_op jit(solution)/shard_map/all_gather | solution.py:361
  8.2 4.3 %collective-permute-start = (bf16[40,640]{1,0:T(8,128)(2,1)S(1)}, bf16[40,640]{1,0:T(8,128)(2,1)S(1)}, u32[]{:S(2)}, u32[]{:S(2)}) collective-permute-start(bf16[40,640]{1,0:T(8,128)(2,1)S(1)} %get-tuple-element.34), channel_id=1, source_target_pairs={{0,1},{1,0},{2,3},{3,2},{4,5},{5,4},{6,7},{7,6},{8,9},{9,8},{10,11... | collective-permute-start | bytes 153608 | tf_op jit(solution)/shard_map/ppermute | solution.py:320
  10.2 10.0 %collective-permute-start.4 = (bf16[144,512]{1,0:T(8,128)(2,1)S(1)}, bf16[144,512]{1,0:T(8,128)(2,1)S(1)}, u32[]{:S(2)}, u32[]{:S(2)}) collective-permute-start(bf16[144,512]{1,0:T(8,128)(2,1)S(1)} %get-tuple-element.35), channel_id=1, source_target_pairs={{0,1},{1,0},{2,3},{3,2},{4,5},{5,4},{6,7},{7,6},{8,9},{9,8},{10,11... | collective-permute-start | bytes 442376 | tf_op jit(solution)/shard_map/ppermute | solution.py:320
  12.6 15.7 %collective-permute-start.2 = (bf16[2,40,640]{2,1,0:T(8,128)(2,1)S(1)}, bf16[2,40,640]{2,1,0:T(8,128)(2,1)S(1)}, u32[]{:S(2)}, u32[]{:S(2)}) collective-permute-start(bf16[2,40,640]{2,1,0:T(8,128)(2,1)S(1)} %get-tuple-element.69), channel_id=1, source_target_pairs={{0,128},{64,192},{128,0},{192,64},{1,129},{65,193},{129,1},{193,65... | collective-permute-start | bytes 307208 | tf_op jit(solution)/shard_map/ppermute | solution.py:320
  20.2 15.0 %collective-permute-start.6 = (bf16[2,144,512]{2,1,0:T(8,128)(2,1)S(1)}, bf16[2,144,512]{2,1,0:T(8,128)(2,1)S(1)}, u32[]{:S(2)}, u32[]{:S(2)}) collective-permute-start(bf16[2,144,512]{2,1,0:T(8,128)(2,1)S(1)} %get-tuple-element.67), channel_id=1, source_target_pairs={{0,4},{2,6},{4,0},{6,2},{1,5},{3,7},{5,1},{7,3},{8,12},{10,14},{12... | collective-permute-start | bytes 884744 | tf_op jit(solution)/shard_map/ppermute | solution.py:320
  23.5 11.8 %collective-permute-start.5 = (bf16[2,144,512]{2,1,0:T(8,128)(2,1)S(1)}, bf16[2,144,512]{2,1,0:T(8,128)(2,1)S(1)}, u32[]{:S(2)}, u32[]{:S(2)}) collective-permute-start(bf16[2,144,512]{2,1,0:T(8,128)(2,1)S(1)} %get-tuple-element.67), channel_id=1, source_target_pairs={{0,2},{2,4},{4,6},{6,0},{1,3},{3,5},{5,7},{7,1},{8,10},{10,12},{12... | collective-permute-start | bytes 884744 | tf_op jit(solution)/shard_map/ppermute | solution.py:320
  24.2 11.2 %collective-permute-start.7 = (bf16[2,144,512]{2,1,0:T(8,128)(2,1)S(1)}, bf16[2,144,512]{2,1,0:T(8,128)(2,1)S(1)}, u32[]{:S(2)}, u32[]{:S(2)}) collective-permute-start(bf16[2,144,512]{2,1,0:T(8,128)(2,1)S(1)} %get-tuple-element.67), channel_id=1, source_target_pairs={{0,6},{2,0},{4,2},{6,4},{1,7},{3,1},{5,3},{7,5},{8,14},{10,8},{12,... | collective-permute-start | bytes 884744 | tf_op jit(solution)/shard_map/ppermute | solution.py:320
  26.8 6.9 %collective-permute-start.1 = (bf16[2,40,640]{2,1,0:T(8,128)(2,1)S(1)}, bf16[2,40,640]{2,1,0:T(8,128)(2,1)S(1)}, u32[]{:S(2)}, u32[]{:S(2)}) collective-permute-start(bf16[2,40,640]{2,1,0:T(8,128)(2,1)S(1)} %get-tuple-element.69), channel_id=1, source_target_pairs={{0,64},{64,128},{128,192},{192,0},{1,65},{65,129},{129,193},{193,1... | collective-permute-start | bytes 307208 | tf_op jit(solution)/shard_map/ppermute | solution.py:320
  28.2 7.0 %collective-permute-start.3 = (bf16[2,40,640]{2,1,0:T(8,128)(2,1)S(1)}, bf16[2,40,640]{2,1,0:T(8,128)(2,1)S(1)}, u32[]{:S(2)}, u32[]{:S(2)}) collective-permute-start(bf16[2,40,640]{2,1,0:T(8,128)(2,1)S(1)} %get-tuple-element.69), channel_id=1, source_target_pairs={{0,192},{64,0},{128,64},{192,128},{1,193},{65,1},{129,65},{193,129... | collective-permute-start | bytes 307208 | tf_op jit(solution)/shard_map/ppermute | solution.py:320
  35.3 33.2 %copy-start.2 = (bf16[4,2,40,640]{3,2,1,0:T(8,128)(2,1)}, bf16[4,2,40,640]{3,2,1,0:T(8,128)(2,1)S(1)}, u32[]{:S(2)}) copy-start(bf16[4,2,40,640]{3,2,1,0:T(8,128)(2,1)S(1)} %pad_maximum_fusion.1.refs_0_) | copy-start | bytes 1228804
  35.5 14.0 %collective-permute-start.8 = (bf16[4,2,144,512]{3,2,1,0:T(8,128)(2,1)S(1)}, bf16[4,2,144,512]{3,2,1,0:T(8,128)(2,1)S(1)}, u32[]{:S(2)}, u32[]{:S(2)}) collective-permute-start(bf16[4,2,144,512]{3,2,1,0:T(8,128)(2,1)S(1)} %pad_maximum_fusion.refs_0_.own), channel_id=1, source_target_pairs={{0,8},{8,0},{1,9},{9,1},{2,10},{10,2},{3,11},{11,3},{4,12},{12,4},... | collective-permute-start | bytes 3538952 | tf_op jit(solution)/shard_map/ppermute | solution.py:320
  35.6 24.9 %all-to-all-start = ((bf16[32,8,1024]{2,1,0:T(8,128)(2,1)}), bf16[32,8,1024]{2,1,0:T(8,128)(2,1)S(1)}, u32[]{:S(2)}, u32[]{:S(2)}) async-start(bf16[32,8,1024]{2,1,0:T(8,128)(2,1)} %bitcast.20), calls=%async_computation | async-start | bytes 1048576 | tf_op jit(solution)/shard_map/all_to_all | solution.py:364
  44.0 20.5 %collective-permute-start.10 = (bf16[4,2,40,640]{3,2,1,0:T(8,128)(2,1)S(1)}, bf16[4,2,40,640]{3,2,1,0:T(8,128)(2,1)}, u32[]{:S(2)}, u32[]{:S(2)}) collective-permute-start(bf16[4,2,40,640]{3,2,1,0:T(8,128)(2,1)S(1)} %pad_maximum_fusion.1.refs_0_), channel_id=1, source_target_pairs={{0,48},{16,0},{32,16},{48,32},{1,49},{17,1},{33,17},{49,33},{2,50}... | collective-permute-start | bytes 1228808 | tf_op jit(solution)/shard_map/ppermute | solution.py:320
  44.3 20.2 %collective-permute-start.9 = (bf16[4,2,40,640]{3,2,1,0:T(8,128)(2,1)S(1)}, bf16[4,2,40,640]{3,2,1,0:T(8,128)(2,1)}, u32[]{:S(2)}, u32[]{:S(2)}) collective-permute-start(bf16[4,2,40,640]{3,2,1,0:T(8,128)(2,1)S(1)} %pad_maximum_fusion.1.refs_0_), channel_id=1, source_target_pairs={{0,16},{16,32},{32,48},{48,0},{1,17},{17,33},{33,49},{49,1},{2,18}... | collective-permute-start | bytes 1228808 | tf_op jit(solution)/shard_map/ppermute | solution.py:320
  46.1 24.3 %collective-permute-start.11 = (bf16[4,2,40,640]{3,2,1,0:T(8,128)(2,1)S(1)}, bf16[4,2,40,640]{3,2,1,0:T(8,128)(2,1)}, u32[]{:S(2)}, u32[]{:S(2)}) collective-permute-start(bf16[4,2,40,640]{3,2,1,0:T(8,128)(2,1)S(1)} %pad_maximum_fusion.1.refs_0_), channel_id=1, source_target_pairs={{0,32},{16,48},{32,0},{48,16},{1,33},{17,49},{33,1},{49,17},{2,34}... | collective-permute-start | bytes 1228808 | tf_op jit(solution)/shard_map/ppermute | solution.py:320
  50.1 1.1 copy-start
  63.6 0.9 copy-start.1
  64.5 17.5 %all-to-all-start.1 = ((bf16[4,208,512]{2,1,0:T(8,128)(2,1)}), bf16[4,208,512]{2,1,0:T(8,128)(2,1)S(1)}, u32[]{:S(2)}, u32[]{:S(2)}) async-start(bf16[4,208,512]{2,1,0:T(8,128)(2,1)} %copy-done.1), calls=%async_computation.1 | async-start | bytes 1703936 | tf_op jit(solution)/shard_map/all_to_all | solution.py:389
  68.4 2.6 %collective-permute-start.12 = (bf16[4,2,40,640]{3,2,1,0:T(8,128)(2,1)S(1)}, bf16[4,2,40,640]{3,2,1,0:T(8,128)(2,1)S(1)}, u32[]{:S(2)}, u32[]{:S(2)}) collective-permute-start(bf16[4,2,40,640]{3,2,1,0:T(8,128)(2,1)S(1)} %pad_maximum_fusion.1.refs_0_), channel_id=1, source_target_pairs={{0,8},{8,0},{1,9},{9,1},{2,10},{10,2},{3,11},{11,3},{4,12},{12,4},... | collective-permute-start | bytes 1228808 | tf_op jit(solution)/shard_map/ppermute | solution.py:320
  70.5 2.0 %collective-permute-start.14 = (bf16[4,2,40,640]{3,2,1,0:T(8,128)(2,1)}, bf16[4,2,40,640]{3,2,1,0:T(8,128)(2,1)S(1)}, u32[]{:S(2)}, u32[]{:S(2)}) collective-permute-start(bf16[4,2,40,640]{3,2,1,0:T(8,128)(2,1)} %collective-permute-done.11.refs_2_), channel_id=1, source_target_pairs={{0,8},{8,0},{1,9},{9,1},{2,10},{10,2},{3,11},{11,3},{4,12},{12,4},... | collective-permute-start | bytes 1228808 | tf_op jit(solution)/shard_map/ppermute | solution.py:320
  70.5 2.5 %collective-permute-start.13 = (bf16[4,2,40,640]{3,2,1,0:T(8,128)(2,1)}, bf16[4,2,40,640]{3,2,1,0:T(8,128)(2,1)S(1)}, u32[]{:S(2)}, u32[]{:S(2)}) collective-permute-start(bf16[4,2,40,640]{3,2,1,0:T(8,128)(2,1)} %collective-permute-done.9.refs_1_), channel_id=1, source_target_pairs={{0,8},{8,0},{1,9},{9,1},{2,10},{10,2},{3,11},{11,3},{4,12},{12,4},... | collective-permute-start | bytes 1228808 | tf_op jit(solution)/shard_map/ppermute | solution.py:320
  71.0 2.6 %collective-permute-start.15 = (bf16[4,2,40,640]{3,2,1,0:T(8,128)(2,1)}, bf16[4,2,40,640]{3,2,1,0:T(8,128)(2,1)S(1)}, u32[]{:S(2)}, u32[]{:S(2)}) collective-permute-start(bf16[4,2,40,640]{3,2,1,0:T(8,128)(2,1)} %collective-permute-done.10.refs_3_), channel_id=1, source_target_pairs={{0,8},{8,0},{1,9},{9,1},{2,10},{10,2},{3,11},{11,3},{4,12},{12,4},... | collective-permute-start | bytes 1228808 | tf_op jit(solution)/shard_map/ppermute | solution.py:320
  71.1 11.0 %copy-start.3 = (bf16[4,2,40,640]{3,2,1,0:T(8,128)(2,1)}, bf16[4,2,40,640]{3,2,1,0:T(8,128)(2,1)S(1)}, u32[]{:S(2)}) copy-start(bf16[4,2,40,640]{3,2,1,0:T(8,128)(2,1)S(1)} %collective-permute-done.12.refs_4_) | copy-start | bytes 1228804
  72.4 9.6 %copy-start.4 = (bf16[4,2,40,640]{3,2,1,0:T(8,128)(2,1)}, bf16[4,2,40,640]{3,2,1,0:T(8,128)(2,1)S(1)}, u32[]{:S(2)}) copy-start(bf16[4,2,40,640]{3,2,1,0:T(8,128)(2,1)S(1)} %collective-permute-done.14.refs_6_) | copy-start | bytes 1228804
  73.0 9.0 %copy-start.5 = (bf16[4,2,40,640]{3,2,1,0:T(8,128)(2,1)}, bf16[4,2,40,640]{3,2,1,0:T(8,128)(2,1)S(1)}, u32[]{:S(2)}) copy-start(bf16[4,2,40,640]{3,2,1,0:T(8,128)(2,1)S(1)} %collective-permute-done.13.refs_5_) | copy-start | bytes 1228804
  73.6 8.4 %copy-start.6 = (bf16[4,2,40,640]{3,2,1,0:T(8,128)(2,1)}, bf16[4,2,40,640]{3,2,1,0:T(8,128)(2,1)S(1)}, u32[]{:S(2)}) copy-start(bf16[4,2,40,640]{3,2,1,0:T(8,128)(2,1)S(1)} %collective-permute-done.15.refs_7_) | copy-start | bytes 1228804
  102.8 3.6 %collective-permute-start.16 = (bf16[4,8,40,640]{3,2,1,0:T(8,128)(2,1)S(1)}, bf16[4,8,40,640]{3,2,1,0:T(8,128)(2,1)S(1)}, u32[]{:S(2)}, u32[]{:S(2)}) collective-permute-start(bf16[4,8,40,640]{3,2,1,0:T(8,128)(2,1)S(1)} %get-tuple-element.51), channel_id=1, source_target_pairs={{0,8},{8,0},{1,9},{9,1},{2,10},{10,2},{3,11},{11,3},{4,12},{12,4},... | collective-permute-start | bytes 4915208 | tf_op jit(solution)/shard_map/ppermute | solution.py:320
  106.8 14.5 %collective-permute-start.20 = (bf16[8,40,640]{2,1,0:T(8,128)(2,1)S(1)}, bf16[8,40,640]{2,1,0:T(8,128)(2,1)S(1)}, u32[]{:S(2)}, u32[]{:S(2)}) collective-permute-start(bf16[8,40,640]{2,1,0:T(8,128)(2,1)S(1)} %get-tuple-element.57), channel_id=1, source_target_pairs={{0,16},{16,32},{32,48},{48,0},{1,17},{17,33},{33,49},{49,1},{2,18}... | collective-permute-start | bytes 1228808 | tf_op jit(solution)/shard_map/ppermute | solution.py:320
  107.4 16.0 %collective-permute-start.21 = (bf16[8,40,640]{2,1,0:T(8,128)(2,1)S(1)}, bf16[8,40,640]{2,1,0:T(8,128)(2,1)S(1)}, u32[]{:S(2)}, u32[]{:S(2)}) collective-permute-start(bf16[8,40,640]{2,1,0:T(8,128)(2,1)S(1)} %get-tuple-element.58), channel_id=1, source_target_pairs={{0,32},{16,48},{32,0},{48,16},{1,33},{17,49},{33,1},{49,17},{2,34}... | collective-permute-start | bytes 1228808 | tf_op jit(solution)/shard_map/ppermute | solution.py:320
  113.1 18.3 %collective-permute-start.22 = (bf16[8,40,640]{2,1,0:T(8,128)(2,1)S(1)}, bf16[8,40,640]{2,1,0:T(8,128)(2,1)S(1)}, u32[]{:S(2)}, u32[]{:S(2)}) collective-permute-start(bf16[8,40,640]{2,1,0:T(8,128)(2,1)S(1)} %get-tuple-element.59), channel_id=1, source_target_pairs={{0,48},{16,0},{32,16},{48,32},{1,49},{17,1},{33,17},{49,33},{2,50}... | collective-permute-start | bytes 1228808 | tf_op jit(solution)/shard_map/ppermute | solution.py:320
  113.1 31.4 %collective-permute-start.17 = (bf16[192,1280]{1,0:T(8,128)(2,1)S(1)}, bf16[192,1280]{1,0:T(8,128)(2,1)S(1)}, u32[]{:S(2)}, u32[]{:S(2)}) collective-permute-start(bf16[192,1280]{1,0:T(8,128)(2,1)S(1)} %get-tuple-element.53), channel_id=1, source_target_pairs={{0,6},{2,0},{4,2},{6,4},{1,7},{3,1},{5,3},{7,5},{8,14},{10,8},{12,... | collective-permute-start | bytes 1474568 | tf_op jit(solution)/shard_map/ppermute | solution.py:320
  114.2 33.2 %collective-permute-start.18 = (bf16[192,1280]{1,0:T(8,128)(2,1)S(1)}, bf16[192,1280]{1,0:T(8,128)(2,1)S(1)}, u32[]{:S(2)}, u32[]{:S(2)}) collective-permute-start(bf16[192,1280]{1,0:T(8,128)(2,1)S(1)} %get-tuple-element.54), channel_id=1, source_target_pairs={{0,4},{2,6},{4,0},{6,2},{1,5},{3,7},{5,1},{7,3},{8,12},{10,14},{12... | collective-permute-start | bytes 1474568 | tf_op jit(solution)/shard_map/ppermute | solution.py:320
  121.2 26.2 %collective-permute-start.19 = (bf16[192,1280]{1,0:T(8,128)(2,1)S(1)}, bf16[192,1280]{1,0:T(8,128)(2,1)S(1)}, u32[]{:S(2)}, u32[]{:S(2)}) collective-permute-start(bf16[192,1280]{1,0:T(8,128)(2,1)S(1)} %get-tuple-element.55), channel_id=1, source_target_pairs={{0,2},{2,4},{4,6},{6,0},{1,3},{3,5},{5,7},{7,1},{8,10},{10,12},{12... | collective-permute-start | bytes 1474568 | tf_op jit(solution)/shard_map/ppermute | solution.py:320
  131.5 9.4 %collective-permute-start.23 = (bf16[4,40,640]{2,1,0:T(8,128)(2,1)S(1)}, bf16[4,40,640]{2,1,0:T(8,128)(2,1)S(1)}, u32[]{:S(2)}, u32[]{:S(2)}) collective-permute-start(bf16[4,40,640]{2,1,0:T(8,128)(2,1)S(1)} %get-tuple-element.61), channel_id=1, source_target_pairs={{0,1},{1,0},{2,3},{3,2},{4,5},{5,4},{6,7},{7,6},{8,9},{9,8},{10,11... | collective-permute-start | bytes 614408 | tf_op jit(solution)/shard_map/ppermute | solution.py:320
  141.0 7.5 %collective-permute-start.24 = (bf16[40,640]{1,0:T(8,128)(2,1)S(1)}, bf16[40,640]{1,0:T(8,128)(2,1)S(1)}, u32[]{:S(2)}, u32[]{:S(2)}) collective-permute-start(bf16[40,640]{1,0:T(8,128)(2,1)S(1)} %get-tuple-element.63), channel_id=1, source_target_pairs={{0,64},{64,128},{128,192},{192,0},{1,65},{65,129},{129,193},{193,1... | collective-permute-start | bytes 153608 | tf_op jit(solution)/shard_map/ppermute | solution.py:320
  141.1 8.1 %collective-permute-start.25 = (bf16[40,640]{1,0:T(8,128)(2,1)S(1)}, bf16[40,640]{1,0:T(8,128)(2,1)S(1)}, u32[]{:S(2)}, u32[]{:S(2)}) collective-permute-start(bf16[40,640]{1,0:T(8,128)(2,1)S(1)} %get-tuple-element.64), channel_id=1, source_target_pairs={{0,128},{64,192},{128,0},{192,64},{1,129},{65,193},{129,1},{193,65... | collective-permute-start | bytes 153608 | tf_op jit(solution)/shard_map/ppermute | solution.py:320
  144.5 6.8 %collective-permute-start.26 = (bf16[40,640]{1,0:T(8,128)(2,1)S(1)}, bf16[40,640]{1,0:T(8,128)(2,1)S(1)}, u32[]{:S(2)}, u32[]{:S(2)}) collective-permute-start(bf16[40,640]{1,0:T(8,128)(2,1)S(1)} %get-tuple-element.65), channel_id=1, source_target_pairs={{0,192},{64,0},{128,64},{192,128},{1,193},{65,1},{129,65},{193,129... | collective-permute-start | bytes 153608 | tf_op jit(solution)/shard_map/ppermute | solution.py:320
Sparse Core Ops, SparseCore 0:
  35.7 31.0 all-gather.2

commit v11 on v10

--- a/solution.py
+++ b/solution.py
@@ -236,34 +236,25 @@
         flags = jnp.sum(jnp.where(wide, flags, 0.0), axis=1, keepdims=True)
         live[step] = (flags == 2.0).astype(f32)
 
-    def forward(step, carry):
-        rows = pl.ds(pl.multiple_of(step * SLOTS, SLOTS), SLOTS)
+    for step in range(4):
+        rows = slice(step * SLOTS, (step + 1) * SLOTS)
+        masked = (cot[rows, :].astype(f32) * live[step]).astype(bf16)
+        grad_out[rows, :] = masked
         stream = dot(feats[step, :SLOTS, :], proj[...]).astype(bf16).astype(f32)
-        normed[rows, :] = normalize(stream).astype(bf16)
-        pre = dot(normed[rows, :], up[...])
+        grad_hidden = dot(masked, down[...])
+        level = normalize(stream).astype(bf16)
+        normed[rows, :] = level
+        pre = dot(level, up[...])
         cumulative = 0.5 * (1.0 + lax.erf(pre * 0.7071067811865476))
         density = jnp.exp(-0.5 * pre * pre) * 0.3989422804014327
-        hidden[rows, :] = (pre * cumulative).astype(bf16)
-        slope = cumulative + pre * density
-        partial = dot(hidden[rows, :], down[...], ((1,), (1,)))
-
-        @pl.when(step == 0)
-        def _():
+        active = (pre * cumulative).astype(bf16)
+        hidden[rows, :] = active
+        grad_pre[rows, :] = (grad_hidden * (cumulative + pre * density)).astype(bf16)
+        partial = dot(active, down[...], ((1,), (1,)))
+        if step == 0:
             own[...] = partial + stream
-
-        for k, away in enumerate((away1, away2, away3)):
-
-            @pl.when(step == k + 1)
-            def _():
-                away[...] = partial.astype(bf16)
-
-        masked = cot[rows, :].astype(f32) * live[step]
-        grad_out[rows, :] = masked.astype(bf16)
-        grad_hidden = dot(grad_out[rows, :], down[...])
-        grad_pre[rows, :] = (grad_hidden * slope).astype(bf16)
-        return carry
-
-    lax.fori_loop(0, 4, forward, 0)
+        else:
+            (away1, away2, away3)[step - 1][...] = partial.astype(bf16)
 
     def backward(part, carry):
         columns = pl.ds(pl.multiple_of(part * 640, 640), 640)

time: 159 us -> 155 us (0.975)
  Pallas kernels: 29 us -> 24.6 us
    pallas_call x9, Pallas kernels: 29 us -> 24.6 us  [call(): pl.pallas_call(kernel, out_shape=out_shape, in_specs=[SMEM] * smem + [VME...]
where the time goes in v11:
time: 155 us
  starting transfers between devices  59.2 us (38%)
  waiting for transfers between devices  52.9 us (34%)
  Pallas kernels  24.6 us (16%)
  between operations  14.2 us (9%)
  local copies, waits for them, and re-layouts  2.06 us (1%)
    ppermute x27, starting transfers between devices, ring(): lax.ppermute(values, axis, [(k, (k + step) % size) for k in range(size)])  46.9 us
    ppermute x27, waiting for transfers between devices, ring(): lax.ppermute(values, axis, [(k, (k + step) % size) for k in range(size)])  35.1 us
    pallas_call x9, Pallas kernels, call(): pl.pallas_call(kernel, out_shape=out_shape, in_specs=[SMEM] * smem + [VME...  24.6 us
    all_to_all x1, waiting for transfers between devices, per_device(): lax.all_to_all(outgoing.reshape(N_DP, PAD, 1024), dp, split_axis=0, conca...  9.32 us
    all_to_all x1, waiting for transfers between devices, per_device(): blocks = lax.all_to_all(block, 'y', split_axis=0, concat_axis=0, tiled=True)  8.43 us
    all_to_all x1, starting transfers between devices, per_device(): lax.all_to_all(outgoing.reshape(N_DP, PAD, 1024), dp, split_axis=0, conca...  8.39 us
    all_to_all x1, starting transfers between devices, per_device(): blocks = lax.all_to_all(block, 'y', split_axis=0, concat_axis=0, tiled=True)  3.91 us
  transfers between devices with their start and end apart: 30, of which 17 were waited for; matrix products, arithmetic and copies ran while one was open for 1% of the time, Pallas kernels for 4%

profile of v11, /device:TPU:2, one launch (start us, length us, event | category | flops | bytes accessed | tf_op | source)
XLA Modules:
  0.0 154.5 jit_solution(15482222276939452916)
XLA Ops:
  7.2 0.0 all-gather.3.cloned.1.call-start
  7.2 1.0 pack.1
  8.2 2.0 %collective-permute-start = (bf16[40,640]{1,0:T(8,128)(2,1)S(1)}, bf16[40,640]{1,0:T(8,128)(2,1)S(1)}, u32[]{:S(2)}, u32[]{:S(2)}) collective-permute-start(bf16[40,640]{1,0:T(8,128)(2,1)S(1)} %get-tuple-element.34), channel_id=1, source_target_pairs={{0,1},{1,0},{2,3},{3,2},{4,5},{5,4},{6,7},{7,6},{8,9},{9,8},{10,11... | collective-permute-start | bytes 153608 | tf_op jit(solution)/shard_map/ppermute | solution.py:311
  10.2 0.1 collective-permute-start.4
  10.3 2.2 %collective-permute-done = bf16[40,640]{1,0:T(8,128)(2,1)S(1)} collective-permute-done((bf16[40,640]{1,0:T(8,128)(2,1)S(1)}, bf16[40,640]{1,0:T(8,128)(2,1)S(1)}, u32[]{:S(2)}, u32[]{:S(2)}) %collective-permute-start) | collective-permute-done | bytes 51232 | tf_op jit(solution)/shard_map/ppermute | solution.py:311
  12.6 7.6 %collective-permute-start.2 = (bf16[2,40,640]{2,1,0:T(8,128)(2,1)S(1)}, bf16[2,40,640]{2,1,0:T(8,128)(2,1)S(1)}, u32[]{:S(2)}, u32[]{:S(2)}) collective-permute-start(bf16[2,40,640]{2,1,0:T(8,128)(2,1)S(1)} %get-tuple-element.69), channel_id=1, source_target_pairs={{0,128},{64,192},{128,0},{192,64},{1,129},{65,193},{129,1},{193,65... | collective-permute-start | bytes 307208 | tf_op jit(solution)/shard_map/ppermute | solution.py:311
  20.2 3.3 %collective-permute-start.6 = (bf16[2,144,512]{2,1,0:T(8,128)(2,1)S(1)}, bf16[2,144,512]{2,1,0:T(8,128)(2,1)S(1)}, u32[]{:S(2)}, u32[]{:S(2)}) collective-permute-start(bf16[2,144,512]{2,1,0:T(8,128)(2,1)S(1)} %get-tuple-element.67), channel_id=1, source_target_pairs={{0,4},{2,6},{4,0},{6,2},{1,5},{3,7},{5,1},{7,3},{8,12},{10,14},{12... | collective-permute-start | bytes 884744 | tf_op jit(solution)/shard_map/ppermute | solution.py:311
  23.5 0.7 collective-permute-start.5
  24.2 2.6 %collective-permute-start.7 = (bf16[2,144,512]{2,1,0:T(8,128)(2,1)S(1)}, bf16[2,144,512]{2,1,0:T(8,128)(2,1)S(1)}, u32[]{:S(2)}, u32[]{:S(2)}) collective-permute-start(bf16[2,144,512]{2,1,0:T(8,128)(2,1)S(1)} %get-tuple-element.67), channel_id=1, source_target_pairs={{0,6},{2,0},{4,2},{6,4},{1,7},{3,1},{5,3},{7,5},{8,14},{10,8},{12,... | collective-permute-start | bytes 884744 | tf_op jit(solution)/shard_map/ppermute | solution.py:311
  26.8 1.5 collective-permute-start.1
  28.2 2.7 %collective-permute-start.3 = (bf16[2,40,640]{2,1,0:T(8,128)(2,1)S(1)}, bf16[2,40,640]{2,1,0:T(8,128)(2,1)S(1)}, u32[]{:S(2)}, u32[]{:S(2)}) collective-permute-start(bf16[2,40,640]{2,1,0:T(8,128)(2,1)S(1)} %get-tuple-element.69), channel_id=1, source_target_pairs={{0,192},{64,0},{128,64},{192,128},{1,193},{65,1},{129,65},{193,129... | collective-permute-start | bytes 307208 | tf_op jit(solution)/shard_map/ppermute | solution.py:311
  30.9 2.2 %route.1 = bf16[256,1024]{1,0:T(8,128)(2,1)} custom-call(s32[1,128]{1,0:T(1,128)} %bitcast.39, s32[1,128]{1,0:T(1,128)} %bitcast.40, bf16[128,1024]{1,0:T(8,128)(2,1)} %rows_in.1), custom_call_target="tpu_custom_call" | custom-call | flops 75497472 | bytes 1048576 | tf_op jit(solution)/shard_map/route/pallas_call | solution.py:53
  33.1 0.6 collective-permute-done.1
  33.7 1.5 collective-permute-done.3
  35.2 0.1 pad_maximum_fusion.1.refs_0_
  35.3 0.0 copy-start.2
  35.3 0.1 collective-permute-done.7
  35.4 0.1 pad_maximum_fusion.refs_0_.own
  35.5 0.0 all-gather.3.cloned.1.call-update
  35.5 0.1 collective-permute-start.8
  35.6 8.4 %all-to-all-start = ((bf16[32,8,1024]{2,1,0:T(8,128)(2,1)}), bf16[32,8,1024]{2,1,0:T(8,128)(2,1)S(1)}, u32[]{:S(2)}, u32[]{:S(2)}) async-start(bf16[32,8,1024]{2,1,0:T(8,128)(2,1)} %bitcast.20), calls=%async_computation | async-start | bytes 1048576 | tf_op jit(solution)/shard_map/all_to_all | solution.py:355
  44.0 0.3 collective-permute-start.10
  44.3 1.8 %collective-permute-start.9 = (bf16[4,2,40,640]{3,2,1,0:T(8,128)(2,1)S(1)}, bf16[4,2,40,640]{3,2,1,0:T(8,128)(2,1)}, u32[]{:S(2)}, u32[]{:S(2)}) collective-permute-start(bf16[4,2,40,640]{3,2,1,0:T(8,128)(2,1)S(1)} %pad_maximum_fusion.1.refs_0_), channel_id=1, source_target_pairs={{0,16},{16,32},{32,48},{48,0},{1,17},{17,33},{33,49},{49,1},{2,18}... | collective-permute-start | bytes 1228808 | tf_op jit(solution)/shard_map/ppermute | solution.py:311
  46.1 3.3 %collective-permute-start.11 = (bf16[4,2,40,640]{3,2,1,0:T(8,128)(2,1)S(1)}, bf16[4,2,40,640]{3,2,1,0:T(8,128)(2,1)}, u32[]{:S(2)}, u32[]{:S(2)}) collective-permute-start(bf16[4,2,40,640]{3,2,1,0:T(8,128)(2,1)S(1)} %pad_maximum_fusion.1.refs_0_), channel_id=1, source_target_pairs={{0,32},{16,48},{32,0},{48,16},{1,33},{17,49},{33,1},{49,17},{2,34}... | collective-permute-start | bytes 1228808 | tf_op jit(solution)/shard_map/ppermute | solution.py:311
  49.4 0.1 pad_add_fusion.place
  49.5 0.6 proj.1.refs_9_
  50.1 1.0 copy-done
  51.2 9.3 %all-to-all-done = bf16[32,8,1024]{2,1,0:T(8,128)(2,1)S(1)} async-done(((bf16[32,8,1024]{2,1,0:T(8,128)(2,1)}), bf16[32,8,1024]{2,1,0:T(8,128)(2,1)S(1)}, u32[]{:S(2)}, u32[]{:S(2)}) %all-to-all-start) | async-done | bytes 524320 | tf_op jit(solution)/shard_map/all_to_all | solution.py:355
  60.5 3.1 %front.1 = (bf16[4,208,512]{2,1,0:T(8,128)(2,1)S(1)}, f32[192,1]{1,0:T(8,128)S(1)}) custom-call(s32[3]{0:T(128)S(1)} %pad_add_fusion.place, bf16[256,1024]{1,0:T(8,128)(2,1)S(1)} %bitcast.26, bf16[4,2,144,512]{3,2,1,0:T(8,128)(2,1)S(1)} %pad_maximum_fusion.refs_0_.own, bf16[4,2,144,512]{3,2,1,0:T(8,128)(2,1)S(1)} %collective-permute-done.8.refs_1_.other), custom_call_target="tpu_custom_call" | custom-call | flops 268435456 | bytes 2097152 | tf_op jit(solution)/shard_map/front/pallas_call | solution.py:53
  63.6 0.9 copy-done.1
  64.5 3.9 %all-to-all-start.1 = ((bf16[4,208,512]{2,1,0:T(8,128)(2,1)}), bf16[4,208,512]{2,1,0:T(8,128)(2,1)S(1)}, u32[]{:S(2)}, u32[]{:S(2)}) async-start(bf16[4,208,512]{2,1,0:T(8,128)(2,1)} %copy-done.1), calls=%async_computation.1 | async-start | bytes 1703936 | tf_op jit(solution)/shard_map/all_to_all | solution.py:380
  68.4 0.3 collective-permute-start.12
  68.7 1.7 %collective-permute-done.11.refs_2_ = bf16[4,2,40,640]{3,2,1,0:T(8,128)(2,1)} collective-permute-done((bf16[4,2,40,640]{3,2,1,0:T(8,128)(2,1)S(1)}, bf16[4,2,40,640]{3,2,1,0:T(8,128)(2,1)}, u32[]{:S(2)}, u32[]{:S(2)}) %collective-permute-start.11) | collective-permute-done | bytes 409632 | tf_op jit(solution)/shard_map/ppermute | solution.py:311
  70.5 0.5 collective-permute-start.13
  71.0 0.0 collective-permute-start.15
  71.0 0.1 stack.77.place
  71.1 1.4 collective-permute-done.14.refs_6_
  72.4 0.6 collective-permute-done.13.refs_5_
  73.0 0.6 collective-permute-done.15.refs_7_
  73.6 8.4 %all-to-all-done.1.blocks = bf16[4,208,512]{2,1,0:T(8,128)(2,1)S(1)} async-done(((bf16[4,208,512]{2,1,0:T(8,128)(2,1)}), bf16[4,208,512]{2,1,0:T(8,128)(2,1)S(1)}, u32[]{:S(2)}, u32[]{:S(2)}) %all-to-all-start.1) | async-done | bytes 852000 | tf_op jit(solution)/shard_map/all_to_all | solution.py:380
  82.1 16.4 %ffn.1 = (f32[192,1280]{1,0:T(8,128)S(1)}, bf16[192,1280]{1,0:T(8,128)(2,1)S(1)}, bf16[192,1280]{1,0:T(8,128)(2,1)S(1)}, bf16[192,1280]{1,0:T(8,128)(2,1)S(1)}, ...) custom-call(s32[5]{0:T(128)S(1)} %stack.77.place, ...), custom_call_target="tpu_custom_call" | custom-call | flops 8556380160 | bytes 16777216 | tf_op jit(solution)/shard_map/ffn/pallas_call | solution.py:53
  98.4 0.1 collective-permute-start.16
  98.5 3.5 %collective-permute-done.16.arrived = bf16[4,8,40,640]{3,2,1,0:T(8,128)(2,1)S(1)} collective-permute-done((bf16[4,8,40,640]{3,2,1,0:T(8,128)(2,1)S(1)}, bf16[4,8,40,640]{3,2,1,0:T(8,128)(2,1)S(1)}, u32[]{:S(2)}, u32[]{:S(2)}) %collective-permute-start.16) | collective-permute-done | bytes 1638432 | tf_op jit(solution)/shard_map/ppermute | solution.py:311
  102.0 0.4 core_sum.1
  102.4 0.6 collective-permute-start.20
  103.0 5.7 %collective-permute-start.21 = (bf16[8,40,640]{2,1,0:T(8,128)(2,1)S(1)}, bf16[8,40,640]{2,1,0:T(8,128)(2,1)S(1)}, u32[]{:S(2)}, u32[]{:S(2)}) collective-permute-start(bf16[8,40,640]{2,1,0:T(8,128)(2,1)S(1)} %get-tuple-element.58), channel_id=1, source_target_pairs={{0,32},{16,48},{32,0},{48,16},{1,33},{17,49},{33,1},{49,17},{2,34}... | collective-permute-start | bytes 1228808 | tf_op jit(solution)/shard_map/ppermute | solution.py:311
  108.7 1.2 collective-permute-start.17
  109.9 1.5 collective-permute-start.18
  111.3 5.5 %collective-permute-done.20.refs_1_ = bf16[8,40,640]{2,1,0:T(8,128)(2,1)S(1)} collective-permute-done((bf16[8,40,640]{2,1,0:T(8,128)(2,1)S(1)}, bf16[8,40,640]{2,1,0:T(8,128)(2,1)S(1)}, u32[]{:S(2)}, u32[]{:S(2)}) %collective-permute-start.20) | collective-permute-done | bytes 409632 | tf_op jit(solution)/shard_map/ppermute | solution.py:311
  116.9 0.6 collective-permute-start.19
  117.5 1.6 %collective-permute-done.21.refs_2_ = bf16[8,40,640]{2,1,0:T(8,128)(2,1)S(1)} collective-permute-done((bf16[8,40,640]{2,1,0:T(8,128)(2,1)S(1)}, bf16[8,40,640]{2,1,0:T(8,128)(2,1)S(1)}, u32[]{:S(2)}, u32[]{:S(2)}) %collective-permute-start.21) | collective-permute-done | bytes 409632 | tf_op jit(solution)/shard_map/ppermute | solution.py:311
  119.0 7.9 %collective-permute-done.22.refs_3_ = bf16[8,40,640]{2,1,0:T(8,128)(2,1)S(1)} collective-permute-done((bf16[8,40,640]{2,1,0:T(8,128)(2,1)S(1)}, bf16[8,40,640]{2,1,0:T(8,128)(2,1)S(1)}, u32[]{:S(2)}, u32[]{:S(2)}) %collective-permute-start.22) | collective-permute-done | bytes 409632 | tf_op jit(solution)/shard_map/ppermute | solution.py:311
  127.0 0.2 x_sum.1
  127.2 4.1 %collective-permute-start.23 = (bf16[4,40,640]{2,1,0:T(8,128)(2,1)S(1)}, bf16[4,40,640]{2,1,0:T(8,128)(2,1)S(1)}, u32[]{:S(2)}, u32[]{:S(2)}) collective-permute-start(bf16[4,40,640]{2,1,0:T(8,128)(2,1)S(1)} %get-tuple-element.61), channel_id=1, source_target_pairs={{0,1},{1,0},{2,3},{3,2},{4,5},{5,4},{6,7},{7,6},{8,9},{9,8},{10,11... | collective-permute-start | bytes 614408 | tf_op jit(solution)/shard_map/ppermute | solution.py:311
  131.3 0.1 convert_reduce_fusion
  131.4 5.2 %collective-permute-done.23.arrived = bf16[4,40,640]{2,1,0:T(8,128)(2,1)S(1)} collective-permute-done((bf16[4,40,640]{2,1,0:T(8,128)(2,1)S(1)}, bf16[4,40,640]{2,1,0:T(8,128)(2,1)S(1)}, u32[]{:S(2)}, u32[]{:S(2)}) %collective-permute-start.23) | collective-permute-done | bytes 204832 | tf_op jit(solution)/shard_map/ppermute | solution.py:311
  136.6 0.1 z_sum.1
  136.6 0.1 collective-permute-start.24
  136.7 3.4 %collective-permute-start.25 = (bf16[40,640]{1,0:T(8,128)(2,1)S(1)}, bf16[40,640]{1,0:T(8,128)(2,1)S(1)}, u32[]{:S(2)}, u32[]{:S(2)}) collective-permute-start(bf16[40,640]{1,0:T(8,128)(2,1)S(1)} %get-tuple-element.64), channel_id=1, source_target_pairs={{0,128},{64,192},{128,0},{192,64},{1,129},{65,193},{129,1},{193,65... | collective-permute-start | bytes 153608 | tf_op jit(solution)/shard_map/ppermute | solution.py:311
  140.1 2.9 %collective-permute-start.26 = (bf16[40,640]{1,0:T(8,128)(2,1)S(1)}, bf16[40,640]{1,0:T(8,128)(2,1)S(1)}, u32[]{:S(2)}, u32[]{:S(2)}) collective-permute-start(bf16[40,640]{1,0:T(8,128)(2,1)S(1)} %get-tuple-element.65), channel_id=1, source_target_pairs={{0,192},{64,0},{128,64},{192,128},{1,193},{65,1},{129,65},{193,129... | collective-permute-start | bytes 153608 | tf_op jit(solution)/shard_map/ppermute | solution.py:311
  143.1 1.1 multiply_convert_fusion
  144.1 0.7 collective-permute-done.25.refs_2_
  144.8 2.1 %collective-permute-done.26.refs_3_ = bf16[40,640]{1,0:T(8,128)(2,1)S(1)} collective-permute-done((bf16[40,640]{1,0:T(8,128)(2,1)S(1)}, bf16[40,640]{1,0:T(8,128)(2,1)S(1)}, u32[]{:S(2)}, u32[]{:S(2)}) %collective-permute-start.26) | collective-permute-done | bytes 51232 | tf_op jit(solution)/shard_map/ppermute | solution.py:311
  146.9 0.7 last.1
  (28 shorter events, 0.1 us)
Async XLA Ops:
  7.2 74.9 %all-gather.3.cloned.1.call-start = ((), (), s32[]{:S(2)}) async-start(), calls=%async_computation.2 | async-start | bytes 2457600 | tf_op jit(solution)/shard_map/all_gather | solution.py:352
  8.2 4.3 %collective-permute-start = (bf16[40,640]{1,0:T(8,128)(2,1)S(1)}, bf16[40,640]{1,0:T(8,128)(2,1)S(1)}, u32[]{:S(2)}, u32[]{:S(2)}) collective-permute-start(bf16[40,640]{1,0:T(8,128)(2,1)S(1)} %get-tuple-element.34), channel_id=1, source_target_pairs={{0,1},{1,0},{2,3},{3,2},{4,5},{5,4},{6,7},{7,6},{8,9},{9,8},{10,11... | collective-permute-start | bytes 153608 | tf_op jit(solution)/shard_map/ppermute | solution.py:311
  10.2 10.0 %collective-permute-start.4 = (bf16[144,512]{1,0:T(8,128)(2,1)S(1)}, bf16[144,512]{1,0:T(8,128)(2,1)S(1)}, u32[]{:S(2)}, u32[]{:S(2)}) collective-permute-start(bf16[144,512]{1,0:T(8,128)(2,1)S(1)} %get-tuple-element.35), channel_id=1, source_target_pairs={{0,1},{1,0},{2,3},{3,2},{4,5},{5,4},{6,7},{7,6},{8,9},{9,8},{10,11... | collective-permute-start | bytes 442376 | tf_op jit(solution)/shard_map/ppermute | solution.py:311
  12.6 15.7 %collective-permute-start.2 = (bf16[2,40,640]{2,1,0:T(8,128)(2,1)S(1)}, bf16[2,40,640]{2,1,0:T(8,128)(2,1)S(1)}, u32[]{:S(2)}, u32[]{:S(2)}) collective-permute-start(bf16[2,40,640]{2,1,0:T(8,128)(2,1)S(1)} %get-tuple-element.69), channel_id=1, source_target_pairs={{0,128},{64,192},{128,0},{192,64},{1,129},{65,193},{129,1},{193,65... | collective-permute-start | bytes 307208 | tf_op jit(solution)/shard_map/ppermute | solution.py:311
  20.2 15.0 %collective-permute-start.6 = (bf16[2,144,512]{2,1,0:T(8,128)(2,1)S(1)}, bf16[2,144,512]{2,1,0:T(8,128)(2,1)S(1)}, u32[]{:S(2)}, u32[]{:S(2)}) collective-permute-start(bf16[2,144,512]{2,1,0:T(8,128)(2,1)S(1)} %get-tuple-element.67), channel_id=1, source_target_pairs={{0,4},{2,6},{4,0},{6,2},{1,5},{3,7},{5,1},{7,3},{8,12},{10,14},{12... | collective-permute-start | bytes 884744 | tf_op jit(solution)/shard_map/ppermute | solution.py:311
  23.5 11.8 %collective-permute-start.5 = (bf16[2,144,512]{2,1,0:T(8,128)(2,1)S(1)}, bf16[2,144,512]{2,1,0:T(8,128)(2,1)S(1)}, u32[]{:S(2)}, u32[]{:S(2)}) collective-permute-start(bf16[2,144,512]{2,1,0:T(8,128)(2,1)S(1)} %get-tuple-element.67), channel_id=1, source_target_pairs={{0,2},{2,4},{4,6},{6,0},{1,3},{3,5},{5,7},{7,1},{8,10},{10,12},{12... | collective-permute-start | bytes 884744 | tf_op jit(solution)/shard_map/ppermute | solution.py:311
  24.2 11.2 %collective-permute-start.7 = (bf16[2,144,512]{2,1,0:T(8,128)(2,1)S(1)}, bf16[2,144,512]{2,1,0:T(8,128)(2,1)S(1)}, u32[]{:S(2)}, u32[]{:S(2)}) collective-permute-start(bf16[2,144,512]{2,1,0:T(8,128)(2,1)S(1)} %get-tuple-element.67), channel_id=1, source_target_pairs={{0,6},{2,0},{4,2},{6,4},{1,7},{3,1},{5,3},{7,5},{8,14},{10,8},{12,... | collective-permute-start | bytes 884744 | tf_op jit(solution)/shard_map/ppermute | solution.py:311
  26.8 6.9 %collective-permute-start.1 = (bf16[2,40,640]{2,1,0:T(8,128)(2,1)S(1)}, bf16[2,40,640]{2,1,0:T(8,128)(2,1)S(1)}, u32[]{:S(2)}, u32[]{:S(2)}) collective-permute-start(bf16[2,40,640]{2,1,0:T(8,128)(2,1)S(1)} %get-tuple-element.69), channel_id=1, source_target_pairs={{0,64},{64,128},{128,192},{192,0},{1,65},{65,129},{129,193},{193,1... | collective-permute-start | bytes 307208 | tf_op jit(solution)/shard_map/ppermute | solution.py:311
  28.2 7.0 %collective-permute-start.3 = (bf16[2,40,640]{2,1,0:T(8,128)(2,1)S(1)}, bf16[2,40,640]{2,1,0:T(8,128)(2,1)S(1)}, u32[]{:S(2)}, u32[]{:S(2)}) collective-permute-start(bf16[2,40,640]{2,1,0:T(8,128)(2,1)S(1)} %get-tuple-element.69), channel_id=1, source_target_pairs={{0,192},{64,0},{128,64},{192,128},{1,193},{65,1},{129,65},{193,129... | collective-permute-start | bytes 307208 | tf_op jit(solution)/shard_map/ppermute | solution.py:311
  35.3 33.2 %copy-start.2 = (bf16[4,2,40,640]{3,2,1,0:T(8,128)(2,1)}, bf16[4,2,40,640]{3,2,1,0:T(8,128)(2,1)S(1)}, u32[]{:S(2)}) copy-start(bf16[4,2,40,640]{3,2,1,0:T(8,128)(2,1)S(1)} %pad_maximum_fusion.1.refs_0_) | copy-start | bytes 1228804
  35.5 14.0 %collective-permute-start.8 = (bf16[4,2,144,512]{3,2,1,0:T(8,128)(2,1)S(1)}, bf16[4,2,144,512]{3,2,1,0:T(8,128)(2,1)S(1)}, u32[]{:S(2)}, u32[]{:S(2)}) collective-permute-start(bf16[4,2,144,512]{3,2,1,0:T(8,128)(2,1)S(1)} %pad_maximum_fusion.refs_0_.own), channel_id=1, source_target_pairs={{0,8},{8,0},{1,9},{9,1},{2,10},{10,2},{3,11},{11,3},{4,12},{12,4},... | collective-permute-start | bytes 3538952 | tf_op jit(solution)/shard_map/ppermute | solution.py:311
  35.6 24.9 %all-to-all-start = ((bf16[32,8,1024]{2,1,0:T(8,128)(2,1)}), bf16[32,8,1024]{2,1,0:T(8,128)(2,1)S(1)}, u32[]{:S(2)}, u32[]{:S(2)}) async-start(bf16[32,8,1024]{2,1,0:T(8,128)(2,1)} %bitcast.20), calls=%async_computation | async-start | bytes 1048576 | tf_op jit(solution)/shard_map/all_to_all | solution.py:355
  44.0 20.5 %collective-permute-start.10 = (bf16[4,2,40,640]{3,2,1,0:T(8,128)(2,1)S(1)}, bf16[4,2,40,640]{3,2,1,0:T(8,128)(2,1)}, u32[]{:S(2)}, u32[]{:S(2)}) collective-permute-start(bf16[4,2,40,640]{3,2,1,0:T(8,128)(2,1)S(1)} %pad_maximum_fusion.1.refs_0_), channel_id=1, source_target_pairs={{0,48},{16,0},{32,16},{48,32},{1,49},{17,1},{33,17},{49,33},{2,50}... | collective-permute-start | bytes 1228808 | tf_op jit(solution)/shard_map/ppermute | solution.py:311
  44.3 20.2 %collective-permute-start.9 = (bf16[4,2,40,640]{3,2,1,0:T(8,128)(2,1)S(1)}, bf16[4,2,40,640]{3,2,1,0:T(8,128)(2,1)}, u32[]{:S(2)}, u32[]{:S(2)}) collective-permute-start(bf16[4,2,40,640]{3,2,1,0:T(8,128)(2,1)S(1)} %pad_maximum_fusion.1.refs_0_), channel_id=1, source_target_pairs={{0,16},{16,32},{32,48},{48,0},{1,17},{17,33},{33,49},{49,1},{2,18}... | collective-permute-start | bytes 1228808 | tf_op jit(solution)/shard_map/ppermute | solution.py:311
  46.1 24.3 %collective-permute-start.11 = (bf16[4,2,40,640]{3,2,1,0:T(8,128)(2,1)S(1)}, bf16[4,2,40,640]{3,2,1,0:T(8,128)(2,1)}, u32[]{:S(2)}, u32[]{:S(2)}) collective-permute-start(bf16[4,2,40,640]{3,2,1,0:T(8,128)(2,1)S(1)} %pad_maximum_fusion.1.refs_0_), channel_id=1, source_target_pairs={{0,32},{16,48},{32,0},{48,16},{1,33},{17,49},{33,1},{49,17},{2,34}... | collective-permute-start | bytes 1228808 | tf_op jit(solution)/shard_map/ppermute | solution.py:311
  50.1 1.1 copy-start
  63.6 0.9 copy-start.1
  64.5 17.5 %all-to-all-start.1 = ((bf16[4,208,512]{2,1,0:T(8,128)(2,1)}), bf16[4,208,512]{2,1,0:T(8,128)(2,1)S(1)}, u32[]{:S(2)}, u32[]{:S(2)}) async-start(bf16[4,208,512]{2,1,0:T(8,128)(2,1)} %copy-done.1), calls=%async_computation.1 | async-start | bytes 1703936 | tf_op jit(solution)/shard_map/all_to_all | solution.py:380
  68.4 2.6 %collective-permute-start.12 = (bf16[4,2,40,640]{3,2,1,0:T(8,128)(2,1)S(1)}, bf16[4,2,40,640]{3,2,1,0:T(8,128)(2,1)S(1)}, u32[]{:S(2)}, u32[]{:S(2)}) collective-permute-start(bf16[4,2,40,640]{3,2,1,0:T(8,128)(2,1)S(1)} %pad_maximum_fusion.1.refs_0_), channel_id=1, source_target_pairs={{0,8},{8,0},{1,9},{9,1},{2,10},{10,2},{3,11},{11,3},{4,12},{12,4},... | collective-permute-start | bytes 1228808 | tf_op jit(solution)/shard_map/ppermute | solution.py:311
  70.5 2.0 %collective-permute-start.14 = (bf16[4,2,40,640]{3,2,1,0:T(8,128)(2,1)}, bf16[4,2,40,640]{3,2,1,0:T(8,128)(2,1)S(1)}, u32[]{:S(2)}, u32[]{:S(2)}) collective-permute-start(bf16[4,2,40,640]{3,2,1,0:T(8,128)(2,1)} %collective-permute-done.11.refs_2_), channel_id=1, source_target_pairs={{0,8},{8,0},{1,9},{9,1},{2,10},{10,2},{3,11},{11,3},{4,12},{12,4},... | collective-permute-start | bytes 1228808 | tf_op jit(solution)/shard_map/ppermute | solution.py:311
  70.5 2.5 %collective-permute-start.13 = (bf16[4,2,40,640]{3,2,1,0:T(8,128)(2,1)}, bf16[4,2,40,640]{3,2,1,0:T(8,128)(2,1)S(1)}, u32[]{:S(2)}, u32[]{:S(2)}) collective-permute-start(bf16[4,2,40,640]{3,2,1,0:T(8,128)(2,1)} %collective-permute-done.9.refs_1_), channel_id=1, source_target_pairs={{0,8},{8,0},{1,9},{9,1},{2,10},{10,2},{3,11},{11,3},{4,12},{12,4},... | collective-permute-start | bytes 1228808 | tf_op jit(solution)/shard_map/ppermute | solution.py:311
  71.0 2.6 %collective-permute-start.15 = (bf16[4,2,40,640]{3,2,1,0:T(8,128)(2,1)}, bf16[4,2,40,640]{3,2,1,0:T(8,128)(2,1)S(1)}, u32[]{:S(2)}, u32[]{:S(2)}) collective-permute-start(bf16[4,2,40,640]{3,2,1,0:T(8,128)(2,1)} %collective-permute-done.10.refs_3_), channel_id=1, source_target_pairs={{0,8},{8,0},{1,9},{9,1},{2,10},{10,2},{3,11},{11,3},{4,12},{12,4},... | collective-permute-start | bytes 1228808 | tf_op jit(solution)/shard_map/ppermute | solution.py:311
  71.1 11.0 %copy-start.3 = (bf16[4,2,40,640]{3,2,1,0:T(8,128)(2,1)}, bf16[4,2,40,640]{3,2,1,0:T(8,128)(2,1)S(1)}, u32[]{:S(2)}) copy-start(bf16[4,2,40,640]{3,2,1,0:T(8,128)(2,1)S(1)} %collective-permute-done.12.refs_4_) | copy-start | bytes 1228804
  72.4 9.6 %copy-start.4 = (bf16[4,2,40,640]{3,2,1,0:T(8,128)(2,1)}, bf16[4,2,40,640]{3,2,1,0:T(8,128)(2,1)S(1)}, u32[]{:S(2)}) copy-start(bf16[4,2,40,640]{3,2,1,0:T(8,128)(2,1)S(1)} %collective-permute-done.14.refs_6_) | copy-start | bytes 1228804
  73.0 9.0 %copy-start.5 = (bf16[4,2,40,640]{3,2,1,0:T(8,128)(2,1)}, bf16[4,2,40,640]{3,2,1,0:T(8,128)(2,1)S(1)}, u32[]{:S(2)}) copy-start(bf16[4,2,40,640]{3,2,1,0:T(8,128)(2,1)S(1)} %collective-permute-done.13.refs_5_) | copy-start | bytes 1228804
  73.6 8.4 %copy-start.6 = (bf16[4,2,40,640]{3,2,1,0:T(8,128)(2,1)}, bf16[4,2,40,640]{3,2,1,0:T(8,128)(2,1)S(1)}, u32[]{:S(2)}) copy-start(bf16[4,2,40,640]{3,2,1,0:T(8,128)(2,1)S(1)} %collective-permute-done.15.refs_7_) | copy-start | bytes 1228804
  98.4 3.6 %collective-permute-start.16 = (bf16[4,8,40,640]{3,2,1,0:T(8,128)(2,1)S(1)}, bf16[4,8,40,640]{3,2,1,0:T(8,128)(2,1)S(1)}, u32[]{:S(2)}, u32[]{:S(2)}) collective-permute-start(bf16[4,8,40,640]{3,2,1,0:T(8,128)(2,1)S(1)} %get-tuple-element.51), channel_id=1, source_target_pairs={{0,8},{8,0},{1,9},{9,1},{2,10},{10,2},{3,11},{11,3},{4,12},{12,4},... | collective-permute-start | bytes 4915208 | tf_op jit(solution)/shard_map/ppermute | solution.py:311
  102.4 14.5 %collective-permute-start.20 = (bf16[8,40,640]{2,1,0:T(8,128)(2,1)S(1)}, bf16[8,40,640]{2,1,0:T(8,128)(2,1)S(1)}, u32[]{:S(2)}, u32[]{:S(2)}) collective-permute-start(bf16[8,40,640]{2,1,0:T(8,128)(2,1)S(1)} %get-tuple-element.57), channel_id=1, source_target_pairs={{0,16},{16,32},{32,48},{48,0},{1,17},{17,33},{33,49},{49,1},{2,18}... | collective-permute-start | bytes 1228808 | tf_op jit(solution)/shard_map/ppermute | solution.py:311
  103.0 16.0 %collective-permute-start.21 = (bf16[8,40,640]{2,1,0:T(8,128)(2,1)S(1)}, bf16[8,40,640]{2,1,0:T(8,128)(2,1)S(1)}, u32[]{:S(2)}, u32[]{:S(2)}) collective-permute-start(bf16[8,40,640]{2,1,0:T(8,128)(2,1)S(1)} %get-tuple-element.58), channel_id=1, source_target_pairs={{0,32},{16,48},{32,0},{48,16},{1,33},{17,49},{33,1},{49,17},{2,34}... | collective-permute-start | bytes 1228808 | tf_op jit(solution)/shard_map/ppermute | solution.py:311
  108.7 18.3 %collective-permute-start.22 = (bf16[8,40,640]{2,1,0:T(8,128)(2,1)S(1)}, bf16[8,40,640]{2,1,0:T(8,128)(2,1)S(1)}, u32[]{:S(2)}, u32[]{:S(2)}) collective-permute-start(bf16[8,40,640]{2,1,0:T(8,128)(2,1)S(1)} %get-tuple-element.59), channel_id=1, source_target_pairs={{0,48},{16,0},{32,16},{48,32},{1,49},{17,1},{33,17},{49,33},{2,50}... | collective-permute-start | bytes 1228808 | tf_op jit(solution)/shard_map/ppermute | solution.py:311
  108.7 31.4 %collective-permute-start.17 = (bf16[192,1280]{1,0:T(8,128)(2,1)S(1)}, bf16[192,1280]{1,0:T(8,128)(2,1)S(1)}, u32[]{:S(2)}, u32[]{:S(2)}) collective-permute-start(bf16[192,1280]{1,0:T(8,128)(2,1)S(1)} %get-tuple-element.53), channel_id=1, source_target_pairs={{0,6},{2,0},{4,2},{6,4},{1,7},{3,1},{5,3},{7,5},{8,14},{10,8},{12,... | collective-permute-start | bytes 1474568 | tf_op jit(solution)/shard_map/ppermute | solution.py:311
  109.9 33.2 %collective-permute-start.18 = (bf16[192,1280]{1,0:T(8,128)(2,1)S(1)}, bf16[192,1280]{1,0:T(8,128)(2,1)S(1)}, u32[]{:S(2)}, u32[]{:S(2)}) collective-permute-start(bf16[192,1280]{1,0:T(8,128)(2,1)S(1)} %get-tuple-element.54), channel_id=1, source_target_pairs={{0,4},{2,6},{4,0},{6,2},{1,5},{3,7},{5,1},{7,3},{8,12},{10,14},{12... | collective-permute-start | bytes 1474568 | tf_op jit(solution)/shard_map/ppermute | solution.py:311
  116.9 26.2 %collective-permute-start.19 = (bf16[192,1280]{1,0:T(8,128)(2,1)S(1)}, bf16[192,1280]{1,0:T(8,128)(2,1)S(1)}, u32[]{:S(2)}, u32[]{:S(2)}) collective-permute-start(bf16[192,1280]{1,0:T(8,128)(2,1)S(1)} %get-tuple-element.55), channel_id=1, source_target_pairs={{0,2},{2,4},{4,6},{6,0},{1,3},{3,5},{5,7},{7,1},{8,10},{10,12},{12... | collective-permute-start | bytes 1474568 | tf_op jit(solution)/shard_map/ppermute | solution.py:311
  127.2 9.4 %collective-permute-start.23 = (bf16[4,40,640]{2,1,0:T(8,128)(2,1)S(1)}, bf16[4,40,640]{2,1,0:T(8,128)(2,1)S(1)}, u32[]{:S(2)}, u32[]{:S(2)}) collective-permute-start(bf16[4,40,640]{2,1,0:T(8,128)(2,1)S(1)} %get-tuple-element.61), channel_id=1, source_target_pairs={{0,1},{1,0},{2,3},{3,2},{4,5},{5,4},{6,7},{7,6},{8,9},{9,8},{10,11... | collective-permute-start | bytes 614408 | tf_op jit(solution)/shard_map/ppermute | solution.py:311
  136.6 7.5 %collective-permute-start.24 = (bf16[40,640]{1,0:T(8,128)(2,1)S(1)}, bf16[40,640]{1,0:T(8,128)(2,1)S(1)}, u32[]{:S(2)}, u32[]{:S(2)}) collective-permute-start(bf16[40,640]{1,0:T(8,128)(2,1)S(1)} %get-tuple-element.63), channel_id=1, source_target_pairs={{0,64},{64,128},{128,192},{192,0},{1,65},{65,129},{129,193},{193,1... | collective-permute-start | bytes 153608 | tf_op jit(solution)/shard_map/ppermute | solution.py:311
  136.7 8.1 %collective-permute-start.25 = (bf16[40,640]{1,0:T(8,128)(2,1)S(1)}, bf16[40,640]{1,0:T(8,128)(2,1)S(1)}, u32[]{:S(2)}, u32[]{:S(2)}) collective-permute-start(bf16[40,640]{1,0:T(8,128)(2,1)S(1)} %get-tuple-element.64), channel_id=1, source_target_pairs={{0,128},{64,192},{128,0},{192,64},{1,129},{65,193},{129,1},{193,65... | collective-permute-start | bytes 153608 | tf_op jit(solution)/shard_map/ppermute | solution.py:311
  140.1 6.8 %collective-permute-start.26 = (bf16[40,640]{1,0:T(8,128)(2,1)S(1)}, bf16[40,640]{1,0:T(8,128)(2,1)S(1)}, u32[]{:S(2)}, u32[]{:S(2)}) collective-permute-start(bf16[40,640]{1,0:T(8,128)(2,1)S(1)} %get-tuple-element.65), channel_id=1, source_target_pairs={{0,192},{64,0},{128,64},{192,128},{1,193},{65,1},{129,65},{193,129... | collective-permute-start | bytes 153608 | tf_op jit(solution)/shard_map/ppermute | solution.py:311
Sparse Core Ops, SparseCore 0:
  35.7 31.0 all-gather.2

commit v12 on v11

--- a/solution.py
+++ b/solution.py
@@ -256,27 +256,24 @@
         else:
             (away1, away2, away3)[step - 1][...] = partial.astype(bf16)
 
-    def backward(part, carry):
-        columns = pl.ds(pl.multiple_of(part * 640, 640), 640)
+    for part in range(2):
+        columns = slice(part * 640, (part + 1) * 640)
         first = ((0,), (0,))
-        wide_up[...] = dot(normed[:, columns], grad_pre[...], first)
-        wide_down[...] = dot(grad_out[:, columns], hidden[...], first)
+        wide_up[part] = dot(normed[:, columns], grad_pre[...], first)
+        wide_down[part] = dot(grad_out[:, columns], hidden[...], first)
 
         def place_block(k, carry):
-            zh, x = k // 4, lax.rem(k, 4)
+            high, along = k // 4, lax.rem(k, 4)
             for other, out in enumerate((kept, sent)):
-                row = zh * 320 + x * 80 + lax.rem(c + other, 2) * BLOCK
+                row = high * 320 + along * 80 + lax.rem(c + other, 2) * BLOCK
                 rows = pl.ds(pl.multiple_of(row, 8), BLOCK)
                 for half in range(2):
                     lanes = slice(half * LANES, (half + 1) * LANES)
-                    block = pack_pair(wide_up[rows, lanes], wide_down[rows, lanes])
-                    out[x, (part * 2 + zh) * 2 + half] = block.astype(bf16)
+                    block = pack_pair(wide_up[part, rows, lanes], wide_down[part, rows, lanes])
+                    out[along, (part * 2 + high) * 2 + half] = block.astype(bf16)
             return carry
 
-        lax.fori_loop(0, 8, place_block, 0)
-        return carry
-
-    lax.fori_loop(0, 2, backward, 0)
+        lax.fori_loop(0, 8, place_block, 0, unroll=True)
 
 
 def core_sum_kernel(place, kept, arrived, *outs):
@@ -396,8 +393,8 @@
             pltpu.VMEM((rows, WIDE), bf16),
             pltpu.VMEM((rows, WIDE), bf16),
             pltpu.VMEM((rows, D), bf16),
-            pltpu.VMEM((640, WIDE), f32),
-            pltpu.VMEM((640, WIDE), f32),
+            pltpu.VMEM((2, 640, WIDE), f32),
+            pltpu.VMEM((2, 640, WIDE), f32),
             pltpu.VMEM((rows, D), bf16),
             pltpu.VMEM((D, WIDE), bf16),
             pltpu.VMEM((D, WIDE), bf16),

time: 155 us -> 154 us (level)
  no operation moved by 1% of the time
where the time goes in v12:
time: 154 us
  starting transfers between devices  59.4 us (39%)
  waiting for transfers between devices  52.9 us (34%)
  Pallas kernels  23.7 us (15%)
  between operations  14.2 us (9%)
  local copies, waits for them, and re-layouts  2.06 us (1%)
    ppermute x27, starting transfers between devices, ring(): lax.ppermute(values, axis, [(k, (k + step) % size) for k in range(size)])  47.1 us
    ppermute x27, waiting for transfers between devices, ring(): lax.ppermute(values, axis, [(k, (k + step) % size) for k in range(size)])  35.1 us
    pallas_call x9, Pallas kernels, call(): pl.pallas_call(kernel, out_shape=out_shape, in_specs=[SMEM] * smem + [VME...  23.7 us
    all_to_all x1, waiting for transfers between devices, per_device(): lax.all_to_all(outgoing.reshape(N_DP, PAD, 1024), dp, split_axis=0, conca...  9.32 us
    all_to_all x1, waiting for transfers between devices, per_device(): blocks = lax.all_to_all(block, 'y', split_axis=0, concat_axis=0, tiled=True)  8.43 us
    all_to_all x1, starting transfers between devices, per_device(): lax.all_to_all(outgoing.reshape(N_DP, PAD, 1024), dp, split_axis=0, conca...  8.39 us
    all_to_all x1, starting transfers between devices, per_device(): blocks = lax.all_to_all(block, 'y', split_axis=0, concat_axis=0, tiled=True)  3.91 us
  transfers between devices with their start and end apart: 30, of which 17 were waited for; matrix products, arithmetic and copies ran while one was open for 1% of the time, Pallas kernels for 4%

profile of v12, /device:TPU:2, one launch (start us, length us, event | category | flops | bytes accessed | tf_op | source)
XLA Modules:
  0.0 153.8 jit_solution(16911051358033736403)
XLA Ops:
  7.2 0.0 all-gather.3.cloned.1.call-start
  7.2 1.0 pack.1
  8.2 2.0 %collective-permute-start = (bf16[40,640]{1,0:T(8,128)(2,1)S(1)}, bf16[40,640]{1,0:T(8,128)(2,1)S(1)}, u32[]{:S(2)}, u32[]{:S(2)}) collective-permute-start(bf16[40,640]{1,0:T(8,128)(2,1)S(1)} %get-tuple-element.34), channel_id=1, source_target_pairs={{0,1},{1,0},{2,3},{3,2},{4,5},{5,4},{6,7},{7,6},{8,9},{9,8},{10,11... | collective-permute-start | bytes 153608 | tf_op jit(solution)/shard_map/ppermute | solution.py:308
  10.2 0.1 collective-permute-start.4
  10.3 2.2 %collective-permute-done = bf16[40,640]{1,0:T(8,128)(2,1)S(1)} collective-permute-done((bf16[40,640]{1,0:T(8,128)(2,1)S(1)}, bf16[40,640]{1,0:T(8,128)(2,1)S(1)}, u32[]{:S(2)}, u32[]{:S(2)}) %collective-permute-start) | collective-permute-done | bytes 51232 | tf_op jit(solution)/shard_map/ppermute | solution.py:308
  12.6 7.6 %collective-permute-start.2 = (bf16[2,40,640]{2,1,0:T(8,128)(2,1)S(1)}, bf16[2,40,640]{2,1,0:T(8,128)(2,1)S(1)}, u32[]{:S(2)}, u32[]{:S(2)}) collective-permute-start(bf16[2,40,640]{2,1,0:T(8,128)(2,1)S(1)} %get-tuple-element.69), channel_id=1, source_target_pairs={{0,128},{64,192},{128,0},{192,64},{1,129},{65,193},{129,1},{193,65... | collective-permute-start | bytes 307208 | tf_op jit(solution)/shard_map/ppermute | solution.py:308
  20.2 3.3 %collective-permute-start.6 = (bf16[2,144,512]{2,1,0:T(8,128)(2,1)S(1)}, bf16[2,144,512]{2,1,0:T(8,128)(2,1)S(1)}, u32[]{:S(2)}, u32[]{:S(2)}) collective-permute-start(bf16[2,144,512]{2,1,0:T(8,128)(2,1)S(1)} %get-tuple-element.67), channel_id=1, source_target_pairs={{0,4},{2,6},{4,0},{6,2},{1,5},{3,7},{5,1},{7,3},{8,12},{10,14},{12... | collective-permute-start | bytes 884744 | tf_op jit(solution)/shard_map/ppermute | solution.py:308
  23.5 0.7 collective-permute-start.5
  24.2 2.6 %collective-permute-start.7 = (bf16[2,144,512]{2,1,0:T(8,128)(2,1)S(1)}, bf16[2,144,512]{2,1,0:T(8,128)(2,1)S(1)}, u32[]{:S(2)}, u32[]{:S(2)}) collective-permute-start(bf16[2,144,512]{2,1,0:T(8,128)(2,1)S(1)} %get-tuple-element.67), channel_id=1, source_target_pairs={{0,6},{2,0},{4,2},{6,4},{1,7},{3,1},{5,3},{7,5},{8,14},{10,8},{12,... | collective-permute-start | bytes 884744 | tf_op jit(solution)/shard_map/ppermute | solution.py:308
  26.8 1.5 collective-permute-start.1
  28.2 2.7 %collective-permute-start.3 = (bf16[2,40,640]{2,1,0:T(8,128)(2,1)S(1)}, bf16[2,40,640]{2,1,0:T(8,128)(2,1)S(1)}, u32[]{:S(2)}, u32[]{:S(2)}) collective-permute-start(bf16[2,40,640]{2,1,0:T(8,128)(2,1)S(1)} %get-tuple-element.69), channel_id=1, source_target_pairs={{0,192},{64,0},{128,64},{192,128},{1,193},{65,1},{129,65},{193,129... | collective-permute-start | bytes 307208 | tf_op jit(solution)/shard_map/ppermute | solution.py:308
  30.9 2.2 %route.1 = bf16[256,1024]{1,0:T(8,128)(2,1)} custom-call(s32[1,128]{1,0:T(1,128)} %bitcast.39, s32[1,128]{1,0:T(1,128)} %bitcast.40, bf16[128,1024]{1,0:T(8,128)(2,1)} %rows_in.1), custom_call_target="tpu_custom_call" | custom-call | flops 75497472 | bytes 1048576 | tf_op jit(solution)/shard_map/route/pallas_call | solution.py:53
  33.1 0.6 collective-permute-done.1
  33.7 1.5 collective-permute-done.3
  35.2 0.1 pad_maximum_fusion.1.refs_0_
  35.3 0.0 copy-start.2
  35.3 0.1 collective-permute-done.7
  35.4 0.1 pad_maximum_fusion.refs_0_.own
  35.5 0.0 all-gather.3.cloned.1.call-update
  35.5 0.1 collective-permute-start.8
  35.6 8.4 %all-to-all-start = ((bf16[32,8,1024]{2,1,0:T(8,128)(2,1)}), bf16[32,8,1024]{2,1,0:T(8,128)(2,1)S(1)}, u32[]{:S(2)}, u32[]{:S(2)}) async-start(bf16[32,8,1024]{2,1,0:T(8,128)(2,1)} %bitcast.20), calls=%async_computation | async-start | bytes 1048576 | tf_op jit(solution)/shard_map/all_to_all | solution.py:352
  44.0 0.3 collective-permute-start.10
  44.3 1.8 %collective-permute-start.9 = (bf16[4,2,40,640]{3,2,1,0:T(8,128)(2,1)S(1)}, bf16[4,2,40,640]{3,2,1,0:T(8,128)(2,1)}, u32[]{:S(2)}, u32[]{:S(2)}) collective-permute-start(bf16[4,2,40,640]{3,2,1,0:T(8,128)(2,1)S(1)} %pad_maximum_fusion.1.refs_0_), channel_id=1, source_target_pairs={{0,16},{16,32},{32,48},{48,0},{1,17},{17,33},{33,49},{49,1},{2,18}... | collective-permute-start | bytes 1228808 | tf_op jit(solution)/shard_map/ppermute | solution.py:308
  46.1 3.3 %collective-permute-start.11 = (bf16[4,2,40,640]{3,2,1,0:T(8,128)(2,1)S(1)}, bf16[4,2,40,640]{3,2,1,0:T(8,128)(2,1)}, u32[]{:S(2)}, u32[]{:S(2)}) collective-permute-start(bf16[4,2,40,640]{3,2,1,0:T(8,128)(2,1)S(1)} %pad_maximum_fusion.1.refs_0_), channel_id=1, source_target_pairs={{0,32},{16,48},{32,0},{48,16},{1,33},{17,49},{33,1},{49,17},{2,34}... | collective-permute-start | bytes 1228808 | tf_op jit(solution)/shard_map/ppermute | solution.py:308
  49.4 0.1 pad_add_fusion.place
  49.5 0.6 proj.1.refs_9_
  50.1 1.0 copy-done
  51.2 9.3 %all-to-all-done = bf16[32,8,1024]{2,1,0:T(8,128)(2,1)S(1)} async-done(((bf16[32,8,1024]{2,1,0:T(8,128)(2,1)}), bf16[32,8,1024]{2,1,0:T(8,128)(2,1)S(1)}, u32[]{:S(2)}, u32[]{:S(2)}) %all-to-all-start) | async-done | bytes 524320 | tf_op jit(solution)/shard_map/all_to_all | solution.py:352
  60.5 3.1 %front.1 = (bf16[4,208,512]{2,1,0:T(8,128)(2,1)S(1)}, f32[192,1]{1,0:T(8,128)S(1)}) custom-call(s32[3]{0:T(128)S(1)} %pad_add_fusion.place, bf16[256,1024]{1,0:T(8,128)(2,1)S(1)} %bitcast.26, bf16[4,2,144,512]{3,2,1,0:T(8,128)(2,1)S(1)} %pad_maximum_fusion.refs_0_.own, bf16[4,2,144,512]{3,2,1,0:T(8,128)(2,1)S(1)} %collective-permute-done.8.refs_1_.other), custom_call_target="tpu_custom_call" | custom-call | flops 268435456 | bytes 2097152 | tf_op jit(solution)/shard_map/front/pallas_call | solution.py:53
  63.6 0.9 copy-done.1
  64.5 3.9 %all-to-all-start.1 = ((bf16[4,208,512]{2,1,0:T(8,128)(2,1)}), bf16[4,208,512]{2,1,0:T(8,128)(2,1)S(1)}, u32[]{:S(2)}, u32[]{:S(2)}) async-start(bf16[4,208,512]{2,1,0:T(8,128)(2,1)} %copy-done.1), calls=%async_computation.1 | async-start | bytes 1703936 | tf_op jit(solution)/shard_map/all_to_all | solution.py:377
  68.4 0.3 collective-permute-start.12
  68.7 1.7 %collective-permute-done.11.refs_2_ = bf16[4,2,40,640]{3,2,1,0:T(8,128)(2,1)} collective-permute-done((bf16[4,2,40,640]{3,2,1,0:T(8,128)(2,1)S(1)}, bf16[4,2,40,640]{3,2,1,0:T(8,128)(2,1)}, u32[]{:S(2)}, u32[]{:S(2)}) %collective-permute-start.11) | collective-permute-done | bytes 409632 | tf_op jit(solution)/shard_map/ppermute | solution.py:308
  70.5 0.5 collective-permute-start.13
  71.0 0.0 collective-permute-start.15
  71.0 0.1 stack.77.place
  71.1 1.4 collective-permute-done.14.refs_6_
  72.4 0.6 collective-permute-done.13.refs_5_
  73.0 0.6 collective-permute-done.15.refs_7_
  73.6 8.4 %all-to-all-done.1.blocks = bf16[4,208,512]{2,1,0:T(8,128)(2,1)S(1)} async-done(((bf16[4,208,512]{2,1,0:T(8,128)(2,1)}), bf16[4,208,512]{2,1,0:T(8,128)(2,1)S(1)}, u32[]{:S(2)}, u32[]{:S(2)}) %all-to-all-start.1) | async-done | bytes 852000 | tf_op jit(solution)/shard_map/all_to_all | solution.py:377
  82.1 15.4 %ffn.1 = (f32[192,1280]{1,0:T(8,128)S(1)}, bf16[192,1280]{1,0:T(8,128)(2,1)S(1)}, bf16[192,1280]{1,0:T(8,128)(2,1)S(1)}, bf16[192,1280]{1,0:T(8,128)(2,1)S(1)}, ...) custom-call(s32[5]{0:T(128)S(1)} %stack.77.place, ...), custom_call_target="tpu_custom_call" | custom-call | flops 8556380160 | bytes 16777216 | tf_op jit(solution)/shard_map/ffn/pallas_call | solution.py:53
  97.5 0.1 collective-permute-start.16
  97.6 3.5 %collective-permute-done.16.arrived = bf16[4,8,40,640]{3,2,1,0:T(8,128)(2,1)S(1)} collective-permute-done((bf16[4,8,40,640]{3,2,1,0:T(8,128)(2,1)S(1)}, bf16[4,8,40,640]{3,2,1,0:T(8,128)(2,1)S(1)}, u32[]{:S(2)}, u32[]{:S(2)}) %collective-permute-start.16) | collective-permute-done | bytes 1638432 | tf_op jit(solution)/shard_map/ppermute | solution.py:308
  101.1 0.4 core_sum.1
  101.5 0.9 collective-permute-start.20
  102.3 5.7 %collective-permute-start.21 = (bf16[8,40,640]{2,1,0:T(8,128)(2,1)S(1)}, bf16[8,40,640]{2,1,0:T(8,128)(2,1)S(1)}, u32[]{:S(2)}, u32[]{:S(2)}) collective-permute-start(bf16[8,40,640]{2,1,0:T(8,128)(2,1)S(1)} %get-tuple-element.58), channel_id=1, source_target_pairs={{0,32},{16,48},{32,0},{48,16},{1,33},{17,49},{33,1},{49,17},{2,34}... | collective-permute-start | bytes 1228808 | tf_op jit(solution)/shard_map/ppermute | solution.py:308
  108.0 1.2 collective-permute-start.17
  109.2 1.5 collective-permute-start.18
  110.6 5.5 %collective-permute-done.20.refs_1_ = bf16[8,40,640]{2,1,0:T(8,128)(2,1)S(1)} collective-permute-done((bf16[8,40,640]{2,1,0:T(8,128)(2,1)S(1)}, bf16[8,40,640]{2,1,0:T(8,128)(2,1)S(1)}, u32[]{:S(2)}, u32[]{:S(2)}) %collective-permute-start.20) | collective-permute-done | bytes 409632 | tf_op jit(solution)/shard_map/ppermute | solution.py:308
  116.2 0.6 collective-permute-start.19
  116.7 1.6 %collective-permute-done.21.refs_2_ = bf16[8,40,640]{2,1,0:T(8,128)(2,1)S(1)} collective-permute-done((bf16[8,40,640]{2,1,0:T(8,128)(2,1)S(1)}, bf16[8,40,640]{2,1,0:T(8,128)(2,1)S(1)}, u32[]{:S(2)}, u32[]{:S(2)}) %collective-permute-start.21) | collective-permute-done | bytes 409632 | tf_op jit(solution)/shard_map/ppermute | solution.py:308
  118.3 7.9 %collective-permute-done.22.refs_3_ = bf16[8,40,640]{2,1,0:T(8,128)(2,1)S(1)} collective-permute-done((bf16[8,40,640]{2,1,0:T(8,128)(2,1)S(1)}, bf16[8,40,640]{2,1,0:T(8,128)(2,1)S(1)}, u32[]{:S(2)}, u32[]{:S(2)}) %collective-permute-start.22) | collective-permute-done | bytes 409632 | tf_op jit(solution)/shard_map/ppermute | solution.py:308
  126.3 0.2 x_sum.1
  126.5 4.1 %collective-permute-start.23 = (bf16[4,40,640]{2,1,0:T(8,128)(2,1)S(1)}, bf16[4,40,640]{2,1,0:T(8,128)(2,1)S(1)}, u32[]{:S(2)}, u32[]{:S(2)}) collective-permute-start(bf16[4,40,640]{2,1,0:T(8,128)(2,1)S(1)} %get-tuple-element.61), channel_id=1, source_target_pairs={{0,1},{1,0},{2,3},{3,2},{4,5},{5,4},{6,7},{7,6},{8,9},{9,8},{10,11... | collective-permute-start | bytes 614408 | tf_op jit(solution)/shard_map/ppermute | solution.py:308
  130.6 0.1 convert_reduce_fusion
  130.7 5.2 %collective-permute-done.23.arrived = bf16[4,40,640]{2,1,0:T(8,128)(2,1)S(1)} collective-permute-done((bf16[4,40,640]{2,1,0:T(8,128)(2,1)S(1)}, bf16[4,40,640]{2,1,0:T(8,128)(2,1)S(1)}, u32[]{:S(2)}, u32[]{:S(2)}) %collective-permute-start.23) | collective-permute-done | bytes 204832 | tf_op jit(solution)/shard_map/ppermute | solution.py:308
  135.8 0.1 z_sum.1
  135.9 0.1 collective-permute-start.24
  136.0 3.4 %collective-permute-start.25 = (bf16[40,640]{1,0:T(8,128)(2,1)S(1)}, bf16[40,640]{1,0:T(8,128)(2,1)S(1)}, u32[]{:S(2)}, u32[]{:S(2)}) collective-permute-start(bf16[40,640]{1,0:T(8,128)(2,1)S(1)} %get-tuple-element.64), channel_id=1, source_target_pairs={{0,128},{64,192},{128,0},{192,64},{1,129},{65,193},{129,1},{193,65... | collective-permute-start | bytes 153608 | tf_op jit(solution)/shard_map/ppermute | solution.py:308
  139.4 2.9 %collective-permute-start.26 = (bf16[40,640]{1,0:T(8,128)(2,1)S(1)}, bf16[40,640]{1,0:T(8,128)(2,1)S(1)}, u32[]{:S(2)}, u32[]{:S(2)}) collective-permute-start(bf16[40,640]{1,0:T(8,128)(2,1)S(1)} %get-tuple-element.65), channel_id=1, source_target_pairs={{0,192},{64,0},{128,64},{192,128},{1,193},{65,1},{129,65},{193,129... | collective-permute-start | bytes 153608 | tf_op jit(solution)/shard_map/ppermute | solution.py:308
  142.4 1.1 multiply_convert_fusion
  143.4 0.7 collective-permute-done.25.refs_2_
  144.1 2.1 %collective-permute-done.26.refs_3_ = bf16[40,640]{1,0:T(8,128)(2,1)S(1)} collective-permute-done((bf16[40,640]{1,0:T(8,128)(2,1)S(1)}, bf16[40,640]{1,0:T(8,128)(2,1)S(1)}, u32[]{:S(2)}, u32[]{:S(2)}) %collective-permute-start.26) | collective-permute-done | bytes 51232 | tf_op jit(solution)/shard_map/ppermute | solution.py:308
  146.2 0.7 last.1
  (28 shorter events, 0.1 us)
Async XLA Ops:
  7.2 74.9 %all-gather.3.cloned.1.call-start = ((), (), s32[]{:S(2)}) async-start(), calls=%async_computation.2 | async-start | bytes 2457600 | tf_op jit(solution)/shard_map/all_gather | solution.py:349
  8.2 4.3 %collective-permute-start = (bf16[40,640]{1,0:T(8,128)(2,1)S(1)}, bf16[40,640]{1,0:T(8,128)(2,1)S(1)}, u32[]{:S(2)}, u32[]{:S(2)}) collective-permute-start(bf16[40,640]{1,0:T(8,128)(2,1)S(1)} %get-tuple-element.34), channel_id=1, source_target_pairs={{0,1},{1,0},{2,3},{3,2},{4,5},{5,4},{6,7},{7,6},{8,9},{9,8},{10,11... | collective-permute-start | bytes 153608 | tf_op jit(solution)/shard_map/ppermute | solution.py:308
  10.2 10.0 %collective-permute-start.4 = (bf16[144,512]{1,0:T(8,128)(2,1)S(1)}, bf16[144,512]{1,0:T(8,128)(2,1)S(1)}, u32[]{:S(2)}, u32[]{:S(2)}) collective-permute-start(bf16[144,512]{1,0:T(8,128)(2,1)S(1)} %get-tuple-element.35), channel_id=1, source_target_pairs={{0,1},{1,0},{2,3},{3,2},{4,5},{5,4},{6,7},{7,6},{8,9},{9,8},{10,11... | collective-permute-start | bytes 442376 | tf_op jit(solution)/shard_map/ppermute | solution.py:308
  12.6 15.7 %collective-permute-start.2 = (bf16[2,40,640]{2,1,0:T(8,128)(2,1)S(1)}, bf16[2,40,640]{2,1,0:T(8,128)(2,1)S(1)}, u32[]{:S(2)}, u32[]{:S(2)}) collective-permute-start(bf16[2,40,640]{2,1,0:T(8,128)(2,1)S(1)} %get-tuple-element.69), channel_id=1, source_target_pairs={{0,128},{64,192},{128,0},{192,64},{1,129},{65,193},{129,1},{193,65... | collective-permute-start | bytes 307208 | tf_op jit(solution)/shard_map/ppermute | solution.py:308
  20.2 15.0 %collective-permute-start.6 = (bf16[2,144,512]{2,1,0:T(8,128)(2,1)S(1)}, bf16[2,144,512]{2,1,0:T(8,128)(2,1)S(1)}, u32[]{:S(2)}, u32[]{:S(2)}) collective-permute-start(bf16[2,144,512]{2,1,0:T(8,128)(2,1)S(1)} %get-tuple-element.67), channel_id=1, source_target_pairs={{0,4},{2,6},{4,0},{6,2},{1,5},{3,7},{5,1},{7,3},{8,12},{10,14},{12... | collective-permute-start | bytes 884744 | tf_op jit(solution)/shard_map/ppermute | solution.py:308
  23.5 11.8 %collective-permute-start.5 = (bf16[2,144,512]{2,1,0:T(8,128)(2,1)S(1)}, bf16[2,144,512]{2,1,0:T(8,128)(2,1)S(1)}, u32[]{:S(2)}, u32[]{:S(2)}) collective-permute-start(bf16[2,144,512]{2,1,0:T(8,128)(2,1)S(1)} %get-tuple-element.67), channel_id=1, source_target_pairs={{0,2},{2,4},{4,6},{6,0},{1,3},{3,5},{5,7},{7,1},{8,10},{10,12},{12... | collective-permute-start | bytes 884744 | tf_op jit(solution)/shard_map/ppermute | solution.py:308
  24.2 11.2 %collective-permute-start.7 = (bf16[2,144,512]{2,1,0:T(8,128)(2,1)S(1)}, bf16[2,144,512]{2,1,0:T(8,128)(2,1)S(1)}, u32[]{:S(2)}, u32[]{:S(2)}) collective-permute-start(bf16[2,144,512]{2,1,0:T(8,128)(2,1)S(1)} %get-tuple-element.67), channel_id=1, source_target_pairs={{0,6},{2,0},{4,2},{6,4},{1,7},{3,1},{5,3},{7,5},{8,14},{10,8},{12,... | collective-permute-start | bytes 884744 | tf_op jit(solution)/shard_map/ppermute | solution.py:308
  26.8 6.9 %collective-permute-start.1 = (bf16[2,40,640]{2,1,0:T(8,128)(2,1)S(1)}, bf16[2,40,640]{2,1,0:T(8,128)(2,1)S(1)}, u32[]{:S(2)}, u32[]{:S(2)}) collective-permute-start(bf16[2,40,640]{2,1,0:T(8,128)(2,1)S(1)} %get-tuple-element.69), channel_id=1, source_target_pairs={{0,64},{64,128},{128,192},{192,0},{1,65},{65,129},{129,193},{193,1... | collective-permute-start | bytes 307208 | tf_op jit(solution)/shard_map/ppermute | solution.py:308
  28.2 7.0 %collective-permute-start.3 = (bf16[2,40,640]{2,1,0:T(8,128)(2,1)S(1)}, bf16[2,40,640]{2,1,0:T(8,128)(2,1)S(1)}, u32[]{:S(2)}, u32[]{:S(2)}) collective-permute-start(bf16[2,40,640]{2,1,0:T(8,128)(2,1)S(1)} %get-tuple-element.69), channel_id=1, source_target_pairs={{0,192},{64,0},{128,64},{192,128},{1,193},{65,1},{129,65},{193,129... | collective-permute-start | bytes 307208 | tf_op jit(solution)/shard_map/ppermute | solution.py:308
  35.3 33.2 %copy-start.2 = (bf16[4,2,40,640]{3,2,1,0:T(8,128)(2,1)}, bf16[4,2,40,640]{3,2,1,0:T(8,128)(2,1)S(1)}, u32[]{:S(2)}) copy-start(bf16[4,2,40,640]{3,2,1,0:T(8,128)(2,1)S(1)} %pad_maximum_fusion.1.refs_0_) | copy-start | bytes 1228804
  35.5 14.0 %collective-permute-start.8 = (bf16[4,2,144,512]{3,2,1,0:T(8,128)(2,1)S(1)}, bf16[4,2,144,512]{3,2,1,0:T(8,128)(2,1)S(1)}, u32[]{:S(2)}, u32[]{:S(2)}) collective-permute-start(bf16[4,2,144,512]{3,2,1,0:T(8,128)(2,1)S(1)} %pad_maximum_fusion.refs_0_.own), channel_id=1, source_target_pairs={{0,8},{8,0},{1,9},{9,1},{2,10},{10,2},{3,11},{11,3},{4,12},{12,4},... | collective-permute-start | bytes 3538952 | tf_op jit(solution)/shard_map/ppermute | solution.py:308
  35.6 24.9 %all-to-all-start = ((bf16[32,8,1024]{2,1,0:T(8,128)(2,1)}), bf16[32,8,1024]{2,1,0:T(8,128)(2,1)S(1)}, u32[]{:S(2)}, u32[]{:S(2)}) async-start(bf16[32,8,1024]{2,1,0:T(8,128)(2,1)} %bitcast.20), calls=%async_computation | async-start | bytes 1048576 | tf_op jit(solution)/shard_map/all_to_all | solution.py:352
  44.0 20.5 %collective-permute-start.10 = (bf16[4,2,40,640]{3,2,1,0:T(8,128)(2,1)S(1)}, bf16[4,2,40,640]{3,2,1,0:T(8,128)(2,1)}, u32[]{:S(2)}, u32[]{:S(2)}) collective-permute-start(bf16[4,2,40,640]{3,2,1,0:T(8,128)(2,1)S(1)} %pad_maximum_fusion.1.refs_0_), channel_id=1, source_target_pairs={{0,48},{16,0},{32,16},{48,32},{1,49},{17,1},{33,17},{49,33},{2,50}... | collective-permute-start | bytes 1228808 | tf_op jit(solution)/shard_map/ppermute | solution.py:308
  44.3 20.2 %collective-permute-start.9 = (bf16[4,2,40,640]{3,2,1,0:T(8,128)(2,1)S(1)}, bf16[4,2,40,640]{3,2,1,0:T(8,128)(2,1)}, u32[]{:S(2)}, u32[]{:S(2)}) collective-permute-start(bf16[4,2,40,640]{3,2,1,0:T(8,128)(2,1)S(1)} %pad_maximum_fusion.1.refs_0_), channel_id=1, source_target_pairs={{0,16},{16,32},{32,48},{48,0},{1,17},{17,33},{33,49},{49,1},{2,18}... | collective-permute-start | bytes 1228808 | tf_op jit(solution)/shard_map/ppermute | solution.py:308
  46.1 24.3 %collective-permute-start.11 = (bf16[4,2,40,640]{3,2,1,0:T(8,128)(2,1)S(1)}, bf16[4,2,40,640]{3,2,1,0:T(8,128)(2,1)}, u32[]{:S(2)}, u32[]{:S(2)}) collective-permute-start(bf16[4,2,40,640]{3,2,1,0:T(8,128)(2,1)S(1)} %pad_maximum_fusion.1.refs_0_), channel_id=1, source_target_pairs={{0,32},{16,48},{32,0},{48,16},{1,33},{17,49},{33,1},{49,17},{2,34}... | collective-permute-start | bytes 1228808 | tf_op jit(solution)/shard_map/ppermute | solution.py:308
  50.1 1.1 copy-start
  63.6 0.9 copy-start.1
  64.5 17.5 %all-to-all-start.1 = ((bf16[4,208,512]{2,1,0:T(8,128)(2,1)}), bf16[4,208,512]{2,1,0:T(8,128)(2,1)S(1)}, u32[]{:S(2)}, u32[]{:S(2)}) async-start(bf16[4,208,512]{2,1,0:T(8,128)(2,1)} %copy-done.1), calls=%async_computation.1 | async-start | bytes 1703936 | tf_op jit(solution)/shard_map/all_to_all | solution.py:377
  68.4 2.6 %collective-permute-start.12 = (bf16[4,2,40,640]{3,2,1,0:T(8,128)(2,1)S(1)}, bf16[4,2,40,640]{3,2,1,0:T(8,128)(2,1)S(1)}, u32[]{:S(2)}, u32[]{:S(2)}) collective-permute-start(bf16[4,2,40,640]{3,2,1,0:T(8,128)(2,1)S(1)} %pad_maximum_fusion.1.refs_0_), channel_id=1, source_target_pairs={{0,8},{8,0},{1,9},{9,1},{2,10},{10,2},{3,11},{11,3},{4,12},{12,4},... | collective-permute-start | bytes 1228808 | tf_op jit(solution)/shard_map/ppermute | solution.py:308
  70.5 2.0 %collective-permute-start.14 = (bf16[4,2,40,640]{3,2,1,0:T(8,128)(2,1)}, bf16[4,2,40,640]{3,2,1,0:T(8,128)(2,1)S(1)}, u32[]{:S(2)}, u32[]{:S(2)}) collective-permute-start(bf16[4,2,40,640]{3,2,1,0:T(8,128)(2,1)} %collective-permute-done.11.refs_2_), channel_id=1, source_target_pairs={{0,8},{8,0},{1,9},{9,1},{2,10},{10,2},{3,11},{11,3},{4,12},{12,4},... | collective-permute-start | bytes 1228808 | tf_op jit(solution)/shard_map/ppermute | solution.py:308
  70.5 2.5 %collective-permute-start.13 = (bf16[4,2,40,640]{3,2,1,0:T(8,128)(2,1)}, bf16[4,2,40,640]{3,2,1,0:T(8,128)(2,1)S(1)}, u32[]{:S(2)}, u32[]{:S(2)}) collective-permute-start(bf16[4,2,40,640]{3,2,1,0:T(8,128)(2,1)} %collective-permute-done.9.refs_1_), channel_id=1, source_target_pairs={{0,8},{8,0},{1,9},{9,1},{2,10},{10,2},{3,11},{11,3},{4,12},{12,4},... | collective-permute-start | bytes 1228808 | tf_op jit(solution)/shard_map/ppermute | solution.py:308
  71.0 2.6 %collective-permute-start.15 = (bf16[4,2,40,640]{3,2,1,0:T(8,128)(2,1)}, bf16[4,2,40,640]{3,2,1,0:T(8,128)(2,1)S(1)}, u32[]{:S(2)}, u32[]{:S(2)}) collective-permute-start(bf16[4,2,40,640]{3,2,1,0:T(8,128)(2,1)} %collective-permute-done.10.refs_3_), channel_id=1, source_target_pairs={{0,8},{8,0},{1,9},{9,1},{2,10},{10,2},{3,11},{11,3},{4,12},{12,4},... | collective-permute-start | bytes 1228808 | tf_op jit(solution)/shard_map/ppermute | solution.py:308
  71.1 11.0 %copy-start.3 = (bf16[4,2,40,640]{3,2,1,0:T(8,128)(2,1)}, bf16[4,2,40,640]{3,2,1,0:T(8,128)(2,1)S(1)}, u32[]{:S(2)}) copy-start(bf16[4,2,40,640]{3,2,1,0:T(8,128)(2,1)S(1)} %collective-permute-done.12.refs_4_) | copy-start | bytes 1228804
  72.4 9.6 %copy-start.4 = (bf16[4,2,40,640]{3,2,1,0:T(8,128)(2,1)}, bf16[4,2,40,640]{3,2,1,0:T(8,128)(2,1)S(1)}, u32[]{:S(2)}) copy-start(bf16[4,2,40,640]{3,2,1,0:T(8,128)(2,1)S(1)} %collective-permute-done.14.refs_6_) | copy-start | bytes 1228804
  73.0 9.0 %copy-start.5 = (bf16[4,2,40,640]{3,2,1,0:T(8,128)(2,1)}, bf16[4,2,40,640]{3,2,1,0:T(8,128)(2,1)S(1)}, u32[]{:S(2)}) copy-start(bf16[4,2,40,640]{3,2,1,0:T(8,128)(2,1)S(1)} %collective-permute-done.13.refs_5_) | copy-start | bytes 1228804
  73.6 8.4 %copy-start.6 = (bf16[4,2,40,640]{3,2,1,0:T(8,128)(2,1)}, bf16[4,2,40,640]{3,2,1,0:T(8,128)(2,1)S(1)}, u32[]{:S(2)}) copy-start(bf16[4,2,40,640]{3,2,1,0:T(8,128)(2,1)S(1)} %collective-permute-done.15.refs_7_) | copy-start | bytes 1228804
  97.5 3.6 %collective-permute-start.16 = (bf16[4,8,40,640]{3,2,1,0:T(8,128)(2,1)S(1)}, bf16[4,8,40,640]{3,2,1,0:T(8,128)(2,1)S(1)}, u32[]{:S(2)}, u32[]{:S(2)}) collective-permute-start(bf16[4,8,40,640]{3,2,1,0:T(8,128)(2,1)S(1)} %get-tuple-element.51), channel_id=1, source_target_pairs={{0,8},{8,0},{1,9},{9,1},{2,10},{10,2},{3,11},{11,3},{4,12},{12,4},... | collective-permute-start | bytes 4915208 | tf_op jit(solution)/shard_map/ppermute | solution.py:308
  101.5 14.7 %collective-permute-start.20 = (bf16[8,40,640]{2,1,0:T(8,128)(2,1)S(1)}, bf16[8,40,640]{2,1,0:T(8,128)(2,1)S(1)}, u32[]{:S(2)}, u32[]{:S(2)}) collective-permute-start(bf16[8,40,640]{2,1,0:T(8,128)(2,1)S(1)} %get-tuple-element.57), channel_id=1, source_target_pairs={{0,16},{16,32},{32,48},{48,0},{1,17},{17,33},{33,49},{49,1},{2,18}... | collective-permute-start | bytes 1228808 | tf_op jit(solution)/shard_map/ppermute | solution.py:308
  102.3 16.0 %collective-permute-start.21 = (bf16[8,40,640]{2,1,0:T(8,128)(2,1)S(1)}, bf16[8,40,640]{2,1,0:T(8,128)(2,1)S(1)}, u32[]{:S(2)}, u32[]{:S(2)}) collective-permute-start(bf16[8,40,640]{2,1,0:T(8,128)(2,1)S(1)} %get-tuple-element.58), channel_id=1, source_target_pairs={{0,32},{16,48},{32,0},{48,16},{1,33},{17,49},{33,1},{49,17},{2,34}... | collective-permute-start | bytes 1228808 | tf_op jit(solution)/shard_map/ppermute | solution.py:308
  108.0 18.3 %collective-permute-start.22 = (bf16[8,40,640]{2,1,0:T(8,128)(2,1)S(1)}, bf16[8,40,640]{2,1,0:T(8,128)(2,1)S(1)}, u32[]{:S(2)}, u32[]{:S(2)}) collective-permute-start(bf16[8,40,640]{2,1,0:T(8,128)(2,1)S(1)} %get-tuple-element.59), channel_id=1, source_target_pairs={{0,48},{16,0},{32,16},{48,32},{1,49},{17,1},{33,17},{49,33},{2,50}... | collective-permute-start | bytes 1228808 | tf_op jit(solution)/shard_map/ppermute | solution.py:308
  108.0 31.4 %collective-permute-start.17 = (bf16[192,1280]{1,0:T(8,128)(2,1)S(1)}, bf16[192,1280]{1,0:T(8,128)(2,1)S(1)}, u32[]{:S(2)}, u32[]{:S(2)}) collective-permute-start(bf16[192,1280]{1,0:T(8,128)(2,1)S(1)} %get-tuple-element.53), channel_id=1, source_target_pairs={{0,6},{2,0},{4,2},{6,4},{1,7},{3,1},{5,3},{7,5},{8,14},{10,8},{12,... | collective-permute-start | bytes 1474568 | tf_op jit(solution)/shard_map/ppermute | solution.py:308
  109.2 33.2 %collective-permute-start.18 = (bf16[192,1280]{1,0:T(8,128)(2,1)S(1)}, bf16[192,1280]{1,0:T(8,128)(2,1)S(1)}, u32[]{:S(2)}, u32[]{:S(2)}) collective-permute-start(bf16[192,1280]{1,0:T(8,128)(2,1)S(1)} %get-tuple-element.54), channel_id=1, source_target_pairs={{0,4},{2,6},{4,0},{6,2},{1,5},{3,7},{5,1},{7,3},{8,12},{10,14},{12... | collective-permute-start | bytes 1474568 | tf_op jit(solution)/shard_map/ppermute | solution.py:308
  116.2 26.2 %collective-permute-start.19 = (bf16[192,1280]{1,0:T(8,128)(2,1)S(1)}, bf16[192,1280]{1,0:T(8,128)(2,1)S(1)}, u32[]{:S(2)}, u32[]{:S(2)}) collective-permute-start(bf16[192,1280]{1,0:T(8,128)(2,1)S(1)} %get-tuple-element.55), channel_id=1, source_target_pairs={{0,2},{2,4},{4,6},{6,0},{1,3},{3,5},{5,7},{7,1},{8,10},{10,12},{12... | collective-permute-start | bytes 1474568 | tf_op jit(solution)/shard_map/ppermute | solution.py:308
  126.5 9.4 %collective-permute-start.23 = (bf16[4,40,640]{2,1,0:T(8,128)(2,1)S(1)}, bf16[4,40,640]{2,1,0:T(8,128)(2,1)S(1)}, u32[]{:S(2)}, u32[]{:S(2)}) collective-permute-start(bf16[4,40,640]{2,1,0:T(8,128)(2,1)S(1)} %get-tuple-element.61), channel_id=1, source_target_pairs={{0,1},{1,0},{2,3},{3,2},{4,5},{5,4},{6,7},{7,6},{8,9},{9,8},{10,11... | collective-permute-start | bytes 614408 | tf_op jit(solution)/shard_map/ppermute | solution.py:308
  135.9 7.5 %collective-permute-start.24 = (bf16[40,640]{1,0:T(8,128)(2,1)S(1)}, bf16[40,640]{1,0:T(8,128)(2,1)S(1)}, u32[]{:S(2)}, u32[]{:S(2)}) collective-permute-start(bf16[40,640]{1,0:T(8,128)(2,1)S(1)} %get-tuple-element.63), channel_id=1, source_target_pairs={{0,64},{64,128},{128,192},{192,0},{1,65},{65,129},{129,193},{193,1... | collective-permute-start | bytes 153608 | tf_op jit(solution)/shard_map/ppermute | solution.py:308
  136.0 8.1 %collective-permute-start.25 = (bf16[40,640]{1,0:T(8,128)(2,1)S(1)}, bf16[40,640]{1,0:T(8,128)(2,1)S(1)}, u32[]{:S(2)}, u32[]{:S(2)}) collective-permute-start(bf16[40,640]{1,0:T(8,128)(2,1)S(1)} %get-tuple-element.64), channel_id=1, source_target_pairs={{0,128},{64,192},{128,0},{192,64},{1,129},{65,193},{129,1},{193,65... | collective-permute-start | bytes 153608 | tf_op jit(solution)/shard_map/ppermute | solution.py:308
  139.4 6.8 %collective-permute-start.26 = (bf16[40,640]{1,0:T(8,128)(2,1)S(1)}, bf16[40,640]{1,0:T(8,128)(2,1)S(1)}, u32[]{:S(2)}, u32[]{:S(2)}) collective-permute-start(bf16[40,640]{1,0:T(8,128)(2,1)S(1)} %get-tuple-element.65), channel_id=1, source_target_pairs={{0,192},{64,0},{128,64},{192,128},{1,193},{65,1},{129,65},{193,129... | collective-permute-start | bytes 153608 | tf_op jit(solution)/shard_map/ppermute | solution.py:308
Sparse Core Ops, SparseCore 0:
  35.7 31.0 all-gather.2
